TPU v7x, 32 devices: a whole 2x2x4 slice. The times are simulated.
32 devices in a mesh: grp: 2 (over y), aux: 4 (over x, core), occ: 4 (over z).
Axes of the slice: x: 2, y: 2, z: 4, core: 2. Of those that a mesh axis runs over, the one named last changes fastest.
Arguments:
- integrals: bfloat16 [256, 4, 16, 128, 128], P(('grp', 'aux', 'occ')), parts along dimension 0, may hold values from -6 to 6
- pair_list: int32 [256, 4], P(('grp', 'aux', 'occ')), parts along dimension 0, may hold values from 0 to 3, as said below
- pair_count: int32 [256], P(('grp', 'aux', 'occ')), parts along dimension 0, may hold values from 1 to 4, as said below
- coefficients: bfloat16 [512, 384], P('grp'), parts along dimension 0, may hold values from -1 to 1
- metric: bfloat16 [4096, 2048], P(('grp', 'aux', 'occ')), parts along dimension 0, as said below
Outputs:
- exchange: float32 [512, 256], P(('grp', 'aux', 'occ')), parts along dimension 0
There are 2 independent parts, one for each index of `grp`. A program takes and returns all parts, laid end to end along the dimension named above; each array names one. Nothing has to cross between parts.
Inputs may be any that keep to these rules, and one draw needn't show every extreme that they name: `pair_list`: each row names 4 distinct block pairs; only the first pair_count entries of a row are used. `pair_count`: some screening block uses all 4 slots. `metric`: zero above the diagonal; diagonal entries between 0.5 and 2.
All inputs are finite; a program needn't handle non-finite values.
Results may differ from a plain program's by a relative error of at most 0.0003.
Values may be sent and summed in bfloat16 or wider, within the bound.
No kernel may reach another device: no remote copies, remote signals or barrier semaphores. Data moves between devices by JAX's collectives and lax.ppermute only.
A program may use at most 256 MiB of HBM per device.

v0:
```python
import jax
import jax.numpy as jnp
from jax import lax
from jax.sharding import PartitionSpec as P


def block_half(ints_block, list_block, count_block, coefficients, blocks_per_side):
    slots = ints_block.shape[0]
    aux_width = ints_block.shape[1]
    size_block = ints_block.shape[2]
    basis_total, orbitals = coefficients.shape
    row_blocks = list_block // blocks_per_side
    col_blocks = list_block % blocks_per_side
    coef_table = coefficients.reshape(blocks_per_side, size_block, orbitals)
    coef_slots = coef_table[col_blocks]
    contrib = jnp.einsum(
        "spxn,sni->spix", ints_block, coef_slots, preferred_element_type=jnp.float32
    )
    used = jnp.arange(slots) < count_block
    placing = jnp.logical_and(
        row_blocks[:, None] == jnp.arange(blocks_per_side)[None, :], used[:, None]
    ).astype(jnp.float32)
    totals = jnp.einsum("sm,spix->pimx", placing, contrib, precision=lax.Precision.HIGHEST)
    return totals.reshape(aux_width, orbitals, basis_total)


def fitting(factor, columns):
    step_rows = factor.shape[0] // 8
    pieces = []
    for block_number in range(8):
        upper_end = (block_number + 1) * step_rows
        product = jnp.dot(
            factor[block_number * step_rows : upper_end, :upper_end],
            columns[:upper_end],
            preferred_element_type=jnp.float32,
        )
        pieces.append(product.astype(jnp.bfloat16))
    return jnp.concatenate(pieces, axis=0)


def per_device(integrals, pair_list, pair_count, coefficients, metric):
    basis_total, orbitals = coefficients.shape
    size_block = integrals.shape[3]
    blocks_per_side = basis_total // size_block
    aux_total = metric.shape[1]
    aux_devices = lax.axis_size("aux")
    occ_devices = lax.axis_size("occ")

    def transform(operands):
        return block_half(
            operands[0], operands[1], operands[2], coefficients, blocks_per_side
        ).astype(jnp.bfloat16)

    halves = lax.map(transform, (integrals, pair_list, pair_count))
    halves = halves.reshape(1, -1, orbitals, basis_total)
    gathered = lax.all_gather(metric, ("aux", "occ"), axis=0, tiled=True)
    arrived = lax.all_to_all(
        lax.all_to_all(halves, "aux", split_axis=3, concat_axis=0, tiled=True),
        "occ",
        split_axis=2,
        concat_axis=1,
        tiled=True,
    )
    fitted = fitting(gathered, arrived.reshape(aux_total, -1))
    fitted = fitted.reshape(aux_total, orbitals // occ_devices, basis_total // aux_devices)
    owned_rows = lax.all_to_all(fitted, "aux", split_axis=0, concat_axis=2, tiled=True)
    flattened = owned_rows.reshape(-1, basis_total)
    partial_value = lax.dot_general(
        flattened, flattened, (((0,), (0,)), ((), ())), preferred_element_type=jnp.float32
    )
    return lax.psum_scatter(partial_value, ("aux", "occ"), scatter_dimension=0, tiled=True)


def solution(mesh):
    in_specs = (
        P(("grp", "aux", "occ"), None, None, None, None),
        P(("grp", "aux", "occ"), None),
        P(("grp", "aux", "occ")),
        P("grp", None),
        P(("grp", "aux", "occ"), None),
    )
    out_specs = P(("grp", "aux", "occ"), None)
    return jax.shard_map(
        per_device, mesh=mesh, in_specs=in_specs, out_specs=out_specs, check_vma=False
    )
```

profile of v0, /device:TPU:0, one launch (start us, length us, event | category | flops | bytes accessed | tf_op | source)
XLA Modules:
  0.0 2104.8 jit_solution(13473715750538975504)
XLA Ops:
  7.3 249.4 %while.12 = (s32[]{:T(128)}, bf16[8,16,384,256]{2,1,0,3:T(8,128)(2,1)}, bf16[256,384]{1,0:T(8,128)(2,1)}, s32[8,4]{1,0:T(8,128)S(1)}, bf16[8,4,16,128,128]{4,3,2,1,0:T(8,128)(2,1)}, /*index=5*/s32[8]{0:T(128)}, s32[]{:T(128)}) while((s32[]{:T(128)}, bf16[8,16,384,256]{2,1,0,3:T(8,128)(2,1)}, bf16[256,384]{1,0:T(8,128)(2,1)}, ...), condition=%wide.region_1.2_spmd, body=%wide.region_0.1_spmd.sunk | while | flops 882377856 | bytes 44175596 | solution.py:54
  10.7 3.4 convolution_bitcast_fusion.2
  14.1 16.4 fusion.91
  30.5 4.0 copy.86
  34.5 3.9 constant_dynamic-update-slice_fusion.2
  41.8 3.4 convolution_bitcast_fusion.2
  45.2 16.4 fusion.91
  61.6 4.0 copy.86
  65.6 3.9 constant_dynamic-update-slice_fusion.2
  73.0 3.4 convolution_bitcast_fusion.2
  76.4 16.4 fusion.91
  92.8 4.0 copy.86
  96.8 4.0 constant_dynamic-update-slice_fusion.2
  104.2 3.4 convolution_bitcast_fusion.2
  107.6 16.4 fusion.91
  124.0 4.0 copy.86
  128.0 4.0 constant_dynamic-update-slice_fusion.2
  135.4 3.4 convolution_bitcast_fusion.2
  138.8 16.4 fusion.91
  155.2 4.0 copy.86
  159.2 4.0 constant_dynamic-update-slice_fusion.2
  166.5 3.4 convolution_bitcast_fusion.2
  170.0 16.4 fusion.91
  186.4 4.0 copy.86
  190.4 4.0 constant_dynamic-update-slice_fusion.2
  197.8 3.4 convolution_bitcast_fusion.2
  201.2 16.4 fusion.91
  217.6 4.0 copy.86
  221.6 3.9 constant_dynamic-update-slice_fusion.2
  228.9 3.4 convolution_bitcast_fusion.2
  232.4 16.4 fusion.91
  248.8 4.0 copy.86
  252.8 4.0 constant_dynamic-update-slice_fusion.2
  256.7 288.2 %all_to_all.48 = bf16[1,128,384,256]{2,1,0,3:T(8,128)(2,1)} all-to-all(bf16[1,128,384,256]{2,1,0,3:T(8,128)(2,1)} %bitcast.130), channel_id=1, replica_groups=mesh['grp'=2,'aux'=4,'occ'=4] {'aux'}, dimensions={3} | all-to-all | bytes 50331648 | tf_op jit(solution)/shard_map/all_to_all | solution.py:58
  544.9 32.1 %copy.52 = bf16[4,128,384,64]{1,3,0,2:T(8,128)(2,1)} copy(bf16[4,128,384,64]{2,1,3,0:T(8,128)(2,1)} %bitcast.128) | data formatting | bytes 50331648 | tf_op jit(solution)/shard_map/all_to_all | solution.py:58
  577.0 8.4 all-to-all-start.1
  586.4 592.9 %all-to-all-done.1 = bf16[4,128,384,64]{1,3,0,2:T(8,128)(2,1)} async-done(((bf16[4,128,384,64]{1,3,0,2:T(8,128)(2,1)}), bf16[4,128,384,64]{1,3,0,2:T(8,128)(2,1)}, u32[]{:S(2)}, u32[]{:S(2)}) %all-to-all-start.1) | async-done | bytes 25165856 | tf_op jit(solution)/shard_map/all_to_all | solution.py:57
  1179.3 20.7 copy.53
  1200.0 6.9 slice.76
  1206.9 12.0 slice.80
  1218.9 4.5 copy-done
  1223.4 8.7 slice.84
  1232.1 28.9 %copy.54 = bf16[4,4,128,96,64]{2,1,0,4,3:T(4,128)(2,1)} copy(bf16[4,4,128,96,64]{2,4,0,3,1:T(8,128)(2,1)} %bitcast.18) | data formatting | bytes 50331648 | tf_op jit(solution)/shard_map/all_to_all | solution.py:57
  1261.0 41.0 %reshape.135 = bf16[2048,6144]{0,1:T(8,128)(2,1)} reshape(bf16[4,4,128,96,64]{2,1,0,4,3:T(4,128)(2,1)} %copy.54) | data formatting | bytes 50331648 | tf_op jit(solution)/shard_map/reshape | solution.py:64
  1302.0 18.4 copy.55
  1320.4 22.3 %copy.57 = bf16[3,4,128,96,64]{2,1,0,4,3:T(4,128)(2,1)} copy(bf16[3,4,128,96,64]{2,4,3,1,0:T(8,128)(2,1)} %slice.84) | data formatting | bytes 37748736 | tf_op jit(solution)/shard_map/slice | solution.py:34
  1342.7 30.9 %slice.67 = bf16[1536,6144]{0,1:T(8,128)(2,1)} reshape(bf16[3,4,128,96,64]{2,1,0,4,3:T(4,128)(2,1)} %copy.57) | data formatting | bytes 37748736 | tf_op jit(solution)/shard_map/slice | solution.py:34
  1373.6 15.6 copy.56
  1389.2 20.8 slice.62
  1410.0 4.8 fusion.48
  1414.8 6.5 fusion.50
  1421.3 8.1 fusion.38
  1429.5 5.0 fusion.46
  1434.5 11.4 fusion.54
  1445.8 19.8 fusion.42
  1465.7 11.5 fusion.60
  1477.2 12.8 fusion.44
  1489.9 33.0 %copy.58 = bf16[2048,6144]{0,1:T(8,128)(2,1)} copy(bf16[2048,6144]{1,0:T(8,128)(2,1)} %fusion.44) | data formatting | bytes 50331648 | tf_op jit(solution)/shard_map/concatenate | solution.py:38
  1522.9 47.5 %copy.59 = bf16[2048,96,64]{1,2,0:T(8,128)(2,1)} copy(bf16[2048,96,64]{0,2,1:T(8,128)(2,1)} %bitcast.129) | data formatting | bytes 50331648 | tf_op jit(solution)/shard_map/reshape | solution.py:65
  1570.5 381.0 %all_to_all.49 = bf16[2048,96,64]{1,2,0:T(8,128)(2,1)} all-to-all(bf16[2048,96,64]{1,2,0:T(8,128)(2,1)} %copy.59), channel_id=1, replica_groups=mesh['grp'=2,'aux'=4,'occ'=4] {'aux'}, dimensions={0} | all-to-all | bytes 50331648 | tf_op jit(solution)/shard_map/all_to_all | solution.py:66
  1951.4 23.6 %copy.82 = bf16[4,512,96,64]{2,1,3,0:T(8,128)(2,1)} copy(bf16[4,512,96,64]{2,3,1,0:T(8,128)(2,1)} %bitcast.127) | data formatting | bytes 50331648 | tf_op jit(solution)/shard_map/all_to_all | solution.py:66
  1975.0 50.3 %reshape.137 = bf16[49152,256]{0,1:T(8,128)(2,1)} reshape(bf16[512,96,4,64]{1,0,3,2:T(8,128)(2,1)} %bitcast.126) | data formatting | bytes 50331648 | tf_op jit(solution)/shard_map/reshape | solution.py:67
  2025.4 18.6 fusion.74
  2044.0 53.7 %reduce-scatter.2.cloned.1.call-done = f32[16,256]{1,0:T(8,128)} async-done(((f32[256,256]{1,0:T(8,128)}), f32[16,256]{1,0:T(8,128)}) %reduce-scatter.2.cloned.1.call-update) | async-done | bytes 16400 | tf_op jit(solution)/shard_map/reduce_scatter | solution.py:71
  (68 shorter events, 28.6 us)
Async XLA Ops:
  577.0 602.3 %all-to-all-start.1 = ((bf16[4,128,384,64]{1,3,0,2:T(8,128)(2,1)}), bf16[4,128,384,64]{1,3,0,2:T(8,128)(2,1)}, u32[]{:S(2)}, u32[]{:S(2)}) async-start(bf16[4,128,384,64]{1,3,0,2:T(8,128)(2,1)} %copy.52), calls=%async_computation.1 | async-start | bytes 50331648 | tf_op jit(solution)/shard_map/all_to_all | solution.py:57
  585.4 824.6 %all-gather.2.cloned.1.call-start = ((), (), s32[]{:S(2)}) async-start(), calls=%async_computation.4 | async-start | bytes 8912896 | tf_op jit(solution)/shard_map/all_gather | solution.py:56
  586.1 1511.6 %reduce-scatter.2.cloned.1.call-start = ((), (), s32[]{:S(2)}) async-start(), calls=%async_computation.5 | async-start | bytes 278528 | tf_op jit(solution)/shard_map/reduce_scatter | solution.py:71
  1206.9 16.5 copy-start
  1410.0 11.3 slice-start.3
  1414.8 6.5 slice-start.4
  1414.8 14.6 slice-start
  1414.8 14.6 slice-start.1
  1421.3 8.1 slice-start.2
Sparse Core Ops, SparseCore 0:
  588.4 233.3 all-gather.1
  2044.1 53.5 reduce-scatter.1
where the time goes:
time: 2120 us; the launch traced here: 2100 us
  blocking collectives  669 us (32%)
  waiting for transfers between devices  647 us (31%)
  local copies, waits for them, and re-layouts  504 us (24%)
  matrix products  257 us (12%)
    all_to_all x1, waiting for transfers between devices, per_device(): lax.all_to_all(lax.all_to_all(halves, 'aux', split_axis=3, concat_axis=0,...  593 us
    all_to_all x1, blocking collectives, per_device(): lax.all_to_all(fitted, 'aux', split_axis=0, concat_axis=2, tiled=True)  381 us
    all_to_all x1, blocking collectives, per_device(): lax.all_to_all(halves, 'aux', split_axis=3, concat_axis=0, tiled=True)  288 us
    slice x8, local copies, waits for them, and re-layouts, fitting(): columns[:upper_end]  136 us
    dot_general x8, matrix products, block_half(): jnp.einsum('sm,spix->pimx', placing, contrib, precision=lax.Precision.HIG...  131 us
    dot_general x8, matrix products, fitting(): jnp.dot(factor[block_number * step_rows:upper_end, :upper_end], columns[:...  79.9 us
    dynamic_update_slice x16, local copies, waits for them, and re-layouts, per_device(): halves = lax.map(transform, (integrals, pair_list, pair_count))  63.9 us
    reduce_scatter x1, waiting for transfers between devices, per_device(): lax.psum_scatter(partial_value, ('aux', 'occ'), scatter_dimension=0, tile...  53.7 us
  transfers between devices with their start and end apart: 3, of which 2 were waited for; matrix products, arithmetic and copies ran while one was open for 11% of the time, Pallas kernels for 0%

commit v1 on v0

v1 whole, which is shorter than its diff:
```python
import functools

import jax
import jax.numpy as jnp
from jax import lax
from jax.experimental import pallas as pl
from jax.experimental.pallas import tpu as pltpu
from jax.sharding import PartitionSpec as P

BOTH = ("aux", "occ")
VMEM_BYTES = 58 * 2**20


def half_kernel(list_ref, count_ref, ints_ref, basis_ref, out_ref, rows_ref):
    block = pl.program_id(0)
    slots, aux_width, size_block = ints_ref.shape[1:4]
    vectors, basis_total = basis_ref.shape
    side = basis_total // size_block
    where_slot, is_used = [], []
    for pair in range(side * side):
        slot_of = jnp.int32(0)
        used = jnp.int32(0)
        for slot in range(slots):
            hit = jnp.logical_and(
                list_ref[block, slot] == pair, slot < count_ref[block]
            ).astype(jnp.int32)
            slot_of = slot_of + hit * slot
            used = used + hit
        where_slot.append(slot_of)
        is_used.append(used > 0)

    def one(p, carry):
        rows = []
        for m in range(side):
            row = []
            for n in range(side):
                pair = m * side + n
                tile = ints_ref[0, where_slot[pair], p]
                row.append(jnp.where(is_used[pair], tile, jnp.zeros_like(tile)))
            rows.append(jnp.concatenate(row, axis=1))
        window = jnp.concatenate(rows, axis=0)
        product = lax.dot_general(
            basis_ref[...], window, (((1,), (1,)), ((), ())), preferred_element_type=jnp.float32
        )
        for m in range(side):
            rows_ref[m, pl.ds(p, vectors, stride=aux_width), :] = product[
                :, m * size_block : (m + 1) * size_block
            ]
        return carry

    lax.fori_loop(0, aux_width, one, 0, unroll=2)
    for m in range(side):
        out_ref[..., m * size_block : (m + 1) * size_block] = (
            rows_ref[m].astype(jnp.bfloat16).reshape(out_ref.shape[:-1] + (size_block,))
        )


def half_transform(integrals, pair_list, pair_count, basis_rows, devices):
    blocks, slots, aux_width, size_block, _ = integrals.shape
    vectors, basis_total = basis_rows.shape
    own = vectors // devices
    return pl.pallas_call(
        half_kernel,
        out_shape=jax.ShapeDtypeStruct(
            (devices, own, blocks * aux_width, basis_total), jnp.bfloat16
        ),
        grid_spec=pltpu.PrefetchScalarGridSpec(
            num_scalar_prefetch=2,
            grid=(blocks,),
            in_specs=[
                pl.BlockSpec(
                    (1, slots, aux_width, size_block, size_block), lambda b, *_: (b, 0, 0, 0, 0)
                ),
                pl.BlockSpec((vectors, basis_total), lambda b, *_: (0, 0)),
            ],
            out_specs=pl.BlockSpec(
                (devices, own, aux_width, basis_total), lambda b, *_: (0, 0, b, 0)
            ),
            scratch_shapes=[pltpu.VMEM(
                    (basis_total // size_block, vectors * aux_width, size_block), jnp.float32
                )],
        ),
        compiler_params=pltpu.CompilerParams(vmem_limit_bytes=VMEM_BYTES),
        cost_estimate=pl.CostEstimate(
            flops=2 * blocks * aux_width * vectors * basis_total * basis_total,
            bytes_accessed=integrals.size * 2 + vectors * blocks * aux_width * basis_total * 2,
            transcendentals=0,
        ),
        name="half_transform",
    )(pair_list, pair_count, integrals, basis_rows)


def fit_kernel(step_rows, factor_ref, half_ref, out_ref):
    aux_total = factor_ref.shape[0]
    columns = half_ref[...].reshape(aux_total, half_ref.shape[-1])
    total = jnp.zeros(out_ref.shape, jnp.float32)
    for low in range(0, aux_total, step_rows):
        high = low + step_rows
        fitted = jnp.dot(
            factor_ref[low:high, :high], columns[:high], preferred_element_type=jnp.float32
        ).astype(jnp.bfloat16)
        total = total + lax.dot_general(
            fitted, fitted, (((0,), (0,)), ((), ())), preferred_element_type=jnp.float32
        )

    @pl.when(pl.program_id(0) == 0)
    def _():
        out_ref[...] = total

    @pl.when(pl.program_id(0) > 0)
    def _():
        out_ref[...] += total


def fit_exchange(factor, arrived):
    devices, own, aux_local, basis_total = arrived.shape
    aux_total = factor.shape[0]
    return pl.pallas_call(
        functools.partial(fit_kernel, aux_total // 8),
        out_shape=jax.ShapeDtypeStruct((basis_total, basis_total), jnp.float32),
        grid=(own,),
        in_specs=[
            pl.BlockSpec(
                (aux_total, aux_total), lambda k: (0, 0), pipeline_mode=pl.Buffered(1)
            ),
            pl.BlockSpec((devices, 1, aux_local, basis_total), lambda k: (0, k, 0, 0)),
        ],
        out_specs=pl.BlockSpec((basis_total, basis_total), lambda k: (0, 0)),
        compiler_params=pltpu.CompilerParams(vmem_limit_bytes=VMEM_BYTES),
        cost_estimate=pl.CostEstimate(
            flops=own * aux_total * basis_total * (aux_total * 9 // 8 + 2 * basis_total),
            bytes_accessed=(factor.size + arrived.size) * 2,
            transcendentals=0,
        ),
        name="fit_exchange",
    )(factor, arrived)


def per_device(integrals, pair_list, pair_count, coefficients, metric):
    devices = lax.axis_size("aux") * lax.axis_size("occ")
    basis_total = coefficients.shape[0]
    factor = lax.all_gather(metric, BOTH, axis=0, tiled=True)
    half = half_transform(integrals, pair_list, pair_count, coefficients.T, devices)
    arrived = lax.all_to_all(half, BOTH, split_axis=0, concat_axis=0, tiled=True)
    partial_value = fit_exchange(factor, arrived)
    shares = partial_value.reshape(devices, basis_total // devices, basis_total)
    return jnp.sum(lax.all_to_all(shares, BOTH, split_axis=0, concat_axis=0, tiled=True).reshape(shares.shape), axis=0)


def solution(mesh):
    in_specs = (
        P(("grp", "aux", "occ"), None, None, None, None),
        P(("grp", "aux", "occ"), None),
        P(("grp", "aux", "occ")),
        P("grp", None),
        P(("grp", "aux", "occ"), None),
    )
    out_specs = P(("grp", "aux", "occ"), None)
    return jax.shard_map(
        per_device, mesh=mesh, in_specs=in_specs, out_specs=out_specs, check_vma=False
    )
```

time: 2120 us -> 729 us (0.34)
  blocking collectives: 669 us -> 13.5 us
  local copies, waits for them, and re-layouts: 504 us -> 3.08 us
  matrix products: 257 us -> 0 us
  Pallas kernels: 0 us -> 95.8 us
  waiting for transfers between devices: 647 us -> 594 us
    all_to_all x2 -> x1, blocking collectives: 669 us -> 13.5 us  [per_device(): lax.all_to_all(shares, BOTH, split_axis=0, concat_axis=0, tiled=True)]
    all_gather x1, waiting for transfers between devices: 0.01 us -> 410 us  [per_device(): factor = lax.all_gather(metric, BOTH, axis=0, tiled=True)]
    all_to_all x1, waiting for transfers between devices: 593 us -> 184 us  [per_device(): lax.all_to_all(half, BOTH, split_axis=0, concat_axis=0, tiled=True)]
    dot_general x25 -> x0, matrix products: 257 us -> none  [the longest x8 131 us: block_half(): jnp.einsum('sm,spix->pimx', placing, contrib, precision=lax.Precision.HIG...]
    reshape x3 -> x0, local copies, waits for them, and re-layouts: 139 us -> none  [the longest x1 50.3 us: per_device(): flattened = owned_rows.reshape(-1, basis_total)]
    slice x8 -> x0, local copies, waits for them, and re-layouts: 136 us -> none  [fitting(): columns[:upper_end]]
    all_to_all x4 -> x0, local copies, waits for them, and re-layouts: 105 us -> none  [the longest x2 49.6 us: per_device(): lax.all_to_all(lax.all_to_all(halves, 'aux', split_axis=3, concat_axis=0,...]
    pallas_call x0 -> x2, Pallas kernels: none -> 95.8 us  [the longest x1 60.1 us: fit_exchange(): pl.pallas_call(functools.partial(fit_kernel, aux_total // 8), out_shape=j...]
  transfers between devices with their start and end apart: 3 -> 2, of which waited for: 2 -> 2; matrix products, arithmetic and copies ran while one was open for 11% -> 0% of each run, Pallas kernels for 0% -> 0%
where the time goes in v1:
time: 729 us; the launch traced here: 728 us
  waiting for transfers between devices  594 us (81%)
  Pallas kernels  95.8 us (13%)
  blocking collectives  13.5 us (2%)
  between operations  13.4 us (2%)
  starting transfers between devices  7.44 us (1%)
    all_gather x1, waiting for transfers between devices, per_device(): factor = lax.all_gather(metric, BOTH, axis=0, tiled=True)  410 us
    all_to_all x1, waiting for transfers between devices, per_device(): lax.all_to_all(half, BOTH, split_axis=0, concat_axis=0, tiled=True)  184 us
    pallas_call x1, Pallas kernels, fit_exchange(): pl.pallas_call(functools.partial(fit_kernel, aux_total // 8), out_shape=j...  60.1 us
    pallas_call x1, Pallas kernels, half_transform(): pl.pallas_call(half_kernel, out_shape=jax.ShapeDtypeStruct((devices, own,...  35.8 us
  transfers between devices with their start and end apart: 2, of which 2 were waited for; matrix products, arithmetic and copies ran while one was open for 0% of the time, Pallas kernels for 0%

profile of v1, /device:TPU:0, one launch (start us, length us, event | category | flops | bytes accessed | tf_op | source)
XLA Modules:
  0.0 728.3 jit_solution(7554429012325690993)
XLA Ops:
  6.5 1.7 copy.6
  8.3 1.3 copy.7.list_ref
  9.6 35.8 %half_transform.1 = bf16[16,24,128,256]{3,2,1,0:T(8,128)(2,1)} custom-call(s32[8,4]{1,0:T(8,128)} %copy.7.list_ref, s32[8]{0:T(128)} %count_ref.1, bf16[8,4,16,128,128]{4,3,2,1,0:T(8,128)(2,1)} %ints_ref.1, bf16[384,256]{1,0:T(8,128)(2,1)} %bitcast.2), custom_call_target="tpu_custom_call" | custom-call | flops 6442450944 | bytes 41943040 | tf_op jit(solution)/shard_map/half_transform/pallas_call | solution.py:62
  45.4 7.4 %all-to-all-start = ((bf16[16,24,128,256]{3,2,1,0:T(8,128)(2,1)}), bf16[16,24,128,256]{3,2,1,0:T(8,128)(2,1)}, u32[]{:S(2)}, u32[]{:S(2)}) async-start(bf16[16,24,128,256]{3,2,1,0:T(8,128)(2,1)} %half_transform.1), calls=%async_computation | async-start | bytes 50331648 | tf_op jit(solution)/shard_map/all_to_all | solution.py:144
  52.8 0.0 all-gather.2.cloned.1.call-start
  52.8 0.7 all-gather.2.cloned.1.call-update
  53.5 410.0 %all-gather.2.cloned.1.call-done.factor_ref = bf16[2048,2048]{1,0:T(8,128)(2,1)} async-done(((bf16[128,2048]{1,0:T(8,128)(2,1)}), bf16[2048,2048]{1,0:T(8,128)(2,1)}) %all-gather.2.cloned.1.call-update) | async-done | bytes 8388624 | tf_op jit(solution)/shard_map/all_gather | solution.py:142
  463.5 183.7 %all-to-all-done.half_ref = bf16[16,24,128,256]{3,2,1,0:T(8,128)(2,1)} async-done(((bf16[16,24,128,256]{3,2,1,0:T(8,128)(2,1)}), bf16[16,24,128,256]{3,2,1,0:T(8,128)(2,1)}, u32[]{:S(2)}, u32[]{:S(2)}) %all-to-all-start) | async-done | bytes 25165856 | tf_op jit(solution)/shard_map/all_to_all | solution.py:144
  647.2 60.1 %fit_exchange.1 = f32[256,256]{1,0:T(8,128)} custom-call(bf16[2048,2048]{1,0:T(8,128)(2,1)} %all-gather.2.cloned.1.call-done.factor_ref, bf16[16,24,128,256]{3,2,1,0:T(8,128)(2,1)} %all-to-all-done.half_ref), custom_call_target="tpu_custom_call" | custom-call | flops 35433480192 | bytes 33554432 | tf_op jit(solution)/shard_map/fit_exchange/pallas_call | solution.py:118
  707.3 13.5 %all_to_all.10 = f32[16,16,256]{2,1,0:T(8,128)S(1)} all-to-all(f32[16,16,256]{2,1,0:T(8,128)} %bitcast.3), channel_id=1, replica_groups=mesh['grp'=2,'aux'=4,'occ'=4] {'aux','occ'}, dimensions={0} | all-to-all | bytes 524288 | tf_op jit(solution)/shard_map/all_to_all | solution.py:147
  720.8 0.6 reduce_sum.9
Async XLA Ops:
  45.4 601.8 %all-to-all-start = ((bf16[16,24,128,256]{3,2,1,0:T(8,128)(2,1)}), bf16[16,24,128,256]{3,2,1,0:T(8,128)(2,1)}, u32[]{:S(2)}, u32[]{:S(2)}) async-start(bf16[16,24,128,256]{3,2,1,0:T(8,128)(2,1)} %half_transform.1), calls=%async_computation | async-start | bytes 50331648 | tf_op jit(solution)/shard_map/all_to_all | solution.py:144
  52.8 410.7 %all-gather.2.cloned.1.call-start = ((), (), s32[]{:S(2)}) async-start(), calls=%async_computation.2 | async-start | bytes 8912896 | tf_op jit(solution)/shard_map/all_gather | solution.py:142
Sparse Core Ops, SparseCore 0:
  55.8 407.6 all-gather.1

commit v2 on v1

--- a/solution.py
+++ b/solution.py
@@ -9,13 +9,113 @@
 
 BOTH = ("aux", "occ")
 VMEM_BYTES = 58 * 2**20
-
-
-def half_kernel(list_ref, count_ref, ints_ref, basis_ref, out_ref, rows_ref):
+PANEL = 16
+SCALE = 2.0**40
+PIVOT_FLOOR = 1e-6
+
+
+def root(value):
+    return value * lax.rsqrt(jnp.maximum(value, 1e-37))
+
+
+def factor_kernel(start, *refs):
+    if start == 0:
+        coef_ref, rows_ref, rest_ref, diag_ref = refs
+        scaled = (coef_ref[...].astype(jnp.float32) * SCALE).astype(jnp.bfloat16)
+        gram = lax.dot_general(
+            scaled, scaled, (((1,), (1,)), ((), ())), preferred_element_type=jnp.float32
+        )
+        total = gram.shape[0]
+        on_diagonal = lax.broadcasted_iota(jnp.int32, gram.shape, 0) == (
+            lax.broadcasted_iota(jnp.int32, gram.shape, 1)
+        )
+        diagonal = jnp.sum(jnp.where(on_diagonal, gram, 0.0), axis=0, keepdims=True)
+        which = lax.broadcasted_iota(jnp.int32, diag_ref.shape, 0)
+        diag_ref[...] = jnp.where(
+            which == 0, diagonal, jnp.maximum(diagonal * PIVOT_FLOOR, 1e-37)
+        )
+        rest_ref[...] = gram
+    else:
+        rest_in_ref, diag_in_ref, rows_ref, rest_ref, diag_ref = refs
+        rest_ref[...] = rest_in_ref[...]
+        diag_ref[...] = diag_in_ref[...]
+        total = rest_ref.shape[1]
+    own = rows_ref.shape[0] // 2
+    lanes = min(total, 128)
+    lane = lax.broadcasted_iota(jnp.int32, (PANEL, total), 1)
+    row = lax.broadcasted_iota(jnp.int32, (PANEL, total), 0)
+    row_of_column = lax.broadcasted_iota(jnp.int32, (PANEL, 1), 0)
+
+    def panel(number, carry):
+        low = pl.multiple_of(start + number * PANEL, PANEL)
+        rest = rest_ref[pl.ds(low, PANEL), :]
+        left = diag_ref[0:1, :]
+        floor = diag_ref[1:2, :]
+        on_diagonal = lane == low + row
+        left_column = jnp.sum(jnp.where(on_diagonal, left, 0.0), axis=1, keepdims=True)
+        floor_column = jnp.sum(jnp.where(on_diagonal, floor, 0.0), axis=1, keepdims=True)
+        corner = rest[:, :lanes]
+        for part in range(1, total // lanes):
+            corner = jnp.where(
+                low >= part * lanes, rest[:, part * lanes : (part + 1) * lanes], corner
+            )
+        corner = pltpu.roll(corner, lax.rem(lanes - lax.rem(low, lanes), lanes), 1)
+        done = jnp.zeros((PANEL, total), jnp.float32)
+        for t in range(PANEL):
+            pivot = jnp.maximum(left_column[t : t + 1], floor_column[t : t + 1])
+            inverse = lax.rsqrt(pivot)
+            inverse = inverse * (1.5 - 0.5 * (pivot * inverse) * inverse)
+            most = root(left)
+            here = jnp.clip(rest[t : t + 1] * inverse, -most, most)
+            here = jnp.where(lane[:1] > low + t, here, 0.0)
+            left = jnp.maximum(left - here * here, 0.0)
+            here = jnp.where(lane[:1] == low + t, pivot * inverse, here)
+            done = jnp.where(row == t, here, done)
+            most = root(left_column)
+            weight = jnp.clip(corner[:, t : t + 1] * inverse, -most, most)
+            weight = jnp.where(row_of_column > t, weight, 0.0)
+            left_column = jnp.maximum(left_column - weight * weight, 0.0)
+            rest = rest - weight * here
+            corner = corner - weight * (corner[t : t + 1] * inverse)
+        diag_ref[0:1, :] = left
+        rest_ref[...] -= lax.dot_general(
+            done,
+            done,
+            (((0,), (0,)), ((), ())),
+            precision=lax.Precision.HIGHEST,
+            preferred_element_type=jnp.float32,
+        )
+        done = done * (1.0 / SCALE)
+        high = done.astype(jnp.bfloat16)
+        place = pl.multiple_of(number * PANEL, PANEL)
+        rows_ref[pl.ds(place, PANEL), :] = high
+        rows_ref[pl.ds(own + place, PANEL), :] = (done - high.astype(jnp.float32)).astype(
+            jnp.bfloat16
+        )
+        return carry
+
+    lax.fori_loop(0, own // PANEL, panel, 0)
+
+
+def factor_rows(start, own, total, operands):
+    rows, rest, diagonals = pl.pallas_call(
+        functools.partial(factor_kernel, start),
+        out_shape=(
+            jax.ShapeDtypeStruct((2 * own, total), jnp.bfloat16),
+            jax.ShapeDtypeStruct((total, total), jnp.float32),
+            jax.ShapeDtypeStruct((8, total), jnp.float32),
+        ),
+        compiler_params=pltpu.CompilerParams(vmem_limit_bytes=VMEM_BYTES),
+        name="factor_rows",
+    )(*operands)
+    return rows, (rest, diagonals)
+
+
+def half_kernel(low_block, list_ref, count_ref, ints_ref, basis_ref, out_ref, rows_ref):
     block = pl.program_id(0)
     slots, aux_width, size_block = ints_ref.shape[1:4]
-    vectors, basis_total = basis_ref.shape
-    side = basis_total // size_block
+    vectors = basis_ref.shape[0] // 2
+    side = basis_ref.shape[1] // size_block
     where_slot, is_used = [], []
     for pair in range(side * side):
         slot_of = jnp.int32(0)
@@ -33,15 +133,19 @@
         rows = []
         for m in range(side):
             row = []
-            for n in range(side):
+            for n in range(low_block, side):
                 pair = m * side + n
                 tile = ints_ref[0, where_slot[pair], p]
                 row.append(jnp.where(is_used[pair], tile, jnp.zeros_like(tile)))
             rows.append(jnp.concatenate(row, axis=1))
         window = jnp.concatenate(rows, axis=0)
         product = lax.dot_general(
-            basis_ref[...], window, (((1,), (1,)), ((), ())), preferred_element_type=jnp.float32
-        )
+            basis_ref[:, low_block * size_block :],
+            window,
+            (((1,), (1,)), ((), ())),
+            preferred_element_type=jnp.float32,
+        )
+        product = product[:vectors] + product[vectors:]
         for m in range(side):
             rows_ref[m, pl.ds(p, vectors, stride=aux_width), :] = product[
                 :, m * size_block : (m + 1) * size_block
@@ -55,12 +159,12 @@
         )
 
 
-def half_transform(integrals, pair_list, pair_count, basis_rows, devices):
+def half_transform(integrals, pair_list, pair_count, basis_rows, start, devices):
     blocks, slots, aux_width, size_block, _ = integrals.shape
-    vectors, basis_total = basis_rows.shape
+    vectors, basis_total = basis_rows.shape[0] // 2, basis_rows.shape[1]
     own = vectors // devices
     return pl.pallas_call(
-        half_kernel,
+        functools.partial(half_kernel, start // size_block),
         out_shape=jax.ShapeDtypeStruct(
             (devices, own, blocks * aux_width, basis_total), jnp.bfloat16
         ),
@@ -71,18 +175,20 @@
                 pl.BlockSpec(
                     (1, slots, aux_width, size_block, size_block), lambda b, *_: (b, 0, 0, 0, 0)
                 ),
-                pl.BlockSpec((vectors, basis_total), lambda b, *_: (0, 0)),
+                pl.BlockSpec(basis_rows.shape, lambda b, *_: (0, 0)),
             ],
             out_specs=pl.BlockSpec(
                 (devices, own, aux_width, basis_total), lambda b, *_: (0, 0, b, 0)
             ),
-            scratch_shapes=[pltpu.VMEM(
+            scratch_shapes=[
+                pltpu.VMEM(
                     (basis_total // size_block, vectors * aux_width, size_block), jnp.float32
-                )],
+                )
+            ],
         ),
         compiler_params=pltpu.CompilerParams(vmem_limit_bytes=VMEM_BYTES),
         cost_estimate=pl.CostEstimate(
-            flops=2 * blocks * aux_width * vectors * basis_total * basis_total,
+            flops=4 * blocks * aux_width * vectors * basis_total * basis_total,
             bytes_accessed=integrals.size * 2 + vectors * blocks * aux_width * basis_total * 2,
             transcendentals=0,
         ),
@@ -90,7 +196,7 @@
     )(pair_list, pair_count, integrals, basis_rows)
 
 
-def fit_kernel(step_rows, factor_ref, half_ref, out_ref):
+def fit_kernel(step_rows, factor_ref, half_ref, before_ref, out_ref):
     aux_total = factor_ref.shape[0]
     columns = half_ref[...].reshape(aux_total, half_ref.shape[-1])
     total = jnp.zeros(out_ref.shape, jnp.float32)
@@ -105,14 +211,14 @@
 
     @pl.when(pl.program_id(0) == 0)
     def _():
-        out_ref[...] = total
+        out_ref[...] = before_ref[...] + total
 
     @pl.when(pl.program_id(0) > 0)
     def _():
         out_ref[...] += total
 
 
-def fit_exchange(factor, arrived):
+def fit_exchange(factor, arrived, before):
     devices, own, aux_local, basis_total = arrived.shape
     aux_total = factor.shape[0]
     return pl.pallas_call(
@@ -124,6 +230,7 @@
                 (aux_total, aux_total), lambda k: (0, 0), pipeline_mode=pl.Buffered(1)
             ),
             pl.BlockSpec((devices, 1, aux_local, basis_total), lambda k: (0, k, 0, 0)),
+            pl.BlockSpec((basis_total, basis_total), lambda k: (0, 0)),
         ],
         out_specs=pl.BlockSpec((basis_total, basis_total), lambda k: (0, 0)),
         compiler_params=pltpu.CompilerParams(vmem_limit_bytes=VMEM_BYTES),
@@ -133,18 +240,25 @@
             transcendentals=0,
         ),
         name="fit_exchange",
-    )(factor, arrived)
+    )(factor, arrived, before)
 
 
 def per_device(integrals, pair_list, pair_count, coefficients, metric):
     devices = lax.axis_size("aux") * lax.axis_size("occ")
     basis_total = coefficients.shape[0]
+    chunks = min(4, basis_total // devices)
+    width = basis_total // chunks
     factor = lax.all_gather(metric, BOTH, axis=0, tiled=True)
-    half = half_transform(integrals, pair_list, pair_count, coefficients.T, devices)
-    arrived = lax.all_to_all(half, BOTH, split_axis=0, concat_axis=0, tiled=True)
-    partial_value = fit_exchange(factor, arrived)
-    shares = partial_value.reshape(devices, basis_total // devices, basis_total)
-    return jnp.sum(lax.all_to_all(shares, BOTH, split_axis=0, concat_axis=0, tiled=True).reshape(shares.shape), axis=0)
+    total = jnp.zeros((basis_total, basis_total), jnp.float32)
+    state = (coefficients,)
+    for chunk in range(chunks):
+        rows, state = factor_rows(chunk * width, width, basis_total, state)
+        half = half_transform(integrals, pair_list, pair_count, rows, chunk * width, devices)
+        half, state = lax.optimization_barrier((half, state))
+        arrived = lax.all_to_all(half, BOTH, split_axis=0, concat_axis=0, tiled=True)
+        total = fit_exchange(factor, arrived, total)
+    shares = total.reshape(devices, basis_total // devices, basis_total)
+    return jnp.sum(lax.all_to_all(shares, BOTH, split_axis=0, concat_axis=0, tiled=True), axis=0)
 
 
 def solution(mesh):

time: 729 us -> 526 us (0.72)
  waiting for transfers between devices: 594 us -> 290 us
  Pallas kernels: 95.8 us -> 185 us
  starting transfers between devices: 7.44 us -> 21.3 us
    all_gather x1, waiting for transfers between devices: 410 us -> 0.02 us  [per_device(): factor = lax.all_gather(metric, BOTH, axis=0, tiled=True)]
    all_to_all x1 -> x4, waiting for transfers between devices: 184 us -> 289 us  [per_device(): lax.all_to_all(half, BOTH, split_axis=0, concat_axis=0, tiled=True)]
    pallas_call x1 -> x8, Pallas kernels: 35.8 us -> 130 us  [the longest x4 76.7 us: half_transform(): pl.pallas_call(functools.partial(half_kernel, start // size_block), out_s...]
    all_to_all x1 -> x4, starting transfers between devices: 7.4 us -> 21.3 us  [per_device(): lax.all_to_all(half, BOTH, split_axis=0, concat_axis=0, tiled=True)]
    pallas_call x1 -> x4, Pallas kernels: 60.1 us -> 54.9 us  [fit_exchange(): pl.pallas_call(functools.partial(fit_kernel, aux_total // 8), out_shape=j...]
  transfers between devices with their start and end apart: 2 -> 5, of which waited for: 2 -> 4; matrix products, arithmetic and copies ran while one was open for 0% -> 0% of each run, Pallas kernels for 0% -> 26%
where the time goes in v2:
time: 526 us
  waiting for transfers between devices  290 us (55%)
  Pallas kernels  185 us (35%)
  starting transfers between devices  21.3 us (4%)
  blocking collectives  13.5 us (3%)
  between operations  13.4 us (3%)
    all_to_all x4, waiting for transfers between devices, per_device(): lax.all_to_all(half, BOTH, split_axis=0, concat_axis=0, tiled=True)  289 us
    pallas_call x4, Pallas kernels, half_transform(): pl.pallas_call(functools.partial(half_kernel, start // size_block), out_s...  76.7 us
    pallas_call x4, Pallas kernels, fit_exchange(): pl.pallas_call(functools.partial(fit_kernel, aux_total // 8), out_shape=j...  54.9 us
    pallas_call x4, Pallas kernels, factor_rows(): pl.pallas_call(functools.partial(factor_kernel, start), out_shape=(jax.Sh...  53 us
    all_to_all x4, starting transfers between devices, per_device(): lax.all_to_all(half, BOTH, split_axis=0, concat_axis=0, tiled=True)  21.3 us
    all_to_all x1, blocking collectives, per_device(): lax.all_to_all(shares, BOTH, split_axis=0, concat_axis=0, tiled=True)  13.5 us
  transfers between devices with their start and end apart: 5, of which 4 were waited for; matrix products, arithmetic and copies ran while one was open for 0% of the time, Pallas kernels for 26%

profile of v2, /device:TPU:0, one launch (start us, length us, event | category | flops | bytes accessed | tf_op | source)
XLA Modules:
  0.0 525.5 jit_solution(2738283196090945038)
XLA Ops:
  6.5 1.3 copy.9.list_ref
  7.9 13.4 %factor_rows.4 = (bf16[128,256]{1,0:T(8,128)(2,1)}, f32[256,256]{1,0:T(8,128)}, f32[8,256]{1,0:T(8,128)}) custom-call(bf16[256,384]{1,0:T(8,128)(2,1)} %refs_0_.1), custom_call_target="tpu_custom_call" | custom-call | tf_op jit(solution)/shard_map/factor_rows/pallas_call | solution.py:101
  21.3 20.3 %half_transform.4 = bf16[16,4,128,256]{3,2,1,0:T(8,128)(2,1)} custom-call(s32[8,4]{1,0:T(8,128)} %copy.9.list_ref, s32[8]{0:T(128)} %count_ref.7, bf16[8,4,16,128,128]{4,3,2,1,0:T(8,128)(2,1)} %ints_ref.7, bf16[128,256]{1,0:T(8,128)(2,1)} %get-tuple-element.24.basis_ref), custom_call_target="tpu_custom_call" | custom-call | flops 2147483648 | bytes 20971520 | tf_op jit(solution)/shard_map/half_transform/pallas_call | solution.py:166
  41.6 7.4 %all-to-all-start.3 = ((bf16[16,4,128,256]{3,2,1,0:T(8,128)(2,1)}), bf16[16,4,128,256]{3,2,1,0:T(8,128)(2,1)}, u32[]{:S(2)}, u32[]{:S(2)}) async-start(bf16[16,4,128,256]{3,2,1,0:T(8,128)(2,1)} %half_transform.4), calls=%async_computation.3 | async-start | bytes 8388608 | tf_op jit(solution)/shard_map/all_to_all | solution.py:258
  49.0 13.2 %factor_rows.5 = (bf16[128,256]{1,0:T(8,128)(2,1)}, f32[256,256]{1,0:T(8,128)}, f32[8,256]{1,0:T(8,128)}) custom-call(f32[256,256]{1,0:T(8,128)} %get-tuple-element.27.refs_0_, f32[8,256]{1,0:T(8,128)} %get-tuple-element.28.refs_1_), custom_call_target="tpu_custom_call" | custom-call | tf_op jit(solution)/shard_map/factor_rows/pallas_call | solution.py:101
  62.2 20.3 %half_transform.5 = bf16[16,4,128,256]{3,2,1,0:T(8,128)(2,1)} custom-call(s32[8,4]{1,0:T(8,128)} %copy.9.list_ref, s32[8]{0:T(128)} %count_ref.7, bf16[8,4,16,128,128]{4,3,2,1,0:T(8,128)(2,1)} %ints_ref.7, bf16[128,256]{1,0:T(8,128)(2,1)} %get-tuple-element.29.basis_ref), custom_call_target="tpu_custom_call" | custom-call | flops 2147483648 | bytes 20971520 | tf_op jit(solution)/shard_map/half_transform/pallas_call | solution.py:166
  82.5 61.0 %all-to-all-done.3.half_ref = bf16[16,4,128,256]{3,2,1,0:T(8,128)(2,1)} async-done(((bf16[16,4,128,256]{3,2,1,0:T(8,128)(2,1)}), bf16[16,4,128,256]{3,2,1,0:T(8,128)(2,1)}, u32[]{:S(2)}, u32[]{:S(2)}) %all-to-all-start.3) | async-done | bytes 4194336 | tf_op jit(solution)/shard_map/all_to_all | solution.py:258
  143.4 4.5 all-to-all-start.2
  148.0 0.0 all-gather.2.cloned.1.call-start
  148.0 0.7 all-gather.2.cloned.1.call-update
  148.7 13.2 %factor_rows.6 = (bf16[128,256]{1,0:T(8,128)(2,1)}, f32[256,256]{1,0:T(8,128)}, f32[8,256]{1,0:T(8,128)}) custom-call(f32[256,256]{1,0:T(8,128)} %get-tuple-element.32.refs_0_, f32[8,256]{1,0:T(8,128)} %get-tuple-element.33.refs_1_), custom_call_target="tpu_custom_call" | custom-call | tf_op jit(solution)/shard_map/factor_rows/pallas_call | solution.py:101
  161.9 18.1 %half_transform.6 = bf16[16,4,128,256]{3,2,1,0:T(8,128)(2,1)} custom-call(s32[8,4]{1,0:T(8,128)} %copy.9.list_ref, s32[8]{0:T(128)} %count_ref.7, bf16[8,4,16,128,128]{4,3,2,1,0:T(8,128)(2,1)} %ints_ref.7, bf16[128,256]{1,0:T(8,128)(2,1)} %get-tuple-element.34.basis_ref), custom_call_target="tpu_custom_call" | custom-call | flops 2147483648 | bytes 20971520 | tf_op jit(solution)/shard_map/half_transform/pallas_call | solution.py:166
  180.0 112.9 %all-to-all-done.2.half_ref = bf16[16,4,128,256]{3,2,1,0:T(8,128)(2,1)} async-done(((bf16[16,4,128,256]{3,2,1,0:T(8,128)(2,1)}), bf16[16,4,128,256]{3,2,1,0:T(8,128)(2,1)}, u32[]{:S(2)}, u32[]{:S(2)}) %all-to-all-start.2) | async-done | bytes 4194336 | tf_op jit(solution)/shard_map/all_to_all | solution.py:258
  292.9 4.6 all-to-all-start.1
  297.4 13.2 %factor_rows.7 = (bf16[128,256]{1,0:T(8,128)(2,1)}, f32[256,256]{1,0:T(8,128)}, f32[8,256]{1,0:T(8,128)}) custom-call(f32[256,256]{1,0:T(8,128)} %get-tuple-element.37.refs_0_, f32[8,256]{1,0:T(8,128)} %get-tuple-element.38.refs_1_), custom_call_target="tpu_custom_call" | custom-call | tf_op jit(solution)/shard_map/factor_rows/pallas_call | solution.py:101
  310.6 18.1 %half_transform.7 = bf16[16,4,128,256]{3,2,1,0:T(8,128)(2,1)} custom-call(s32[8,4]{1,0:T(8,128)} %copy.9.list_ref, s32[8]{0:T(128)} %count_ref.7, bf16[8,4,16,128,128]{4,3,2,1,0:T(8,128)(2,1)} %ints_ref.7, bf16[128,256]{1,0:T(8,128)(2,1)} %get-tuple-element.39.basis_ref), custom_call_target="tpu_custom_call" | custom-call | flops 2147483648 | bytes 20971520 | tf_op jit(solution)/shard_map/half_transform/pallas_call | solution.py:166
  328.7 63.1 %all-to-all-done.1.half_ref = bf16[16,4,128,256]{3,2,1,0:T(8,128)(2,1)} async-done(((bf16[16,4,128,256]{3,2,1,0:T(8,128)(2,1)}), bf16[16,4,128,256]{3,2,1,0:T(8,128)(2,1)}, u32[]{:S(2)}, u32[]{:S(2)}) %all-to-all-start.1) | async-done | bytes 4194336 | tf_op jit(solution)/shard_map/all_to_all | solution.py:258
  391.8 4.8 all-to-all-start
  396.6 0.0 all-gather.2.cloned.1.call-done.factor_ref
  396.6 0.7 broadcast_in_dim.3.before_ref
  397.3 13.7 %fit_exchange.4.before_ref = f32[256,256]{1,0:T(8,128)} custom-call(bf16[2048,2048]{1,0:T(8,128)(2,1)} %all-gather.2.cloned.1.call-done.factor_ref, bf16[16,4,128,256]{3,2,1,0:T(8,128)(2,1)} %all-to-all-done.3.half_ref, f32[256,256]{1,0:T(8,128)} %broadcast_in_dim.3.before_ref), custom_call_target="tpu_custom_call" | custom-call | flops 5905580032 | bytes 12582912 | tf_op jit(solution)/shard_map/fit_exchange/pallas_call | solution.py:224
  411.0 13.7 %fit_exchange.5.before_ref = f32[256,256]{1,0:T(8,128)} custom-call(bf16[2048,2048]{1,0:T(8,128)(2,1)} %all-gather.2.cloned.1.call-done.factor_ref, bf16[16,4,128,256]{3,2,1,0:T(8,128)(2,1)} %all-to-all-done.2.half_ref, f32[256,256]{1,0:T(8,128)} %fit_exchange.4.before_ref), custom_call_target="tpu_custom_call" | custom-call | flops 5905580032 | bytes 12582912 | tf_op jit(solution)/shard_map/fit_exchange/pallas_call | solution.py:224
  424.8 13.7 %fit_exchange.6.before_ref = f32[256,256]{1,0:T(8,128)} custom-call(bf16[2048,2048]{1,0:T(8,128)(2,1)} %all-gather.2.cloned.1.call-done.factor_ref, bf16[16,4,128,256]{3,2,1,0:T(8,128)(2,1)} %all-to-all-done.1.half_ref, f32[256,256]{1,0:T(8,128)} %fit_exchange.5.before_ref), custom_call_target="tpu_custom_call" | custom-call | flops 5905580032 | bytes 12582912 | tf_op jit(solution)/shard_map/fit_exchange/pallas_call | solution.py:224
  438.5 52.3 %all-to-all-done.half_ref = bf16[16,4,128,256]{3,2,1,0:T(8,128)(2,1)} async-done(((bf16[16,4,128,256]{3,2,1,0:T(8,128)(2,1)}), bf16[16,4,128,256]{3,2,1,0:T(8,128)(2,1)}, u32[]{:S(2)}, u32[]{:S(2)}) %all-to-all-start) | async-done | bytes 4194336 | tf_op jit(solution)/shard_map/all_to_all | solution.py:258
  490.8 13.7 %fit_exchange.7 = f32[256,256]{1,0:T(8,128)} custom-call(bf16[2048,2048]{1,0:T(8,128)(2,1)} %all-gather.2.cloned.1.call-done.factor_ref, bf16[16,4,128,256]{3,2,1,0:T(8,128)(2,1)} %all-to-all-done.half_ref, f32[256,256]{1,0:T(8,128)} %fit_exchange.6.before_ref), custom_call_target="tpu_custom_call" | custom-call | flops 5905580032 | bytes 12582912 | tf_op jit(solution)/shard_map/fit_exchange/pallas_call | solution.py:224
  504.5 13.5 %all_to_all.25 = f32[16,16,256]{2,1,0:T(8,128)S(1)} all-to-all(f32[16,16,256]{2,1,0:T(8,128)} %bitcast.1), channel_id=1, replica_groups=mesh['grp'=2,'aux'=4,'occ'=4] {'aux','occ'}, dimensions={0} | all-to-all | bytes 524288 | tf_op jit(solution)/shard_map/all_to_all | solution.py:261
  518.0 0.6 reduce_sum.9
Async XLA Ops:
  41.6 101.8 %all-to-all-start.3 = ((bf16[16,4,128,256]{3,2,1,0:T(8,128)(2,1)}), bf16[16,4,128,256]{3,2,1,0:T(8,128)(2,1)}, u32[]{:S(2)}, u32[]{:S(2)}) async-start(bf16[16,4,128,256]{3,2,1,0:T(8,128)(2,1)} %half_transform.4), calls=%async_computation.3 | async-start | bytes 8388608 | tf_op jit(solution)/shard_map/all_to_all | solution.py:258
  143.4 149.4 %all-to-all-start.2 = ((bf16[16,4,128,256]{3,2,1,0:T(8,128)(2,1)}), bf16[16,4,128,256]{3,2,1,0:T(8,128)(2,1)}, u32[]{:S(2)}, u32[]{:S(2)}) async-start(bf16[16,4,128,256]{3,2,1,0:T(8,128)(2,1)} %half_transform.5), calls=%async_computation.2 | async-start | bytes 8388608 | tf_op jit(solution)/shard_map/all_to_all | solution.py:258
  148.0 248.6 %all-gather.2.cloned.1.call-start = ((), (), s32[]{:S(2)}) async-start(), calls=%async_computation.5 | async-start | bytes 8912896 | tf_op jit(solution)/shard_map/all_gather | solution.py:251
  292.9 98.9 %all-to-all-start.1 = ((bf16[16,4,128,256]{3,2,1,0:T(8,128)(2,1)}), bf16[16,4,128,256]{3,2,1,0:T(8,128)(2,1)}, u32[]{:S(2)}, u32[]{:S(2)}) async-start(bf16[16,4,128,256]{3,2,1,0:T(8,128)(2,1)} %half_transform.6), calls=%async_computation.1 | async-start | bytes 8388608 | tf_op jit(solution)/shard_map/all_to_all | solution.py:258
  391.8 99.0 %all-to-all-start = ((bf16[16,4,128,256]{3,2,1,0:T(8,128)(2,1)}), bf16[16,4,128,256]{3,2,1,0:T(8,128)(2,1)}, u32[]{:S(2)}, u32[]{:S(2)}) async-start(bf16[16,4,128,256]{3,2,1,0:T(8,128)(2,1)} %half_transform.7), calls=%async_computation | async-start | bytes 8388608 | tf_op jit(solution)/shard_map/all_to_all | solution.py:258
Sparse Core Ops, SparseCore 0:
  151.0 138.8 all-gather.1

commit v3 on v2

--- a/solution.py
+++ b/solution.py
@@ -10,6 +10,7 @@
 BOTH = ("aux", "occ")
 VMEM_BYTES = 58 * 2**20
 PANEL = 16
+GROUP = 4
 SCALE = 2.0**40
 PIVOT_FLOOR = 1e-6
 
@@ -111,7 +112,7 @@
     return rows, (rest, diagonals)
 
 
-def half_kernel(low_block, list_ref, count_ref, ints_ref, basis_ref, out_ref, rows_ref):
+def half_kernel(low_block, list_ref, count_ref, ints_ref, basis_ref, out_ref, rows_ref, window_ref):
     block = pl.program_id(0)
     slots, aux_width, size_block = ints_ref.shape[1:4]
     vectors = basis_ref.shape[0] // 2
@@ -129,30 +130,34 @@
         where_slot.append(slot_of)
         is_used.append(used > 0)
 
-    def one(p, carry):
-        rows = []
-        for m in range(side):
-            row = []
-            for n in range(low_block, side):
-                pair = m * side + n
-                tile = ints_ref[0, where_slot[pair], p]
-                row.append(jnp.where(is_used[pair], tile, jnp.zeros_like(tile)))
-            rows.append(jnp.concatenate(row, axis=1))
-        window = jnp.concatenate(rows, axis=0)
+    for m in range(side):
+        for n in range(low_block, side):
+            pair = m * side + n
+            tile = ints_ref[0, where_slot[pair]]
+            column = (n - low_block) * size_block
+            window_ref[:, m * size_block : (m + 1) * size_block, column : column + size_block] = (
+                jnp.where(is_used[pair], tile, jnp.zeros_like(tile))
+            )
+
+    def some(group, carry):
+        low = group * GROUP
+        window = window_ref[pl.ds(low, GROUP)]
         product = lax.dot_general(
             basis_ref[:, low_block * size_block :],
-            window,
+            window.reshape(GROUP * window.shape[1], window.shape[2]),
             (((1,), (1,)), ((), ())),
             preferred_element_type=jnp.float32,
         )
         product = product[:vectors] + product[vectors:]
-        for m in range(side):
-            rows_ref[m, pl.ds(p, vectors, stride=aux_width), :] = product[
-                :, m * size_block : (m + 1) * size_block
-            ]
+        for p in range(GROUP):
+            for m in range(side):
+                column = (p * side + m) * size_block
+                rows_ref[m, pl.ds(low + p, vectors, stride=aux_width), :] = product[
+                    :, column : column + size_block
+                ]
         return carry
 
-    lax.fori_loop(0, aux_width, one, 0, unroll=2)
+    lax.fori_loop(0, aux_width // GROUP, some, 0)
     for m in range(side):
         out_ref[..., m * size_block : (m + 1) * size_block] = (
             rows_ref[m].astype(jnp.bfloat16).reshape(out_ref.shape[:-1] + (size_block,))
@@ -183,7 +188,11 @@
             scratch_shapes=[
                 pltpu.VMEM(
                     (basis_total // size_block, vectors * aux_width, size_block), jnp.float32
-                )
+                ),
+                pltpu.VMEM(
+                    (aux_width, basis_total, basis_total - start // size_block * size_block),
+                    jnp.bfloat16,
+                ),
             ],
         ),
         compiler_params=pltpu.CompilerParams(vmem_limit_bytes=VMEM_BYTES),
@@ -198,16 +207,22 @@
 
 def fit_kernel(step_rows, factor_ref, half_ref, before_ref, out_ref):
     aux_total = factor_ref.shape[0]
-    columns = half_ref[...].reshape(aux_total, half_ref.shape[-1])
+    basis_total = out_ref.shape[0]
+    steps = half_ref.shape[1]
+    columns = jnp.concatenate(
+        [half_ref[:, k].reshape(aux_total, basis_total) for k in range(steps)], axis=1
+    )
     total = jnp.zeros(out_ref.shape, jnp.float32)
     for low in range(0, aux_total, step_rows):
         high = low + step_rows
         fitted = jnp.dot(
             factor_ref[low:high, :high], columns[:high], preferred_element_type=jnp.float32
         ).astype(jnp.bfloat16)
-        total = total + lax.dot_general(
-            fitted, fitted, (((0,), (0,)), ((), ())), preferred_element_type=jnp.float32
-        )
+        for k in range(steps):
+            one = fitted[:, k * basis_total : (k + 1) * basis_total]
+            total = total + lax.dot_general(
+                one, one, (((0,), (0,)), ((), ())), preferred_element_type=jnp.float32
+            )
 
     @pl.when(pl.program_id(0) == 0)
     def _():
@@ -221,15 +236,16 @@
 def fit_exchange(factor, arrived, before):
     devices, own, aux_local, basis_total = arrived.shape
     aux_total = factor.shape[0]
+    steps = 2 if own % 2 == 0 else 1
     return pl.pallas_call(
         functools.partial(fit_kernel, aux_total // 8),
         out_shape=jax.ShapeDtypeStruct((basis_total, basis_total), jnp.float32),
-        grid=(own,),
+        grid=(own // steps,),
         in_specs=[
             pl.BlockSpec(
                 (aux_total, aux_total), lambda k: (0, 0), pipeline_mode=pl.Buffered(1)
             ),
-            pl.BlockSpec((devices, 1, aux_local, basis_total), lambda k: (0, k, 0, 0)),
+            pl.BlockSpec((devices, steps, aux_local, basis_total), lambda k: (0, k, 0, 0)),
             pl.BlockSpec((basis_total, basis_total), lambda k: (0, 0)),
         ],
         out_specs=pl.BlockSpec((basis_total, basis_total), lambda k: (0, 0)),
@@ -243,20 +259,67 @@
     )(factor, arrived, before)
 
 
+def line_step(step, upward, downward, axis):
+    devices = lax.axis_size(axis)
+    upward = lax.ppermute(upward, axis, [(i, i + 1) for i in range(step, devices - 1)])
+    downward = lax.ppermute(downward, axis, [(i, i - 1) for i in range(1, devices - step)])
+    return upward, downward
+
+
+def line_blocks(block, passed, axis):
+    devices = lax.axis_size(axis)
+    up, down = [pair[0] for pair in passed], [pair[1] for pair in passed]
+    around = jnp.stack(up[::-1] + [block] + down)
+    first = devices - 1 - lax.axis_index(axis)
+    blocks = lax.dynamic_slice_in_dim(around, first, devices, 0)
+    return blocks.reshape(devices * block.shape[0], block.shape[1])
+
+
+def chunk_sizes(own):
+    if own % 8 == 0:
+        return [own // 8, 3 * own // 8, 3 * own // 8, own // 8]
+    return [1] * own
+
+
 def per_device(integrals, pair_list, pair_count, coefficients, metric):
     devices = lax.axis_size("aux") * lax.axis_size("occ")
     basis_total = coefficients.shape[0]
-    chunks = min(4, basis_total // devices)
-    width = basis_total // chunks
-    factor = lax.all_gather(metric, BOTH, axis=0, tiled=True)
+    passed = [line_step(0, metric, metric, "occ")]
     total = jnp.zeros((basis_total, basis_total), jnp.float32)
     state = (coefficients,)
-    for chunk in range(chunks):
-        rows, state = factor_rows(chunk * width, width, basis_total, state)
-        half = half_transform(integrals, pair_list, pair_count, rows, chunk * width, devices)
-        half, state = lax.optimization_barrier((half, state))
+    start = 0
+    arrived = None
+    factor = None
+    waiting = []
+    for chunk, own in enumerate(chunk_sizes(basis_total // devices)):
+        width = own * devices
+        rows, state = factor_rows(start, width, basis_total, state)
+        if chunk == 0:
+            rows, passed[0] = lax.optimization_barrier((rows, passed[0]))
+            passed.append(line_step(1, *passed[0], "occ"))
+        half = half_transform(integrals, pair_list, pair_count, rows, start, devices)
+        if chunk == 0:
+            half, state, passed[1] = lax.optimization_barrier((half, state, passed[1]))
+            for step in range(2, lax.axis_size("occ") - 1):
+                passed.append(line_step(step, *passed[-1], "occ"))
+            line = line_blocks(metric, passed, "occ")
+        elif chunk == 1:
+            half, state, arrived, line = lax.optimization_barrier((half, state, arrived, line))
+            factor = lax.all_gather(line, "aux", axis=0, tiled=True)
+        elif chunk == 2:
+            half, state, arrived, factor = lax.optimization_barrier(
+                (half, state, arrived, factor)
+            )
+        else:
+            half, state, arrived = lax.optimization_barrier((half, state, arrived))
+        if chunk > 0:
+            waiting.append(arrived)
+        if chunk > 1:
+            total = fit_exchange(factor, waiting.pop(0), total)
         arrived = lax.all_to_all(half, BOTH, split_axis=0, concat_axis=0, tiled=True)
-        total = fit_exchange(factor, arrived, total)
+        start += width
+    for piece in waiting + [arrived]:
+        total = fit_exchange(factor, piece, total)
     shares = total.reshape(devices, basis_total // devices, basis_total)
     return jnp.sum(lax.all_to_all(shares, BOTH, split_axis=0, concat_axis=0, tiled=True), axis=0)
 

time: 526 us -> 485 us (0.922)
  waiting for transfers between devices: 290 us -> 234 us
  starting transfers between devices: 21.3 us -> 34.4 us
  Pallas kernels: 185 us -> 178 us
  local copies, waits for them, and re-layouts: 2.08 us -> 8.66 us
    all_to_all x4, waiting for transfers between devices: 289 us -> 225 us  [per_device(): lax.all_to_all(half, BOTH, split_axis=0, concat_axis=0, tiled=True)]
    ppermute x0 -> x6, starting transfers between devices: none -> 11.7 us  [the longest x3 7.84 us: line_step(): lax.ppermute(upward, axis, [(i, i + 1) for i in range(step, devices - 1)])]
    ppermute x0 -> x6, waiting for transfers between devices: none -> 9.08 us  [the longest x3 6.55 us: line_step(): lax.ppermute(downward, axis, [(i, i - 1) for i in range(1, devices - step)])]
    pallas_call x4, Pallas kernels: 76.7 us -> 68.3 us  [half_transform(): pl.pallas_call(functools.partial(half_kernel, start // size_block), out_s...]
  transfers between devices with their start and end apart: 5 -> 11, of which waited for: 4 -> 7; matrix products, arithmetic and copies ran while one was open for 0% -> 1% of each run, Pallas kernels for 26% -> 35%
where the time goes in v3:
time: 485 us; the launch traced here: 484 us
  waiting for transfers between devices  234 us (48%)
  Pallas kernels  178 us (37%)
  starting transfers between devices  34.4 us (7%)
  blocking collectives  14.6 us (3%)
  between operations  13.6 us (3%)
  local copies, waits for them, and re-layouts  8.66 us (2%)
    all_to_all x4, waiting for transfers between devices, per_device(): lax.all_to_all(half, BOTH, split_axis=0, concat_axis=0, tiled=True)  225 us
    pallas_call x4, Pallas kernels, half_transform(): pl.pallas_call(functools.partial(half_kernel, start // size_block), out_s...  68.3 us
    pallas_call x4, Pallas kernels, fit_exchange(): pl.pallas_call(functools.partial(fit_kernel, aux_total // 8), out_shape=j...  56.6 us
    pallas_call x4, Pallas kernels, factor_rows(): pl.pallas_call(functools.partial(factor_kernel, start), out_shape=(jax.Sh...  53 us
    all_to_all x4, starting transfers between devices, per_device(): lax.all_to_all(half, BOTH, split_axis=0, concat_axis=0, tiled=True)  22.6 us
    all_to_all x1, blocking collectives, per_device(): lax.all_to_all(shares, BOTH, split_axis=0, concat_axis=0, tiled=True)  14.6 us
  transfers between devices with their start and end apart: 11, of which 7 were waited for; matrix products, arithmetic and copies ran while one was open for 1% of the time, Pallas kernels for 35%

profile of v3, /device:TPU:0, one launch (start us, length us, event | category | flops | bytes accessed | tf_op | source)
XLA Modules:
  0.0 483.6 jit_solution(10041132471620595772)
XLA Ops:
  6.5 5.0 %collective-permute-start = (bf16[128,2048]{1,0:T(8,128)(2,1)}, bf16[128,2048]{1,0:T(8,128)(2,1)S(1)}, u32[]{:S(2)}, u32[]{:S(2)}) collective-permute-start(bf16[128,2048]{1,0:T(8,128)(2,1)} %param.9), channel_id=1, source_target_pairs={{0,1},{1,2},{2,3},{4,5},{5,6},{6,7},{8,9},{9,10},{10,11},{12,13},{... | collective-permute-start | bytes 1572872 | tf_op jit(solution)/shard_map/ppermute | solution.py:264
  11.5 1.3 collective-permute-start.1
  12.8 7.6 %factor_rows.4 = (bf16[64,256]{1,0:T(8,128)(2,1)}, f32[256,256]{1,0:T(8,128)}, f32[8,256]{1,0:T(8,128)}) custom-call(bf16[256,384]{1,0:T(8,128)(2,1)} %refs_0_.1), custom_call_target="tpu_custom_call" | custom-call | tf_op jit(solution)/shard_map/factor_rows/pallas_call | solution.py:102
  20.4 2.5 collective-permute-done
  22.9 4.0 collective-permute-done.1
  27.0 1.4 collective-permute-start.2
  28.4 1.3 collective-permute-start.3
  29.7 1.3 copy.8.list_ref
  31.1 16.8 %half_transform.4 = bf16[16,2,128,256]{3,2,1,0:T(8,128)(2,1)} custom-call(s32[8,4]{1,0:T(8,128)} %copy.8.list_ref, s32[8]{0:T(128)} %count_ref.7, bf16[8,4,16,128,128]{4,3,2,1,0:T(8,128)(2,1)} %ints_ref.7, bf16[64,256]{1,0:T(8,128)(2,1)} %get-tuple-element.36.basis_ref), custom_call_target="tpu_custom_call" | custom-call | flops 1073741824 | bytes 18874368 | tf_op jit(solution)/shard_map/half_transform/pallas_call | solution.py:171
  47.9 0.0 collective-permute-done.2
  47.9 0.0 collective-permute-done.3
  47.9 0.0 copy-start.3
  47.9 1.4 collective-permute-start.4
  49.4 0.0 copy-done.3
  49.4 9.4 %all-to-all-start = ((bf16[16,2,128,256]{3,2,1,0:T(8,128)(2,1)}), bf16[16,2,128,256]{3,2,1,0:T(8,128)(2,1)S(1)}, u32[]{:S(2)}, u32[]{:S(2)}) async-start(bf16[16,2,128,256]{3,2,1,0:T(8,128)(2,1)} %half_transform.4), calls=%async_computation | async-start | bytes 4194304 | tf_op jit(solution)/shard_map/all_to_all | solution.py:319
  58.8 0.0 all-gather.2.cloned.1.call-start
  58.8 1.3 collective-permute-start.5
  60.1 18.9 %factor_rows.5 = (bf16[192,256]{1,0:T(8,128)(2,1)}, f32[256,256]{1,0:T(8,128)}, f32[8,256]{1,0:T(8,128)}) custom-call(f32[256,256]{1,0:T(8,128)} %get-tuple-element.41.refs_0_, f32[8,256]{1,0:T(8,128)} %get-tuple-element.42.refs_1_), custom_call_target="tpu_custom_call" | custom-call | tf_op jit(solution)/shard_map/factor_rows/pallas_call | solution.py:102
  79.1 0.0 copy-start.2
  79.1 20.0 %half_transform.5 = bf16[16,6,128,256]{3,2,1,0:T(8,128)(2,1)} custom-call(s32[8,4]{1,0:T(8,128)} %copy.8.list_ref, s32[8]{0:T(128)} %count_ref.7, bf16[8,4,16,128,128]{4,3,2,1,0:T(8,128)(2,1)} %ints_ref.7, bf16[192,256]{1,0:T(8,128)(2,1)} %get-tuple-element.43.basis_ref), custom_call_target="tpu_custom_call" | custom-call | flops 3221225472 | bytes 23068672 | tf_op jit(solution)/shard_map/half_transform/pallas_call | solution.py:171
  99.1 0.0 copy-start.4
  99.1 0.0 collective-permute-done.4
  99.1 1.1 bitcast_dynamic-update-slice_fusion.6
  100.3 1.1 bitcast_dynamic-update-slice_fusion.5
  101.4 0.0 copy-done.2
  101.5 0.0 copy-done.4
  101.5 2.5 collective-permute-done.5
  104.1 1.5 constant_dynamic-slice_fusion
  105.6 2.7 all-to-all-done.half_ref
  108.2 0.0 copy-start
  108.2 0.0 all-gather.2.cloned.1.call-update
  108.3 1.3 copy-done
  109.6 4.7 all-to-all-start.1
  114.2 19.0 %factor_rows.6 = (bf16[192,256]{1,0:T(8,128)(2,1)}, f32[256,256]{1,0:T(8,128)}, f32[8,256]{1,0:T(8,128)}) custom-call(f32[256,256]{1,0:T(8,128)} %get-tuple-element.49.refs_0_, f32[8,256]{1,0:T(8,128)} %get-tuple-element.50.refs_1_), custom_call_target="tpu_custom_call" | custom-call | tf_op jit(solution)/shard_map/factor_rows/pallas_call | solution.py:102
  133.2 17.1 %half_transform.6 = bf16[16,6,128,256]{3,2,1,0:T(8,128)(2,1)} custom-call(s32[8,4]{1,0:T(8,128)} %copy.8.list_ref, s32[8]{0:T(128)} %count_ref.7, bf16[8,4,16,128,128]{4,3,2,1,0:T(8,128)(2,1)} %ints_ref.7, bf16[192,256]{1,0:T(8,128)(2,1)} %get-tuple-element.51.basis_ref), custom_call_target="tpu_custom_call" | custom-call | flops 3221225472 | bytes 23068672 | tf_op jit(solution)/shard_map/half_transform/pallas_call | solution.py:171
  150.3 103.3 %all-to-all-done.1.half_ref = bf16[16,6,128,256]{3,2,1,0:T(8,128)(2,1)} async-done(((bf16[16,6,128,256]{3,2,1,0:T(8,128)(2,1)}), bf16[16,6,128,256]{3,2,1,0:T(8,128)(2,1)}, u32[]{:S(2)}, u32[]{:S(2)}) %all-to-all-start.1) | async-done | bytes 6291488 | tf_op jit(solution)/shard_map/all_to_all | solution.py:319
  253.6 0.0 all-gather.2.cloned.1.call-done.factor_ref
  253.6 4.6 all-to-all-start.2
  258.3 7.5 %factor_rows.7 = (bf16[64,256]{1,0:T(8,128)(2,1)}, f32[256,256]{1,0:T(8,128)}, f32[8,256]{1,0:T(8,128)}) custom-call(f32[256,256]{1,0:T(8,128)} %get-tuple-element.57.refs_0_, f32[8,256]{1,0:T(8,128)} %get-tuple-element.58.refs_1_), custom_call_target="tpu_custom_call" | custom-call | tf_op jit(solution)/shard_map/factor_rows/pallas_call | solution.py:102
  265.7 14.3 %half_transform.7 = bf16[16,2,128,256]{3,2,1,0:T(8,128)(2,1)} custom-call(s32[8,4]{1,0:T(8,128)} %copy.8.list_ref, s32[8]{0:T(128)} %count_ref.7, bf16[8,4,16,128,128]{4,3,2,1,0:T(8,128)(2,1)} %ints_ref.7, bf16[64,256]{1,0:T(8,128)(2,1)} %get-tuple-element.59.basis_ref), custom_call_target="tpu_custom_call" | custom-call | flops 1073741824 | bytes 18874368 | tf_op jit(solution)/shard_map/half_transform/pallas_call | solution.py:171
  280.0 117.6 %all-to-all-done.2.half_ref = bf16[16,6,128,256]{3,2,1,0:T(8,128)(2,1)} async-done(((bf16[16,6,128,256]{3,2,1,0:T(8,128)(2,1)}), bf16[16,6,128,256]{3,2,1,0:T(8,128)(2,1)}, u32[]{:S(2)}, u32[]{:S(2)}) %all-to-all-start.2) | async-done | bytes 6291488 | tf_op jit(solution)/shard_map/all_to_all | solution.py:319
  397.6 3.9 all-to-all-start.3
  401.5 0.7 broadcast_in_dim.3.before_ref
  402.2 9.4 %fit_exchange.4.before_ref = f32[256,256]{1,0:T(8,128)} custom-call(bf16[2048,2048]{1,0:T(8,128)(2,1)} %all-gather.2.cloned.1.call-done.factor_ref, bf16[16,2,128,256]{3,2,1,0:T(8,128)(2,1)} %copy-done, f32[256,256]{1,0:T(8,128)} %broadcast_in_dim.3.before_ref), custom_call_target="tpu_custom_call" | custom-call | flops 2952790016 | bytes 10485760 | tf_op jit(solution)/shard_map/fit_exchange/pallas_call | solution.py:240
  411.7 18.9 %fit_exchange.5.before_ref = f32[256,256]{1,0:T(8,128)} custom-call(bf16[2048,2048]{1,0:T(8,128)(2,1)} %all-gather.2.cloned.1.call-done.factor_ref, bf16[16,6,128,256]{3,2,1,0:T(8,128)(2,1)} %all-to-all-done.1.half_ref, f32[256,256]{1,0:T(8,128)} %fit_exchange.4.before_ref), custom_call_target="tpu_custom_call" | custom-call | flops 8858370048 | bytes 14680064 | tf_op jit(solution)/shard_map/fit_exchange/pallas_call | solution.py:240
  430.6 18.9 %fit_exchange.6.before_ref = f32[256,256]{1,0:T(8,128)} custom-call(bf16[2048,2048]{1,0:T(8,128)(2,1)} %all-gather.2.cloned.1.call-done.factor_ref, bf16[16,6,128,256]{3,2,1,0:T(8,128)(2,1)} %all-to-all-done.2.half_ref, f32[256,256]{1,0:T(8,128)} %fit_exchange.5.before_ref), custom_call_target="tpu_custom_call" | custom-call | flops 8858370048 | bytes 14680064 | tf_op jit(solution)/shard_map/fit_exchange/pallas_call | solution.py:240
  449.5 1.2 all-to-all-done.3.half_ref
  450.7 0.0 copy-start.1
  450.7 1.4 copy-done.1
  452.1 9.4 %fit_exchange.7 = f32[256,256]{1,0:T(8,128)} custom-call(bf16[2048,2048]{1,0:T(8,128)(2,1)} %all-gather.2.cloned.1.call-done.factor_ref, bf16[16,2,128,256]{3,2,1,0:T(8,128)(2,1)} %copy-done.1, f32[256,256]{1,0:T(8,128)} %fit_exchange.6.before_ref), custom_call_target="tpu_custom_call" | custom-call | flops 2952790016 | bytes 10485760 | tf_op jit(solution)/shard_map/fit_exchange/pallas_call | solution.py:240
  461.5 14.6 %all_to_all.25 = f32[16,16,256]{2,1,0:T(8,128)S(1)} all-to-all(f32[16,16,256]{2,1,0:T(8,128)} %bitcast.17), channel_id=1, replica_groups=mesh['grp'=2,'aux'=4,'occ'=4] {'aux','occ'}, dimensions={0} | all-to-all | bytes 524288 | tf_op jit(solution)/shard_map/all_to_all | solution.py:324
  476.1 0.6 reduce_sum.9
  (5 shorter events, 0.2 us)
Async XLA Ops:
  6.5 16.4 %collective-permute-start = (bf16[128,2048]{1,0:T(8,128)(2,1)}, bf16[128,2048]{1,0:T(8,128)(2,1)S(1)}, u32[]{:S(2)}, u32[]{:S(2)}) collective-permute-start(bf16[128,2048]{1,0:T(8,128)(2,1)} %param.9), channel_id=1, source_target_pairs={{0,1},{1,2},{2,3},{4,5},{5,6},{6,7},{8,9},{9,10},{10,11},{12,13},{... | collective-permute-start | bytes 1572872 | tf_op jit(solution)/shard_map/ppermute | solution.py:264
  11.5 15.5 %collective-permute-start.1 = (bf16[128,2048]{1,0:T(8,128)(2,1)}, bf16[128,2048]{1,0:T(8,128)(2,1)S(1)}, u32[]{:S(2)}, u32[]{:S(2)}) collective-permute-start(bf16[128,2048]{1,0:T(8,128)(2,1)} %param.9), channel_id=1, source_target_pairs={{1,0},{2,1},{3,2},{5,4},{6,5},{7,6},{9,8},{10,9},{11,10},{13,12},{... | collective-permute-start | bytes 1572872 | tf_op jit(solution)/shard_map/ppermute | solution.py:265
  27.0 20.9 %collective-permute-start.2 = (bf16[128,2048]{1,0:T(8,128)(2,1)S(1)}, bf16[128,2048]{1,0:T(8,128)(2,1)}, u32[]{:S(2)}, u32[]{:S(2)}) collective-permute-start(bf16[128,2048]{1,0:T(8,128)(2,1)S(1)} %collective-permute-done), channel_id=1, source_target_pairs={{1,2},{2,3},{5,6},{6,7},{9,10},{10,11},{13,14},{14,15},{17,18},{18... | collective-permute-start | bytes 1572872 | tf_op jit(solution)/shard_map/ppermute | solution.py:264
  28.4 19.5 %collective-permute-start.3 = (bf16[128,2048]{1,0:T(8,128)(2,1)S(1)}, bf16[128,2048]{1,0:T(8,128)(2,1)S(1)}, u32[]{:S(2)}, u32[]{:S(2)}) collective-permute-start(bf16[128,2048]{1,0:T(8,128)(2,1)S(1)} %collective-permute-done.1), channel_id=1, source_target_pairs={{1,0},{2,1},{5,4},{6,5},{9,8},{10,9},{13,12},{14,13},{17,16},{18,1... | collective-permute-start | bytes 1572872 | tf_op jit(solution)/shard_map/ppermute | solution.py:265
  47.9 1.5 copy-start.3
  47.9 51.2 %collective-permute-start.4 = (bf16[128,2048]{1,0:T(8,128)(2,1)}, bf16[128,2048]{1,0:T(8,128)(2,1)}, u32[]{:S(2)}, u32[]{:S(2)}) collective-permute-start(bf16[128,2048]{1,0:T(8,128)(2,1)} %collective-permute-done.2), channel_id=1, source_target_pairs={{2,3},{6,7},{10,11},{14,15},{18,19},{22,23},{26,27},{30,31}} | collective-permute-start | bytes 1572872 | tf_op jit(solution)/shard_map/ppermute | solution.py:264
  49.4 58.9 %all-to-all-start = ((bf16[16,2,128,256]{3,2,1,0:T(8,128)(2,1)}), bf16[16,2,128,256]{3,2,1,0:T(8,128)(2,1)S(1)}, u32[]{:S(2)}, u32[]{:S(2)}) async-start(bf16[16,2,128,256]{3,2,1,0:T(8,128)(2,1)} %half_transform.4), calls=%async_computation | async-start | bytes 4194304 | tf_op jit(solution)/shard_map/all_to_all | solution.py:319
  58.8 194.8 %all-gather.2.cloned.1.call-start = ((), (), s32[]{:S(2)}) async-start(), calls=%async_computation.5 | async-start | bytes 10485760 | tf_op jit(solution)/shard_map/all_gather | solution.py:308
  58.8 45.2 %collective-permute-start.5 = (bf16[128,2048]{1,0:T(8,128)(2,1)}, bf16[128,2048]{1,0:T(8,128)(2,1)S(1)}, u32[]{:S(2)}, u32[]{:S(2)}) collective-permute-start(bf16[128,2048]{1,0:T(8,128)(2,1)} %copy-done.3), channel_id=1, source_target_pairs={{1,0},{5,4},{9,8},{13,12},{17,16},{21,20},{25,24},{29,28}} | collective-permute-start | bytes 1572872 | tf_op jit(solution)/shard_map/ppermute | solution.py:265
  79.1 22.3 %copy-start.2 = (bf16[128,2048]{1,0:T(8,128)(2,1)S(1)}, bf16[128,2048]{1,0:T(8,128)(2,1)}, u32[]{:S(2)}) copy-start(bf16[128,2048]{1,0:T(8,128)(2,1)} %param.9) | copy-start | bytes 1572868
  99.1 2.4 copy-start.4
  108.2 1.3 copy-start
  109.6 144.0 %all-to-all-start.1 = ((bf16[16,6,128,256]{3,2,1,0:T(8,128)(2,1)}), bf16[16,6,128,256]{3,2,1,0:T(8,128)(2,1)}, u32[]{:S(2)}, u32[]{:S(2)}) async-start(bf16[16,6,128,256]{3,2,1,0:T(8,128)(2,1)} %half_transform.5), calls=%async_computation.1 | async-start | bytes 12582912 | tf_op jit(solution)/shard_map/all_to_all | solution.py:319
  253.6 144.0 %all-to-all-start.2 = ((bf16[16,6,128,256]{3,2,1,0:T(8,128)(2,1)}), bf16[16,6,128,256]{3,2,1,0:T(8,128)(2,1)}, u32[]{:S(2)}, u32[]{:S(2)}) async-start(bf16[16,6,128,256]{3,2,1,0:T(8,128)(2,1)} %half_transform.6), calls=%async_computation.2 | async-start | bytes 12582912 | tf_op jit(solution)/shard_map/all_to_all | solution.py:319
  397.6 53.1 %all-to-all-start.3 = ((bf16[16,2,128,256]{3,2,1,0:T(8,128)(2,1)}), bf16[16,2,128,256]{3,2,1,0:T(8,128)(2,1)S(1)}, u32[]{:S(2)}, u32[]{:S(2)}) async-start(bf16[16,2,128,256]{3,2,1,0:T(8,128)(2,1)} %half_transform.7), calls=%async_computation.3 | async-start | bytes 4194304 | tf_op jit(solution)/shard_map/all_to_all | solution.py:319
  450.7 1.4 copy-start.1
Sparse Core Ops, SparseCore 0:
  108.4 118.7 all-gather.1

commit v4 on v3

--- a/solution.py
+++ b/solution.py
@@ -112,7 +112,8 @@
     return rows, (rest, diagonals)
 
 
-def half_kernel(low_block, list_ref, count_ref, ints_ref, basis_ref, out_ref, rows_ref, window_ref):
+def half_kernel(low_block, list_ref, count_ref, me_ref, ints_ref, basis_ref, *refs):
+    out_refs, (rows_ref, window_ref) = refs[:-2], refs[-2:]
     block = pl.program_id(0)
     slots, aux_width, size_block = ints_ref.shape[1:4]
     vectors = basis_ref.shape[0] // 2
@@ -158,23 +159,29 @@
         return carry
 
     lax.fori_loop(0, aux_width // GROUP, some, 0)
-    for m in range(side):
-        out_ref[..., m * size_block : (m + 1) * size_block] = (
-            rows_ref[m].astype(jnp.bfloat16).reshape(out_ref.shape[:-1] + (size_block,))
-        )
-
-
-def half_transform(integrals, pair_list, pair_count, basis_rows, start, devices):
+    share = vectors // len(out_refs) * aux_width
+    for slot, out_ref in enumerate(out_refs):
+        low = pl.multiple_of((me_ref[0] ^ slot) * share, share)
+        for m in range(side):
+            out_ref[..., m * size_block : (m + 1) * size_block] = (
+                rows_ref[m, pl.ds(low, share), :]
+                .astype(jnp.bfloat16)
+                .reshape(out_ref.shape[:-1] + (size_block,))
+            )
+
+
+def half_transform(integrals, pair_list, pair_count, me, basis_rows, start, devices):
     blocks, slots, aux_width, size_block, _ = integrals.shape
     vectors, basis_total = basis_rows.shape[0] // 2, basis_rows.shape[1]
     own = vectors // devices
     return pl.pallas_call(
         functools.partial(half_kernel, start // size_block),
-        out_shape=jax.ShapeDtypeStruct(
-            (devices, own, blocks * aux_width, basis_total), jnp.bfloat16
-        ),
+        out_shape=[
+            jax.ShapeDtypeStruct((own, blocks * aux_width, basis_total), jnp.bfloat16)
+        ]
+        * devices,
         grid_spec=pltpu.PrefetchScalarGridSpec(
-            num_scalar_prefetch=2,
+            num_scalar_prefetch=3,
             grid=(blocks,),
             in_specs=[
                 pl.BlockSpec(
@@ -182,9 +189,8 @@
                 ),
                 pl.BlockSpec(basis_rows.shape, lambda b, *_: (0, 0)),
             ],
-            out_specs=pl.BlockSpec(
-                (devices, own, aux_width, basis_total), lambda b, *_: (0, 0, b, 0)
-            ),
+            out_specs=[pl.BlockSpec((own, aux_width, basis_total), lambda b, *_: (0, b, 0))]
+            * devices,
             scratch_shapes=[
                 pltpu.VMEM(
                     (basis_total // size_block, vectors * aux_width, size_block), jnp.float32
@@ -202,21 +208,25 @@
             transcendentals=0,
         ),
         name="half_transform",
-    )(pair_list, pair_count, integrals, basis_rows)
-
-
-def fit_kernel(step_rows, factor_ref, half_ref, before_ref, out_ref):
+    )(pair_list, pair_count, me, integrals, basis_rows)
+
+
+def fit_kernel(step_rows, me_ref, factor_ref, before_ref, *refs):
+    half_refs, (out_ref, columns_ref) = refs[:-2], refs[-2:]
     aux_total = factor_ref.shape[0]
     basis_total = out_ref.shape[0]
-    steps = half_ref.shape[1]
-    columns = jnp.concatenate(
-        [half_ref[:, k].reshape(aux_total, basis_total) for k in range(steps)], axis=1
-    )
+    steps, aux_local = half_refs[0].shape[:2]
+    for slot, half_ref in enumerate(half_refs):
+        low = pl.multiple_of((me_ref[0] ^ slot) * aux_local, aux_local)
+        for k in range(steps):
+            columns_ref[pl.ds(low, aux_local), k * basis_total : (k + 1) * basis_total] = (
+                half_ref[k]
+            )
     total = jnp.zeros(out_ref.shape, jnp.float32)
     for low in range(0, aux_total, step_rows):
         high = low + step_rows
         fitted = jnp.dot(
-            factor_ref[low:high, :high], columns[:high], preferred_element_type=jnp.float32
+            factor_ref[low:high, :high], columns_ref[:high], preferred_element_type=jnp.float32
         ).astype(jnp.bfloat16)
         for k in range(steps):
             one = fitted[:, k * basis_total : (k + 1) * basis_total]
@@ -233,46 +243,68 @@
         out_ref[...] += total
 
 
-def fit_exchange(factor, arrived, before):
-    devices, own, aux_local, basis_total = arrived.shape
+def fit_exchange(me, factor, arrived, before):
+    own, aux_local, basis_total = arrived[0].shape
     aux_total = factor.shape[0]
     steps = 2 if own % 2 == 0 else 1
     return pl.pallas_call(
         functools.partial(fit_kernel, aux_total // 8),
         out_shape=jax.ShapeDtypeStruct((basis_total, basis_total), jnp.float32),
-        grid=(own // steps,),
-        in_specs=[
-            pl.BlockSpec(
-                (aux_total, aux_total), lambda k: (0, 0), pipeline_mode=pl.Buffered(1)
-            ),
-            pl.BlockSpec((devices, steps, aux_local, basis_total), lambda k: (0, k, 0, 0)),
-            pl.BlockSpec((basis_total, basis_total), lambda k: (0, 0)),
-        ],
-        out_specs=pl.BlockSpec((basis_total, basis_total), lambda k: (0, 0)),
+        grid_spec=pltpu.PrefetchScalarGridSpec(
+            num_scalar_prefetch=1,
+            grid=(own // steps,),
+            in_specs=[
+                pl.BlockSpec(
+                    (aux_total, aux_total), lambda k, *_: (0, 0), pipeline_mode=pl.Buffered(1)
+                ),
+                pl.BlockSpec((basis_total, basis_total), lambda k, *_: (0, 0)),
+            ]
+            + [pl.BlockSpec((steps, aux_local, basis_total), lambda k, *_: (k, 0, 0))]
+            * len(arrived),
+            out_specs=pl.BlockSpec((basis_total, basis_total), lambda k, *_: (0, 0)),
+            scratch_shapes=[pltpu.VMEM((aux_total, steps * basis_total), jnp.bfloat16)],
+        ),
         compiler_params=pltpu.CompilerParams(vmem_limit_bytes=VMEM_BYTES),
         cost_estimate=pl.CostEstimate(
             flops=own * aux_total * basis_total * (aux_total * 9 // 8 + 2 * basis_total),
-            bytes_accessed=(factor.size + arrived.size) * 2,
+            bytes_accessed=(factor.size + own * aux_total * basis_total) * 2,
             transcendentals=0,
         ),
         name="fit_exchange",
-    )(factor, arrived, before)
-
-
-def line_step(step, upward, downward, axis):
-    devices = lax.axis_size(axis)
-    upward = lax.ppermute(upward, axis, [(i, i + 1) for i in range(step, devices - 1)])
-    downward = lax.ppermute(downward, axis, [(i, i - 1) for i in range(1, devices - step)])
-    return upward, downward
-
-
-def line_blocks(block, passed, axis):
-    devices = lax.axis_size(axis)
-    up, down = [pair[0] for pair in passed], [pair[1] for pair in passed]
-    around = jnp.stack(up[::-1] + [block] + down)
-    first = devices - 1 - lax.axis_index(axis)
-    blocks = lax.dynamic_slice_in_dim(around, first, devices, 0)
-    return blocks.reshape(devices * block.shape[0], block.shape[1])
+    )(me, factor, before, *arrived)
+
+
+def line_near(block):
+    up = lax.ppermute(block, "occ", [(0, 1), (1, 2), (2, 3)])
+    down = lax.ppermute(block, "occ", [(3, 2), (2, 1), (1, 0)])
+    far = lax.ppermute(block, "occ", [(0, 2), (3, 1)])
+    return up, down, far
+
+
+def line_ends(block, up, down, far):
+    me = lax.axis_index("occ")
+    left = me < 2
+    later = lax.ppermute(
+        jnp.stack([jnp.where(left, down, up), far]), "occ", [(1, 0), (2, 3)]
+    )
+    order = lax.switch(
+        me,
+        [
+            lambda: (block, down, later[0], later[1]),
+            lambda: (up, block, down, far),
+            lambda: (far, up, block, down),
+            lambda: (later[1], later[0], up, block),
+        ],
+    )
+    return jnp.concatenate(order)
+
+
+def exchange(pieces):
+    count = len(pieces)
+    return [pieces[0]] + [
+        lax.ppermute(pieces[slot], BOTH, [(i, i ^ slot) for i in range(count)])
+        for slot in range(1, count)
+    ]
 
 
 def chunk_sizes(own):
@@ -284,42 +316,36 @@
 def per_device(integrals, pair_list, pair_count, coefficients, metric):
     devices = lax.axis_size("aux") * lax.axis_size("occ")
     basis_total = coefficients.shape[0]
-    passed = [line_step(0, metric, metric, "occ")]
+    me = lax.axis_index(BOTH).reshape(1)
+    in_line = lax.axis_size("occ") == 4
+    near = line_near(metric) if in_line else ()
     total = jnp.zeros((basis_total, basis_total), jnp.float32)
     state = (coefficients,)
     start = 0
-    arrived = None
+    arrived = []
     factor = None
-    waiting = []
     for chunk, own in enumerate(chunk_sizes(basis_total // devices)):
         width = own * devices
         rows, state = factor_rows(start, width, basis_total, state)
+        half = half_transform(integrals, pair_list, pair_count, me, rows, start, devices)
         if chunk == 0:
-            rows, passed[0] = lax.optimization_barrier((rows, passed[0]))
-            passed.append(line_step(1, *passed[0], "occ"))
-        half = half_transform(integrals, pair_list, pair_count, rows, start, devices)
-        if chunk == 0:
-            half, state, passed[1] = lax.optimization_barrier((half, state, passed[1]))
-            for step in range(2, lax.axis_size("occ") - 1):
-                passed.append(line_step(step, *passed[-1], "occ"))
-            line = line_blocks(metric, passed, "occ")
-        elif chunk == 1:
-            half, state, arrived, line = lax.optimization_barrier((half, state, arrived, line))
-            factor = lax.all_gather(line, "aux", axis=0, tiled=True)
+            half, state, near = lax.optimization_barrier((half, state, near))
+            if in_line:
+                factor = lax.all_gather(line_ends(metric, *near), "aux", axis=0, tiled=True)
+            else:
+                factor = lax.all_gather(metric, BOTH, axis=0, tiled=True)
         elif chunk == 2:
-            half, state, arrived, factor = lax.optimization_barrier(
-                (half, state, arrived, factor)
+            half, state, arrived[0] = lax.optimization_barrier((half, state, arrived[0]))
+        elif chunk > 2:
+            half, state, arrived[chunk - 2], factor = lax.optimization_barrier(
+                (half, state, arrived[chunk - 2], factor)
             )
         else:
-            half, state, arrived = lax.optimization_barrier((half, state, arrived))
-        if chunk > 0:
-            waiting.append(arrived)
-        if chunk > 1:
-            total = fit_exchange(factor, waiting.pop(0), total)
-        arrived = lax.all_to_all(half, BOTH, split_axis=0, concat_axis=0, tiled=True)
+            half, state = lax.optimization_barrier((half, state))
+        arrived.append(exchange(half))
         start += width
-    for piece in waiting + [arrived]:
-        total = fit_exchange(factor, piece, total)
+    for pieces in arrived:
+        total = fit_exchange(me, factor, pieces, total)
     shares = total.reshape(devices, basis_total // devices, basis_total)
     return jnp.sum(lax.all_to_all(shares, BOTH, split_axis=0, concat_axis=0, tiled=True), axis=0)
 

time: 485 us -> 540 us (1.11)
  starting transfers between devices: 34.4 us -> 203 us
  waiting for transfers between devices: 234 us -> 115 us
    all_to_all x4 -> x0, waiting for transfers between devices: 225 us -> none  [per_device(): lax.all_to_all(half, BOTH, split_axis=0, concat_axis=0, tiled=True)]
    ppermute x6 -> x64, starting transfers between devices: 11.7 us -> 203 us  [the longest x60 190 us: exchange(): lax.ppermute(pieces[slot], BOTH, [(i, i ^ slot) for i in range(count)])]
    ppermute x6 -> x64, waiting for transfers between devices: 9.08 us -> 115 us  [the longest x60 90.1 us: exchange(): lax.ppermute(pieces[slot], BOTH, [(i, i ^ slot) for i in range(count)])]
    all_to_all x4 -> x0, starting transfers between devices: 22.6 us -> none  [per_device(): lax.all_to_all(half, BOTH, split_axis=0, concat_axis=0, tiled=True)]
  transfers between devices with their start and end apart: 11 -> 65, of which waited for: 7 -> 12; matrix products, arithmetic and copies ran while one was open for 1% -> 0% of each run, Pallas kernels for 35% -> 32%
where the time goes in v4:
time: 540 us; the launch traced here: 539 us
  starting transfers between devices  203 us (38%)
  Pallas kernels  182 us (34%)
  waiting for transfers between devices  115 us (21%)
  between operations  14.4 us (3%)
  blocking collectives  14.1 us (3%)
  local copies, waits for them, and re-layouts  6.37 us (1%)
    ppermute x60, starting transfers between devices, exchange(): lax.ppermute(pieces[slot], BOTH, [(i, i ^ slot) for i in range(count)])  190 us
    ppermute x60, waiting for transfers between devices, exchange(): lax.ppermute(pieces[slot], BOTH, [(i, i ^ slot) for i in range(count)])  90.1 us
    pallas_call x4, Pallas kernels, half_transform(): pl.pallas_call(functools.partial(half_kernel, start // size_block), out_s...  70 us
    pallas_call x4, Pallas kernels, fit_exchange(): pl.pallas_call(functools.partial(fit_kernel, aux_total // 8), out_shape=j...  58.7 us
    pallas_call x4, Pallas kernels, factor_rows(): pl.pallas_call(functools.partial(factor_kernel, start), out_shape=(jax.Sh...  53 us
    ppermute x1, waiting for transfers between devices, line_ends(): lax.ppermute(jnp.stack([jnp.where(left, down, up), far]), 'occ', [(1, 0),...  24.8 us
    all_to_all x1, blocking collectives, per_device(): lax.all_to_all(shares, BOTH, split_axis=0, concat_axis=0, tiled=True)  14.1 us
  transfers between devices with their start and end apart: 65, of which 12 were waited for; matrix products, arithmetic and copies ran while one was open for 0% of the time, Pallas kernels for 32%

profile of v4, /device:TPU:0, one launch (start us, length us, event | category | flops | bytes accessed | tf_op | source)
XLA Modules:
  0.0 539.2 jit_solution(1247027108452376735)
XLA Ops:
  6.5 6.0 %collective-permute-start.2 = (bf16[128,2048]{1,0:T(8,128)(2,1)}, bf16[128,2048]{1,0:T(8,128)(2,1)S(1)}, u32[]{:S(2)}, u32[]{:S(2)}) collective-permute-start(bf16[128,2048]{1,0:T(8,128)(2,1)} %param.13), channel_id=1, source_target_pairs={{0,2},{3,1},{4,6},{7,5},{8,10},{11,9},{12,14},{15,13},{16,18},{19,... | collective-permute-start | bytes 1572872 | tf_op jit(solution)/shard_map/ppermute | solution.py:280
  12.5 1.3 collective-permute-start.1
  13.8 4.6 collective-permute-start
  18.4 1.3 copy.9.list_ref
  19.8 7.7 %factor_rows.4 = (bf16[64,256]{1,0:T(8,128)(2,1)}, f32[256,256]{1,0:T(8,128)}, f32[8,256]{1,0:T(8,128)}) custom-call(bf16[256,384]{1,0:T(8,128)(2,1)} %refs_0_.1), custom_call_target="tpu_custom_call" | custom-call | tf_op jit(solution)/shard_map/factor_rows/pallas_call | solution.py:102
  27.4 17.8 %half_transform.4 = (bf16[2,128,256]{2,1,0:T(8,128)(2,1)}, bf16[2,128,256]{2,1,0:T(8,128)(2,1)}, bf16[2,128,256]{2,1,0:T(8,128)(2,1)}, bf16[2,128,256]{2,1,0:T(8...) custom-call(s32[8,4]{1,0:T(8,128)} %copy.9.list_ref, ...), custom_call_target="tpu_custom_call" | custom-call | flops 1073741824 | bytes 18874368 | tf_op jit(solution)/shard_map/half_transform/pallas_call | solution.py:177
  46.4 1.3 collective-permute-start.33
  47.7 24.8 %collective-permute-done.33 = bf16[2,128,2048]{2,1,0:T(8,128)(2,1)S(1)} collective-permute-done((bf16[2,128,2048]{2,1,0:T(8,128)(2,1)}, bf16[2,128,2048]{2,1,0:T(8,128)(2,1)S(1)}, u32[]{:S(2)}, u32[]{:S(2)}) %collective-permute-start.33) | collective-permute-done | bytes 1048608 | tf_op jit(solution)/shard_map/ppermute | solution.py:287
  72.5 2.6 conditional.1
  75.3 3.3 pad_maximum_fusion
  78.8 4.2 collective-permute-start.5
  83.1 2.4 collective-permute-done.3.refs_1_
  85.6 5.8 %collective-permute-done.4.refs_2_ = bf16[2,128,256]{2,1,0:T(8,128)(2,1)S(1)} collective-permute-done((bf16[2,128,256]{2,1,0:T(8,128)(2,1)S(1)}, bf16[2,128,256]{2,1,0:T(8,128)(2,1)S(1)}, u32[]{:S(2)}, u32[]{:S(2)}) %collective-permute-start.4) | collective-permute-done | bytes 131104 | tf_op jit(solution)/shard_map/ppermute | solution.py:305
  91.4 1.7 collective-permute-start.10
  93.1 7.4 %collective-permute-start.11 = (bf16[2,128,256]{2,1,0:T(8,128)(2,1)S(1)}, bf16[2,128,256]{2,1,0:T(8,128)(2,1)S(1)}, u32[]{:S(2)}, u32[]{:S(2)}) collective-permute-start(bf16[2,128,256]{2,1,0:T(8,128)(2,1)S(1)} %copy-done.55), channel_id=1, source_target_pairs={{0,9},{1,8},{2,11},{3,10},{4,13},{5,12},{6,15},{7,14},{8,1},{9,0},... | collective-permute-start | bytes 393224 | tf_op jit(solution)/shard_map/ppermute | solution.py:305
  100.8 18.9 %factor_rows.5 = (bf16[192,256]{1,0:T(8,128)(2,1)}, f32[256,256]{1,0:T(8,128)}, f32[8,256]{1,0:T(8,128)}) custom-call(f32[256,256]{1,0:T(8,128)} %get-tuple-element.242.refs_0_, f32[8,256]{1,0:T(8,128)} %get-tuple-element.243.refs_1_), custom_call_target="tpu_custom_call" | custom-call | tf_op jit(solution)/shard_map/factor_rows/pallas_call | solution.py:102
  119.7 3.3 collective-permute-start.13
  123.2 2.2 collective-permute-start.15
  126.1 3.5 collective-permute-start.17
  129.5 20.7 %half_transform.5 = (bf16[6,128,256]{2,1,0:T(8,128)(2,1)}, bf16[6,128,256]{2,1,0:T(8,128)(2,1)}, bf16[6,128,256]{2,1,0:T(8,128)(2,1)}, bf16[6,128,256]{2,1,0:T(8...) custom-call(s32[8,4]{1,0:T(8,128)} %copy.9.list_ref, ...), custom_call_target="tpu_custom_call" | custom-call | flops 3221225472 | bytes 23068672 | tf_op jit(solution)/shard_map/half_transform/pallas_call | solution.py:177
  150.5 2.1 collective-permute-start.19
  152.6 2.2 collective-permute-start.20
  155.0 15.7 %collective-permute-done.18.refs_1_ = bf16[6,128,256]{2,1,0:T(8,128)(2,1)S(1)} collective-permute-done((bf16[6,128,256]{2,1,0:T(8,128)(2,1)}, bf16[6,128,256]{2,1,0:T(8,128)(2,1)S(1)}, u32[]{:S(2)}, u32[]{:S(2)}) %collective-permute-start.18) | collective-permute-done | bytes 393248 | tf_op jit(solution)/shard_map/ppermute | solution.py:305
  170.7 9.9 %collective-permute-done.19.refs_2_ = bf16[6,128,256]{2,1,0:T(8,128)(2,1)S(1)} collective-permute-done((bf16[6,128,256]{2,1,0:T(8,128)(2,1)}, bf16[6,128,256]{2,1,0:T(8,128)(2,1)S(1)}, u32[]{:S(2)}, u32[]{:S(2)}) %collective-permute-start.19) | collective-permute-done | bytes 393248 | tf_op jit(solution)/shard_map/ppermute | solution.py:305
  180.6 1.6 collective-permute-start.25
  182.2 25.7 %collective-permute-start.26 = (bf16[6,128,256]{2,1,0:T(8,128)(2,1)}, bf16[6,128,256]{2,1,0:T(8,128)(2,1)}, u32[]{:S(2)}, u32[]{:S(2)}) collective-permute-start(bf16[6,128,256]{2,1,0:T(8,128)(2,1)} %get-tuple-element.328), channel_id=1, source_target_pairs={{0,9},{1,8},{2,11},{3,10},{4,13},{5,12},{6,15},{7,14},{8,1},{9,0},... | collective-permute-start | bytes 1179656 | tf_op jit(solution)/shard_map/ppermute | solution.py:305
  208.1 7.9 %collective-permute-done.23.refs_6_ = bf16[6,128,256]{2,1,0:T(8,128)(2,1)S(1)} collective-permute-done((bf16[6,128,256]{2,1,0:T(8,128)(2,1)}, bf16[6,128,256]{2,1,0:T(8,128)(2,1)S(1)}, u32[]{:S(2)}, u32[]{:S(2)}) %collective-permute-start.23) | collective-permute-done | bytes 393248 | tf_op jit(solution)/shard_map/ppermute | solution.py:305
  217.0 12.3 %collective-permute-start.29 = (bf16[6,128,256]{2,1,0:T(8,128)(2,1)}, bf16[6,128,256]{2,1,0:T(8,128)(2,1)}, u32[]{:S(2)}, u32[]{:S(2)}) collective-permute-start(bf16[6,128,256]{2,1,0:T(8,128)(2,1)} %get-tuple-element.331), channel_id=1, source_target_pairs={{0,12},{1,13},{2,14},{3,15},{4,8},{5,9},{6,10},{7,11},{8,4},{9,5},... | collective-permute-start | bytes 1179656 | tf_op jit(solution)/shard_map/ppermute | solution.py:305
  229.3 11.3 %collective-permute-start.30 = (bf16[6,128,256]{2,1,0:T(8,128)(2,1)}, bf16[6,128,256]{2,1,0:T(8,128)(2,1)}, u32[]{:S(2)}, u32[]{:S(2)}) collective-permute-start(bf16[6,128,256]{2,1,0:T(8,128)(2,1)} %get-tuple-element.332), channel_id=1, source_target_pairs={{0,13},{1,12},{2,15},{3,14},{4,9},{5,8},{6,11},{7,10},{8,5},{9,4},... | collective-permute-start | bytes 1179656 | tf_op jit(solution)/shard_map/ppermute | solution.py:305
  240.9 8.3 %collective-permute-done.27.refs_10_ = bf16[6,128,256]{2,1,0:T(8,128)(2,1)} collective-permute-done((bf16[6,128,256]{2,1,0:T(8,128)(2,1)}, bf16[6,128,256]{2,1,0:T(8,128)(2,1)}, u32[]{:S(2)}, u32[]{:S(2)}) %collective-permute-start.27) | collective-permute-done | bytes 393248 | tf_op jit(solution)/shard_map/ppermute | solution.py:305
  249.2 18.9 %factor_rows.6 = (bf16[192,256]{1,0:T(8,128)(2,1)}, f32[256,256]{1,0:T(8,128)}, f32[8,256]{1,0:T(8,128)}) custom-call(f32[256,256]{1,0:T(8,128)} %get-tuple-element.263.refs_0_, f32[8,256]{1,0:T(8,128)} %get-tuple-element.264.refs_1_), custom_call_target="tpu_custom_call" | custom-call | tf_op jit(solution)/shard_map/factor_rows/pallas_call | solution.py:102
  268.2 17.0 %half_transform.6 = (bf16[6,128,256]{2,1,0:T(8,128)(2,1)}, bf16[6,128,256]{2,1,0:T(8,128)(2,1)}, bf16[6,128,256]{2,1,0:T(8,128)(2,1)}, bf16[6,128,256]{2,1,0:T(8...) custom-call(s32[8,4]{1,0:T(8,128)} %copy.9.list_ref, ...), custom_call_target="tpu_custom_call" | custom-call | flops 3221225472 | bytes 23068672 | tf_op jit(solution)/shard_map/half_transform/pallas_call | solution.py:177
  285.4 2.1 collective-permute-start.35
  287.5 2.2 collective-permute-start.36
  290.5 6.1 %collective-permute-start.38 = (bf16[6,128,256]{2,1,0:T(8,128)(2,1)}, bf16[6,128,256]{2,1,0:T(8,128)(2,1)S(1)}, u32[]{:S(2)}, u32[]{:S(2)}) collective-permute-start(bf16[6,128,256]{2,1,0:T(8,128)(2,1)} %get-tuple-element.380), channel_id=1, source_target_pairs={{0,5},{1,4},{2,7},{3,6},{4,1},{5,0},{6,3},{7,2},{8,13},{9,12},{10,... | collective-permute-start | bytes 1179656 | tf_op jit(solution)/shard_map/ppermute | solution.py:305
  296.6 3.3 collective-permute-done.34.refs_1_
  299.9 2.1 collective-permute-start.39
  301.9 19.2 %collective-permute-done.35.refs_2_ = bf16[6,128,256]{2,1,0:T(8,128)(2,1)S(1)} collective-permute-done((bf16[6,128,256]{2,1,0:T(8,128)(2,1)}, bf16[6,128,256]{2,1,0:T(8,128)(2,1)S(1)}, u32[]{:S(2)}, u32[]{:S(2)}) %collective-permute-start.35) | collective-permute-done | bytes 393248 | tf_op jit(solution)/shard_map/ppermute | solution.py:305
  321.1 1.1 collective-permute-start.41
  322.2 26.0 %collective-permute-start.42 = (bf16[6,128,256]{2,1,0:T(8,128)(2,1)}, bf16[6,128,256]{2,1,0:T(8,128)(2,1)S(1)}, u32[]{:S(2)}, u32[]{:S(2)}) collective-permute-start(bf16[6,128,256]{2,1,0:T(8,128)(2,1)} %get-tuple-element.384), channel_id=1, source_target_pairs={{0,9},{1,8},{2,11},{3,10},{4,13},{5,12},{6,15},{7,14},{8,1},{9,0},... | collective-permute-start | bytes 1179656 | tf_op jit(solution)/shard_map/ppermute | solution.py:305
  348.7 3.4 collective-permute-done.39.refs_6_
  352.1 1.6 collective-permute-start.44
  353.8 5.0 collective-permute-start.45
  358.8 21.3 %collective-permute-start.46 = (bf16[6,128,256]{2,1,0:T(8,128)(2,1)}, bf16[6,128,256]{2,1,0:T(8,128)(2,1)}, u32[]{:S(2)}, u32[]{:S(2)}) collective-permute-start(bf16[6,128,256]{2,1,0:T(8,128)(2,1)} %get-tuple-element.388), channel_id=1, source_target_pairs={{0,13},{1,12},{2,15},{3,14},{4,9},{5,8},{6,11},{7,10},{8,5},{9,4},... | collective-permute-start | bytes 1179656 | tf_op jit(solution)/shard_map/ppermute | solution.py:305
  380.1 1.8 collective-permute-start.47
  381.9 6.4 %collective-permute-done.43.refs_10_ = bf16[6,128,256]{2,1,0:T(8,128)(2,1)} collective-permute-done((bf16[6,128,256]{2,1,0:T(8,128)(2,1)}, bf16[6,128,256]{2,1,0:T(8,128)(2,1)}, u32[]{:S(2)}, u32[]{:S(2)}) %collective-permute-start.43) | collective-permute-done | bytes 393248 | tf_op jit(solution)/shard_map/ppermute | solution.py:305
  388.2 7.4 %factor_rows.7 = (bf16[64,256]{1,0:T(8,128)(2,1)}, f32[256,256]{1,0:T(8,128)}, f32[8,256]{1,0:T(8,128)}) custom-call(f32[256,256]{1,0:T(8,128)} %get-tuple-element.300.refs_0_, f32[8,256]{1,0:T(8,128)} %get-tuple-element.301.refs_1_), custom_call_target="tpu_custom_call" | custom-call | tf_op jit(solution)/shard_map/factor_rows/pallas_call | solution.py:102
  395.7 14.5 %half_transform.7 = (bf16[2,128,256]{2,1,0:T(8,128)(2,1)}, bf16[2,128,256]{2,1,0:T(8,128)(2,1)}, bf16[2,128,256]{2,1,0:T(8,128)(2,1)}, bf16[2,128,256]{2,1,0:T(8...) custom-call(s32[8,4]{1,0:T(8,128)} %copy.9.list_ref, ...), custom_call_target="tpu_custom_call" | custom-call | flops 1073741824 | bytes 18874368 | tf_op jit(solution)/shard_map/half_transform/pallas_call | solution.py:177
  410.3 9.6 %collective-permute-start.49 = (bf16[2,128,256]{2,1,0:T(8,128)(2,1)}, bf16[2,128,256]{2,1,0:T(8,128)(2,1)S(1)}, u32[]{:S(2)}, u32[]{:S(2)}) collective-permute-start(bf16[2,128,256]{2,1,0:T(8,128)(2,1)} %get-tuple-element.392), channel_id=1, source_target_pairs={{0,1},{1,0},{2,3},{3,2},{4,5},{5,4},{6,7},{7,6},{8,9},{9,8},{10,11... | collective-permute-start | bytes 393224 | tf_op jit(solution)/shard_map/ppermute | solution.py:305
  420.8 1.5 collective-permute-start.51
  422.4 7.6 %collective-permute-done.47.refs_14_ = bf16[6,128,256]{2,1,0:T(8,128)(2,1)} collective-permute-done((bf16[6,128,256]{2,1,0:T(8,128)(2,1)}, bf16[6,128,256]{2,1,0:T(8,128)(2,1)}, u32[]{:S(2)}, u32[]{:S(2)}) %collective-permute-start.47) | collective-permute-done | bytes 393248 | tf_op jit(solution)/shard_map/ppermute | solution.py:305
  430.0 3.3 collective-permute-start.52
  433.3 8.6 %collective-permute-start.53 = (bf16[2,128,256]{2,1,0:T(8,128)(2,1)}, bf16[2,128,256]{2,1,0:T(8,128)(2,1)S(1)}, u32[]{:S(2)}, u32[]{:S(2)}) collective-permute-start(bf16[2,128,256]{2,1,0:T(8,128)(2,1)} %get-tuple-element.396), channel_id=1, source_target_pairs={{0,5},{1,4},{2,7},{3,6},{4,1},{5,0},{6,3},{7,2},{8,13},{9,12},{10,... | collective-permute-start | bytes 393224 | tf_op jit(solution)/shard_map/ppermute | solution.py:305
  442.6 9.6 %fit_exchange.4.before_ref = f32[256,256]{1,0:T(8,128)} custom-call(s32[1]{0:T(128)} %bitcast.4.me_ref, bf16[2048,2048]{1,0:T(8,128)(2,1)} %all-gather.2.cloned.1.call-done.factor_ref, f32[256,256]{1,0:T(8,128)} %broadcast_in_dim.3.before_ref, bf16[2,128,256]{2,1,0:T(8,128)(2,1)} %get-tuple-element.343.refs_0_, bf16[2,128,256]{2,1,0:T(8,128)(2,1)} %copy-done.1, ...), custom_call_target="tpu_custom_call" | custom-call | flops 2952790016 | bytes 10485760 | tf_op jit(solution)/shard_map/fit_exchange/pallas_call | solution.py:250
  453.4 1.3 collective-permute-start.56
  454.8 2.5 collective-permute-start.57
  458.3 19.6 %fit_exchange.5.before_ref = f32[256,256]{1,0:T(8,128)} custom-call(s32[1]{0:T(128)} %bitcast.4.me_ref, bf16[2048,2048]{1,0:T(8,128)(2,1)} %all-gather.2.cloned.1.call-done.factor_ref, f32[256,256]{1,0:T(8,128)} %fit_exchange.4.before_ref, bf16[6,128,256]{2,1,0:T(8,128)(2,1)} %get-tuple-element.359.refs_0_, bf16[6,128,256]{2,1,0:T(8,128)(2,1)} %copy-done.31, ...), custom_call_target="tpu_custom_call" | custom-call | flops 8858370048 | bytes 14680064 | tf_op jit(solution)/shard_map/fit_exchange/pallas_call | solution.py:250
  478.0 2.2 collective-permute-start.59
  480.8 1.9 collective-permute-start.61
  482.8 1.7 collective-permute-start.62
  484.5 2.1 collective-permute-start.63
  486.6 19.8 %fit_exchange.6.before_ref = f32[256,256]{1,0:T(8,128)} custom-call(s32[1]{0:T(128)} %bitcast.4.me_ref, bf16[2048,2048]{1,0:T(8,128)(2,1)} %all-gather.2.cloned.1.call-done.factor_ref, f32[256,256]{1,0:T(8,128)} %fit_exchange.5.before_ref, bf16[6,128,256]{2,1,0:T(8,128)(2,1)} %get-tuple-element.375.refs_0_, bf16[6,128,256]{2,1,0:T(8,128)(2,1)} %copy-done.38, ...), custom_call_target="tpu_custom_call" | custom-call | flops 8858370048 | bytes 14680064 | tf_op jit(solution)/shard_map/fit_exchange/pallas_call | solution.py:250
  507.9 9.7 %fit_exchange.7 = f32[256,256]{1,0:T(8,128)} custom-call(s32[1]{0:T(128)} %bitcast.4.me_ref, bf16[2048,2048]{1,0:T(8,128)(2,1)} %all-gather.2.cloned.1.call-done.factor_ref, f32[256,256]{1,0:T(8,128)} %fit_exchange.6.before_ref, bf16[2,128,256]{2,1,0:T(8,128)(2,1)} %get-tuple-element.391.refs_0_, bf16[2,128,256]{2,1,0:T(8,128)(2,1)} %copy-done.16, ...), custom_call_target="tpu_custom_call" | custom-call | flops 2952790016 | bytes 10485760 | tf_op jit(solution)/shard_map/fit_exchange/pallas_call | solution.py:250
  517.7 14.1 %all_to_all.5 = f32[16,16,256]{2,1,0:T(8,128)S(1)} all-to-all(f32[16,16,256]{2,1,0:T(8,128)} %bitcast.14), channel_id=1, replica_groups=mesh['grp'=2,'aux'=4,'occ'=4] {'aux','occ'}, dimensions={0} | all-to-all | bytes 524288 | tf_op jit(solution)/shard_map/all_to_all | solution.py:350
  (238 shorter events, 14.9 us)
Async XLA Ops:
  6.5 403.8 %all-gather.2.cloned.1.call-start = ((), (), s32[]{:S(2)}) async-start(), calls=%async_computation.1 | async-start | bytes 10485760 | tf_op jit(solution)/shard_map/all_gather | solution.py:334
  6.5 38.7 %collective-permute-start.2 = (bf16[128,2048]{1,0:T(8,128)(2,1)}, bf16[128,2048]{1,0:T(8,128)(2,1)S(1)}, u32[]{:S(2)}, u32[]{:S(2)}) collective-permute-start(bf16[128,2048]{1,0:T(8,128)(2,1)} %param.13), channel_id=1, source_target_pairs={{0,2},{3,1},{4,6},{7,5},{8,10},{11,9},{12,14},{15,13},{16,18},{19,... | collective-permute-start | bytes 1572872 | tf_op jit(solution)/shard_map/ppermute | solution.py:280
  12.5 32.7 %collective-permute-start.1 = (bf16[128,2048]{1,0:T(8,128)(2,1)}, bf16[128,2048]{1,0:T(8,128)(2,1)S(1)}, u32[]{:S(2)}, u32[]{:S(2)}) collective-permute-start(bf16[128,2048]{1,0:T(8,128)(2,1)} %param.13), channel_id=1, source_target_pairs={{3,2},{2,1},{1,0},{7,6},{6,5},{5,4},{11,10},{10,9},{9,8},{15,14},{... | collective-permute-start | bytes 1572872 | tf_op jit(solution)/shard_map/ppermute | solution.py:279
  13.8 31.4 %collective-permute-start = (bf16[128,2048]{1,0:T(8,128)(2,1)}, bf16[128,2048]{1,0:T(8,128)(2,1)S(1)}, u32[]{:S(2)}, u32[]{:S(2)}) collective-permute-start(bf16[128,2048]{1,0:T(8,128)(2,1)} %param.13), channel_id=1, source_target_pairs={{0,1},{1,2},{2,3},{4,5},{5,6},{6,7},{8,9},{9,10},{10,11},{12,13},{... | collective-permute-start | bytes 1572872 | tf_op jit(solution)/shard_map/ppermute | solution.py:278
  46.4 26.1 %collective-permute-start.33 = (bf16[2,128,2048]{2,1,0:T(8,128)(2,1)}, bf16[2,128,2048]{2,1,0:T(8,128)(2,1)S(1)}, u32[]{:S(2)}, u32[]{:S(2)}) collective-permute-start(bf16[2,128,2048]{2,1,0:T(8,128)(2,1)} %pad_maximum_fusion.1), channel_id=1, source_target_pairs={{1,0},{2,3},{5,4},{6,7},{9,8},{10,11},{13,12},{14,15},{17,16},{18,... | collective-permute-start | bytes 3145736 | tf_op jit(solution)/shard_map/ppermute | solution.py:287
  78.8 12.6 %collective-permute-start.4 = (bf16[2,128,256]{2,1,0:T(8,128)(2,1)S(1)}, bf16[2,128,256]{2,1,0:T(8,128)(2,1)S(1)}, u32[]{:S(2)}, u32[]{:S(2)}) collective-permute-start(bf16[2,128,256]{2,1,0:T(8,128)(2,1)S(1)} %copy-done.70), channel_id=1, source_target_pairs={{0,2},{1,3},{2,0},{3,1},{4,6},{5,7},{6,4},{7,5},{8,10},{9,11},{10,... | collective-permute-start | bytes 393224 | tf_op jit(solution)/shard_map/ppermute | solution.py:305
  78.8 12.6 %collective-permute-start.5 = (bf16[2,128,256]{2,1,0:T(8,128)(2,1)S(1)}, bf16[2,128,256]{2,1,0:T(8,128)(2,1)S(1)}, u32[]{:S(2)}, u32[]{:S(2)}) collective-permute-start(bf16[2,128,256]{2,1,0:T(8,128)(2,1)S(1)} %copy-done.68), channel_id=1, source_target_pairs={{0,3},{1,2},{2,1},{3,0},{4,7},{5,6},{6,5},{7,4},{8,11},{9,10},{10,... | collective-permute-start | bytes 393224 | tf_op jit(solution)/shard_map/ppermute | solution.py:305
  83.0 10.1 %collective-permute-start.6 = (bf16[2,128,256]{2,1,0:T(8,128)(2,1)S(1)}, bf16[2,128,256]{2,1,0:T(8,128)(2,1)S(1)}, u32[]{:S(2)}, u32[]{:S(2)}) collective-permute-start(bf16[2,128,256]{2,1,0:T(8,128)(2,1)S(1)} %copy-done.66), channel_id=1, source_target_pairs={{0,4},{1,5},{2,6},{3,7},{4,0},{5,1},{6,2},{7,3},{8,12},{9,13},{10,... | collective-permute-start | bytes 393224 | tf_op jit(solution)/shard_map/ppermute | solution.py:305
  83.0 17.6 %collective-permute-start.7 = (bf16[2,128,256]{2,1,0:T(8,128)(2,1)S(1)}, bf16[2,128,256]{2,1,0:T(8,128)(2,1)S(1)}, u32[]{:S(2)}, u32[]{:S(2)}) collective-permute-start(bf16[2,128,256]{2,1,0:T(8,128)(2,1)S(1)} %copy-done.64), channel_id=1, source_target_pairs={{0,5},{1,4},{2,7},{3,6},{4,1},{5,0},{6,3},{7,2},{8,13},{9,12},{10,... | collective-permute-start | bytes 393224 | tf_op jit(solution)/shard_map/ppermute | solution.py:305
  85.5 34.2 %collective-permute-start.8 = (bf16[2,128,256]{2,1,0:T(8,128)(2,1)S(1)}, bf16[2,128,256]{2,1,0:T(8,128)(2,1)S(1)}, u32[]{:S(2)}, u32[]{:S(2)}) collective-permute-start(bf16[2,128,256]{2,1,0:T(8,128)(2,1)S(1)} %copy-done.63), channel_id=1, source_target_pairs={{0,6},{1,7},{2,4},{3,5},{4,2},{5,3},{6,0},{7,1},{8,14},{9,15},{10,... | collective-permute-start | bytes 393224 | tf_op jit(solution)/shard_map/ppermute | solution.py:305
  91.4 31.7 %collective-permute-start.9 = (bf16[2,128,256]{2,1,0:T(8,128)(2,1)S(1)}, bf16[2,128,256]{2,1,0:T(8,128)(2,1)S(1)}, u32[]{:S(2)}, u32[]{:S(2)}) collective-permute-start(bf16[2,128,256]{2,1,0:T(8,128)(2,1)S(1)} %copy-done.61), channel_id=1, source_target_pairs={{0,7},{1,6},{2,5},{3,4},{4,3},{5,2},{6,1},{7,0},{8,15},{9,14},{10,... | collective-permute-start | bytes 393224 | tf_op jit(solution)/shard_map/ppermute | solution.py:305
  91.4 31.8 %collective-permute-start.10 = (bf16[2,128,256]{2,1,0:T(8,128)(2,1)S(1)}, bf16[2,128,256]{2,1,0:T(8,128)(2,1)S(1)}, u32[]{:S(2)}, u32[]{:S(2)}) collective-permute-start(bf16[2,128,256]{2,1,0:T(8,128)(2,1)S(1)} %copy-done.58), channel_id=1, source_target_pairs={{0,8},{1,9},{2,10},{3,11},{4,12},{5,13},{6,14},{7,15},{8,0},{9,1},... | collective-permute-start | bytes 393224 | tf_op jit(solution)/shard_map/ppermute | solution.py:305
  93.1 32.2 %collective-permute-start.11 = (bf16[2,128,256]{2,1,0:T(8,128)(2,1)S(1)}, bf16[2,128,256]{2,1,0:T(8,128)(2,1)S(1)}, u32[]{:S(2)}, u32[]{:S(2)}) collective-permute-start(bf16[2,128,256]{2,1,0:T(8,128)(2,1)S(1)} %copy-done.55), channel_id=1, source_target_pairs={{0,9},{1,8},{2,11},{3,10},{4,13},{5,12},{6,15},{7,14},{8,1},{9,0},... | collective-permute-start | bytes 393224 | tf_op jit(solution)/shard_map/ppermute | solution.py:305
  100.6 25.5 %collective-permute-start.12 = (bf16[2,128,256]{2,1,0:T(8,128)(2,1)S(1)}, bf16[2,128,256]{2,1,0:T(8,128)(2,1)S(1)}, u32[]{:S(2)}, u32[]{:S(2)}) collective-permute-start(bf16[2,128,256]{2,1,0:T(8,128)(2,1)S(1)} %copy-done.54), channel_id=1, source_target_pairs={{0,10},{1,11},{2,8},{3,9},{4,14},{5,15},{6,12},{7,13},{8,2},{9,3},... | collective-permute-start | bytes 393224 | tf_op jit(solution)/shard_map/ppermute | solution.py:305
  119.7 30.6 %collective-permute-start.13 = (bf16[2,128,256]{2,1,0:T(8,128)(2,1)S(1)}, bf16[2,128,256]{2,1,0:T(8,128)(2,1)S(1)}, u32[]{:S(2)}, u32[]{:S(2)}) collective-permute-start(bf16[2,128,256]{2,1,0:T(8,128)(2,1)S(1)} %copy-done.53), channel_id=1, source_target_pairs={{0,11},{1,10},{2,9},{3,8},{4,15},{5,14},{6,13},{7,12},{8,3},{9,2},... | collective-permute-start | bytes 393224 | tf_op jit(solution)/shard_map/ppermute | solution.py:305
  123.1 27.4 %collective-permute-start.14 = (bf16[2,128,256]{2,1,0:T(8,128)(2,1)S(1)}, bf16[2,128,256]{2,1,0:T(8,128)(2,1)S(1)}, u32[]{:S(2)}, u32[]{:S(2)}) collective-permute-start(bf16[2,128,256]{2,1,0:T(8,128)(2,1)S(1)} %copy-done.52), channel_id=1, source_target_pairs={{0,12},{1,13},{2,14},{3,15},{4,8},{5,9},{6,10},{7,11},{8,4},{9,5},... | collective-permute-start | bytes 393224 | tf_op jit(solution)/shard_map/ppermute | solution.py:305
  123.2 29.4 %collective-permute-start.15 = (bf16[2,128,256]{2,1,0:T(8,128)(2,1)S(1)}, bf16[2,128,256]{2,1,0:T(8,128)(2,1)S(1)}, u32[]{:S(2)}, u32[]{:S(2)}) collective-permute-start(bf16[2,128,256]{2,1,0:T(8,128)(2,1)S(1)} %copy-done.51), channel_id=1, source_target_pairs={{0,13},{1,12},{2,15},{3,14},{4,9},{5,8},{6,11},{7,10},{8,5},{9,4},... | collective-permute-start | bytes 393224 | tf_op jit(solution)/shard_map/ppermute | solution.py:305
  125.4 29.5 %collective-permute-start.16 = (bf16[2,128,256]{2,1,0:T(8,128)(2,1)S(1)}, bf16[2,128,256]{2,1,0:T(8,128)(2,1)S(1)}, u32[]{:S(2)}, u32[]{:S(2)}) collective-permute-start(bf16[2,128,256]{2,1,0:T(8,128)(2,1)S(1)} %copy-done.50), channel_id=1, source_target_pairs={{0,14},{1,15},{2,12},{3,13},{4,10},{5,11},{6,8},{7,9},{8,6},{9,7},... | collective-permute-start | bytes 393224 | tf_op jit(solution)/shard_map/ppermute | solution.py:305
  126.1 28.8 %collective-permute-start.17 = (bf16[2,128,256]{2,1,0:T(8,128)(2,1)S(1)}, bf16[2,128,256]{2,1,0:T(8,128)(2,1)S(1)}, u32[]{:S(2)}, u32[]{:S(2)}) collective-permute-start(bf16[2,128,256]{2,1,0:T(8,128)(2,1)S(1)} %copy-done.49), channel_id=1, source_target_pairs={{0,15},{1,14},{2,13},{3,12},{4,11},{5,10},{6,9},{7,8},{8,7},{9,6},... | collective-permute-start | bytes 393224 | tf_op jit(solution)/shard_map/ppermute | solution.py:305
  150.4 20.3 %collective-permute-start.18 = (bf16[6,128,256]{2,1,0:T(8,128)(2,1)}, bf16[6,128,256]{2,1,0:T(8,128)(2,1)S(1)}, u32[]{:S(2)}, u32[]{:S(2)}) collective-permute-start(bf16[6,128,256]{2,1,0:T(8,128)(2,1)} %get-tuple-element.320), channel_id=1, source_target_pairs={{0,1},{1,0},{2,3},{3,2},{4,5},{5,4},{6,7},{7,6},{8,9},{9,8},{10,11... | collective-permute-start | bytes 1179656 | tf_op jit(solution)/shard_map/ppermute | solution.py:305
  150.5 30.1 %collective-permute-start.19 = (bf16[6,128,256]{2,1,0:T(8,128)(2,1)}, bf16[6,128,256]{2,1,0:T(8,128)(2,1)S(1)}, u32[]{:S(2)}, u32[]{:S(2)}) collective-permute-start(bf16[6,128,256]{2,1,0:T(8,128)(2,1)} %get-tuple-element.321), channel_id=1, source_target_pairs={{0,2},{1,3},{2,0},{3,1},{4,6},{5,7},{6,4},{7,5},{8,10},{9,11},{10,... | collective-permute-start | bytes 1179656 | tf_op jit(solution)/shard_map/ppermute | solution.py:305
  152.6 28.0 %collective-permute-start.20 = (bf16[6,128,256]{2,1,0:T(8,128)(2,1)}, bf16[6,128,256]{2,1,0:T(8,128)(2,1)S(1)}, u32[]{:S(2)}, u32[]{:S(2)}) collective-permute-start(bf16[6,128,256]{2,1,0:T(8,128)(2,1)} %get-tuple-element.322), channel_id=1, source_target_pairs={{0,3},{1,2},{2,1},{3,0},{4,7},{5,6},{6,5},{7,4},{8,11},{9,10},{10,... | collective-permute-start | bytes 1179656 | tf_op jit(solution)/shard_map/ppermute | solution.py:305
  154.9 27.4 %collective-permute-start.21 = (bf16[6,128,256]{2,1,0:T(8,128)(2,1)}, bf16[6,128,256]{2,1,0:T(8,128)(2,1)S(1)}, u32[]{:S(2)}, u32[]{:S(2)}) collective-permute-start(bf16[6,128,256]{2,1,0:T(8,128)(2,1)} %get-tuple-element.323), channel_id=1, source_target_pairs={{0,4},{1,5},{2,6},{3,7},{4,0},{5,1},{6,2},{7,3},{8,12},{9,13},{10,... | collective-permute-start | bytes 1179656 | tf_op jit(solution)/shard_map/ppermute | solution.py:305
  154.9 53.0 %collective-permute-start.22 = (bf16[6,128,256]{2,1,0:T(8,128)(2,1)}, bf16[6,128,256]{2,1,0:T(8,128)(2,1)S(1)}, u32[]{:S(2)}, u32[]{:S(2)}) collective-permute-start(bf16[6,128,256]{2,1,0:T(8,128)(2,1)} %get-tuple-element.324), channel_id=1, source_target_pairs={{0,5},{1,4},{2,7},{3,6},{4,1},{5,0},{6,3},{7,2},{8,13},{9,12},{10,... | collective-permute-start | bytes 1179656 | tf_op jit(solution)/shard_map/ppermute | solution.py:305
  170.7 45.3 %collective-permute-start.23 = (bf16[6,128,256]{2,1,0:T(8,128)(2,1)}, bf16[6,128,256]{2,1,0:T(8,128)(2,1)S(1)}, u32[]{:S(2)}, u32[]{:S(2)}) collective-permute-start(bf16[6,128,256]{2,1,0:T(8,128)(2,1)} %get-tuple-element.325), channel_id=1, source_target_pairs={{0,6},{1,7},{2,4},{3,5},{4,2},{5,3},{6,0},{7,1},{8,14},{9,15},{10,... | collective-permute-start | bytes 1179656 | tf_op jit(solution)/shard_map/ppermute | solution.py:305
  180.6 36.4 %collective-permute-start.24 = (bf16[6,128,256]{2,1,0:T(8,128)(2,1)}, bf16[6,128,256]{2,1,0:T(8,128)(2,1)S(1)}, u32[]{:S(2)}, u32[]{:S(2)}) collective-permute-start(bf16[6,128,256]{2,1,0:T(8,128)(2,1)} %get-tuple-element.326), channel_id=1, source_target_pairs={{0,7},{1,6},{2,5},{3,4},{4,3},{5,2},{6,1},{7,0},{8,15},{9,14},{10,... | collective-permute-start | bytes 1179656 | tf_op jit(solution)/shard_map/ppermute | solution.py:305
  180.6 48.7 %collective-permute-start.25 = (bf16[6,128,256]{2,1,0:T(8,128)(2,1)}, bf16[6,128,256]{2,1,0:T(8,128)(2,1)}, u32[]{:S(2)}, u32[]{:S(2)}) collective-permute-start(bf16[6,128,256]{2,1,0:T(8,128)(2,1)} %get-tuple-element.327), channel_id=1, source_target_pairs={{0,8},{1,9},{2,10},{3,11},{4,12},{5,13},{6,14},{7,15},{8,0},{9,1},... | collective-permute-start | bytes 1179656 | tf_op jit(solution)/shard_map/ppermute | solution.py:305
  182.2 58.4 %collective-permute-start.26 = (bf16[6,128,256]{2,1,0:T(8,128)(2,1)}, bf16[6,128,256]{2,1,0:T(8,128)(2,1)}, u32[]{:S(2)}, u32[]{:S(2)}) collective-permute-start(bf16[6,128,256]{2,1,0:T(8,128)(2,1)} %get-tuple-element.328), channel_id=1, source_target_pairs={{0,9},{1,8},{2,11},{3,10},{4,13},{5,12},{6,15},{7,14},{8,1},{9,0},... | collective-permute-start | bytes 1179656 | tf_op jit(solution)/shard_map/ppermute | solution.py:305
  207.9 41.3 %collective-permute-start.27 = (bf16[6,128,256]{2,1,0:T(8,128)(2,1)}, bf16[6,128,256]{2,1,0:T(8,128)(2,1)}, u32[]{:S(2)}, u32[]{:S(2)}) collective-permute-start(bf16[6,128,256]{2,1,0:T(8,128)(2,1)} %get-tuple-element.329), channel_id=1, source_target_pairs={{0,10},{1,11},{2,8},{3,9},{4,14},{5,15},{6,12},{7,13},{8,2},{9,3},... | collective-permute-start | bytes 1179656 | tf_op jit(solution)/shard_map/ppermute | solution.py:305
  216.0 69.3 %collective-permute-start.28 = (bf16[6,128,256]{2,1,0:T(8,128)(2,1)}, bf16[6,128,256]{2,1,0:T(8,128)(2,1)}, u32[]{:S(2)}, u32[]{:S(2)}) collective-permute-start(bf16[6,128,256]{2,1,0:T(8,128)(2,1)} %get-tuple-element.330), channel_id=1, source_target_pairs={{0,11},{1,10},{2,9},{3,8},{4,15},{5,14},{6,13},{7,12},{8,3},{9,2},... | collective-permute-start | bytes 1179656 | tf_op jit(solution)/shard_map/ppermute | solution.py:305
  217.0 68.3 %collective-permute-start.29 = (bf16[6,128,256]{2,1,0:T(8,128)(2,1)}, bf16[6,128,256]{2,1,0:T(8,128)(2,1)}, u32[]{:S(2)}, u32[]{:S(2)}) collective-permute-start(bf16[6,128,256]{2,1,0:T(8,128)(2,1)} %get-tuple-element.331), channel_id=1, source_target_pairs={{0,12},{1,13},{2,14},{3,15},{4,8},{5,9},{6,10},{7,11},{8,4},{9,5},... | collective-permute-start | bytes 1179656 | tf_op jit(solution)/shard_map/ppermute | solution.py:305
  229.3 58.2 %collective-permute-start.30 = (bf16[6,128,256]{2,1,0:T(8,128)(2,1)}, bf16[6,128,256]{2,1,0:T(8,128)(2,1)}, u32[]{:S(2)}, u32[]{:S(2)}) collective-permute-start(bf16[6,128,256]{2,1,0:T(8,128)(2,1)} %get-tuple-element.332), channel_id=1, source_target_pairs={{0,13},{1,12},{2,15},{3,14},{4,9},{5,8},{6,11},{7,10},{8,5},{9,4},... | collective-permute-start | bytes 1179656 | tf_op jit(solution)/shard_map/ppermute | solution.py:305
  240.7 49.1 %collective-permute-start.31 = (bf16[6,128,256]{2,1,0:T(8,128)(2,1)}, bf16[6,128,256]{2,1,0:T(8,128)(2,1)S(1)}, u32[]{:S(2)}, u32[]{:S(2)}) collective-permute-start(bf16[6,128,256]{2,1,0:T(8,128)(2,1)} %get-tuple-element.333), channel_id=1, source_target_pairs={{0,14},{1,15},{2,12},{3,13},{4,10},{5,11},{6,8},{7,9},{8,6},{9,7},... | collective-permute-start | bytes 1179656 | tf_op jit(solution)/shard_map/ppermute | solution.py:305
  249.2 41.3 %collective-permute-start.32 = (bf16[6,128,256]{2,1,0:T(8,128)(2,1)}, bf16[6,128,256]{2,1,0:T(8,128)(2,1)S(1)}, u32[]{:S(2)}, u32[]{:S(2)}) collective-permute-start(bf16[6,128,256]{2,1,0:T(8,128)(2,1)} %get-tuple-element.334), channel_id=1, source_target_pairs={{0,15},{1,14},{2,13},{3,12},{4,11},{5,10},{6,9},{7,8},{8,7},{9,6},... | collective-permute-start | bytes 1179656 | tf_op jit(solution)/shard_map/ppermute | solution.py:305
  285.3 14.6 %collective-permute-start.34 = (bf16[6,128,256]{2,1,0:T(8,128)(2,1)}, bf16[6,128,256]{2,1,0:T(8,128)(2,1)S(1)}, u32[]{:S(2)}, u32[]{:S(2)}) collective-permute-start(bf16[6,128,256]{2,1,0:T(8,128)(2,1)} %get-tuple-element.376), channel_id=1, source_target_pairs={{0,1},{1,0},{2,3},{3,2},{4,5},{5,4},{6,7},{7,6},{8,9},{9,8},{10,11... | collective-permute-start | bytes 1179656 | tf_op jit(solution)/shard_map/ppermute | solution.py:305
  285.4 35.7 %collective-permute-start.35 = (bf16[6,128,256]{2,1,0:T(8,128)(2,1)}, bf16[6,128,256]{2,1,0:T(8,128)(2,1)S(1)}, u32[]{:S(2)}, u32[]{:S(2)}) collective-permute-start(bf16[6,128,256]{2,1,0:T(8,128)(2,1)} %get-tuple-element.377), channel_id=1, source_target_pairs={{0,2},{1,3},{2,0},{3,1},{4,6},{5,7},{6,4},{7,5},{8,10},{9,11},{10,... | collective-permute-start | bytes 1179656 | tf_op jit(solution)/shard_map/ppermute | solution.py:305
  287.5 33.6 %collective-permute-start.36 = (bf16[6,128,256]{2,1,0:T(8,128)(2,1)}, bf16[6,128,256]{2,1,0:T(8,128)(2,1)S(1)}, u32[]{:S(2)}, u32[]{:S(2)}) collective-permute-start(bf16[6,128,256]{2,1,0:T(8,128)(2,1)} %get-tuple-element.378), channel_id=1, source_target_pairs={{0,3},{1,2},{2,1},{3,0},{4,7},{5,6},{6,5},{7,4},{8,11},{9,10},{10,... | collective-permute-start | bytes 1179656 | tf_op jit(solution)/shard_map/ppermute | solution.py:305
  289.7 32.5 %collective-permute-start.37 = (bf16[6,128,256]{2,1,0:T(8,128)(2,1)}, bf16[6,128,256]{2,1,0:T(8,128)(2,1)S(1)}, u32[]{:S(2)}, u32[]{:S(2)}) collective-permute-start(bf16[6,128,256]{2,1,0:T(8,128)(2,1)} %get-tuple-element.379), channel_id=1, source_target_pairs={{0,4},{1,5},{2,6},{3,7},{4,0},{5,1},{6,2},{7,3},{8,12},{9,13},{10,... | collective-permute-start | bytes 1179656 | tf_op jit(solution)/shard_map/ppermute | solution.py:305
  290.5 57.8 %collective-permute-start.38 = (bf16[6,128,256]{2,1,0:T(8,128)(2,1)}, bf16[6,128,256]{2,1,0:T(8,128)(2,1)S(1)}, u32[]{:S(2)}, u32[]{:S(2)}) collective-permute-start(bf16[6,128,256]{2,1,0:T(8,128)(2,1)} %get-tuple-element.380), channel_id=1, source_target_pairs={{0,5},{1,4},{2,7},{3,6},{4,1},{5,0},{6,3},{7,2},{8,13},{9,12},{10,... | collective-permute-start | bytes 1179656 | tf_op jit(solution)/shard_map/ppermute | solution.py:305
  299.9 52.3 %collective-permute-start.39 = (bf16[6,128,256]{2,1,0:T(8,128)(2,1)}, bf16[6,128,256]{2,1,0:T(8,128)(2,1)S(1)}, u32[]{:S(2)}, u32[]{:S(2)}) collective-permute-start(bf16[6,128,256]{2,1,0:T(8,128)(2,1)} %get-tuple-element.381), channel_id=1, source_target_pairs={{0,6},{1,7},{2,4},{3,5},{4,2},{5,3},{6,0},{7,1},{8,14},{9,15},{10,... | collective-permute-start | bytes 1179656 | tf_op jit(solution)/shard_map/ppermute | solution.py:305
  321.1 32.7 %collective-permute-start.40 = (bf16[6,128,256]{2,1,0:T(8,128)(2,1)}, bf16[6,128,256]{2,1,0:T(8,128)(2,1)S(1)}, u32[]{:S(2)}, u32[]{:S(2)}) collective-permute-start(bf16[6,128,256]{2,1,0:T(8,128)(2,1)} %get-tuple-element.382), channel_id=1, source_target_pairs={{0,7},{1,6},{2,5},{3,4},{4,3},{5,2},{6,1},{7,0},{8,15},{9,14},{10,... | collective-permute-start | bytes 1179656 | tf_op jit(solution)/shard_map/ppermute | solution.py:305
  321.1 37.7 %collective-permute-start.41 = (bf16[6,128,256]{2,1,0:T(8,128)(2,1)}, bf16[6,128,256]{2,1,0:T(8,128)(2,1)S(1)}, u32[]{:S(2)}, u32[]{:S(2)}) collective-permute-start(bf16[6,128,256]{2,1,0:T(8,128)(2,1)} %get-tuple-element.383), channel_id=1, source_target_pairs={{0,8},{1,9},{2,10},{3,11},{4,12},{5,13},{6,14},{7,15},{8,0},{9,1},... | collective-permute-start | bytes 1179656 | tf_op jit(solution)/shard_map/ppermute | solution.py:305
  322.2 57.8 %collective-permute-start.42 = (bf16[6,128,256]{2,1,0:T(8,128)(2,1)}, bf16[6,128,256]{2,1,0:T(8,128)(2,1)S(1)}, u32[]{:S(2)}, u32[]{:S(2)}) collective-permute-start(bf16[6,128,256]{2,1,0:T(8,128)(2,1)} %get-tuple-element.384), channel_id=1, source_target_pairs={{0,9},{1,8},{2,11},{3,10},{4,13},{5,12},{6,15},{7,14},{8,1},{9,0},... | collective-permute-start | bytes 1179656 | tf_op jit(solution)/shard_map/ppermute | solution.py:305
  348.3 39.9 %collective-permute-start.43 = (bf16[6,128,256]{2,1,0:T(8,128)(2,1)}, bf16[6,128,256]{2,1,0:T(8,128)(2,1)}, u32[]{:S(2)}, u32[]{:S(2)}) collective-permute-start(bf16[6,128,256]{2,1,0:T(8,128)(2,1)} %get-tuple-element.385), channel_id=1, source_target_pairs={{0,10},{1,11},{2,8},{3,9},{4,14},{5,15},{6,12},{7,13},{8,2},{9,3},... | collective-permute-start | bytes 1179656 | tf_op jit(solution)/shard_map/ppermute | solution.py:305
  352.1 58.2 %collective-permute-start.44 = (bf16[6,128,256]{2,1,0:T(8,128)(2,1)}, bf16[6,128,256]{2,1,0:T(8,128)(2,1)}, u32[]{:S(2)}, u32[]{:S(2)}) collective-permute-start(bf16[6,128,256]{2,1,0:T(8,128)(2,1)} %get-tuple-element.386), channel_id=1, source_target_pairs={{0,11},{1,10},{2,9},{3,8},{4,15},{5,14},{6,13},{7,12},{8,3},{9,2},... | collective-permute-start | bytes 1179656 | tf_op jit(solution)/shard_map/ppermute | solution.py:305
  353.8 66.1 %collective-permute-start.45 = (bf16[6,128,256]{2,1,0:T(8,128)(2,1)}, bf16[6,128,256]{2,1,0:T(8,128)(2,1)}, u32[]{:S(2)}, u32[]{:S(2)}) collective-permute-start(bf16[6,128,256]{2,1,0:T(8,128)(2,1)} %get-tuple-element.387), channel_id=1, source_target_pairs={{0,12},{1,13},{2,14},{3,15},{4,8},{5,9},{6,10},{7,11},{8,4},{9,5},... | collective-permute-start | bytes 1179656 | tf_op jit(solution)/shard_map/ppermute | solution.py:305
  358.8 62.1 %collective-permute-start.46 = (bf16[6,128,256]{2,1,0:T(8,128)(2,1)}, bf16[6,128,256]{2,1,0:T(8,128)(2,1)}, u32[]{:S(2)}, u32[]{:S(2)}) collective-permute-start(bf16[6,128,256]{2,1,0:T(8,128)(2,1)} %get-tuple-element.388), channel_id=1, source_target_pairs={{0,13},{1,12},{2,15},{3,14},{4,9},{5,8},{6,11},{7,10},{8,5},{9,4},... | collective-permute-start | bytes 1179656 | tf_op jit(solution)/shard_map/ppermute | solution.py:305
  380.1 49.9 %collective-permute-start.47 = (bf16[6,128,256]{2,1,0:T(8,128)(2,1)}, bf16[6,128,256]{2,1,0:T(8,128)(2,1)}, u32[]{:S(2)}, u32[]{:S(2)}) collective-permute-start(bf16[6,128,256]{2,1,0:T(8,128)(2,1)} %get-tuple-element.389), channel_id=1, source_target_pairs={{0,14},{1,15},{2,12},{3,13},{4,10},{5,11},{6,8},{7,9},{8,6},{9,7},... | collective-permute-start | bytes 1179656 | tf_op jit(solution)/shard_map/ppermute | solution.py:305
  388.2 45.1 %collective-permute-start.48 = (bf16[6,128,256]{2,1,0:T(8,128)(2,1)}, bf16[6,128,256]{2,1,0:T(8,128)(2,1)}, u32[]{:S(2)}, u32[]{:S(2)}) collective-permute-start(bf16[6,128,256]{2,1,0:T(8,128)(2,1)} %get-tuple-element.390), channel_id=1, source_target_pairs={{0,15},{1,14},{2,13},{3,12},{4,11},{5,10},{6,9},{7,8},{8,7},{9,6},... | collective-permute-start | bytes 1179656 | tf_op jit(solution)/shard_map/ppermute | solution.py:305
  410.3 42.0 %collective-permute-start.49 = (bf16[2,128,256]{2,1,0:T(8,128)(2,1)}, bf16[2,128,256]{2,1,0:T(8,128)(2,1)S(1)}, u32[]{:S(2)}, u32[]{:S(2)}) collective-permute-start(bf16[2,128,256]{2,1,0:T(8,128)(2,1)} %get-tuple-element.392), channel_id=1, source_target_pairs={{0,1},{1,0},{2,3},{3,2},{4,5},{5,4},{6,7},{7,6},{8,9},{9,8},{10,11... | collective-permute-start | bytes 393224 | tf_op jit(solution)/shard_map/ppermute | solution.py:305
  419.9 33.4 %collective-permute-start.50 = (bf16[2,128,256]{2,1,0:T(8,128)(2,1)}, bf16[2,128,256]{2,1,0:T(8,128)(2,1)S(1)}, u32[]{:S(2)}, u32[]{:S(2)}) collective-permute-start(bf16[2,128,256]{2,1,0:T(8,128)(2,1)} %get-tuple-element.393), channel_id=1, source_target_pairs={{0,2},{1,3},{2,0},{3,1},{4,6},{5,7},{6,4},{7,5},{8,10},{9,11},{10,... | collective-permute-start | bytes 393224 | tf_op jit(solution)/shard_map/ppermute | solution.py:305
  420.8 32.6 %collective-permute-start.51 = (bf16[2,128,256]{2,1,0:T(8,128)(2,1)}, bf16[2,128,256]{2,1,0:T(8,128)(2,1)S(1)}, u32[]{:S(2)}, u32[]{:S(2)}) collective-permute-start(bf16[2,128,256]{2,1,0:T(8,128)(2,1)} %get-tuple-element.394), channel_id=1, source_target_pairs={{0,3},{1,2},{2,1},{3,0},{4,7},{5,6},{6,5},{7,4},{8,11},{9,10},{10,... | collective-permute-start | bytes 393224 | tf_op jit(solution)/shard_map/ppermute | solution.py:305
  430.0 24.8 %collective-permute-start.52 = (bf16[2,128,256]{2,1,0:T(8,128)(2,1)}, bf16[2,128,256]{2,1,0:T(8,128)(2,1)S(1)}, u32[]{:S(2)}, u32[]{:S(2)}) collective-permute-start(bf16[2,128,256]{2,1,0:T(8,128)(2,1)} %get-tuple-element.395), channel_id=1, source_target_pairs={{0,4},{1,5},{2,6},{3,7},{4,0},{5,1},{6,2},{7,3},{8,12},{9,13},{10,... | collective-permute-start | bytes 393224 | tf_op jit(solution)/shard_map/ppermute | solution.py:305
  433.3 24.0 %collective-permute-start.53 = (bf16[2,128,256]{2,1,0:T(8,128)(2,1)}, bf16[2,128,256]{2,1,0:T(8,128)(2,1)S(1)}, u32[]{:S(2)}, u32[]{:S(2)}) collective-permute-start(bf16[2,128,256]{2,1,0:T(8,128)(2,1)} %get-tuple-element.396), channel_id=1, source_target_pairs={{0,5},{1,4},{2,7},{3,6},{4,1},{5,0},{6,3},{7,2},{8,13},{9,12},{10,... | collective-permute-start | bytes 393224 | tf_op jit(solution)/shard_map/ppermute | solution.py:305
  452.3 25.6 %collective-permute-start.54 = (bf16[2,128,256]{2,1,0:T(8,128)(2,1)S(1)}, bf16[2,128,256]{2,1,0:T(8,128)(2,1)S(1)}, u32[]{:S(2)}, u32[]{:S(2)}) collective-permute-start(bf16[2,128,256]{2,1,0:T(8,128)(2,1)S(1)} %copy-done.73), channel_id=1, source_target_pairs={{0,6},{1,7},{2,4},{3,5},{4,2},{5,3},{6,0},{7,1},{8,14},{9,15},{10,... | collective-permute-start | bytes 393224 | tf_op jit(solution)/shard_map/ppermute | solution.py:305
  453.3 26.8 %collective-permute-start.55 = (bf16[2,128,256]{2,1,0:T(8,128)(2,1)S(1)}, bf16[2,128,256]{2,1,0:T(8,128)(2,1)S(1)}, u32[]{:S(2)}, u32[]{:S(2)}) collective-permute-start(bf16[2,128,256]{2,1,0:T(8,128)(2,1)S(1)} %copy-done.71), channel_id=1, source_target_pairs={{0,7},{1,6},{2,5},{3,4},{4,3},{5,2},{6,1},{7,0},{8,15},{9,14},{10,... | collective-permute-start | bytes 393224 | tf_op jit(solution)/shard_map/ppermute | solution.py:305
  453.4 27.4 %collective-permute-start.56 = (bf16[2,128,256]{2,1,0:T(8,128)(2,1)S(1)}, bf16[2,128,256]{2,1,0:T(8,128)(2,1)S(1)}, u32[]{:S(2)}, u32[]{:S(2)}) collective-permute-start(bf16[2,128,256]{2,1,0:T(8,128)(2,1)S(1)} %copy-done.69), channel_id=1, source_target_pairs={{0,8},{1,9},{2,10},{3,11},{4,12},{5,13},{6,14},{7,15},{8,0},{9,1},... | collective-permute-start | bytes 393224 | tf_op jit(solution)/shard_map/ppermute | solution.py:305
  454.8 28.0 %collective-permute-start.57 = (bf16[2,128,256]{2,1,0:T(8,128)(2,1)S(1)}, bf16[2,128,256]{2,1,0:T(8,128)(2,1)S(1)}, u32[]{:S(2)}, u32[]{:S(2)}) collective-permute-start(bf16[2,128,256]{2,1,0:T(8,128)(2,1)S(1)} %copy-done.67), channel_id=1, source_target_pairs={{0,9},{1,8},{2,11},{3,10},{4,13},{5,12},{6,15},{7,14},{8,1},{9,0},... | collective-permute-start | bytes 393224 | tf_op jit(solution)/shard_map/ppermute | solution.py:305
  457.3 27.2 %collective-permute-start.58 = (bf16[2,128,256]{2,1,0:T(8,128)(2,1)S(1)}, bf16[2,128,256]{2,1,0:T(8,128)(2,1)S(1)}, u32[]{:S(2)}, u32[]{:S(2)}) collective-permute-start(bf16[2,128,256]{2,1,0:T(8,128)(2,1)S(1)} %copy-done.65), channel_id=1, source_target_pairs={{0,10},{1,11},{2,8},{3,9},{4,14},{5,15},{6,12},{7,13},{8,2},{9,3},... | collective-permute-start | bytes 393224 | tf_op jit(solution)/shard_map/ppermute | solution.py:305
  478.0 28.5 %collective-permute-start.59 = (bf16[2,128,256]{2,1,0:T(8,128)(2,1)S(1)}, bf16[2,128,256]{2,1,0:T(8,128)(2,1)S(1)}, u32[]{:S(2)}, u32[]{:S(2)}) collective-permute-start(bf16[2,128,256]{2,1,0:T(8,128)(2,1)S(1)} %copy-done.62), channel_id=1, source_target_pairs={{0,11},{1,10},{2,9},{3,8},{4,15},{5,14},{6,13},{7,12},{8,3},{9,2},... | collective-permute-start | bytes 393224 | tf_op jit(solution)/shard_map/ppermute | solution.py:305
  480.1 26.3 %collective-permute-start.60 = (bf16[2,128,256]{2,1,0:T(8,128)(2,1)S(1)}, bf16[2,128,256]{2,1,0:T(8,128)(2,1)S(1)}, u32[]{:S(2)}, u32[]{:S(2)}) collective-permute-start(bf16[2,128,256]{2,1,0:T(8,128)(2,1)S(1)} %copy-done.60), channel_id=1, source_target_pairs={{0,12},{1,13},{2,14},{3,15},{4,8},{5,9},{6,10},{7,11},{8,4},{9,5},... | collective-permute-start | bytes 393224 | tf_op jit(solution)/shard_map/ppermute | solution.py:305
  480.8 25.6 %collective-permute-start.61 = (bf16[2,128,256]{2,1,0:T(8,128)(2,1)S(1)}, bf16[2,128,256]{2,1,0:T(8,128)(2,1)S(1)}, u32[]{:S(2)}, u32[]{:S(2)}) collective-permute-start(bf16[2,128,256]{2,1,0:T(8,128)(2,1)S(1)} %copy-done.59), channel_id=1, source_target_pairs={{0,13},{1,12},{2,15},{3,14},{4,9},{5,8},{6,11},{7,10},{8,5},{9,4},... | collective-permute-start | bytes 393224 | tf_op jit(solution)/shard_map/ppermute | solution.py:305
  482.8 23.7 %collective-permute-start.62 = (bf16[2,128,256]{2,1,0:T(8,128)(2,1)S(1)}, bf16[2,128,256]{2,1,0:T(8,128)(2,1)S(1)}, u32[]{:S(2)}, u32[]{:S(2)}) collective-permute-start(bf16[2,128,256]{2,1,0:T(8,128)(2,1)S(1)} %copy-done.57), channel_id=1, source_target_pairs={{0,14},{1,15},{2,12},{3,13},{4,10},{5,11},{6,8},{7,9},{8,6},{9,7},... | collective-permute-start | bytes 393224 | tf_op jit(solution)/shard_map/ppermute | solution.py:305
  484.5 22.0 %collective-permute-start.63 = (bf16[2,128,256]{2,1,0:T(8,128)(2,1)S(1)}, bf16[2,128,256]{2,1,0:T(8,128)(2,1)S(1)}, u32[]{:S(2)}, u32[]{:S(2)}) collective-permute-start(bf16[2,128,256]{2,1,0:T(8,128)(2,1)S(1)} %copy-done.56), channel_id=1, source_target_pairs={{0,15},{1,14},{2,13},{3,12},{4,11},{5,10},{6,9},{7,8},{8,7},{9,6},... | collective-permute-start | bytes 393224 | tf_op jit(solution)/shard_map/ppermute | solution.py:305
  (75 other events, 3260.1 us)
Sparse Core Ops, SparseCore 0:
  78.7 79.0 all-gather.1

commit v5 on v3

--- a/solution.py
+++ b/solution.py
@@ -205,18 +205,32 @@
     )(pair_list, pair_count, integrals, basis_rows)
 
 
-def fit_kernel(step_rows, factor_ref, half_ref, before_ref, out_ref):
+def fit_kernel(step_rows, half_ref, before_ref, factor_ref, out_ref, lower_ref, sems):
     aux_total = factor_ref.shape[0]
     basis_total = out_ref.shape[0]
     steps = half_ref.shape[1]
+    lows = range(0, aux_total, step_rows)
+    copies = []
+    for number, low in enumerate(lows):
+        part = (slice(low, low + step_rows), slice(0, low + step_rows))
+        copies.append(
+            pltpu.make_async_copy(factor_ref.at[part], lower_ref.at[part], sems.at[number])
+        )
+
+    @pl.when(pl.program_id(0) == 0)
+    def _():
+        for copy in copies:
+            copy.start()
+
     columns = jnp.concatenate(
         [half_ref[:, k].reshape(aux_total, basis_total) for k in range(steps)], axis=1
     )
     total = jnp.zeros(out_ref.shape, jnp.float32)
-    for low in range(0, aux_total, step_rows):
+    for number, low in enumerate(lows):
         high = low + step_rows
+        pl.when(pl.program_id(0) == 0)(copies[number].wait)
         fitted = jnp.dot(
-            factor_ref[low:high, :high], columns[:high], preferred_element_type=jnp.float32
+            lower_ref[low:high, :high], columns[:high], preferred_element_type=jnp.float32
         ).astype(jnp.bfloat16)
         for k in range(steps):
             one = fitted[:, k * basis_total : (k + 1) * basis_total]
@@ -242,13 +256,15 @@
         out_shape=jax.ShapeDtypeStruct((basis_total, basis_total), jnp.float32),
         grid=(own // steps,),
         in_specs=[
-            pl.BlockSpec(
-                (aux_total, aux_total), lambda k: (0, 0), pipeline_mode=pl.Buffered(1)
-            ),
             pl.BlockSpec((devices, steps, aux_local, basis_total), lambda k: (0, k, 0, 0)),
             pl.BlockSpec((basis_total, basis_total), lambda k: (0, 0)),
+            pl.BlockSpec(memory_space=pl.ANY),
         ],
         out_specs=pl.BlockSpec((basis_total, basis_total), lambda k: (0, 0)),
+        scratch_shapes=[
+            pltpu.VMEM((aux_total, aux_total), jnp.bfloat16),
+            pltpu.SemaphoreType.DMA((8,)),
+        ],
         compiler_params=pltpu.CompilerParams(vmem_limit_bytes=VMEM_BYTES),
         cost_estimate=pl.CostEstimate(
             flops=own * aux_total * basis_total * (aux_total * 9 // 8 + 2 * basis_total),
@@ -256,69 +272,40 @@
             transcendentals=0,
         ),
         name="fit_exchange",
-    )(factor, arrived, before)
-
-
-def line_step(step, upward, downward, axis):
-    devices = lax.axis_size(axis)
-    upward = lax.ppermute(upward, axis, [(i, i + 1) for i in range(step, devices - 1)])
-    downward = lax.ppermute(downward, axis, [(i, i - 1) for i in range(1, devices - step)])
-    return upward, downward
-
-
-def line_blocks(block, passed, axis):
-    devices = lax.axis_size(axis)
-    up, down = [pair[0] for pair in passed], [pair[1] for pair in passed]
-    around = jnp.stack(up[::-1] + [block] + down)
-    first = devices - 1 - lax.axis_index(axis)
-    blocks = lax.dynamic_slice_in_dim(around, first, devices, 0)
-    return blocks.reshape(devices * block.shape[0], block.shape[1])
+    )(arrived, before, factor)
 
 
 def chunk_sizes(own):
-    if own % 8 == 0:
-        return [own // 8, 3 * own // 8, 3 * own // 8, own // 8]
+    if own % 16 == 0:
+        return [own // 8, 3 * own // 8, 7 * own // 16, own // 16]
     return [1] * own
 
 
 def per_device(integrals, pair_list, pair_count, coefficients, metric):
     devices = lax.axis_size("aux") * lax.axis_size("occ")
     basis_total = coefficients.shape[0]
-    passed = [line_step(0, metric, metric, "occ")]
+    line = lax.all_gather(metric, "occ", axis=0, tiled=True)
     total = jnp.zeros((basis_total, basis_total), jnp.float32)
     state = (coefficients,)
     start = 0
-    arrived = None
+    arrived = []
     factor = None
-    waiting = []
     for chunk, own in enumerate(chunk_sizes(basis_total // devices)):
         width = own * devices
         rows, state = factor_rows(start, width, basis_total, state)
-        if chunk == 0:
-            rows, passed[0] = lax.optimization_barrier((rows, passed[0]))
-            passed.append(line_step(1, *passed[0], "occ"))
         half = half_transform(integrals, pair_list, pair_count, rows, start, devices)
         if chunk == 0:
-            half, state, passed[1] = lax.optimization_barrier((half, state, passed[1]))
-            for step in range(2, lax.axis_size("occ") - 1):
-                passed.append(line_step(step, *passed[-1], "occ"))
-            line = line_blocks(metric, passed, "occ")
-        elif chunk == 1:
-            half, state, arrived, line = lax.optimization_barrier((half, state, arrived, line))
+            half, state, line = lax.optimization_barrier((half, state, line))
             factor = lax.all_gather(line, "aux", axis=0, tiled=True)
-        elif chunk == 2:
-            half, state, arrived, factor = lax.optimization_barrier(
-                (half, state, arrived, factor)
+        else:
+            if chunk > 1:
+                total = fit_exchange(factor, arrived[chunk - 2], total)
+            half, state, arrived[chunk - 1], total = lax.optimization_barrier(
+                (half, state, arrived[chunk - 1], total)
             )
-        else:
-            half, state, arrived = lax.optimization_barrier((half, state, arrived))
-        if chunk > 0:
-            waiting.append(arrived)
-        if chunk > 1:
-            total = fit_exchange(factor, waiting.pop(0), total)
-        arrived = lax.all_to_all(half, BOTH, split_axis=0, concat_axis=0, tiled=True)
+        arrived.append(lax.all_to_all(half, BOTH, split_axis=0, concat_axis=0, tiled=True))
         start += width
-    for piece in waiting + [arrived]:
+    for piece in arrived[-2:]:
         total = fit_exchange(factor, piece, total)
     shares = total.reshape(devices, basis_total // devices, basis_total)
     return jnp.sum(lax.all_to_all(shares, BOTH, split_axis=0, concat_axis=0, tiled=True), axis=0)

time: 485 us -> 495 us (1.021)
  starting transfers between devices: 34.4 us -> 17 us
  Pallas kernels: 178 us -> 194 us
  waiting for transfers between devices: 234 us -> 248 us
    all_to_all x4, waiting for transfers between devices: 225 us -> 188 us  [per_device(): lax.all_to_all(half, BOTH, split_axis=0, concat_axis=0, tiled=True)]
    all_gather x1, waiting for transfers between devices: 0.01 us -> 34.7 us  [per_device(): factor = lax.all_gather(line, 'aux', axis=0, tiled=True)]
    all_gather x0 -> x1, waiting for transfers between devices: none -> 24.4 us  [per_device(): line = lax.all_gather(metric, 'occ', axis=0, tiled=True)]
    pallas_call x4, Pallas kernels: 56.6 us -> 72.3 us  [fit_exchange(): pl.pallas_call(functools.partial(fit_kernel, aux_total // 8), out_shape=j...]
    ppermute x6 -> x0, starting transfers between devices: 11.7 us -> none  [the longest x3 7.84 us: line_step(): lax.ppermute(upward, axis, [(i, i + 1) for i in range(step, devices - 1)])]
    ppermute x6 -> x0, waiting for transfers between devices: 9.08 us -> none  [the longest x3 6.55 us: line_step(): lax.ppermute(downward, axis, [(i, i - 1) for i in range(1, devices - step)])]
    all_to_all x4, starting transfers between devices: 22.6 us -> 16.9 us  [per_device(): lax.all_to_all(half, BOTH, split_axis=0, concat_axis=0, tiled=True)]
  transfers between devices with their start and end apart: 11 -> 6, of which waited for: 7 -> 5; matrix products, arithmetic and copies ran while one was open for 1% -> 0% of each run, Pallas kernels for 35% -> 38%
where the time goes in v5:
time: 495 us; the launch traced here: 493 us
  waiting for transfers between devices  248 us (50%)
  Pallas kernels  194 us (39%)
  starting transfers between devices  17 us (3%)
  blocking collectives  16 us (3%)
  between operations  13.5 us (3%)
    all_to_all x4, waiting for transfers between devices, per_device(): lax.all_to_all(half, BOTH, split_axis=0, concat_axis=0, tiled=True)  188 us
    pallas_call x4, Pallas kernels, fit_exchange(): pl.pallas_call(functools.partial(fit_kernel, aux_total // 8), out_shape=j...  72.3 us
    pallas_call x4, Pallas kernels, half_transform(): pl.pallas_call(functools.partial(half_kernel, start // size_block), out_s...  68.3 us
    pallas_call x4, Pallas kernels, factor_rows(): pl.pallas_call(functools.partial(factor_kernel, start), out_shape=(jax.Sh...  52.9 us
    all_gather x1, waiting for transfers between devices, per_device(): factor = lax.all_gather(line, 'aux', axis=0, tiled=True)  34.7 us
    all_gather x1, waiting for transfers between devices, per_device(): line = lax.all_gather(metric, 'occ', axis=0, tiled=True)  24.4 us
    all_to_all x4, starting transfers between devices, per_device(): lax.all_to_all(half, BOTH, split_axis=0, concat_axis=0, tiled=True)  16.9 us
    all_to_all x1, blocking collectives, per_device(): lax.all_to_all(shares, BOTH, split_axis=0, concat_axis=0, tiled=True)  16 us
  transfers between devices with their start and end apart: 6, of which 5 were waited for; matrix products, arithmetic and copies ran while one was open for 0% of the time, Pallas kernels for 38%

profile of v5, /device:TPU:0, one launch (start us, length us, event | category | flops | bytes accessed | tf_op | source)
XLA Modules:
  0.0 493.5 jit_solution(7187739834970529632)
XLA Ops:
  6.5 0.0 all-gather.3.cloned.1.call-start
  6.5 0.7 all-gather.3.cloned.1.call-update
  7.3 1.3 copy.9.list_ref
  8.6 7.7 %factor_rows.4 = (bf16[64,256]{1,0:T(8,128)(2,1)}, f32[256,256]{1,0:T(8,128)}, f32[8,256]{1,0:T(8,128)}) custom-call(bf16[256,384]{1,0:T(8,128)(2,1)} %refs_0_.1), custom_call_target="tpu_custom_call" | custom-call | tf_op jit(solution)/shard_map/factor_rows/pallas_call | solution.py:102
  16.3 16.9 %half_transform.4 = bf16[16,2,128,256]{3,2,1,0:T(8,128)(2,1)} custom-call(s32[8,4]{1,0:T(8,128)} %copy.9.list_ref, s32[8]{0:T(128)} %count_ref.7, bf16[8,4,16,128,128]{4,3,2,1,0:T(8,128)(2,1)} %ints_ref.7, bf16[64,256]{1,0:T(8,128)(2,1)} %get-tuple-element.32.basis_ref), custom_call_target="tpu_custom_call" | custom-call | flops 1073741824 | bytes 18874368 | tf_op jit(solution)/shard_map/half_transform/pallas_call | solution.py:171
  33.2 24.4 %all-gather.3.cloned.1.call-done = bf16[512,2048]{1,0:T(8,128)(2,1)} async-done(((bf16[128,2048]{1,0:T(8,128)(2,1)}), bf16[512,2048]{1,0:T(8,128)(2,1)}) %all-gather.3.cloned.1.call-update) | async-done | bytes 2097168 | tf_op jit(solution)/shard_map/all_gather | solution.py:287
  57.6 3.7 all-to-all-start
  61.4 0.0 all-gather.5.cloned.1.call-start
  61.4 0.7 all-gather.5.cloned.1.call-update
  62.1 19.0 %factor_rows.5 = (bf16[192,256]{1,0:T(8,128)(2,1)}, f32[256,256]{1,0:T(8,128)}, f32[8,256]{1,0:T(8,128)}) custom-call(f32[256,256]{1,0:T(8,128)} %get-tuple-element.35.refs_0_, f32[8,256]{1,0:T(8,128)} %get-tuple-element.36.refs_1_), custom_call_target="tpu_custom_call" | custom-call | tf_op jit(solution)/shard_map/factor_rows/pallas_call | solution.py:102
  81.1 19.9 %half_transform.5 = bf16[16,6,128,256]{3,2,1,0:T(8,128)(2,1)} custom-call(s32[8,4]{1,0:T(8,128)} %copy.9.list_ref, s32[8]{0:T(128)} %count_ref.7, bf16[8,4,16,128,128]{4,3,2,1,0:T(8,128)(2,1)} %ints_ref.7, bf16[192,256]{1,0:T(8,128)(2,1)} %get-tuple-element.37.basis_ref), custom_call_target="tpu_custom_call" | custom-call | flops 3221225472 | bytes 23068672 | tf_op jit(solution)/shard_map/half_transform/pallas_call | solution.py:171
  101.0 9.9 %all-to-all-done.half_ref = bf16[16,2,128,256]{3,2,1,0:T(8,128)(2,1)S(1)} async-done(((bf16[16,2,128,256]{3,2,1,0:T(8,128)(2,1)}), bf16[16,2,128,256]{3,2,1,0:T(8,128)(2,1)S(1)}, u32[]{:S(2)}, u32[]{:S(2)}) %all-to-all-start) | async-done | bytes 2097184 | tf_op jit(solution)/shard_map/all_to_all | solution.py:306
  110.8 0.0 copy-start
  110.8 1.3 copy-done
  112.1 4.7 all-to-all-start.1
  116.8 21.8 %factor_rows.6 = (bf16[224,256]{1,0:T(8,128)(2,1)}, f32[256,256]{1,0:T(8,128)}, f32[8,256]{1,0:T(8,128)}) custom-call(f32[256,256]{1,0:T(8,128)} %get-tuple-element.41.refs_0_, f32[8,256]{1,0:T(8,128)} %get-tuple-element.42.refs_1_), custom_call_target="tpu_custom_call" | custom-call | tf_op jit(solution)/shard_map/factor_rows/pallas_call | solution.py:102
  138.6 17.8 %half_transform.6 = bf16[16,7,128,256]{3,2,1,0:T(8,128)(2,1)} custom-call(s32[8,4]{1,0:T(8,128)} %copy.9.list_ref, s32[8]{0:T(128)} %count_ref.7, bf16[8,4,16,128,128]{4,3,2,1,0:T(8,128)(2,1)} %ints_ref.7, bf16[224,256]{1,0:T(8,128)(2,1)} %get-tuple-element.43.basis_ref), custom_call_target="tpu_custom_call" | custom-call | flops 3758096384 | bytes 24117248 | tf_op jit(solution)/shard_map/half_transform/pallas_call | solution.py:171
  156.4 34.7 %all-gather.5.cloned.1.call-done.factor_ref = bf16[2048,2048]{1,0:T(8,128)(2,1)} async-done(((bf16[512,2048]{1,0:T(8,128)(2,1)}), bf16[2048,2048]{1,0:T(8,128)(2,1)}) %all-gather.5.cloned.1.call-update) | async-done | bytes 8388624 | tf_op jit(solution)/shard_map/all_gather | solution.py:299
  191.1 0.7 broadcast_in_dim.3.before_ref
  191.8 9.0 %fit_exchange.4.before_ref = f32[256,256]{1,0:T(8,128)} custom-call(bf16[16,2,128,256]{3,2,1,0:T(8,128)(2,1)} %copy-done, f32[256,256]{1,0:T(8,128)} %broadcast_in_dim.3.before_ref, bf16[2048,2048]{1,0:T(8,128)(2,1)} %all-gather.5.cloned.1.call-done.factor_ref), custom_call_target="tpu_custom_call" | custom-call | flops 2952790016 | bytes 10485760 | tf_op jit(solution)/shard_map/fit_exchange/pallas_call | solution.py:254
  200.8 55.3 %all-to-all-done.1.half_ref = bf16[16,6,128,256]{3,2,1,0:T(8,128)(2,1)} async-done(((bf16[16,6,128,256]{3,2,1,0:T(8,128)(2,1)}), bf16[16,6,128,256]{3,2,1,0:T(8,128)(2,1)}, u32[]{:S(2)}, u32[]{:S(2)}) %all-to-all-start.1) | async-done | bytes 6291488 | tf_op jit(solution)/shard_map/all_to_all | solution.py:306
  256.1 4.9 all-to-all-start.2
  261.1 4.5 factor_rows.7
  265.6 13.7 %half_transform.7 = bf16[16,1,128,256]{3,2,1,0:T(8,128)(2,1)} custom-call(s32[8,4]{1,0:T(8,128)} %copy.9.list_ref, s32[8]{0:T(128)} %count_ref.7, bf16[8,4,16,128,128]{4,3,2,1,0:T(8,128)(2,1)} %ints_ref.7, bf16[32,256]{1,0:T(8,128)(2,1)} %get-tuple-element.52.basis_ref), custom_call_target="tpu_custom_call" | custom-call | flops 536870912 | bytes 17825792 | tf_op jit(solution)/shard_map/half_transform/pallas_call | solution.py:171
  279.2 20.8 %fit_exchange.5.before_ref = f32[256,256]{1,0:T(8,128)} custom-call(bf16[16,6,128,256]{3,2,1,0:T(8,128)(2,1)} %all-to-all-done.1.half_ref, f32[256,256]{1,0:T(8,128)} %fit_exchange.4.before_ref, bf16[2048,2048]{1,0:T(8,128)(2,1)} %all-gather.5.cloned.1.call-done.factor_ref), custom_call_target="tpu_custom_call" | custom-call | flops 8858370048 | bytes 14680064 | tf_op jit(solution)/shard_map/fit_exchange/pallas_call | solution.py:254
  300.0 122.7 %all-to-all-done.2.half_ref = bf16[16,7,128,256]{3,2,1,0:T(8,128)(2,1)} async-done(((bf16[16,7,128,256]{3,2,1,0:T(8,128)(2,1)}), bf16[16,7,128,256]{3,2,1,0:T(8,128)(2,1)}, u32[]{:S(2)}, u32[]{:S(2)}) %all-to-all-start.2) | async-done | bytes 7340064 | tf_op jit(solution)/shard_map/all_to_all | solution.py:306
  422.7 3.7 all-to-all-start.3
  426.3 35.1 %fit_exchange.6.before_ref = f32[256,256]{1,0:T(8,128)} custom-call(bf16[16,7,128,256]{3,2,1,0:T(8,128)(2,1)} %all-to-all-done.2.half_ref, f32[256,256]{1,0:T(8,128)} %fit_exchange.5.before_ref, bf16[2048,2048]{1,0:T(8,128)(2,1)} %all-gather.5.cloned.1.call-done.factor_ref), custom_call_target="tpu_custom_call" | custom-call | flops 10334765056 | bytes 15728640 | tf_op jit(solution)/shard_map/fit_exchange/pallas_call | solution.py:254
  461.4 0.0 all-to-all-done.3.half_ref
  461.5 0.0 copy-start.1
  461.5 1.0 copy-done.1
  462.5 7.4 %fit_exchange.7 = f32[256,256]{1,0:T(8,128)} custom-call(bf16[16,1,128,256]{3,2,1,0:T(8,128)(2,1)} %copy-done.1, f32[256,256]{1,0:T(8,128)} %fit_exchange.6.before_ref, bf16[2048,2048]{1,0:T(8,128)(2,1)} %all-gather.5.cloned.1.call-done.factor_ref), custom_call_target="tpu_custom_call" | custom-call | flops 1476395008 | bytes 9437184 | tf_op jit(solution)/shard_map/fit_exchange/pallas_call | solution.py:254
  470.0 16.0 %all_to_all.25 = f32[16,16,256]{2,1,0:T(8,128)S(1)} all-to-all(f32[16,16,256]{2,1,0:T(8,128)} %bitcast.1), channel_id=1, replica_groups=mesh['grp'=2,'aux'=4,'occ'=4] {'aux','occ'}, dimensions={0} | all-to-all | bytes 524288 | tf_op jit(solution)/shard_map/all_to_all | solution.py:311
  486.0 0.6 reduce_sum.9
Async XLA Ops:
  6.5 51.1 %all-gather.3.cloned.1.call-start = ((), (), s32[]{:S(2)}) async-start(), calls=%async_computation.5 | async-start | bytes 2621440 | tf_op jit(solution)/shard_map/all_gather | solution.py:287
  57.6 53.2 %all-to-all-start = ((bf16[16,2,128,256]{3,2,1,0:T(8,128)(2,1)}), bf16[16,2,128,256]{3,2,1,0:T(8,128)(2,1)S(1)}, u32[]{:S(2)}, u32[]{:S(2)}) async-start(bf16[16,2,128,256]{3,2,1,0:T(8,128)(2,1)} %half_transform.4), calls=%async_computation | async-start | bytes 4194304 | tf_op jit(solution)/shard_map/all_to_all | solution.py:306
  61.4 129.8 %all-gather.5.cloned.1.call-start = ((), (), s32[]{:S(2)}) async-start(), calls=%async_computation.6 | async-start | bytes 10485760 | tf_op jit(solution)/shard_map/all_gather | solution.py:299
  110.8 1.3 copy-start
  112.1 144.0 %all-to-all-start.1 = ((bf16[16,6,128,256]{3,2,1,0:T(8,128)(2,1)}), bf16[16,6,128,256]{3,2,1,0:T(8,128)(2,1)}, u32[]{:S(2)}, u32[]{:S(2)}) async-start(bf16[16,6,128,256]{3,2,1,0:T(8,128)(2,1)} %half_transform.5), calls=%async_computation.1 | async-start | bytes 12582912 | tf_op jit(solution)/shard_map/all_to_all | solution.py:306
  256.1 166.5 %all-to-all-start.2 = ((bf16[16,7,128,256]{3,2,1,0:T(8,128)(2,1)}), bf16[16,7,128,256]{3,2,1,0:T(8,128)(2,1)}, u32[]{:S(2)}, u32[]{:S(2)}) async-start(bf16[16,7,128,256]{3,2,1,0:T(8,128)(2,1)} %half_transform.6), calls=%async_computation.2 | async-start | bytes 14680064 | tf_op jit(solution)/shard_map/all_to_all | solution.py:306
  422.7 38.8 %all-to-all-start.3 = ((bf16[16,1,128,256]{3,2,1,0:T(8,128)(2,1)}), bf16[16,1,128,256]{3,2,1,0:T(8,128)(2,1)S(1)}, u32[]{:S(2)}, u32[]{:S(2)}) async-start(bf16[16,1,128,256]{3,2,1,0:T(8,128)(2,1)} %half_transform.7), calls=%async_computation.3 | async-start | bytes 2097152 | tf_op jit(solution)/shard_map/all_to_all | solution.py:306
  461.5 1.1 copy-start.1
Sparse Core Ops, SparseCore 0:
  8.9 48.6 all-gather.2
  63.8 127.3 all-gather.4

commit v6 on v5

--- a/solution.py
+++ b/solution.py
@@ -9,6 +9,7 @@
 
 BOTH = ("aux", "occ")
 VMEM_BYTES = 58 * 2**20
+FIT_VMEM_BYTES = 63 * 2**20
 PANEL = 16
 GROUP = 4
 SCALE = 2.0**40
@@ -205,22 +206,36 @@
     )(pair_list, pair_count, integrals, basis_rows)
 
 
-def fit_kernel(step_rows, half_ref, before_ref, factor_ref, out_ref, lower_ref, sems):
-    aux_total = factor_ref.shape[0]
+def fit_kernel(step_rows, half_ref, before_ref, left_ref, right_ref, out_ref, lower_ref, sems):
+    aux_total, split = left_ref.shape
     basis_total = out_ref.shape[0]
     steps = half_ref.shape[1]
     lows = range(0, aux_total, step_rows)
     copies = []
     for number, low in enumerate(lows):
-        part = (slice(low, low + step_rows), slice(0, low + step_rows))
+        high = low + step_rows
+        width = min(high, split)
         copies.append(
-            pltpu.make_async_copy(factor_ref.at[part], lower_ref.at[part], sems.at[number])
-        )
+            [
+                pltpu.make_async_copy(
+                    left_ref.at[low:high, :width], lower_ref.at[low:high, :width], sems.at[0, number]
+                )
+            ]
+        )
+        if high > split:
+            copies[-1].append(
+                pltpu.make_async_copy(
+                    right_ref.at[low:high, : high - split],
+                    lower_ref.at[low:high, split:high],
+                    sems.at[1, number],
+                )
+            )
 
     @pl.when(pl.program_id(0) == 0)
     def _():
-        for copy in copies:
-            copy.start()
+        for pair in copies:
+            for copy in pair:
+                copy.start()
 
     columns = jnp.concatenate(
         [half_ref[:, k].reshape(aux_total, basis_total) for k in range(steps)], axis=1
@@ -228,7 +243,12 @@
     total = jnp.zeros(out_ref.shape, jnp.float32)
     for number, low in enumerate(lows):
         high = low + step_rows
-        pl.when(pl.program_id(0) == 0)(copies[number].wait)
+
+        @pl.when(pl.program_id(0) == 0)
+        def _():
+            for copy in copies[number]:
+                copy.wait()
+
         fitted = jnp.dot(
             lower_ref[low:high, :high], columns[:high], preferred_element_type=jnp.float32
         ).astype(jnp.bfloat16)
@@ -249,7 +269,7 @@
 
 def fit_exchange(factor, arrived, before):
     devices, own, aux_local, basis_total = arrived.shape
-    aux_total = factor.shape[0]
+    aux_total = factor[0].shape[0]
     steps = 2 if own % 2 == 0 else 1
     return pl.pallas_call(
         functools.partial(fit_kernel, aux_total // 8),
@@ -259,32 +279,35 @@
             pl.BlockSpec((devices, steps, aux_local, basis_total), lambda k: (0, k, 0, 0)),
             pl.BlockSpec((basis_total, basis_total), lambda k: (0, 0)),
             pl.BlockSpec(memory_space=pl.ANY),
+            pl.BlockSpec(memory_space=pl.ANY),
         ],
         out_specs=pl.BlockSpec((basis_total, basis_total), lambda k: (0, 0)),
         scratch_shapes=[
             pltpu.VMEM((aux_total, aux_total), jnp.bfloat16),
-            pltpu.SemaphoreType.DMA((8,)),
+            pltpu.SemaphoreType.DMA((2, 8)),
         ],
-        compiler_params=pltpu.CompilerParams(vmem_limit_bytes=VMEM_BYTES),
+        compiler_params=pltpu.CompilerParams(vmem_limit_bytes=FIT_VMEM_BYTES),
         cost_estimate=pl.CostEstimate(
             flops=own * aux_total * basis_total * (aux_total * 9 // 8 + 2 * basis_total),
-            bytes_accessed=(factor.size + arrived.size) * 2,
+            bytes_accessed=(aux_total * aux_total + arrived.size) * 2,
             transcendentals=0,
         ),
         name="fit_exchange",
-    )(arrived, before, factor)
+    )(arrived, before, *factor)
 
 
 def chunk_sizes(own):
-    if own % 16 == 0:
-        return [own // 8, 3 * own // 8, 7 * own // 16, own // 16]
+    if own % 8 == 0:
+        return [own // 4, 5 * own // 8, own // 8]
     return [1] * own
 
 
 def per_device(integrals, pair_list, pair_count, coefficients, metric):
     devices = lax.axis_size("aux") * lax.axis_size("occ")
     basis_total = coefficients.shape[0]
-    line = lax.all_gather(metric, "occ", axis=0, tiled=True)
+    split = metric.shape[1] * 5 // 8
+    left, right = metric[:, :split], metric[:, split:]
+    left = lax.all_gather(left, "occ", axis=0, tiled=True)
     total = jnp.zeros((basis_total, basis_total), jnp.float32)
     state = (coefficients,)
     start = 0
@@ -295,8 +318,9 @@
         rows, state = factor_rows(start, width, basis_total, state)
         half = half_transform(integrals, pair_list, pair_count, rows, start, devices)
         if chunk == 0:
-            half, state, line = lax.optimization_barrier((half, state, line))
-            factor = lax.all_gather(line, "aux", axis=0, tiled=True)
+            half, state, left, right = lax.optimization_barrier((half, state, left, right))
+            right = lax.all_gather(right, "occ", axis=0, tiled=True)
+            factor = [lax.all_gather(part, "aux", axis=0, tiled=True) for part in (left, right)]
         else:
             if chunk > 1:
                 total = fit_exchange(factor, arrived[chunk - 2], total)

time: 495 us -> 563 us (1.14)
  blocking collectives: 16 us -> 256 us
  waiting for transfers between devices: 248 us -> 110 us
  Pallas kernels: 194 us -> 165 us
    all_gather x0 -> x1, blocking collectives: none -> 242 us  [per_device(): right = lax.all_gather(right, 'occ', axis=0, tiled=True)]
    all_to_all x4 -> x3, waiting for transfers between devices: 188 us -> 57.1 us  [per_device(): lax.all_to_all(half, BOTH, split_axis=0, concat_axis=0, tiled=True)]
    pallas_call x4 -> x3, Pallas kernels: 72.3 us -> 56.6 us  [fit_exchange(): pl.pallas_call(functools.partial(fit_kernel, aux_total // 8), out_shape=j...]
    pallas_call x4 -> x3, Pallas kernels: 68.3 us -> 57.1 us  [half_transform(): pl.pallas_call(functools.partial(half_kernel, start // size_block), out_s...]
    all_gather x2 -> x3, waiting for transfers between devices: 59.1 us -> 52.1 us  [the longest x2 48.9 us: per_device(): lax.all_gather(part, 'aux', axis=0, tiled=True)]
    all_to_all x4 -> x3, starting transfers between devices: 16.9 us -> 14.3 us  [per_device(): lax.all_to_all(half, BOTH, split_axis=0, concat_axis=0, tiled=True)]
    pallas_call x4 -> x3, Pallas kernels: 52.9 us -> 51.3 us  [factor_rows(): pl.pallas_call(functools.partial(factor_kernel, start), out_shape=(jax.Sh...]
  transfers between devices with their start and end apart: 6 -> 6, of which waited for: 5 -> 5; matrix products, arithmetic and copies ran while one was open for 0% -> 0% of each run, Pallas kernels for 38% -> 28%
where the time goes in v6:
time: 563 us
  blocking collectives  256 us (45%)
  Pallas kernels  165 us (29%)
  waiting for transfers between devices  110 us (20%)
  starting transfers between devices  14.4 us (3%)
  between operations  13.2 us (2%)
    all_gather x1, blocking collectives, per_device(): right = lax.all_gather(right, 'occ', axis=0, tiled=True)  242 us
    all_to_all x3, waiting for transfers between devices, per_device(): lax.all_to_all(half, BOTH, split_axis=0, concat_axis=0, tiled=True)  57.1 us
    pallas_call x3, Pallas kernels, half_transform(): pl.pallas_call(functools.partial(half_kernel, start // size_block), out_s...  57.1 us
    pallas_call x3, Pallas kernels, fit_exchange(): pl.pallas_call(functools.partial(fit_kernel, aux_total // 8), out_shape=j...  56.6 us
    pallas_call x3, Pallas kernels, factor_rows(): pl.pallas_call(functools.partial(factor_kernel, start), out_shape=(jax.Sh...  51.3 us
    all_gather x2, waiting for transfers between devices, per_device(): lax.all_gather(part, 'aux', axis=0, tiled=True)  48.9 us
    all_to_all x3, starting transfers between devices, per_device(): lax.all_to_all(half, BOTH, split_axis=0, concat_axis=0, tiled=True)  14.3 us
    all_to_all x1, blocking collectives, per_device(): lax.all_to_all(shares, BOTH, split_axis=0, concat_axis=0, tiled=True)  13.6 us
  transfers between devices with their start and end apart: 6, of which 5 were waited for; matrix products, arithmetic and copies ran while one was open for 0% of the time, Pallas kernels for 28%

profile of v6, /device:TPU:0, one launch (start us, length us, event | category | flops | bytes accessed | tf_op | source)
XLA Modules:
  0.0 562.5 jit_solution(8912007272672206649)
XLA Ops:
  6.5 0.0 all-gather.4.cloned.1.call-start
  6.5 1.7 slice.6
  8.3 0.0 all-gather.4.cloned.1.call-update
  8.3 1.3 copy.8.list_ref
  9.6 13.4 %factor_rows.3 = (bf16[128,256]{1,0:T(8,128)(2,1)}, f32[256,256]{1,0:T(8,128)}, f32[8,256]{1,0:T(8,128)}) custom-call(bf16[256,384]{1,0:T(8,128)(2,1)} %refs_0_.1), custom_call_target="tpu_custom_call" | custom-call | tf_op jit(solution)/shard_map/factor_rows/pallas_call | solution.py:103
  23.1 18.6 %half_transform.3 = bf16[16,4,128,256]{3,2,1,0:T(8,128)(2,1)} custom-call(s32[8,4]{1,0:T(8,128)} %copy.8.list_ref, s32[8]{0:T(128)} %count_ref.5, bf16[8,4,16,128,128]{4,3,2,1,0:T(8,128)(2,1)} %ints_ref.5, bf16[128,256]{1,0:T(8,128)(2,1)} %get-tuple-element.25.basis_ref), custom_call_target="tpu_custom_call" | custom-call | flops 2147483648 | bytes 20971520 | tf_op jit(solution)/shard_map/half_transform/pallas_call | solution.py:172
  41.6 3.3 all-gather.4.cloned.1.call-done
  44.9 4.6 all-to-all-start
  49.4 30.4 %factor_rows.4 = (bf16[320,256]{1,0:T(8,128)(2,1)}, f32[256,256]{1,0:T(8,128)}, f32[8,256]{1,0:T(8,128)}) custom-call(f32[256,256]{1,0:T(8,128)} %get-tuple-element.28.refs_0_, f32[8,256]{1,0:T(8,128)} %get-tuple-element.29.refs_1_), custom_call_target="tpu_custom_call" | custom-call | tf_op jit(solution)/shard_map/factor_rows/pallas_call | solution.py:103
  79.9 23.9 %half_transform.4 = bf16[16,10,128,256]{3,2,1,0:T(8,128)(2,1)} custom-call(s32[8,4]{1,0:T(8,128)} %copy.8.list_ref, s32[8]{0:T(128)} %count_ref.5, bf16[8,4,16,128,128]{4,3,2,1,0:T(8,128)(2,1)} %ints_ref.5, bf16[320,256]{1,0:T(8,128)(2,1)} %get-tuple-element.30.basis_ref), custom_call_target="tpu_custom_call" | custom-call | flops 5368709120 | bytes 27262976 | tf_op jit(solution)/shard_map/half_transform/pallas_call | solution.py:172
  103.7 40.1 %all-to-all-done.half_ref = bf16[16,4,128,256]{3,2,1,0:T(8,128)(2,1)} async-done(((bf16[16,4,128,256]{3,2,1,0:T(8,128)(2,1)}), bf16[16,4,128,256]{3,2,1,0:T(8,128)(2,1)}, u32[]{:S(2)}, u32[]{:S(2)}) %all-to-all-start) | async-done | bytes 4194336 | tf_op jit(solution)/shard_map/all_to_all | solution.py:330
  143.9 0.0 slice-start
  143.9 5.0 all-to-all-start.1
  148.8 0.0 all-gather.8.cloned.1.call-start
  148.9 0.0 slice-done
  148.9 242.1 %all_gather.14 = bf16[512,768]{1,0:T(8,128)(2,1)} all-gather(bf16[128,768]{1,0:T(8,128)(2,1)S(1)} %slice-done), channel_id=1, replica_groups=mesh['grp'=2,'aux'=4,'occ'=4] {'occ'}, dimensions={0}, use_global_device_ids=true | all-gather | bytes 983040 | tf_op jit(solution)/shard_map/all_gather | solution.py:322
  391.0 0.0 all-gather.8.cloned.1.call-update
  391.0 0.0 all-gather.6.cloned.1.call-start
  391.1 0.7 all-gather.6.cloned.1.call-update
  391.7 7.4 %factor_rows.5 = (bf16[64,256]{1,0:T(8,128)(2,1)}, f32[256,256]{1,0:T(8,128)}, f32[8,256]{1,0:T(8,128)}) custom-call(f32[256,256]{1,0:T(8,128)} %get-tuple-element.34.refs_0_, f32[8,256]{1,0:T(8,128)} %get-tuple-element.35.refs_1_), custom_call_target="tpu_custom_call" | custom-call | tf_op jit(solution)/shard_map/factor_rows/pallas_call | solution.py:103
  399.2 14.6 %half_transform.5 = bf16[16,2,128,256]{3,2,1,0:T(8,128)(2,1)} custom-call(s32[8,4]{1,0:T(8,128)} %copy.8.list_ref, s32[8]{0:T(128)} %count_ref.5, bf16[8,4,16,128,128]{4,3,2,1,0:T(8,128)(2,1)} %ints_ref.5, bf16[64,256]{1,0:T(8,128)(2,1)} %get-tuple-element.36.basis_ref), custom_call_target="tpu_custom_call" | custom-call | flops 1073741824 | bytes 18874368 | tf_op jit(solution)/shard_map/half_transform/pallas_call | solution.py:172
  413.8 6.8 %all-gather.8.cloned.1.call-done.right_ref = bf16[2048,768]{1,0:T(8,128)(2,1)} async-done(((bf16[512,768]{1,0:T(8,128)(2,1)}), bf16[2048,768]{1,0:T(8,128)(2,1)}) %all-gather.8.cloned.1.call-update) | async-done | bytes 3145744 | tf_op jit(solution)/shard_map/all_gather | solution.py:323
  420.6 42.1 %all-gather.6.cloned.1.call-done.left_ref = bf16[2048,1280]{1,0:T(8,128)(2,1)} async-done(((bf16[512,1280]{1,0:T(8,128)(2,1)}), bf16[2048,1280]{1,0:T(8,128)(2,1)}) %all-gather.6.cloned.1.call-update) | async-done | bytes 5242896 | tf_op jit(solution)/shard_map/all_gather | solution.py:323
  462.7 0.7 broadcast_in_dim.3.before_ref
  463.4 15.1 %fit_exchange.3.before_ref = f32[256,256]{1,0:T(8,128)} custom-call(bf16[16,4,128,256]{3,2,1,0:T(8,128)(2,1)} %all-to-all-done.half_ref, f32[256,256]{1,0:T(8,128)} %broadcast_in_dim.3.before_ref, bf16[2048,1280]{1,0:T(8,128)(2,1)} %all-gather.6.cloned.1.call-done.left_ref, bf16[2048,768]{1,0:T(8,128)(2,1)} %all-gather.8.cloned.1.call-done.right_ref), custom_call_target="tpu_custom_call" | custom-call | flops 5905580032 | bytes 12582912 | tf_op jit(solution)/shard_map/fit_exchange/pallas_call | solution.py:274
  478.5 0.0 all-to-all-done.1.half_ref
  478.5 4.8 all-to-all-start.2
  483.3 32.5 %fit_exchange.4.before_ref = f32[256,256]{1,0:T(8,128)} custom-call(bf16[16,10,128,256]{3,2,1,0:T(8,128)(2,1)} %all-to-all-done.1.half_ref, f32[256,256]{1,0:T(8,128)} %fit_exchange.3.before_ref, bf16[2048,1280]{1,0:T(8,128)(2,1)} %all-gather.6.cloned.1.call-done.left_ref, bf16[2048,768]{1,0:T(8,128)(2,1)} %all-gather.8.cloned.1.call-done.right_ref), custom_call_target="tpu_custom_call" | custom-call | flops 14763950080 | bytes 18874368 | tf_op jit(solution)/shard_map/fit_exchange/pallas_call | solution.py:274
  515.7 17.0 %all-to-all-done.2.half_ref = bf16[16,2,128,256]{3,2,1,0:T(8,128)(2,1)} async-done(((bf16[16,2,128,256]{3,2,1,0:T(8,128)(2,1)}), bf16[16,2,128,256]{3,2,1,0:T(8,128)(2,1)}, u32[]{:S(2)}, u32[]{:S(2)}) %all-to-all-start.2) | async-done | bytes 2097184 | tf_op jit(solution)/shard_map/all_to_all | solution.py:330
  532.7 9.1 %fit_exchange.5 = f32[256,256]{1,0:T(8,128)} custom-call(bf16[16,2,128,256]{3,2,1,0:T(8,128)(2,1)} %all-to-all-done.2.half_ref, f32[256,256]{1,0:T(8,128)} %fit_exchange.4.before_ref, bf16[2048,1280]{1,0:T(8,128)(2,1)} %all-gather.6.cloned.1.call-done.left_ref, bf16[2048,768]{1,0:T(8,128)(2,1)} %all-gather.8.cloned.1.call-done.right_ref), custom_call_target="tpu_custom_call" | custom-call | flops 2952790016 | bytes 10485760 | tf_op jit(solution)/shard_map/fit_exchange/pallas_call | solution.py:274
  541.8 13.6 %all_to_all.20 = f32[16,16,256]{2,1,0:T(8,128)S(1)} all-to-all(f32[16,16,256]{2,1,0:T(8,128)} %bitcast.1), channel_id=1, replica_groups=mesh['grp'=2,'aux'=4,'occ'=4] {'aux','occ'}, dimensions={0} | all-to-all | bytes 524288 | tf_op jit(solution)/shard_map/all_to_all | solution.py:335
  555.4 0.6 reduce_sum.9
Async XLA Ops:
  6.5 38.3 %all-gather.4.cloned.1.call-start = ((), (), s32[]{:S(2)}) async-start(), calls=%async_computation.4 | async-start | bytes 1638400 | tf_op jit(solution)/shard_map/all_gather | solution.py:310
  44.9 99.0 %all-to-all-start = ((bf16[16,4,128,256]{3,2,1,0:T(8,128)(2,1)}), bf16[16,4,128,256]{3,2,1,0:T(8,128)(2,1)}, u32[]{:S(2)}, u32[]{:S(2)}) async-start(bf16[16,4,128,256]{3,2,1,0:T(8,128)(2,1)} %half_transform.3), calls=%async_computation | async-start | bytes 8388608 | tf_op jit(solution)/shard_map/all_to_all | solution.py:330
  143.9 5.0 slice-start
  143.9 334.6 %all-to-all-start.1 = ((bf16[16,10,128,256]{3,2,1,0:T(8,128)(2,1)}), bf16[16,10,128,256]{3,2,1,0:T(8,128)(2,1)}, u32[]{:S(2)}, u32[]{:S(2)}) async-start(bf16[16,10,128,256]{3,2,1,0:T(8,128)(2,1)} %half_transform.4), calls=%async_computation.1 | async-start | bytes 20971520 | tf_op jit(solution)/shard_map/all_to_all | solution.py:330
  148.8 271.7 %all-gather.8.cloned.1.call-start = ((), (), s32[]{:S(2)}) async-start(), calls=%async_computation.6 | async-start | bytes 3932160 | tf_op jit(solution)/shard_map/all_gather | solution.py:323
  391.0 71.6 %all-gather.6.cloned.1.call-start = ((), (), s32[]{:S(2)}) async-start(), calls=%async_computation.5 | async-start | bytes 6553600 | tf_op jit(solution)/shard_map/all_gather | solution.py:323
  478.5 54.3 %all-to-all-start.2 = ((bf16[16,2,128,256]{3,2,1,0:T(8,128)(2,1)}), bf16[16,2,128,256]{3,2,1,0:T(8,128)(2,1)}, u32[]{:S(2)}, u32[]{:S(2)}) async-start(bf16[16,2,128,256]{3,2,1,0:T(8,128)(2,1)} %half_transform.5), calls=%async_computation.2 | async-start | bytes 4194304 | tf_op jit(solution)/shard_map/all_to_all | solution.py:330
Sparse Core Ops, SparseCore 0:
  8.9 35.9 all-gather.3
  391.1 29.4 all-gather.7
  422.1 40.4 all-gather.5

commit v7 on v5

v7 whole, which is shorter than its diff:
```python
import functools

import jax
import jax.numpy as jnp
from jax import lax
from jax.experimental import pallas as pl
from jax.experimental.pallas import tpu as pltpu
from jax.sharding import PartitionSpec as P

BOTH = ("aux", "occ")
VMEM_BYTES = 58 * 2**20
FIT_VMEM_BYTES = 63 * 2**20
PANEL = 16
GROUP = 4
SCALE = 2.0**40
PIVOT_FLOOR = 1e-6


def root(value):
    return value * lax.rsqrt(jnp.maximum(value, 1e-37))


def factor_kernel(start, *refs):
    if start == 0:
        coef_ref, rows_ref, rest_ref, diag_ref = refs
        scaled = (coef_ref[...].astype(jnp.float32) * SCALE).astype(jnp.bfloat16)
        gram = lax.dot_general(
            scaled, scaled, (((1,), (1,)), ((), ())), preferred_element_type=jnp.float32
        )
        total = gram.shape[0]
        on_diagonal = lax.broadcasted_iota(jnp.int32, gram.shape, 0) == (
            lax.broadcasted_iota(jnp.int32, gram.shape, 1)
        )
        diagonal = jnp.sum(jnp.where(on_diagonal, gram, 0.0), axis=0, keepdims=True)
        which = lax.broadcasted_iota(jnp.int32, diag_ref.shape, 0)
        diag_ref[...] = jnp.where(
            which == 0, diagonal, jnp.maximum(diagonal * PIVOT_FLOOR, 1e-37)
        )
        rest_ref[...] = gram
    else:
        rest_in_ref, diag_in_ref, rows_ref, rest_ref, diag_ref = refs
        rest_ref[...] = rest_in_ref[...]
        diag_ref[...] = diag_in_ref[...]
        total = rest_ref.shape[1]
    own = rows_ref.shape[0] // 2
    lanes = min(total, 128)
    parts = [slice(part * lanes, (part + 1) * lanes) for part in range(total // lanes)]
    row = lax.broadcasted_iota(jnp.int32, (PANEL, lanes), 0)
    lane = lax.broadcasted_iota(jnp.int32, (PANEL, lanes), 1)

    def panel(number, carry):
        low = pl.multiple_of(start + number * PANEL, PANEL)
        rest = [rest_ref[pl.ds(low, PANEL), part] for part in parts]
        left = [diag_ref[0:1, part] for part in parts]
        floor = [diag_ref[1:2, part] for part in parts]

        def as_column(values):
            picked = jnp.zeros((PANEL, lanes), jnp.float32)
            for part, value in zip(parts, values):
                picked = picked + jnp.where(lane + part.start == low + row, value, 0.0)
            return jnp.broadcast_to(jnp.sum(picked, axis=1, keepdims=True), (PANEL, lanes))

        left_column, floor_column = as_column(left), as_column(floor)
        corner = rest[0]
        for part, value in zip(parts[1:], rest[1:]):
            corner = jnp.where(low >= part.start, value, corner)
        corner = pltpu.roll(corner, lax.rem(lanes - lax.rem(low, lanes), lanes), 1)
        columns = [
            jnp.broadcast_to(corner[:, t : t + 1], (PANEL, lanes)) for t in range(PANEL)
        ]
        done = [jnp.zeros((PANEL, lanes), jnp.float32) for part in parts]
        for t in range(PANEL):
            pivot = jnp.maximum(left_column[t : t + 1], floor_column[t : t + 1])
            inverse = lax.rsqrt(pivot)
            inverse = inverse * (1.5 - 0.5 * (pivot * inverse) * inverse)
            most = root(left_column)
            weight = jnp.clip(columns[t] * inverse, -most, most)
            weight = jnp.where(row > t, weight, 0.0)
            left_column = jnp.maximum(left_column - weight * weight, 0.0)
            for s in range(t + 1, PANEL):
                columns[s] = columns[s] - weight * weight[s : s + 1]
            for i, part in enumerate(parts):
                place = lane[:1] + part.start
                most = root(left[i])
                here = jnp.clip(rest[i][t : t + 1] * inverse, -most, most)
                here = jnp.where(place > low + t, here, 0.0)
                left[i] = jnp.maximum(left[i] - here * here, 0.0)
                here = jnp.where(place == low + t, pivot * inverse, here)
                done[i] = jnp.where(row == t, here, done[i])
                rest[i] = rest[i] - weight * here
        for part, value in zip(parts, left):
            diag_ref[0:1, part] = value
        done = jnp.concatenate(done, axis=1)
        rest_ref[...] -= lax.dot_general(
            done,
            done,
            (((0,), (0,)), ((), ())),
            precision=lax.Precision.HIGHEST,
            preferred_element_type=jnp.float32,
        )
        done = done * (1.0 / SCALE)
        high = done.astype(jnp.bfloat16)
        place = pl.multiple_of(number * PANEL, PANEL)
        rows_ref[pl.ds(place, PANEL), :] = high
        rows_ref[pl.ds(own + place, PANEL), :] = (done - high.astype(jnp.float32)).astype(
            jnp.bfloat16
        )
        return carry

    lax.fori_loop(0, own // PANEL, panel, 0)


def factor_rows(start, own, total, operands):
    rows, rest, diagonals = pl.pallas_call(
        functools.partial(factor_kernel, start),
        out_shape=(
            jax.ShapeDtypeStruct((2 * own, total), jnp.bfloat16),
            jax.ShapeDtypeStruct((total, total), jnp.float32),
            jax.ShapeDtypeStruct((8, total), jnp.float32),
        ),
        compiler_params=pltpu.CompilerParams(vmem_limit_bytes=VMEM_BYTES),
        name="factor_rows",
    )(*operands)
    return rows, (rest, diagonals)


def half_kernel(low_block, list_ref, count_ref, basis_ref, *refs):
    tile_refs, (out_ref, rows_ref, window_ref) = refs[:-3], refs[-3:]
    block = pl.program_id(0)
    aux_width, size_block = tile_refs[0].shape[2:4]
    vectors = basis_ref.shape[0] // 2
    side = basis_ref.shape[1] // size_block
    pairs = [(m, n) for m in range(side) for n in range(low_block, side)]
    for (m, n), tile_ref in zip(pairs, tile_refs):
        used = jnp.bool_(False)
        for slot in range(list_ref.shape[0]):
            hit = jnp.logical_and(list_ref[slot, block] == m * side + n, slot < count_ref[block])
            used = jnp.logical_or(used, hit)
        tile = tile_ref[0, 0]
        column = (n - low_block) * size_block
        window_ref[:, m * size_block : (m + 1) * size_block, column : column + size_block] = (
            jnp.where(used, tile, jnp.zeros_like(tile))
        )

    def some(group, carry):
        low = group * GROUP
        window = window_ref[pl.ds(low, GROUP)]
        product = lax.dot_general(
            basis_ref[:, low_block * size_block :],
            window.reshape(GROUP * window.shape[1], window.shape[2]),
            (((1,), (1,)), ((), ())),
            preferred_element_type=jnp.float32,
        )
        product = product[:vectors] + product[vectors:]
        for p in range(GROUP):
            for m in range(side):
                column = (p * side + m) * size_block
                rows_ref[m, pl.ds(low + p, vectors, stride=aux_width), :] = product[
                    :, column : column + size_block
                ]
        return carry

    lax.fori_loop(0, aux_width // GROUP, some, 0)
    for m in range(side):
        out_ref[..., m * size_block : (m + 1) * size_block] = (
            rows_ref[m].astype(jnp.bfloat16).reshape(out_ref.shape[:-1] + (size_block,))
        )


def half_transform(integrals, pair_list, pair_count, basis_rows, start, devices):
    blocks, slots, aux_width, size_block, _ = integrals.shape
    vectors, basis_total = basis_rows.shape[0] // 2, basis_rows.shape[1]
    own = vectors // devices
    side = basis_total // size_block
    low_block = start // size_block

    def tile_spec(pair):
        def place(b, list_ref, count_ref):
            slot_of = jnp.int32(0)
            for slot in range(1, slots):
                slot_of = jnp.where(list_ref[slot, b] == pair, slot, slot_of)
            return b, slot_of, 0, 0, 0

        return pl.BlockSpec((1, 1, aux_width, size_block, size_block), place)

    tiles = [tile_spec(m * side + n) for m in range(side) for n in range(low_block, side)]
    return pl.pallas_call(
        functools.partial(half_kernel, low_block),
        out_shape=jax.ShapeDtypeStruct(
            (devices, own, blocks * aux_width, basis_total), jnp.bfloat16
        ),
        grid_spec=pltpu.PrefetchScalarGridSpec(
            num_scalar_prefetch=2,
            grid=(blocks,),
            in_specs=[pl.BlockSpec(basis_rows.shape, lambda b, *_: (0, 0))] + tiles,
            out_specs=pl.BlockSpec(
                (devices, own, aux_width, basis_total), lambda b, *_: (0, 0, b, 0)
            ),
            scratch_shapes=[
                pltpu.VMEM(
                    (basis_total // size_block, vectors * aux_width, size_block), jnp.float32
                ),
                pltpu.VMEM(
                    (aux_width, basis_total, basis_total - low_block * size_block),
                    jnp.bfloat16,
                ),
            ],
        ),
        compiler_params=pltpu.CompilerParams(vmem_limit_bytes=VMEM_BYTES),
        cost_estimate=pl.CostEstimate(
            flops=4 * blocks * aux_width * vectors * basis_total * basis_total,
            bytes_accessed=integrals.size * 2 + vectors * blocks * aux_width * basis_total * 2,
            transcendentals=0,
        ),
        name="half_transform",
    )(pair_list.T, pair_count, basis_rows, *[integrals] * len(tiles))


def fit_kernel(step_rows, before_ref, factor_ref, half_ref, out_ref, lower_ref, columns_ref, factor_sems, half_sems):
    step = pl.program_id(0)
    aux_total = factor_ref.shape[0]
    basis_total = out_ref.shape[0]
    width = columns_ref.shape[-1] // basis_total
    blocks = aux_total // step_rows
    sources = half_ref.shape[0] // blocks

    def factor_copy(number):
        low, high = number * step_rows, (number + 1) * step_rows
        part = (slice(low, high), slice(0, high))
        return pltpu.make_async_copy(
            factor_ref.at[part], lower_ref.at[part], factor_sems.at[number]
        )

    def half_copy(index, number, k):
        slot = lax.rem(index, 2)
        part = slice(number * sources, (number + 1) * sources)
        return pltpu.make_async_copy(
            half_ref.at[part, index * width + k],
            columns_ref.at[slot, part, :, k * basis_total : (k + 1) * basis_total],
            half_sems.at[slot, number, k],
        )

    def start_half(index):
        for number in range(blocks):
            for k in range(width):
                half_copy(index, number, k).start()

    @pl.when(step == 0)
    def _():
        for number in range(blocks):
            for k in range(width):
                half_copy(step, number, k).start()
            factor_copy(number).start()

    pl.when(step + 1 < pl.num_programs(0))(lambda: start_half(step + 1))

    total = jnp.zeros(out_ref.shape, jnp.float32)
    for number in range(blocks):
        low, high = number * step_rows, (number + 1) * step_rows
        for k in range(width):
            half_copy(step, number, k).wait()
        pl.when(step == 0)(lambda number=number: factor_copy(number).wait())
        columns = columns_ref[lax.rem(step, 2), : (number + 1) * sources]
        fitted = jnp.dot(
            lower_ref[low:high, :high],
            columns.reshape(high, columns.shape[-1]),
            preferred_element_type=jnp.float32,
        ).astype(jnp.bfloat16)
        for k in range(width):
            one = fitted[:, k * basis_total : (k + 1) * basis_total]
            total = total + lax.dot_general(
                one, one, (((0,), (0,)), ((), ())), preferred_element_type=jnp.float32
            )

    @pl.when(step == 0)
    def _():
        out_ref[...] = before_ref[...] + total

    @pl.when(step > 0)
    def _():
        out_ref[...] += total


def fit_exchange(factor, arrived, before):
    devices, own, aux_local, basis_total = arrived.shape
    aux_total = factor.shape[0]
    width = 2 if own % 2 == 0 else 1
    return pl.pallas_call(
        functools.partial(fit_kernel, aux_total // 8),
        out_shape=jax.ShapeDtypeStruct((basis_total, basis_total), jnp.float32),
        grid=(own // width,),
        in_specs=[
            pl.BlockSpec((basis_total, basis_total), lambda k: (0, 0)),
            pl.BlockSpec(memory_space=pl.ANY),
            pl.BlockSpec(memory_space=pl.ANY),
        ],
        out_specs=pl.BlockSpec((basis_total, basis_total), lambda k: (0, 0)),
        scratch_shapes=[
            pltpu.VMEM((aux_total, aux_total), jnp.bfloat16),
            pltpu.VMEM((2, devices, aux_local, width * basis_total), jnp.bfloat16),
            pltpu.SemaphoreType.DMA((8,)),
            pltpu.SemaphoreType.DMA((2, 8, width)),
        ],
        compiler_params=pltpu.CompilerParams(vmem_limit_bytes=FIT_VMEM_BYTES),
        cost_estimate=pl.CostEstimate(
            flops=own * aux_total * basis_total * (aux_total * 9 // 8 + 2 * basis_total),
            bytes_accessed=(factor.size + arrived.size) * 2,
            transcendentals=0,
        ),
        name="fit_exchange",
    )(before, factor, arrived)


def line_step(step, upward, downward, axis):
    devices = lax.axis_size(axis)
    upward = lax.ppermute(upward, axis, [(i, i + 1) for i in range(step, devices - 1)])
    downward = lax.ppermute(downward, axis, [(i, i - 1) for i in range(1, devices - step)])
    return upward, downward


def line_blocks(block, passed, axis):
    devices = lax.axis_size(axis)
    up, down = [pair[0] for pair in passed], [pair[1] for pair in passed]
    around = jnp.stack(up[::-1] + [block] + down)
    first = devices - 1 - lax.axis_index(axis)
    blocks = lax.dynamic_slice_in_dim(around, first, devices, 0)
    return blocks.reshape(devices * block.shape[0], block.shape[1])


def chunk_sizes(own):
    if own % 8 == 0:
        return [own // 8, 3 * own // 4, own // 8]
    return [1] * own


def per_device(integrals, pair_list, pair_count, coefficients, metric):
    devices = lax.axis_size("aux") * lax.axis_size("occ")
    basis_total = coefficients.shape[0]
    passed = [line_step(0, metric, metric, "occ")]
    total = jnp.zeros((basis_total, basis_total), jnp.float32)
    state = (coefficients,)
    start = 0
    arrived = []
    factor = None
    for chunk, own in enumerate(chunk_sizes(basis_total // devices)):
        width = own * devices
        rows, state = factor_rows(start, width, basis_total, state)
        half = half_transform(integrals, pair_list, pair_count, rows, start, devices)
        if chunk == 0:
            half, state, passed[0] = lax.optimization_barrier((half, state, passed[0]))
            for step in range(1, lax.axis_size("occ") - 1):
                passed.append(line_step(step, *passed[-1], "occ"))
            line = line_blocks(metric, passed, "occ")
        elif chunk == 1:
            half, state, arrived[0], line = lax.optimization_barrier(
                (half, state, arrived[0], line)
            )
            factor = lax.all_gather(line, "aux", axis=0, tiled=True)
        else:
            total = fit_exchange(factor, arrived[chunk - 2], total)
            half, state, arrived[chunk - 1], total = lax.optimization_barrier(
                (half, state, arrived[chunk - 1], total)
            )
        arrived.append(lax.all_to_all(half, BOTH, split_axis=0, concat_axis=0, tiled=True))
        start += width
    for piece in arrived[-2:]:
        total = fit_exchange(factor, piece, total)
    shares = total.reshape(devices, basis_total // devices, basis_total)
    return jnp.sum(lax.all_to_all(shares, BOTH, split_axis=0, concat_axis=0, tiled=True), axis=0)


def solution(mesh):
    in_specs = (
        P(("grp", "aux", "occ"), None, None, None, None),
        P(("grp", "aux", "occ"), None),
        P(("grp", "aux", "occ")),
        P("grp", None),
        P(("grp", "aux", "occ"), None),
    )
    out_specs = P(("grp", "aux", "occ"), None)
    return jax.shard_map(
        per_device, mesh=mesh, in_specs=in_specs, out_specs=out_specs, check_vma=False
    )
```

time: 495 us -> 484 us (0.978)
  Pallas kernels: 194 us -> 132 us
  waiting for transfers between devices: 248 us -> 290 us
  starting transfers between devices: 17 us -> 28.6 us
    all_gather x1, waiting for transfers between devices: 34.7 us -> 159 us  [per_device(): factor = lax.all_gather(line, 'aux', axis=0, tiled=True)]
    all_to_all x4 -> x3, waiting for transfers between devices: 188 us -> 101 us  [per_device(): lax.all_to_all(half, BOTH, split_axis=0, concat_axis=0, tiled=True)]
    pallas_call x4 -> x3, Pallas kernels: 52.9 us -> 19.8 us  [factor_rows(): pl.pallas_call(functools.partial(factor_kernel, start), out_shape=(jax.Sh...]
    ppermute x0 -> x6, waiting for transfers between devices: none -> 29.6 us  [the longest x3 29.6 us: line_step(): lax.ppermute(downward, axis, [(i, i - 1) for i in range(1, devices - step)])]
    all_gather x1 -> x0, waiting for transfers between devices: 24.4 us -> none  [per_device(): line = lax.all_gather(metric, 'occ', axis=0, tiled=True)]
    pallas_call x4 -> x3, Pallas kernels: 72.3 us -> 54.7 us  [fit_exchange(): pl.pallas_call(functools.partial(fit_kernel, aux_total // 8), out_shape=j...]
    ppermute x0 -> x6, starting transfers between devices: none -> 11 us  [the longest x3 7.1 us: line_step(): lax.ppermute(upward, axis, [(i, i + 1) for i in range(step, devices - 1)])]
    pallas_call x4 -> x3, Pallas kernels: 68.3 us -> 57.7 us  [half_transform(): pl.pallas_call(functools.partial(half_kernel, low_block), out_shape=jax.S...]
  transfers between devices with their start and end apart: 6 -> 10, of which waited for: 5 -> 5; matrix products, arithmetic and copies ran while one was open for 0% -> 1% of each run, Pallas kernels for 38% -> 26%
where the time goes in v7:
time: 484 us; the launch traced here: 483 us
  waiting for transfers between devices  290 us (60%)
  Pallas kernels  132 us (27%)
  starting transfers between devices  28.6 us (6%)
  blocking collectives  13.6 us (3%)
  between operations  13.6 us (3%)
  local copies, waits for them, and re-layouts  4.86 us (1%)
    all_gather x1, waiting for transfers between devices, per_device(): factor = lax.all_gather(line, 'aux', axis=0, tiled=True)  159 us
    all_to_all x3, waiting for transfers between devices, per_device(): lax.all_to_all(half, BOTH, split_axis=0, concat_axis=0, tiled=True)  101 us
    pallas_call x3, Pallas kernels, half_transform(): pl.pallas_call(functools.partial(half_kernel, low_block), out_shape=jax.S...  57.7 us
    pallas_call x3, Pallas kernels, fit_exchange(): pl.pallas_call(functools.partial(fit_kernel, aux_total // 8), out_shape=j...  54.7 us
    ppermute x3, waiting for transfers between devices, line_step(): lax.ppermute(downward, axis, [(i, i - 1) for i in range(1, devices - step)])  29.6 us
    pallas_call x3, Pallas kernels, factor_rows(): pl.pallas_call(functools.partial(factor_kernel, start), out_shape=(jax.Sh...  19.8 us
    all_to_all x3, starting transfers between devices, per_device(): lax.all_to_all(half, BOTH, split_axis=0, concat_axis=0, tiled=True)  17.6 us
    all_to_all x1, blocking collectives, per_device(): lax.all_to_all(shares, BOTH, split_axis=0, concat_axis=0, tiled=True)  13.6 us
  transfers between devices with their start and end apart: 10, of which 5 were waited for; matrix products, arithmetic and copies ran while one was open for 1% of the time, Pallas kernels for 26%

profile of v7, /device:TPU:0, one launch (start us, length us, event | category | flops | bytes accessed | tf_op | source)
XLA Modules:
  0.0 482.9 jit_solution(1240380241769227700)
XLA Ops:
  6.5 5.0 %collective-permute-start = (bf16[128,2048]{1,0:T(8,128)(2,1)}, bf16[128,2048]{1,0:T(8,128)(2,1)S(1)}, u32[]{:S(2)}, u32[]{:S(2)}) collective-permute-start(bf16[128,2048]{1,0:T(8,128)(2,1)} %param.9), channel_id=1, source_target_pairs={{0,1},{1,2},{2,3},{4,5},{5,6},{6,7},{8,9},{9,10},{10,11},{12,13},{... | collective-permute-start | bytes 1572872 | tf_op jit(solution)/shard_map/ppermute | solution.py:316
  11.5 1.3 collective-permute-start.1
  12.8 3.7 factor_rows.3
  16.5 17.5 %half_transform.3 = bf16[16,2,128,256]{3,2,1,0:T(8,128)(2,1)} custom-call(s32[4,8]{1,0:T(4,128)} %bitcast.19, s32[8]{0:T(128)} %count_ref.5, bf16[64,256]{1,0:T(8,128)(2,1)} %get-tuple-element.25.basis_ref, bf16[8,4,16,128,128]{4,3,2,1,0:T(8,128)(2,1)} %refs_1_.5, bf16[8,4,16,128,128]{4,3,2,1,0:T(8,128)(2,1)} %refs_1_.5, ...), custom_call_target="tpu_custom_call" | custom-call | flops 1073741824 | bytes 18874368 | tf_op jit(solution)/shard_map/half_transform/pallas_call | solution.py:187
  34.0 0.0 collective-permute-done
  34.0 0.0 collective-permute-done.1
  34.0 1.5 collective-permute-start.2
  35.5 8.0 %all-to-all-start = ((bf16[16,2,128,256]{3,2,1,0:T(8,128)(2,1)}), bf16[16,2,128,256]{3,2,1,0:T(8,128)(2,1)S(1)}, u32[]{:S(2)}, u32[]{:S(2)}) async-start(bf16[16,2,128,256]{3,2,1,0:T(8,128)(2,1)} %half_transform.3), calls=%async_computation | async-start | bytes 4194304 | tf_op jit(solution)/shard_map/all_to_all | solution.py:364
  43.5 1.3 collective-permute-start.4
  44.8 12.6 %factor_rows.4 = (bf16[384,256]{1,0:T(8,128)(2,1)}, f32[256,256]{1,0:T(8,128)}, f32[8,256]{1,0:T(8,128)}) custom-call(f32[256,256]{1,0:T(8,128)} %get-tuple-element.28.refs_0_, f32[8,256]{1,0:T(8,128)} %get-tuple-element.29.refs_1_), custom_call_target="tpu_custom_call" | custom-call | tf_op jit(solution)/shard_map/factor_rows/pallas_call | solution.py:114
  57.4 0.0 collective-permute-done.2
  57.4 0.7 collective-permute-start.3
  58.1 0.0 copy-start.1
  58.1 27.0 %half_transform.4 = bf16[16,12,128,256]{3,2,1,0:T(8,128)(2,1)} custom-call(s32[4,8]{1,0:T(4,128)} %bitcast.20, s32[8]{0:T(128)} %count_ref.5, bf16[384,256]{1,0:T(8,128)(2,1)} %get-tuple-element.30.basis_ref, bf16[8,4,16,128,128]{4,3,2,1,0:T(8,128)(2,1)} %refs_1_.5, bf16[8,4,16,128,128]{4,3,2,1,0:T(8,128)(2,1)} %refs_1_.5, ...), custom_call_target="tpu_custom_call" | custom-call | flops 6442450944 | bytes 29360128 | tf_op jit(solution)/shard_map/half_transform/pallas_call | solution.py:187
  85.1 3.7 collective-permute-done.4
  88.7 1.3 collective-permute-start.5
  90.0 0.0 collective-permute-done.3
  90.1 1.1 bitcast_dynamic-update-slice_fusion.5
  91.2 0.0 copy-done.1
  91.4 25.9 %collective-permute-done.5 = bf16[128,2048]{1,0:T(8,128)(2,1)S(1)} collective-permute-done((bf16[128,2048]{1,0:T(8,128)(2,1)S(1)}, bf16[128,2048]{1,0:T(8,128)(2,1)S(1)}, u32[]{:S(2)}, u32[]{:S(2)}) %collective-permute-start.5) | collective-permute-done | bytes 524320 | tf_op jit(solution)/shard_map/ppermute | solution.py:317
  117.3 1.5 constant_dynamic-slice_fusion
  118.9 0.0 all-to-all-done.half_ref
  118.9 0.0 copy-start
  118.9 1.3 copy-done
  120.2 5.0 %all-to-all-start.1 = ((bf16[16,12,128,256]{3,2,1,0:T(8,128)(2,1)}), bf16[16,12,128,256]{3,2,1,0:T(8,128)(2,1)}, u32[]{:S(2)}, u32[]{:S(2)}) async-start(bf16[16,12,128,256]{3,2,1,0:T(8,128)(2,1)} %half_transform.4), calls=%async_computation.1 | async-start | bytes 25165824 | tf_op jit(solution)/shard_map/all_to_all | solution.py:364
  125.2 0.0 all-gather.2.cloned.1.call-start
  125.2 0.7 all-gather.2.cloned.1.call-update
  125.9 3.5 factor_rows.5
  129.4 13.2 %half_transform.5 = bf16[16,2,128,256]{3,2,1,0:T(8,128)(2,1)} custom-call(s32[4,8]{1,0:T(4,128)} %bitcast.21, s32[8]{0:T(128)} %count_ref.5, bf16[64,256]{1,0:T(8,128)(2,1)} %get-tuple-element.38.basis_ref, bf16[8,4,16,128,128]{4,3,2,1,0:T(8,128)(2,1)} %refs_1_.5, bf16[8,4,16,128,128]{4,3,2,1,0:T(8,128)(2,1)} %refs_1_.5), custom_call_target="tpu_custom_call" | custom-call | flops 1073741824 | bytes 18874368 | tf_op jit(solution)/shard_map/half_transform/pallas_call | solution.py:187
  142.6 158.7 %all-gather.2.cloned.1.call-done.factor_ref = bf16[2048,2048]{1,0:T(8,128)(2,1)} async-done(((bf16[512,2048]{1,0:T(8,128)(2,1)}), bf16[2048,2048]{1,0:T(8,128)(2,1)}) %all-gather.2.cloned.1.call-update) | async-done | bytes 8388624 | tf_op jit(solution)/shard_map/all_gather | solution.py:358
  301.3 0.7 broadcast_in_dim.3.before_ref
  302.0 8.7 %fit_exchange.3.before_ref = f32[256,256]{1,0:T(8,128)} custom-call(f32[256,256]{1,0:T(8,128)} %broadcast_in_dim.3.before_ref, bf16[2048,2048]{1,0:T(8,128)(2,1)} %all-gather.2.cloned.1.call-done.factor_ref, bf16[16,2,128,256]{3,2,1,0:T(8,128)(2,1)} %copy-done), custom_call_target="tpu_custom_call" | custom-call | flops 2952790016 | bytes 10485760 | tf_op jit(solution)/shard_map/fit_exchange/pallas_call | solution.py:288
  310.7 88.6 %all-to-all-done.1.half_ref = bf16[16,12,128,256]{3,2,1,0:T(8,128)(2,1)} async-done(((bf16[16,12,128,256]{3,2,1,0:T(8,128)(2,1)}), bf16[16,12,128,256]{3,2,1,0:T(8,128)(2,1)}, u32[]{:S(2)}, u32[]{:S(2)}) %all-to-all-start.1) | async-done | bytes 12582944 | tf_op jit(solution)/shard_map/all_to_all | solution.py:364
  399.3 4.6 all-to-all-start.2
  403.9 37.3 %fit_exchange.4.before_ref = f32[256,256]{1,0:T(8,128)} custom-call(f32[256,256]{1,0:T(8,128)} %fit_exchange.3.before_ref, bf16[2048,2048]{1,0:T(8,128)(2,1)} %all-gather.2.cloned.1.call-done.factor_ref, bf16[16,12,128,256]{3,2,1,0:T(8,128)(2,1)} %all-to-all-done.1.half_ref), custom_call_target="tpu_custom_call" | custom-call | flops 17716740096 | bytes 20971520 | tf_op jit(solution)/shard_map/fit_exchange/pallas_call | solution.py:288
  441.3 11.9 %all-to-all-done.2.half_ref = bf16[16,2,128,256]{3,2,1,0:T(8,128)(2,1)} async-done(((bf16[16,2,128,256]{3,2,1,0:T(8,128)(2,1)}), bf16[16,2,128,256]{3,2,1,0:T(8,128)(2,1)}, u32[]{:S(2)}, u32[]{:S(2)}) %all-to-all-start.2) | async-done | bytes 2097184 | tf_op jit(solution)/shard_map/all_to_all | solution.py:364
  453.2 8.7 %fit_exchange.5 = f32[256,256]{1,0:T(8,128)} custom-call(f32[256,256]{1,0:T(8,128)} %fit_exchange.4.before_ref, bf16[2048,2048]{1,0:T(8,128)(2,1)} %all-gather.2.cloned.1.call-done.factor_ref, bf16[16,2,128,256]{3,2,1,0:T(8,128)(2,1)} %all-to-all-done.2.half_ref), custom_call_target="tpu_custom_call" | custom-call | flops 2952790016 | bytes 10485760 | tf_op jit(solution)/shard_map/fit_exchange/pallas_call | solution.py:288
  461.9 13.6 %all_to_all.20 = f32[16,16,256]{2,1,0:T(8,128)S(1)} all-to-all(f32[16,16,256]{2,1,0:T(8,128)} %bitcast.18), channel_id=1, replica_groups=mesh['grp'=2,'aux'=4,'occ'=4] {'aux','occ'}, dimensions={0} | all-to-all | bytes 524288 | tf_op jit(solution)/shard_map/all_to_all | solution.py:369
  475.4 0.6 reduce_sum.9
  (6 shorter events, 0.2 us)
Async XLA Ops:
  6.5 27.4 %collective-permute-start = (bf16[128,2048]{1,0:T(8,128)(2,1)}, bf16[128,2048]{1,0:T(8,128)(2,1)S(1)}, u32[]{:S(2)}, u32[]{:S(2)}) collective-permute-start(bf16[128,2048]{1,0:T(8,128)(2,1)} %param.9), channel_id=1, source_target_pairs={{0,1},{1,2},{2,3},{4,5},{5,6},{6,7},{8,9},{9,10},{10,11},{12,13},{... | collective-permute-start | bytes 1572872 | tf_op jit(solution)/shard_map/ppermute | solution.py:316
  11.5 22.5 %collective-permute-start.1 = (bf16[128,2048]{1,0:T(8,128)(2,1)}, bf16[128,2048]{1,0:T(8,128)(2,1)S(1)}, u32[]{:S(2)}, u32[]{:S(2)}) collective-permute-start(bf16[128,2048]{1,0:T(8,128)(2,1)} %param.9), channel_id=1, source_target_pairs={{1,0},{2,1},{3,2},{5,4},{6,5},{7,6},{9,8},{10,9},{11,10},{13,12},{... | collective-permute-start | bytes 1572872 | tf_op jit(solution)/shard_map/ppermute | solution.py:317
  34.0 23.4 %collective-permute-start.2 = (bf16[128,2048]{1,0:T(8,128)(2,1)S(1)}, bf16[128,2048]{1,0:T(8,128)(2,1)}, u32[]{:S(2)}, u32[]{:S(2)}) collective-permute-start(bf16[128,2048]{1,0:T(8,128)(2,1)S(1)} %collective-permute-done), channel_id=1, source_target_pairs={{1,2},{2,3},{5,6},{6,7},{9,10},{10,11},{13,14},{14,15},{17,18},{18... | collective-permute-start | bytes 1572872 | tf_op jit(solution)/shard_map/ppermute | solution.py:316
  35.5 83.4 %all-to-all-start = ((bf16[16,2,128,256]{3,2,1,0:T(8,128)(2,1)}), bf16[16,2,128,256]{3,2,1,0:T(8,128)(2,1)S(1)}, u32[]{:S(2)}, u32[]{:S(2)}) async-start(bf16[16,2,128,256]{3,2,1,0:T(8,128)(2,1)} %half_transform.3), calls=%async_computation | async-start | bytes 4194304 | tf_op jit(solution)/shard_map/all_to_all | solution.py:364
  43.5 45.3 %collective-permute-start.4 = (bf16[128,2048]{1,0:T(8,128)(2,1)S(1)}, bf16[128,2048]{1,0:T(8,128)(2,1)S(1)}, u32[]{:S(2)}, u32[]{:S(2)}) collective-permute-start(bf16[128,2048]{1,0:T(8,128)(2,1)S(1)} %collective-permute-done.1), channel_id=1, source_target_pairs={{1,0},{2,1},{5,4},{6,5},{9,8},{10,9},{13,12},{14,13},{17,16},{18,1... | collective-permute-start | bytes 1572872 | tf_op jit(solution)/shard_map/ppermute | solution.py:317
  57.4 32.7 %collective-permute-start.3 = (bf16[128,2048]{1,0:T(8,128)(2,1)}, bf16[128,2048]{1,0:T(8,128)(2,1)S(1)}, u32[]{:S(2)}, u32[]{:S(2)}) collective-permute-start(bf16[128,2048]{1,0:T(8,128)(2,1)} %collective-permute-done.2), channel_id=1, source_target_pairs={{2,3},{6,7},{10,11},{14,15},{18,19},{22,23},{26,27},{30,31}} | collective-permute-start | bytes 1572872 | tf_op jit(solution)/shard_map/ppermute | solution.py:316
  58.1 33.1 %copy-start.1 = (bf16[128,2048]{1,0:T(8,128)(2,1)S(1)}, bf16[128,2048]{1,0:T(8,128)(2,1)}, u32[]{:S(2)}) copy-start(bf16[128,2048]{1,0:T(8,128)(2,1)} %param.9) | copy-start | bytes 1572868
  88.7 28.5 %collective-permute-start.5 = (bf16[128,2048]{1,0:T(8,128)(2,1)S(1)}, bf16[128,2048]{1,0:T(8,128)(2,1)S(1)}, u32[]{:S(2)}, u32[]{:S(2)}) collective-permute-start(bf16[128,2048]{1,0:T(8,128)(2,1)S(1)} %collective-permute-done.4), channel_id=1, source_target_pairs={{1,0},{5,4},{9,8},{13,12},{17,16},{21,20},{25,24},{29,28}} | collective-permute-start | bytes 1572872 | tf_op jit(solution)/shard_map/ppermute | solution.py:317
  118.9 1.3 copy-start
  120.2 279.2 %all-to-all-start.1 = ((bf16[16,12,128,256]{3,2,1,0:T(8,128)(2,1)}), bf16[16,12,128,256]{3,2,1,0:T(8,128)(2,1)}, u32[]{:S(2)}, u32[]{:S(2)}) async-start(bf16[16,12,128,256]{3,2,1,0:T(8,128)(2,1)} %half_transform.4), calls=%async_computation.1 | async-start | bytes 25165824 | tf_op jit(solution)/shard_map/all_to_all | solution.py:364
  125.2 176.1 %all-gather.2.cloned.1.call-start = ((), (), s32[]{:S(2)}) async-start(), calls=%async_computation.4 | async-start | bytes 10485760 | tf_op jit(solution)/shard_map/all_gather | solution.py:358
  399.3 53.9 %all-to-all-start.2 = ((bf16[16,2,128,256]{3,2,1,0:T(8,128)(2,1)}), bf16[16,2,128,256]{3,2,1,0:T(8,128)(2,1)}, u32[]{:S(2)}, u32[]{:S(2)}) async-start(bf16[16,2,128,256]{3,2,1,0:T(8,128)(2,1)} %half_transform.5), calls=%async_computation.2 | async-start | bytes 4194304 | tf_op jit(solution)/shard_map/all_to_all | solution.py:364
Sparse Core Ops, SparseCore 0:
  127.6 173.6 all-gather.1

commit v8 on v7

--- a/solution.py
+++ b/solution.py
@@ -11,7 +11,6 @@
 VMEM_BYTES = 58 * 2**20
 FIT_VMEM_BYTES = 63 * 2**20
 PANEL = 16
-GROUP = 4
 SCALE = 2.0**40
 PIVOT_FLOOR = 1e-6
 
@@ -142,17 +141,19 @@
             jnp.where(used, tile, jnp.zeros_like(tile))
         )
 
+    together = aux_width if vectors <= 64 else 4
+
     def some(group, carry):
-        low = group * GROUP
-        window = window_ref[pl.ds(low, GROUP)]
+        low = group * together
+        window = window_ref[pl.ds(low, together)]
         product = lax.dot_general(
             basis_ref[:, low_block * size_block :],
-            window.reshape(GROUP * window.shape[1], window.shape[2]),
+            window.reshape(together * window.shape[1], window.shape[2]),
             (((1,), (1,)), ((), ())),
             preferred_element_type=jnp.float32,
         )
         product = product[:vectors] + product[vectors:]
-        for p in range(GROUP):
+        for p in range(together):
             for m in range(side):
                 column = (p * side + m) * size_block
                 rows_ref[m, pl.ds(low + p, vectors, stride=aux_width), :] = product[
@@ -160,7 +161,7 @@
                 ]
         return carry
 
-    lax.fori_loop(0, aux_width // GROUP, some, 0)
+    lax.fori_loop(0, aux_width // together, some, 0)
     for m in range(side):
         out_ref[..., m * size_block : (m + 1) * size_block] = (
             rows_ref[m].astype(jnp.bfloat16).reshape(out_ref.shape[:-1] + (size_block,))
@@ -216,13 +217,26 @@
     )(pair_list.T, pair_count, basis_rows, *[integrals] * len(tiles))
 
 
-def fit_kernel(step_rows, before_ref, factor_ref, half_ref, out_ref, lower_ref, columns_ref, factor_sems, half_sems):
+def fit_kernel(
+    step_rows,
+    before_ref,
+    factor_ref,
+    half_ref,
+    out_ref,
+    sum_ref,
+    lower_ref,
+    columns_ref,
+    sum_sem,
+    factor_sems,
+    half_sems,
+):
     step = pl.program_id(0)
     aux_total = factor_ref.shape[0]
     basis_total = out_ref.shape[0]
     width = columns_ref.shape[-1] // basis_total
     blocks = aux_total // step_rows
     sources = half_ref.shape[0] // blocks
+    sum_copy = pltpu.make_async_copy(before_ref, sum_ref, sum_sem)
 
     def factor_copy(number):
         low, high = number * step_rows, (number + 1) * step_rows
@@ -251,6 +265,7 @@
             for k in range(width):
                 half_copy(step, number, k).start()
             factor_copy(number).start()
+        sum_copy.start()
 
     pl.when(step + 1 < pl.num_programs(0))(lambda: start_half(step + 1))
 
@@ -274,7 +289,8 @@
 
     @pl.when(step == 0)
     def _():
-        out_ref[...] = before_ref[...] + total
+        sum_copy.wait()
+        out_ref[...] = sum_ref[...] + total
 
     @pl.when(step > 0)
     def _():
@@ -290,14 +306,16 @@
         out_shape=jax.ShapeDtypeStruct((basis_total, basis_total), jnp.float32),
         grid=(own // width,),
         in_specs=[
-            pl.BlockSpec((basis_total, basis_total), lambda k: (0, 0)),
+            pl.BlockSpec(memory_space=pl.ANY),
             pl.BlockSpec(memory_space=pl.ANY),
             pl.BlockSpec(memory_space=pl.ANY),
         ],
         out_specs=pl.BlockSpec((basis_total, basis_total), lambda k: (0, 0)),
         scratch_shapes=[
+            pltpu.VMEM((basis_total, basis_total), jnp.float32),
             pltpu.VMEM((aux_total, aux_total), jnp.bfloat16),
             pltpu.VMEM((2, devices, aux_local, width * basis_total), jnp.bfloat16),
+            pltpu.SemaphoreType.DMA,
             pltpu.SemaphoreType.DMA((8,)),
             pltpu.SemaphoreType.DMA((2, 8, width)),
         ],
@@ -351,11 +369,9 @@
             for step in range(1, lax.axis_size("occ") - 1):
                 passed.append(line_step(step, *passed[-1], "occ"))
             line = line_blocks(metric, passed, "occ")
+            factor = lax.all_gather(line, "aux", axis=0, tiled=True)
         elif chunk == 1:
-            half, state, arrived[0], line = lax.optimization_barrier(
-                (half, state, arrived[0], line)
-            )
-            factor = lax.all_gather(line, "aux", axis=0, tiled=True)
+            half, state, arrived[0] = lax.optimization_barrier((half, state, arrived[0]))
         else:
             total = fit_exchange(factor, arrived[chunk - 2], total)
             half, state, arrived[chunk - 1], total = lax.optimization_barrier(

time: 484 us -> 545 us (1.13)
  waiting for transfers between devices: 290 us -> 361 us
  Pallas kernels: 132 us -> 122 us
    ppermute x3, waiting for transfers between devices: 29.6 us -> 293 us  [line_step(): lax.ppermute(downward, axis, [(i, i - 1) for i in range(1, devices - step)])]
    all_gather x1, waiting for transfers between devices: 159 us -> 45.2 us  [per_device(): factor = lax.all_gather(line, 'aux', axis=0, tiled=True)]
    all_to_all x3, waiting for transfers between devices: 101 us -> 23.1 us  [per_device(): lax.all_to_all(half, BOTH, split_axis=0, concat_axis=0, tiled=True)]
    pallas_call x3, Pallas kernels: 57.7 us -> 50.7 us  [half_transform(): pl.pallas_call(functools.partial(half_kernel, low_block), out_shape=jax.S...]
  transfers between devices with their start and end apart: 10 -> 10, of which waited for: 5 -> 5; matrix products, arithmetic and copies ran while one was open for 1% -> 1% of each run, Pallas kernels for 26% -> 21%
where the time goes in v8:
time: 545 us; the launch traced here: 544 us
  waiting for transfers between devices  361 us (66%)
  Pallas kernels  122 us (22%)
  starting transfers between devices  27 us (5%)
  blocking collectives  13.6 us (2%)
  between operations  13.6 us (2%)
  local copies, waits for them, and re-layouts  5.59 us (1%)
    ppermute x3, waiting for transfers between devices, line_step(): lax.ppermute(downward, axis, [(i, i - 1) for i in range(1, devices - step)])  293 us
    pallas_call x3, Pallas kernels, fit_exchange(): pl.pallas_call(functools.partial(fit_kernel, aux_total // 8), out_shape=j...  51.9 us
    pallas_call x3, Pallas kernels, half_transform(): pl.pallas_call(functools.partial(half_kernel, low_block), out_shape=jax.S...  50.7 us
    all_gather x1, waiting for transfers between devices, per_device(): factor = lax.all_gather(line, 'aux', axis=0, tiled=True)  45.2 us
    all_to_all x3, waiting for transfers between devices, per_device(): lax.all_to_all(half, BOTH, split_axis=0, concat_axis=0, tiled=True)  23.1 us
    pallas_call x3, Pallas kernels, factor_rows(): pl.pallas_call(functools.partial(factor_kernel, start), out_shape=(jax.Sh...  19.8 us
    all_to_all x3, starting transfers between devices, per_device(): lax.all_to_all(half, BOTH, split_axis=0, concat_axis=0, tiled=True)  16.8 us
    all_to_all x1, blocking collectives, per_device(): lax.all_to_all(shares, BOTH, split_axis=0, concat_axis=0, tiled=True)  13.6 us
  transfers between devices with their start and end apart: 10, of which 5 were waited for; matrix products, arithmetic and copies ran while one was open for 1% of the time, Pallas kernels for 21%

profile of v8, /device:TPU:0, one launch (start us, length us, event | category | flops | bytes accessed | tf_op | source)
XLA Modules:
  0.0 544.1 jit_solution(9778052534408946025)
XLA Ops:
  6.5 5.0 collective-permute-start
  11.5 1.3 collective-permute-start.1
  12.8 3.7 factor_rows.3
  16.5 13.3 %half_transform.3 = bf16[16,2,128,256]{3,2,1,0:T(8,128)(2,1)} custom-call(s32[4,8]{1,0:T(4,128)} %bitcast.19, s32[8]{0:T(128)} %count_ref.5, bf16[64,256]{1,0:T(8,128)(2,1)} %get-tuple-element.24.basis_ref, bf16[8,4,16,128,128]{4,3,2,1,0:T(8,128)(2,1)} %refs_1_.5, bf16[8,4,16,128,128]{4,3,2,1,0:T(8,128)(2,1)} %refs_1_.5, ...), custom_call_target="tpu_custom_call" | custom-call | flops 1073741824 | bytes 18874368 | tf_op jit(solution)/shard_map/half_transform/pallas_call | solution.py:188
  29.8 0.0 collective-permute-done
  29.8 0.0 copy-start.2
  29.8 0.0 collective-permute-done.1
  29.8 0.8 copy-done.2
  30.6 7.0 %all-to-all-start = ((bf16[16,2,128,256]{3,2,1,0:T(8,128)(2,1)}), bf16[16,2,128,256]{3,2,1,0:T(8,128)(2,1)S(1)}, u32[]{:S(2)}, u32[]{:S(2)}) async-start(bf16[16,2,128,256]{3,2,1,0:T(8,128)(2,1)} %half_transform.3), calls=%async_computation | async-start | bytes 4194304 | tf_op jit(solution)/shard_map/all_to_all | solution.py:380
  37.6 12.6 %factor_rows.4 = (bf16[384,256]{1,0:T(8,128)(2,1)}, f32[256,256]{1,0:T(8,128)}, f32[8,256]{1,0:T(8,128)}) custom-call(f32[256,256]{1,0:T(8,128)} %get-tuple-element.27.refs_0_, f32[8,256]{1,0:T(8,128)} %get-tuple-element.28.refs_1_), custom_call_target="tpu_custom_call" | custom-call | tf_op jit(solution)/shard_map/factor_rows/pallas_call | solution.py:113
  50.2 26.9 %half_transform.4 = bf16[16,12,128,256]{3,2,1,0:T(8,128)(2,1)} custom-call(s32[4,8]{1,0:T(4,128)} %bitcast.20, s32[8]{0:T(128)} %count_ref.5, bf16[384,256]{1,0:T(8,128)(2,1)} %get-tuple-element.29.basis_ref, bf16[8,4,16,128,128]{4,3,2,1,0:T(8,128)(2,1)} %refs_1_.5, bf16[8,4,16,128,128]{4,3,2,1,0:T(8,128)(2,1)} %refs_1_.5, ...), custom_call_target="tpu_custom_call" | custom-call | flops 6442450944 | bytes 29360128 | tf_op jit(solution)/shard_map/half_transform/pallas_call | solution.py:188
  77.1 10.0 %all-to-all-done.half_ref = bf16[16,2,128,256]{3,2,1,0:T(8,128)(2,1)S(1)} async-done(((bf16[16,2,128,256]{3,2,1,0:T(8,128)(2,1)}), bf16[16,2,128,256]{3,2,1,0:T(8,128)(2,1)S(1)}, u32[]{:S(2)}, u32[]{:S(2)}) %all-to-all-start) | async-done | bytes 2097184 | tf_op jit(solution)/shard_map/all_to_all | solution.py:380
  87.1 0.0 copy-start
  87.1 0.0 copy-start.1
  87.1 1.3 copy-done
  88.4 5.0 all-to-all-start.1
  93.4 0.0 all-gather.2.cloned.1.call-start
  93.4 0.7 collective-permute-start.2
  94.1 1.3 collective-permute-start.4
  95.4 0.0 collective-permute-done.2
  95.4 0.7 collective-permute-start.3
  96.2 196.8 %collective-permute-done.4 = bf16[128,2048]{1,0:T(8,128)(2,1)S(1)} collective-permute-done((bf16[128,2048]{1,0:T(8,128)(2,1)S(1)}, bf16[128,2048]{1,0:T(8,128)(2,1)S(1)}, u32[]{:S(2)}, u32[]{:S(2)}) %collective-permute-start.4) | collective-permute-done | bytes 524320 | tf_op jit(solution)/shard_map/ppermute | solution.py:335
  293.0 1.3 collective-permute-start.5
  294.3 0.0 collective-permute-done.3
  294.4 1.1 bitcast_dynamic-update-slice_fusion.4
  295.4 0.0 copy-done.1
  295.6 96.2 %collective-permute-done.5 = bf16[128,2048]{1,0:T(8,128)(2,1)S(1)} collective-permute-done((bf16[128,2048]{1,0:T(8,128)(2,1)S(1)}, bf16[128,2048]{1,0:T(8,128)(2,1)S(1)}, u32[]{:S(2)}, u32[]{:S(2)}) %collective-permute-start.5) | collective-permute-done | bytes 524320 | tf_op jit(solution)/shard_map/ppermute | solution.py:335
  391.8 1.5 constant_dynamic-slice_fusion
  393.2 0.0 all-gather.2.cloned.1.call-update
  393.3 3.5 factor_rows.5
  396.8 10.6 %half_transform.5 = bf16[16,2,128,256]{3,2,1,0:T(8,128)(2,1)} custom-call(s32[4,8]{1,0:T(4,128)} %bitcast.21, s32[8]{0:T(128)} %count_ref.5, bf16[64,256]{1,0:T(8,128)(2,1)} %get-tuple-element.35.basis_ref, bf16[8,4,16,128,128]{4,3,2,1,0:T(8,128)(2,1)} %refs_1_.5, bf16[8,4,16,128,128]{4,3,2,1,0:T(8,128)(2,1)} %refs_1_.5), custom_call_target="tpu_custom_call" | custom-call | flops 1073741824 | bytes 18874368 | tf_op jit(solution)/shard_map/half_transform/pallas_call | solution.py:188
  407.3 45.2 %all-gather.2.cloned.1.call-done.factor_ref = bf16[2048,2048]{1,0:T(8,128)(2,1)} async-done(((bf16[512,2048]{1,0:T(8,128)(2,1)}), bf16[2048,2048]{1,0:T(8,128)(2,1)}) %all-gather.2.cloned.1.call-update) | async-done | bytes 8388624 | tf_op jit(solution)/shard_map/all_gather | solution.py:372
  452.6 0.7 broadcast_in_dim.3.before_ref
  453.3 7.7 %fit_exchange.3.before_ref = f32[256,256]{1,0:T(8,128)} custom-call(f32[256,256]{1,0:T(8,128)} %broadcast_in_dim.3.before_ref, bf16[2048,2048]{1,0:T(8,128)(2,1)} %all-gather.2.cloned.1.call-done.factor_ref, bf16[16,2,128,256]{3,2,1,0:T(8,128)(2,1)} %copy-done), custom_call_target="tpu_custom_call" | custom-call | flops 2952790016 | bytes 10485760 | tf_op jit(solution)/shard_map/fit_exchange/pallas_call | solution.py:304
  461.0 0.0 all-to-all-done.1.half_ref
  461.0 4.8 all-to-all-start.2
  465.8 36.4 %fit_exchange.4.before_ref = f32[256,256]{1,0:T(8,128)} custom-call(f32[256,256]{1,0:T(8,128)} %fit_exchange.3.before_ref, bf16[2048,2048]{1,0:T(8,128)(2,1)} %all-gather.2.cloned.1.call-done.factor_ref, bf16[16,12,128,256]{3,2,1,0:T(8,128)(2,1)} %all-to-all-done.1.half_ref), custom_call_target="tpu_custom_call" | custom-call | flops 17716740096 | bytes 20971520 | tf_op jit(solution)/shard_map/fit_exchange/pallas_call | solution.py:304
  502.2 13.1 %all-to-all-done.2.half_ref = bf16[16,2,128,256]{3,2,1,0:T(8,128)(2,1)} async-done(((bf16[16,2,128,256]{3,2,1,0:T(8,128)(2,1)}), bf16[16,2,128,256]{3,2,1,0:T(8,128)(2,1)}, u32[]{:S(2)}, u32[]{:S(2)}) %all-to-all-start.2) | async-done | bytes 2097184 | tf_op jit(solution)/shard_map/all_to_all | solution.py:380
  515.3 7.7 %fit_exchange.5 = f32[256,256]{1,0:T(8,128)} custom-call(f32[256,256]{1,0:T(8,128)} %fit_exchange.4.before_ref, bf16[2048,2048]{1,0:T(8,128)(2,1)} %all-gather.2.cloned.1.call-done.factor_ref, bf16[16,2,128,256]{3,2,1,0:T(8,128)(2,1)} %all-to-all-done.2.half_ref), custom_call_target="tpu_custom_call" | custom-call | flops 2952790016 | bytes 10485760 | tf_op jit(solution)/shard_map/fit_exchange/pallas_call | solution.py:304
  523.1 13.6 %all_to_all.20 = f32[16,16,256]{2,1,0:T(8,128)S(1)} all-to-all(f32[16,16,256]{2,1,0:T(8,128)} %bitcast.18), channel_id=1, replica_groups=mesh['grp'=2,'aux'=4,'occ'=4] {'aux','occ'}, dimensions={0} | all-to-all | bytes 524288 | tf_op jit(solution)/shard_map/all_to_all | solution.py:385
  536.6 0.6 reduce_sum.9
  (6 shorter events, 0.2 us)
Async XLA Ops:
  6.5 23.3 %collective-permute-start = (bf16[128,2048]{1,0:T(8,128)(2,1)}, bf16[128,2048]{1,0:T(8,128)(2,1)S(1)}, u32[]{:S(2)}, u32[]{:S(2)}) collective-permute-start(bf16[128,2048]{1,0:T(8,128)(2,1)} %param.9), channel_id=1, source_target_pairs={{0,1},{1,2},{2,3},{4,5},{5,6},{6,7},{8,9},{9,10},{10,11},{12,13},{... | collective-permute-start | bytes 1572872 | tf_op jit(solution)/shard_map/ppermute | solution.py:334
  11.5 18.3 %collective-permute-start.1 = (bf16[128,2048]{1,0:T(8,128)(2,1)}, bf16[128,2048]{1,0:T(8,128)(2,1)S(1)}, u32[]{:S(2)}, u32[]{:S(2)}) collective-permute-start(bf16[128,2048]{1,0:T(8,128)(2,1)} %param.9), channel_id=1, source_target_pairs={{1,0},{2,1},{3,2},{5,4},{6,5},{7,6},{9,8},{10,9},{11,10},{13,12},{... | collective-permute-start | bytes 1572872 | tf_op jit(solution)/shard_map/ppermute | solution.py:335
  29.8 0.8 copy-start.2
  30.6 56.4 %all-to-all-start = ((bf16[16,2,128,256]{3,2,1,0:T(8,128)(2,1)}), bf16[16,2,128,256]{3,2,1,0:T(8,128)(2,1)S(1)}, u32[]{:S(2)}, u32[]{:S(2)}) async-start(bf16[16,2,128,256]{3,2,1,0:T(8,128)(2,1)} %half_transform.3), calls=%async_computation | async-start | bytes 4194304 | tf_op jit(solution)/shard_map/all_to_all | solution.py:380
  87.1 1.3 copy-start
  87.1 208.4 %copy-start.1 = (bf16[128,2048]{1,0:T(8,128)(2,1)S(1)}, bf16[128,2048]{1,0:T(8,128)(2,1)}, u32[]{:S(2)}) copy-start(bf16[128,2048]{1,0:T(8,128)(2,1)} %param.9) | copy-start | bytes 1572868
  88.4 372.7 %all-to-all-start.1 = ((bf16[16,12,128,256]{3,2,1,0:T(8,128)(2,1)}), bf16[16,12,128,256]{3,2,1,0:T(8,128)(2,1)}, u32[]{:S(2)}, u32[]{:S(2)}) async-start(bf16[16,12,128,256]{3,2,1,0:T(8,128)(2,1)} %half_transform.4), calls=%async_computation.1 | async-start | bytes 25165824 | tf_op jit(solution)/shard_map/all_to_all | solution.py:380
  93.4 359.2 %all-gather.2.cloned.1.call-start = ((), (), s32[]{:S(2)}) async-start(), calls=%async_computation.4 | async-start | bytes 10485760 | tf_op jit(solution)/shard_map/all_gather | solution.py:372
  93.4 2.0 collective-permute-start.2
  94.1 198.8 %collective-permute-start.4 = (bf16[128,2048]{1,0:T(8,128)(2,1)S(1)}, bf16[128,2048]{1,0:T(8,128)(2,1)S(1)}, u32[]{:S(2)}, u32[]{:S(2)}) collective-permute-start(bf16[128,2048]{1,0:T(8,128)(2,1)S(1)} %collective-permute-done.1), channel_id=1, source_target_pairs={{1,0},{2,1},{5,4},{6,5},{9,8},{10,9},{13,12},{14,13},{17,16},{18,1... | collective-permute-start | bytes 1572872 | tf_op jit(solution)/shard_map/ppermute | solution.py:335
  95.4 198.8 %collective-permute-start.3 = (bf16[128,2048]{1,0:T(8,128)(2,1)S(1)}, bf16[128,2048]{1,0:T(8,128)(2,1)S(1)}, u32[]{:S(2)}, u32[]{:S(2)}) collective-permute-start(bf16[128,2048]{1,0:T(8,128)(2,1)S(1)} %collective-permute-done.2), channel_id=1, source_target_pairs={{2,3},{6,7},{10,11},{14,15},{18,19},{22,23},{26,27},{30,31}} | collective-permute-start | bytes 1572872 | tf_op jit(solution)/shard_map/ppermute | solution.py:334
  293.0 98.8 %collective-permute-start.5 = (bf16[128,2048]{1,0:T(8,128)(2,1)S(1)}, bf16[128,2048]{1,0:T(8,128)(2,1)S(1)}, u32[]{:S(2)}, u32[]{:S(2)}) collective-permute-start(bf16[128,2048]{1,0:T(8,128)(2,1)S(1)} %collective-permute-done.4), channel_id=1, source_target_pairs={{1,0},{5,4},{9,8},{13,12},{17,16},{21,20},{25,24},{29,28}} | collective-permute-start | bytes 1572872 | tf_op jit(solution)/shard_map/ppermute | solution.py:335
  461.0 54.3 %all-to-all-start.2 = ((bf16[16,2,128,256]{3,2,1,0:T(8,128)(2,1)}), bf16[16,2,128,256]{3,2,1,0:T(8,128)(2,1)}, u32[]{:S(2)}, u32[]{:S(2)}) async-start(bf16[16,2,128,256]{3,2,1,0:T(8,128)(2,1)} %half_transform.5), calls=%async_computation.2 | async-start | bytes 4194304 | tf_op jit(solution)/shard_map/all_to_all | solution.py:380
Sparse Core Ops, SparseCore 0:
  393.4 59.1 all-gather.1

commit v9 on v8

--- a/solution.py
+++ b/solution.py
@@ -329,20 +329,29 @@
     )(before, factor, arrived)
 
 
-def line_step(step, upward, downward, axis):
-    devices = lax.axis_size(axis)
-    upward = lax.ppermute(upward, axis, [(i, i + 1) for i in range(step, devices - 1)])
-    downward = lax.ppermute(downward, axis, [(i, i - 1) for i in range(1, devices - step)])
-    return upward, downward
-
-
-def line_blocks(block, passed, axis):
-    devices = lax.axis_size(axis)
-    up, down = [pair[0] for pair in passed], [pair[1] for pair in passed]
-    around = jnp.stack(up[::-1] + [block] + down)
-    first = devices - 1 - lax.axis_index(axis)
-    blocks = lax.dynamic_slice_in_dim(around, first, devices, 0)
-    return blocks.reshape(devices * block.shape[0], block.shape[1])
+def line_near(block):
+    up = lax.ppermute(block, "occ", [(0, 1), (1, 2), (2, 3)])
+    down = lax.ppermute(block, "occ", [(3, 2), (2, 1), (1, 0)])
+    far = lax.ppermute(block, "occ", [(0, 2), (3, 1)])
+    return up, down, far
+
+
+def line_ends(block, up, down, far):
+    me = lax.axis_index("occ")
+    left = me < 2
+    later = lax.ppermute(
+        jnp.stack([jnp.where(left, down, up), far]), "occ", [(1, 0), (2, 3)]
+    )
+    order = lax.switch(
+        me,
+        [
+            lambda: (block, down, later[0], later[1]),
+            lambda: (up, block, down, far),
+            lambda: (far, up, block, down),
+            lambda: (later[1], later[0], up, block),
+        ],
+    )
+    return jnp.concatenate(order)
 
 
 def chunk_sizes(own):
@@ -354,7 +363,8 @@
 def per_device(integrals, pair_list, pair_count, coefficients, metric):
     devices = lax.axis_size("aux") * lax.axis_size("occ")
     basis_total = coefficients.shape[0]
-    passed = [line_step(0, metric, metric, "occ")]
+    in_line = lax.axis_size("occ") == 4
+    near = line_near(metric) if in_line else ()
     total = jnp.zeros((basis_total, basis_total), jnp.float32)
     state = (coefficients,)
     start = 0
@@ -365,13 +375,11 @@
         rows, state = factor_rows(start, width, basis_total, state)
         half = half_transform(integrals, pair_list, pair_count, rows, start, devices)
         if chunk == 0:
-            half, state, passed[0] = lax.optimization_barrier((half, state, passed[0]))
-            for step in range(1, lax.axis_size("occ") - 1):
-                passed.append(line_step(step, *passed[-1], "occ"))
-            line = line_blocks(metric, passed, "occ")
-            factor = lax.all_gather(line, "aux", axis=0, tiled=True)
+            half, state, near = lax.optimization_barrier((half, state, near))
+            line = line_ends(metric, *near) if in_line else metric
         elif chunk == 1:
-            half, state, arrived[0] = lax.optimization_barrier((half, state, arrived[0]))
+            half, state, line = lax.optimization_barrier((half, state, line))
+            factor = lax.all_gather(line, "aux" if in_line else BOTH, axis=0, tiled=True)
         else:
             total = fit_exchange(factor, arrived[chunk - 2], total)
             half, state, arrived[chunk - 1], total = lax.optimization_barrier(

time: 545 us -> 471 us (0.86)
  waiting for transfers between devices: 361 us -> 282 us
    ppermute x6 -> x4, waiting for transfers between devices: 293 us -> 17.2 us  [the longest x1 17.2 us: line_ends(): lax.ppermute(jnp.stack([jnp.where(left, down, up), far]), 'occ', [(1, 0),...]
    all_gather x1, waiting for transfers between devices: 45.2 us -> 162 us  [per_device(): lax.all_gather(line, 'aux' if in_line else BOTH, axis=0, tiled=True)]
    all_to_all x3, waiting for transfers between devices: 23.1 us -> 102 us  [per_device(): lax.all_to_all(half, BOTH, split_axis=0, concat_axis=0, tiled=True)]
    ppermute x6 -> x4, starting transfers between devices: 10.2 us -> 13.1 us  [the longest x1 5.57 us: line_near(): far = lax.ppermute(block, 'occ', [(0, 2), (3, 1)])]
  transfers between devices with their start and end apart: 10 -> 8, of which waited for: 5 -> 4; matrix products, arithmetic and copies ran while one was open for 1% -> 2% of each run, Pallas kernels for 21% -> 24%
where the time goes in v9:
time: 471 us; the launch traced here: 470 us
  waiting for transfers between devices  282 us (60%)
  Pallas kernels  122 us (26%)
  starting transfers between devices  30.4 us (6%)
  blocking collectives  13.6 us (3%)
  between operations  13.5 us (3%)
  other arithmetic  4.92 us (1%)
    all_gather x1, waiting for transfers between devices, per_device(): lax.all_gather(line, 'aux' if in_line else BOTH, axis=0, tiled=True)  162 us
    all_to_all x3, waiting for transfers between devices, per_device(): lax.all_to_all(half, BOTH, split_axis=0, concat_axis=0, tiled=True)  102 us
    pallas_call x3, Pallas kernels, fit_exchange(): pl.pallas_call(functools.partial(fit_kernel, aux_total // 8), out_shape=j...  51.9 us
    pallas_call x3, Pallas kernels, half_transform(): pl.pallas_call(functools.partial(half_kernel, low_block), out_shape=jax.S...  50.6 us
    pallas_call x3, Pallas kernels, factor_rows(): pl.pallas_call(functools.partial(factor_kernel, start), out_shape=(jax.Sh...  19.8 us
    all_to_all x3, starting transfers between devices, per_device(): lax.all_to_all(half, BOTH, split_axis=0, concat_axis=0, tiled=True)  17.3 us
    ppermute x1, waiting for transfers between devices, line_ends(): lax.ppermute(jnp.stack([jnp.where(left, down, up), far]), 'occ', [(1, 0),...  17.2 us
    all_to_all x1, blocking collectives, per_device(): lax.all_to_all(shares, BOTH, split_axis=0, concat_axis=0, tiled=True)  13.6 us
  transfers between devices with their start and end apart: 8, of which 4 were waited for; matrix products, arithmetic and copies ran while one was open for 2% of the time, Pallas kernels for 24%

profile of v9, /device:TPU:0, one launch (start us, length us, event | category | flops | bytes accessed | tf_op | source)
XLA Modules:
  0.0 470.0 jit_solution(2134205285954442569)
XLA Ops:
  6.5 5.0 %collective-permute-start = (bf16[128,2048]{1,0:T(8,128)(2,1)}, bf16[128,2048]{1,0:T(8,128)(2,1)S(1)}, u32[]{:S(2)}, u32[]{:S(2)}) collective-permute-start(bf16[128,2048]{1,0:T(8,128)(2,1)} %param.13), channel_id=1, source_target_pairs={{0,1},{1,2},{2,3},{4,5},{5,6},{6,7},{8,9},{9,10},{10,11},{12,13},{... | collective-permute-start | bytes 1572872 | tf_op jit(solution)/shard_map/ppermute | solution.py:333
  11.5 1.3 collective-permute-start.1
  12.8 5.6 %collective-permute-start.2 = (bf16[128,2048]{1,0:T(8,128)(2,1)}, bf16[128,2048]{1,0:T(8,128)(2,1)S(1)}, u32[]{:S(2)}, u32[]{:S(2)}) collective-permute-start(bf16[128,2048]{1,0:T(8,128)(2,1)} %param.13), channel_id=1, source_target_pairs={{0,2},{3,1},{4,6},{7,5},{8,10},{11,9},{12,14},{15,13},{16,18},{19,... | collective-permute-start | bytes 1572872 | tf_op jit(solution)/shard_map/ppermute | solution.py:335
  18.4 3.7 factor_rows.3
  22.1 13.3 %half_transform.3 = bf16[16,2,128,256]{3,2,1,0:T(8,128)(2,1)} custom-call(s32[4,8]{1,0:T(4,128)} %bitcast.15, s32[8]{0:T(128)} %count_ref.5, bf16[64,256]{1,0:T(8,128)(2,1)} %get-tuple-element.63.basis_ref, bf16[8,4,16,128,128]{4,3,2,1,0:T(8,128)(2,1)} %refs_1_.5, bf16[8,4,16,128,128]{4,3,2,1,0:T(8,128)(2,1)} %refs_1_.5, ...), custom_call_target="tpu_custom_call" | custom-call | flops 1073741824 | bytes 18874368 | tf_op jit(solution)/shard_map/half_transform/pallas_call | solution.py:188
  35.4 0.0 collective-permute-done
  35.4 0.0 collective-permute-done.1
  35.4 0.0 collective-permute-done.2
  35.4 7.7 %all-to-all-start.1 = ((bf16[16,2,128,256]{3,2,1,0:T(8,128)(2,1)}), bf16[16,2,128,256]{3,2,1,0:T(8,128)(2,1)}, u32[]{:S(2)}, u32[]{:S(2)}) async-start(bf16[16,2,128,256]{3,2,1,0:T(8,128)(2,1)} %half_transform.3), calls=%async_computation.1 | async-start | bytes 4194304 | tf_op jit(solution)/shard_map/all_to_all | solution.py:388
  43.2 0.1 select_bitcast_fusion
  43.2 1.1 pad_maximum_fusion.1
  44.3 1.3 collective-permute-start.3
  45.6 12.6 %factor_rows.4 = (bf16[384,256]{1,0:T(8,128)(2,1)}, f32[256,256]{1,0:T(8,128)}, f32[8,256]{1,0:T(8,128)}) custom-call(f32[256,256]{1,0:T(8,128)} %get-tuple-element.66.refs_0_, f32[8,256]{1,0:T(8,128)} %get-tuple-element.67.refs_1_), custom_call_target="tpu_custom_call" | custom-call | tf_op jit(solution)/shard_map/factor_rows/pallas_call | solution.py:113
  58.2 0.0 copy-start
  58.2 27.0 %half_transform.4 = bf16[16,12,128,256]{3,2,1,0:T(8,128)(2,1)} custom-call(s32[4,8]{1,0:T(4,128)} %bitcast.16, s32[8]{0:T(128)} %count_ref.5, bf16[384,256]{1,0:T(8,128)(2,1)} %get-tuple-element.68.basis_ref, bf16[8,4,16,128,128]{4,3,2,1,0:T(8,128)(2,1)} %refs_1_.5, bf16[8,4,16,128,128]{4,3,2,1,0:T(8,128)(2,1)} %refs_1_.5, ...), custom_call_target="tpu_custom_call" | custom-call | flops 6442450944 | bytes 29360128 | tf_op jit(solution)/shard_map/half_transform/pallas_call | solution.py:188
  85.2 17.2 %collective-permute-done.3 = bf16[2,128,2048]{2,1,0:T(8,128)(2,1)S(1)} collective-permute-done((bf16[2,128,2048]{2,1,0:T(8,128)(2,1)}, bf16[2,128,2048]{2,1,0:T(8,128)(2,1)S(1)}, u32[]{:S(2)}, u32[]{:S(2)}) %collective-permute-start.3) | collective-permute-done | bytes 1048608 | tf_op jit(solution)/shard_map/ppermute | solution.py:342
  102.4 0.0 copy-done
  102.4 2.6 conditional.1
  102.4 0.8 copy.6
  103.2 0.8 copy.7
  104.0 1.0 slice_bitcast_fusion
  105.0 3.2 pad_maximum_fusion
  108.2 0.0 all-to-all-done.1.half_ref
  108.2 5.0 %all-to-all-start = ((bf16[16,12,128,256]{3,2,1,0:T(8,128)(2,1)}), bf16[16,12,128,256]{3,2,1,0:T(8,128)(2,1)}, u32[]{:S(2)}, u32[]{:S(2)}) async-start(bf16[16,12,128,256]{3,2,1,0:T(8,128)(2,1)} %half_transform.4), calls=%async_computation | async-start | bytes 25165824 | tf_op jit(solution)/shard_map/all_to_all | solution.py:388
  113.2 0.0 all-gather.2.cloned.1.call-start
  113.3 0.7 all-gather.2.cloned.1.call-update
  113.9 3.5 factor_rows.5
  117.4 10.3 %half_transform.5 = bf16[16,2,128,256]{3,2,1,0:T(8,128)(2,1)} custom-call(s32[4,8]{1,0:T(4,128)} %bitcast.17, s32[8]{0:T(128)} %count_ref.5, bf16[64,256]{1,0:T(8,128)(2,1)} %get-tuple-element.80.basis_ref, bf16[8,4,16,128,128]{4,3,2,1,0:T(8,128)(2,1)} %refs_1_.5, bf16[8,4,16,128,128]{4,3,2,1,0:T(8,128)(2,1)} %refs_1_.5), custom_call_target="tpu_custom_call" | custom-call | flops 1073741824 | bytes 18874368 | tf_op jit(solution)/shard_map/half_transform/pallas_call | solution.py:188
  127.7 161.6 %all-gather.2.cloned.1.call-done.factor_ref = bf16[2048,2048]{1,0:T(8,128)(2,1)} async-done(((bf16[512,2048]{1,0:T(8,128)(2,1)}), bf16[2048,2048]{1,0:T(8,128)(2,1)}) %all-gather.2.cloned.1.call-update) | async-done | bytes 8388624 | tf_op jit(solution)/shard_map/all_gather | solution.py:382
  289.3 0.7 broadcast_in_dim.3.before_ref
  290.0 7.7 %fit_exchange.3.before_ref = f32[256,256]{1,0:T(8,128)} custom-call(f32[256,256]{1,0:T(8,128)} %broadcast_in_dim.3.before_ref, bf16[2048,2048]{1,0:T(8,128)(2,1)} %all-gather.2.cloned.1.call-done.factor_ref, bf16[16,2,128,256]{3,2,1,0:T(8,128)(2,1)} %all-to-all-done.1.half_ref), custom_call_target="tpu_custom_call" | custom-call | flops 2952790016 | bytes 10485760 | tf_op jit(solution)/shard_map/fit_exchange/pallas_call | solution.py:304
  297.8 89.5 %all-to-all-done.half_ref = bf16[16,12,128,256]{3,2,1,0:T(8,128)(2,1)} async-done(((bf16[16,12,128,256]{3,2,1,0:T(8,128)(2,1)}), bf16[16,12,128,256]{3,2,1,0:T(8,128)(2,1)}, u32[]{:S(2)}, u32[]{:S(2)}) %all-to-all-start) | async-done | bytes 12582944 | tf_op jit(solution)/shard_map/all_to_all | solution.py:388
  387.4 4.6 all-to-all-start.2
  392.0 36.4 %fit_exchange.4.before_ref = f32[256,256]{1,0:T(8,128)} custom-call(f32[256,256]{1,0:T(8,128)} %fit_exchange.3.before_ref, bf16[2048,2048]{1,0:T(8,128)(2,1)} %all-gather.2.cloned.1.call-done.factor_ref, bf16[16,12,128,256]{3,2,1,0:T(8,128)(2,1)} %all-to-all-done.half_ref), custom_call_target="tpu_custom_call" | custom-call | flops 17716740096 | bytes 20971520 | tf_op jit(solution)/shard_map/fit_exchange/pallas_call | solution.py:304
  428.3 12.9 %all-to-all-done.2.half_ref = bf16[16,2,128,256]{3,2,1,0:T(8,128)(2,1)} async-done(((bf16[16,2,128,256]{3,2,1,0:T(8,128)(2,1)}), bf16[16,2,128,256]{3,2,1,0:T(8,128)(2,1)}, u32[]{:S(2)}, u32[]{:S(2)}) %all-to-all-start.2) | async-done | bytes 2097184 | tf_op jit(solution)/shard_map/all_to_all | solution.py:388
  441.2 7.8 %fit_exchange.5 = f32[256,256]{1,0:T(8,128)} custom-call(f32[256,256]{1,0:T(8,128)} %fit_exchange.4.before_ref, bf16[2048,2048]{1,0:T(8,128)(2,1)} %all-gather.2.cloned.1.call-done.factor_ref, bf16[16,2,128,256]{3,2,1,0:T(8,128)(2,1)} %all-to-all-done.2.half_ref), custom_call_target="tpu_custom_call" | custom-call | flops 2952790016 | bytes 10485760 | tf_op jit(solution)/shard_map/fit_exchange/pallas_call | solution.py:304
  449.0 13.6 %all_to_all.20 = f32[16,16,256]{2,1,0:T(8,128)S(1)} all-to-all(f32[16,16,256]{2,1,0:T(8,128)} %bitcast.14), channel_id=1, replica_groups=mesh['grp'=2,'aux'=4,'occ'=4] {'aux','occ'}, dimensions={0} | all-to-all | bytes 524288 | tf_op jit(solution)/shard_map/all_to_all | solution.py:393
  462.5 0.6 reduce_sum.9
Async XLA Ops:
  6.5 28.9 %collective-permute-start = (bf16[128,2048]{1,0:T(8,128)(2,1)}, bf16[128,2048]{1,0:T(8,128)(2,1)S(1)}, u32[]{:S(2)}, u32[]{:S(2)}) collective-permute-start(bf16[128,2048]{1,0:T(8,128)(2,1)} %param.13), channel_id=1, source_target_pairs={{0,1},{1,2},{2,3},{4,5},{5,6},{6,7},{8,9},{9,10},{10,11},{12,13},{... | collective-permute-start | bytes 1572872 | tf_op jit(solution)/shard_map/ppermute | solution.py:333
  11.5 23.9 %collective-permute-start.1 = (bf16[128,2048]{1,0:T(8,128)(2,1)}, bf16[128,2048]{1,0:T(8,128)(2,1)S(1)}, u32[]{:S(2)}, u32[]{:S(2)}) collective-permute-start(bf16[128,2048]{1,0:T(8,128)(2,1)} %param.13), channel_id=1, source_target_pairs={{3,2},{2,1},{1,0},{7,6},{6,5},{5,4},{11,10},{10,9},{9,8},{15,14},{... | collective-permute-start | bytes 1572872 | tf_op jit(solution)/shard_map/ppermute | solution.py:334
  12.8 22.6 %collective-permute-start.2 = (bf16[128,2048]{1,0:T(8,128)(2,1)}, bf16[128,2048]{1,0:T(8,128)(2,1)S(1)}, u32[]{:S(2)}, u32[]{:S(2)}) collective-permute-start(bf16[128,2048]{1,0:T(8,128)(2,1)} %param.13), channel_id=1, source_target_pairs={{0,2},{3,1},{4,6},{7,5},{8,10},{11,9},{12,14},{15,13},{16,18},{19,... | collective-permute-start | bytes 1572872 | tf_op jit(solution)/shard_map/ppermute | solution.py:335
  35.4 72.8 %all-to-all-start.1 = ((bf16[16,2,128,256]{3,2,1,0:T(8,128)(2,1)}), bf16[16,2,128,256]{3,2,1,0:T(8,128)(2,1)}, u32[]{:S(2)}, u32[]{:S(2)}) async-start(bf16[16,2,128,256]{3,2,1,0:T(8,128)(2,1)} %half_transform.3), calls=%async_computation.1 | async-start | bytes 4194304 | tf_op jit(solution)/shard_map/all_to_all | solution.py:388
  44.3 58.1 %collective-permute-start.3 = (bf16[2,128,2048]{2,1,0:T(8,128)(2,1)}, bf16[2,128,2048]{2,1,0:T(8,128)(2,1)S(1)}, u32[]{:S(2)}, u32[]{:S(2)}) collective-permute-start(bf16[2,128,2048]{2,1,0:T(8,128)(2,1)} %pad_maximum_fusion.1), channel_id=1, source_target_pairs={{1,0},{2,3},{5,4},{6,7},{9,8},{10,11},{13,12},{14,15},{17,16},{18,... | collective-permute-start | bytes 3145736 | tf_op jit(solution)/shard_map/ppermute | solution.py:342
  58.2 44.2 %copy-start = (bf16[128,2048]{1,0:T(8,128)(2,1)S(1)}, bf16[128,2048]{1,0:T(8,128)(2,1)}, u32[]{:S(2)}) copy-start(bf16[128,2048]{1,0:T(8,128)(2,1)} %param.13) | copy-start | bytes 1572868
  108.2 279.1 %all-to-all-start = ((bf16[16,12,128,256]{3,2,1,0:T(8,128)(2,1)}), bf16[16,12,128,256]{3,2,1,0:T(8,128)(2,1)}, u32[]{:S(2)}, u32[]{:S(2)}) async-start(bf16[16,12,128,256]{3,2,1,0:T(8,128)(2,1)} %half_transform.4), calls=%async_computation | async-start | bytes 25165824 | tf_op jit(solution)/shard_map/all_to_all | solution.py:388
  113.2 176.1 %all-gather.2.cloned.1.call-start = ((), (), s32[]{:S(2)}) async-start(), calls=%async_computation.4 | async-start | bytes 10485760 | tf_op jit(solution)/shard_map/all_gather | solution.py:382
  387.4 53.9 %all-to-all-start.2 = ((bf16[16,2,128,256]{3,2,1,0:T(8,128)(2,1)}), bf16[16,2,128,256]{3,2,1,0:T(8,128)(2,1)}, u32[]{:S(2)}, u32[]{:S(2)}) async-start(bf16[16,2,128,256]{3,2,1,0:T(8,128)(2,1)} %half_transform.5), calls=%async_computation.2 | async-start | bytes 4194304 | tf_op jit(solution)/shard_map/all_to_all | solution.py:388
Sparse Core Ops, SparseCore 0:
  115.6 173.6 all-gather.1

commit v10 on v9

--- a/solution.py
+++ b/solution.py
@@ -356,7 +356,7 @@
 
 def chunk_sizes(own):
     if own % 8 == 0:
-        return [own // 8, 3 * own // 4, own // 8]
+        return [own // 4, 5 * own // 8, own // 8]
     return [1] * own
 
 

time: 471 us -> 459 us (0.975)
  waiting for transfers between devices: 282 us -> 270 us
    ppermute x1, waiting for transfers between devices: 17.2 us -> 49.1 us  [line_ends(): lax.ppermute(jnp.stack([jnp.where(left, down, up), far]), 'occ', [(1, 0),...]
    all_to_all x3, waiting for transfers between devices: 102 us -> 79.9 us  [per_device(): lax.all_to_all(half, BOTH, split_axis=0, concat_axis=0, tiled=True)]
    all_gather x1, waiting for transfers between devices: 162 us -> 141 us  [per_device(): lax.all_gather(line, 'aux' if in_line else BOTH, axis=0, tiled=True)]
  transfers between devices with their start and end apart: 8 -> 8, of which waited for: 4 -> 5; matrix products, arithmetic and copies ran while one was open for 2% -> 2% of each run, Pallas kernels for 24% -> 25%
where the time goes in v10:
time: 459 us; the launch traced here: 458 us
  waiting for transfers between devices  270 us (59%)
  Pallas kernels  122 us (27%)
  starting transfers between devices  30.4 us (7%)
  blocking collectives  13.6 us (3%)
  between operations  13.5 us (3%)
  other arithmetic  4.84 us (1%)
    all_gather x1, waiting for transfers between devices, per_device(): lax.all_gather(line, 'aux' if in_line else BOTH, axis=0, tiled=True)  141 us
    all_to_all x3, waiting for transfers between devices, per_device(): lax.all_to_all(half, BOTH, split_axis=0, concat_axis=0, tiled=True)  79.9 us
    pallas_call x3, Pallas kernels, fit_exchange(): pl.pallas_call(functools.partial(fit_kernel, aux_total // 8), out_shape=j...  51.8 us
    pallas_call x3, Pallas kernels, half_transform(): pl.pallas_call(functools.partial(half_kernel, low_block), out_shape=jax.S...  49.9 us
    ppermute x1, waiting for transfers between devices, line_ends(): lax.ppermute(jnp.stack([jnp.where(left, down, up), far]), 'occ', [(1, 0),...  49.1 us
    pallas_call x3, Pallas kernels, factor_rows(): pl.pallas_call(functools.partial(factor_kernel, start), out_shape=(jax.Sh...  19.8 us
    all_to_all x3, starting transfers between devices, per_device(): lax.all_to_all(half, BOTH, split_axis=0, concat_axis=0, tiled=True)  17.2 us
    all_to_all x1, blocking collectives, per_device(): lax.all_to_all(shares, BOTH, split_axis=0, concat_axis=0, tiled=True)  13.6 us
  transfers between devices with their start and end apart: 8, of which 5 were waited for; matrix products, arithmetic and copies ran while one was open for 2% of the time, Pallas kernels for 25%

profile of v10, /device:TPU:0, one launch (start us, length us, event | category | flops | bytes accessed | tf_op | source)
XLA Modules:
  0.0 457.5 jit_solution(10372722146344402464)
XLA Ops:
  6.5 5.0 %collective-permute-start = (bf16[128,2048]{1,0:T(8,128)(2,1)}, bf16[128,2048]{1,0:T(8,128)(2,1)S(1)}, u32[]{:S(2)}, u32[]{:S(2)}) collective-permute-start(bf16[128,2048]{1,0:T(8,128)(2,1)} %param.13), channel_id=1, source_target_pairs={{0,1},{1,2},{2,3},{4,5},{5,6},{6,7},{8,9},{9,10},{10,11},{12,13},{... | collective-permute-start | bytes 1572872 | tf_op jit(solution)/shard_map/ppermute | solution.py:333
  11.5 1.3 collective-permute-start.1
  12.8 5.6 %collective-permute-start.2 = (bf16[128,2048]{1,0:T(8,128)(2,1)}, bf16[128,2048]{1,0:T(8,128)(2,1)S(1)}, u32[]{:S(2)}, u32[]{:S(2)}) collective-permute-start(bf16[128,2048]{1,0:T(8,128)(2,1)} %param.13), channel_id=1, source_target_pairs={{0,2},{3,1},{4,6},{7,5},{8,10},{11,9},{12,14},{15,13},{16,18},{19,... | collective-permute-start | bytes 1572872 | tf_op jit(solution)/shard_map/ppermute | solution.py:335
  18.4 5.6 %factor_rows.3 = (bf16[128,256]{1,0:T(8,128)(2,1)}, f32[256,256]{1,0:T(8,128)}, f32[8,256]{1,0:T(8,128)}) custom-call(bf16[256,384]{1,0:T(8,128)(2,1)} %refs_0_.4), custom_call_target="tpu_custom_call" | custom-call | tf_op jit(solution)/shard_map/factor_rows/pallas_call | solution.py:113
  23.9 14.6 %half_transform.3 = bf16[16,4,128,256]{3,2,1,0:T(8,128)(2,1)} custom-call(s32[4,8]{1,0:T(4,128)} %bitcast.15, s32[8]{0:T(128)} %count_ref.5, bf16[128,256]{1,0:T(8,128)(2,1)} %get-tuple-element.63.basis_ref, bf16[8,4,16,128,128]{4,3,2,1,0:T(8,128)(2,1)} %refs_1_.5, bf16[8,4,16,128,128]{4,3,2,1,0:T(8,128)(2,1)} %refs_1_.5, ...), custom_call_target="tpu_custom_call" | custom-call | flops 2147483648 | bytes 20971520 | tf_op jit(solution)/shard_map/half_transform/pallas_call | solution.py:188
  38.5 0.0 collective-permute-done
  38.5 0.0 collective-permute-done.1
  38.5 0.0 collective-permute-done.2
  38.5 4.6 %all-to-all-start.1 = ((bf16[16,4,128,256]{3,2,1,0:T(8,128)(2,1)}), bf16[16,4,128,256]{3,2,1,0:T(8,128)(2,1)}, u32[]{:S(2)}, u32[]{:S(2)}) async-start(bf16[16,4,128,256]{3,2,1,0:T(8,128)(2,1)} %half_transform.3), calls=%async_computation.1 | async-start | bytes 8388608 | tf_op jit(solution)/shard_map/all_to_all | solution.py:388
  43.2 0.1 select_bitcast_fusion
  43.2 1.1 pad_maximum_fusion.1
  44.3 1.3 collective-permute-start.3
  45.6 10.8 %factor_rows.4 = (bf16[320,256]{1,0:T(8,128)(2,1)}, f32[256,256]{1,0:T(8,128)}, f32[8,256]{1,0:T(8,128)}) custom-call(f32[256,256]{1,0:T(8,128)} %get-tuple-element.66.refs_0_, f32[8,256]{1,0:T(8,128)} %get-tuple-element.67.refs_1_), custom_call_target="tpu_custom_call" | custom-call | tf_op jit(solution)/shard_map/factor_rows/pallas_call | solution.py:113
  56.4 0.0 copy-start
  56.4 25.0 %half_transform.4 = bf16[16,10,128,256]{3,2,1,0:T(8,128)(2,1)} custom-call(s32[4,8]{1,0:T(4,128)} %bitcast.16, s32[8]{0:T(128)} %count_ref.5, bf16[320,256]{1,0:T(8,128)(2,1)} %get-tuple-element.68.basis_ref, bf16[8,4,16,128,128]{4,3,2,1,0:T(8,128)(2,1)} %refs_1_.5, bf16[8,4,16,128,128]{4,3,2,1,0:T(8,128)(2,1)} %refs_1_.5, ...), custom_call_target="tpu_custom_call" | custom-call | flops 5368709120 | bytes 27262976 | tf_op jit(solution)/shard_map/half_transform/pallas_call | solution.py:188
  81.4 49.1 %collective-permute-done.3 = bf16[2,128,2048]{2,1,0:T(8,128)(2,1)S(1)} collective-permute-done((bf16[2,128,2048]{2,1,0:T(8,128)(2,1)}, bf16[2,128,2048]{2,1,0:T(8,128)(2,1)S(1)}, u32[]{:S(2)}, u32[]{:S(2)}) %collective-permute-start.3) | collective-permute-done | bytes 1048608 | tf_op jit(solution)/shard_map/ppermute | solution.py:342
  130.5 0.0 copy-done
  130.5 2.6 conditional.1
  130.5 0.8 copy.6
  131.3 0.8 copy.7
  132.1 1.0 slice_bitcast_fusion
  133.1 3.1 pad_maximum_fusion
  136.2 1.4 all-to-all-done.1.half_ref
  137.6 8.0 %all-to-all-start = ((bf16[16,10,128,256]{3,2,1,0:T(8,128)(2,1)}), bf16[16,10,128,256]{3,2,1,0:T(8,128)(2,1)}, u32[]{:S(2)}, u32[]{:S(2)}) async-start(bf16[16,10,128,256]{3,2,1,0:T(8,128)(2,1)} %half_transform.4), calls=%async_computation | async-start | bytes 20971520 | tf_op jit(solution)/shard_map/all_to_all | solution.py:388
  145.6 0.0 all-gather.2.cloned.1.call-start
  145.7 0.7 all-gather.2.cloned.1.call-update
  146.3 3.5 factor_rows.5
  149.8 10.3 %half_transform.5 = bf16[16,2,128,256]{3,2,1,0:T(8,128)(2,1)} custom-call(s32[4,8]{1,0:T(4,128)} %bitcast.17, s32[8]{0:T(128)} %count_ref.5, bf16[64,256]{1,0:T(8,128)(2,1)} %get-tuple-element.80.basis_ref, bf16[8,4,16,128,128]{4,3,2,1,0:T(8,128)(2,1)} %refs_1_.5, bf16[8,4,16,128,128]{4,3,2,1,0:T(8,128)(2,1)} %refs_1_.5), custom_call_target="tpu_custom_call" | custom-call | flops 1073741824 | bytes 18874368 | tf_op jit(solution)/shard_map/half_transform/pallas_call | solution.py:188
  160.1 140.6 %all-gather.2.cloned.1.call-done.factor_ref = bf16[2048,2048]{1,0:T(8,128)(2,1)} async-done(((bf16[512,2048]{1,0:T(8,128)(2,1)}), bf16[2048,2048]{1,0:T(8,128)(2,1)}) %all-gather.2.cloned.1.call-update) | async-done | bytes 8388624 | tf_op jit(solution)/shard_map/all_gather | solution.py:382
  300.8 0.7 broadcast_in_dim.3.before_ref
  301.5 13.4 %fit_exchange.3.before_ref = f32[256,256]{1,0:T(8,128)} custom-call(f32[256,256]{1,0:T(8,128)} %broadcast_in_dim.3.before_ref, bf16[2048,2048]{1,0:T(8,128)(2,1)} %all-gather.2.cloned.1.call-done.factor_ref, bf16[16,4,128,256]{3,2,1,0:T(8,128)(2,1)} %all-to-all-done.1.half_ref), custom_call_target="tpu_custom_call" | custom-call | flops 5905580032 | bytes 12582912 | tf_op jit(solution)/shard_map/fit_exchange/pallas_call | solution.py:304
  314.9 60.0 %all-to-all-done.half_ref = bf16[16,10,128,256]{3,2,1,0:T(8,128)(2,1)} async-done(((bf16[16,10,128,256]{3,2,1,0:T(8,128)(2,1)}), bf16[16,10,128,256]{3,2,1,0:T(8,128)(2,1)}, u32[]{:S(2)}, u32[]{:S(2)}) %all-to-all-start) | async-done | bytes 10485792 | tf_op jit(solution)/shard_map/all_to_all | solution.py:388
  374.9 4.6 %all-to-all-start.2 = ((bf16[16,2,128,256]{3,2,1,0:T(8,128)(2,1)}), bf16[16,2,128,256]{3,2,1,0:T(8,128)(2,1)}, u32[]{:S(2)}, u32[]{:S(2)}) async-start(bf16[16,2,128,256]{3,2,1,0:T(8,128)(2,1)} %half_transform.5), calls=%async_computation.2 | async-start | bytes 4194304 | tf_op jit(solution)/shard_map/all_to_all | solution.py:388
  379.5 30.6 %fit_exchange.4.before_ref = f32[256,256]{1,0:T(8,128)} custom-call(f32[256,256]{1,0:T(8,128)} %fit_exchange.3.before_ref, bf16[2048,2048]{1,0:T(8,128)(2,1)} %all-gather.2.cloned.1.call-done.factor_ref, bf16[16,10,128,256]{3,2,1,0:T(8,128)(2,1)} %all-to-all-done.half_ref), custom_call_target="tpu_custom_call" | custom-call | flops 14763950080 | bytes 18874368 | tf_op jit(solution)/shard_map/fit_exchange/pallas_call | solution.py:304
  410.2 18.6 %all-to-all-done.2.half_ref = bf16[16,2,128,256]{3,2,1,0:T(8,128)(2,1)} async-done(((bf16[16,2,128,256]{3,2,1,0:T(8,128)(2,1)}), bf16[16,2,128,256]{3,2,1,0:T(8,128)(2,1)}, u32[]{:S(2)}, u32[]{:S(2)}) %all-to-all-start.2) | async-done | bytes 2097184 | tf_op jit(solution)/shard_map/all_to_all | solution.py:388
  428.8 7.7 %fit_exchange.5 = f32[256,256]{1,0:T(8,128)} custom-call(f32[256,256]{1,0:T(8,128)} %fit_exchange.4.before_ref, bf16[2048,2048]{1,0:T(8,128)(2,1)} %all-gather.2.cloned.1.call-done.factor_ref, bf16[16,2,128,256]{3,2,1,0:T(8,128)(2,1)} %all-to-all-done.2.half_ref), custom_call_target="tpu_custom_call" | custom-call | flops 2952790016 | bytes 10485760 | tf_op jit(solution)/shard_map/fit_exchange/pallas_call | solution.py:304
  436.5 13.6 %all_to_all.20 = f32[16,16,256]{2,1,0:T(8,128)S(1)} all-to-all(f32[16,16,256]{2,1,0:T(8,128)} %bitcast.14), channel_id=1, replica_groups=mesh['grp'=2,'aux'=4,'occ'=4] {'aux','occ'}, dimensions={0} | all-to-all | bytes 524288 | tf_op jit(solution)/shard_map/all_to_all | solution.py:393
  450.1 0.6 reduce_sum.9
Async XLA Ops:
  6.5 32.0 %collective-permute-start = (bf16[128,2048]{1,0:T(8,128)(2,1)}, bf16[128,2048]{1,0:T(8,128)(2,1)S(1)}, u32[]{:S(2)}, u32[]{:S(2)}) collective-permute-start(bf16[128,2048]{1,0:T(8,128)(2,1)} %param.13), channel_id=1, source_target_pairs={{0,1},{1,2},{2,3},{4,5},{5,6},{6,7},{8,9},{9,10},{10,11},{12,13},{... | collective-permute-start | bytes 1572872 | tf_op jit(solution)/shard_map/ppermute | solution.py:333
  11.5 27.0 %collective-permute-start.1 = (bf16[128,2048]{1,0:T(8,128)(2,1)}, bf16[128,2048]{1,0:T(8,128)(2,1)S(1)}, u32[]{:S(2)}, u32[]{:S(2)}) collective-permute-start(bf16[128,2048]{1,0:T(8,128)(2,1)} %param.13), channel_id=1, source_target_pairs={{3,2},{2,1},{1,0},{7,6},{6,5},{5,4},{11,10},{10,9},{9,8},{15,14},{... | collective-permute-start | bytes 1572872 | tf_op jit(solution)/shard_map/ppermute | solution.py:334
  12.8 25.7 %collective-permute-start.2 = (bf16[128,2048]{1,0:T(8,128)(2,1)}, bf16[128,2048]{1,0:T(8,128)(2,1)S(1)}, u32[]{:S(2)}, u32[]{:S(2)}) collective-permute-start(bf16[128,2048]{1,0:T(8,128)(2,1)} %param.13), channel_id=1, source_target_pairs={{0,2},{3,1},{4,6},{7,5},{8,10},{11,9},{12,14},{15,13},{16,18},{19,... | collective-permute-start | bytes 1572872 | tf_op jit(solution)/shard_map/ppermute | solution.py:335
  38.5 99.0 %all-to-all-start.1 = ((bf16[16,4,128,256]{3,2,1,0:T(8,128)(2,1)}), bf16[16,4,128,256]{3,2,1,0:T(8,128)(2,1)}, u32[]{:S(2)}, u32[]{:S(2)}) async-start(bf16[16,4,128,256]{3,2,1,0:T(8,128)(2,1)} %half_transform.3), calls=%async_computation.1 | async-start | bytes 8388608 | tf_op jit(solution)/shard_map/all_to_all | solution.py:388
  44.3 86.2 %collective-permute-start.3 = (bf16[2,128,2048]{2,1,0:T(8,128)(2,1)}, bf16[2,128,2048]{2,1,0:T(8,128)(2,1)S(1)}, u32[]{:S(2)}, u32[]{:S(2)}) collective-permute-start(bf16[2,128,2048]{2,1,0:T(8,128)(2,1)} %pad_maximum_fusion.1), channel_id=1, source_target_pairs={{1,0},{2,3},{5,4},{6,7},{9,8},{10,11},{13,12},{14,15},{17,16},{18,... | collective-permute-start | bytes 3145736 | tf_op jit(solution)/shard_map/ppermute | solution.py:342
  56.4 74.1 %copy-start = (bf16[128,2048]{1,0:T(8,128)(2,1)S(1)}, bf16[128,2048]{1,0:T(8,128)(2,1)}, u32[]{:S(2)}) copy-start(bf16[128,2048]{1,0:T(8,128)(2,1)} %param.13) | copy-start | bytes 1572868
  137.6 237.3 %all-to-all-start = ((bf16[16,10,128,256]{3,2,1,0:T(8,128)(2,1)}), bf16[16,10,128,256]{3,2,1,0:T(8,128)(2,1)}, u32[]{:S(2)}, u32[]{:S(2)}) async-start(bf16[16,10,128,256]{3,2,1,0:T(8,128)(2,1)} %half_transform.4), calls=%async_computation | async-start | bytes 20971520 | tf_op jit(solution)/shard_map/all_to_all | solution.py:388
  145.6 155.1 %all-gather.2.cloned.1.call-start = ((), (), s32[]{:S(2)}) async-start(), calls=%async_computation.4 | async-start | bytes 10485760 | tf_op jit(solution)/shard_map/all_gather | solution.py:382
  374.9 53.9 %all-to-all-start.2 = ((bf16[16,2,128,256]{3,2,1,0:T(8,128)(2,1)}), bf16[16,2,128,256]{3,2,1,0:T(8,128)(2,1)}, u32[]{:S(2)}, u32[]{:S(2)}) async-start(bf16[16,2,128,256]{3,2,1,0:T(8,128)(2,1)} %half_transform.5), calls=%async_computation.2 | async-start | bytes 4194304 | tf_op jit(solution)/shard_map/all_to_all | solution.py:388
Sparse Core Ops, SparseCore 0:
  148.0 152.7 all-gather.1

commit v11 on v10

--- a/solution.py
+++ b/solution.py
@@ -124,44 +124,38 @@
 
 
 def half_kernel(low_block, list_ref, count_ref, basis_ref, *refs):
-    tile_refs, (out_ref, rows_ref, window_ref) = refs[:-3], refs[-3:]
+    tile_refs, (out_ref, rows_ref) = refs[:-2], refs[-2:]
     block = pl.program_id(0)
     aux_width, size_block = tile_refs[0].shape[2:4]
     vectors = basis_ref.shape[0] // 2
     side = basis_ref.shape[1] // size_block
-    pairs = [(m, n) for m in range(side) for n in range(low_block, side)]
-    for (m, n), tile_ref in zip(pairs, tile_refs):
-        used = jnp.bool_(False)
-        for slot in range(list_ref.shape[0]):
-            hit = jnp.logical_and(list_ref[slot, block] == m * side + n, slot < count_ref[block])
-            used = jnp.logical_or(used, hit)
-        tile = tile_ref[0, 0]
-        column = (n - low_block) * size_block
-        window_ref[:, m * size_block : (m + 1) * size_block, column : column + size_block] = (
-            jnp.where(used, tile, jnp.zeros_like(tile))
-        )
-
-    together = aux_width if vectors <= 64 else 4
-
-    def some(group, carry):
-        low = group * together
-        window = window_ref[pl.ds(low, together)]
+    columns = range(low_block, side)
+    for m in range(side):
+        basis = []
+        for n in columns:
+            used = jnp.bool_(False)
+            for slot in range(list_ref.shape[0]):
+                hit = jnp.logical_and(
+                    list_ref[slot, block] == m * side + n, slot < count_ref[block]
+                )
+                used = jnp.logical_or(used, hit)
+            part = basis_ref[:, n * size_block : (n + 1) * size_block]
+            basis.append(jnp.where(used, part, jnp.zeros_like(part)))
+        tiles = [
+            tile_refs[m * len(columns) + i][0, 0].reshape(aux_width * size_block, size_block)
+            for i in range(len(columns))
+        ]
         product = lax.dot_general(
-            basis_ref[:, low_block * size_block :],
-            window.reshape(together * window.shape[1], window.shape[2]),
+            jnp.concatenate(basis, axis=1),
+            jnp.concatenate(tiles, axis=1),
             (((1,), (1,)), ((), ())),
             preferred_element_type=jnp.float32,
         )
         product = product[:vectors] + product[vectors:]
-        for p in range(together):
-            for m in range(side):
-                column = (p * side + m) * size_block
-                rows_ref[m, pl.ds(low + p, vectors, stride=aux_width), :] = product[
-                    :, column : column + size_block
-                ]
-        return carry
-
-    lax.fori_loop(0, aux_width // together, some, 0)
+        for p in range(aux_width):
+            rows_ref[m, pl.ds(p, vectors, stride=aux_width), :] = product[
+                :, p * size_block : (p + 1) * size_block
+            ]
     for m in range(side):
         out_ref[..., m * size_block : (m + 1) * size_block] = (
             rows_ref[m].astype(jnp.bfloat16).reshape(out_ref.shape[:-1] + (size_block,))
@@ -200,10 +194,6 @@
             scratch_shapes=[
                 pltpu.VMEM(
                     (basis_total // size_block, vectors * aux_width, size_block), jnp.float32
-                ),
-                pltpu.VMEM(
-                    (aux_width, basis_total, basis_total - low_block * size_block),
-                    jnp.bfloat16,
                 ),
             ],
         ),
@@ -330,20 +320,20 @@
 
 
 def line_near(block):
+    far = lax.ppermute(block, "occ", [(0, 2), (3, 1)])
     up = lax.ppermute(block, "occ", [(0, 1), (1, 2), (2, 3)])
     down = lax.ppermute(block, "occ", [(3, 2), (2, 1), (1, 0)])
-    far = lax.ppermute(block, "occ", [(0, 2), (3, 1)])
     return up, down, far
 
 
-def line_ends(block, up, down, far):
-    me = lax.axis_index("occ")
-    left = me < 2
-    later = lax.ppermute(
-        jnp.stack([jnp.where(left, down, up), far]), "occ", [(1, 0), (2, 3)]
-    )
+def line_forward(up, down, far):
+    nearer = jnp.where(lax.axis_index("occ") < 2, down, up)
+    return lax.ppermute(jnp.stack([nearer, far]), "occ", [(1, 0), (2, 3)])
+
+
+def line_order(block, up, down, far, later):
     order = lax.switch(
-        me,
+        lax.axis_index("occ"),
         [
             lambda: (block, down, later[0], later[1]),
             lambda: (up, block, down, far),
@@ -376,10 +366,14 @@
         half = half_transform(integrals, pair_list, pair_count, rows, start, devices)
         if chunk == 0:
             half, state, near = lax.optimization_barrier((half, state, near))
-            line = line_ends(metric, *near) if in_line else metric
+            later = line_forward(*near) if in_line else ()
         elif chunk == 1:
-            half, state, line = lax.optimization_barrier((half, state, line))
-            factor = lax.all_gather(line, "aux" if in_line else BOTH, axis=0, tiled=True)
+            half, state, later = lax.optimization_barrier((half, state, later))
+            if in_line:
+                line = line_order(metric, *near, later)
+                factor = lax.all_gather(line, "aux", axis=0, tiled=True)
+            else:
+                factor = lax.all_gather(metric, BOTH, axis=0, tiled=True)
         else:
             total = fit_exchange(factor, arrived[chunk - 2], total)
             half, state, arrived[chunk - 1], total = lax.optimization_barrier(

time: 459 us -> 456 us (level)
  Pallas kernels: 122 us -> 112 us
  waiting for transfers between devices: 270 us -> 280 us
    pallas_call x3, Pallas kernels: 49.9 us -> 40.1 us  [half_transform(): pl.pallas_call(functools.partial(half_kernel, low_block), out_shape=jax.S...]
    ppermute x1, waiting for transfers between devices: 49.1 us -> 58.4 us  [line_forward(): return lax.ppermute(jnp.stack([nearer, far]), 'occ', [(1, 0), (2, 3)])]
    all_to_all x3, waiting for transfers between devices: 79.9 us -> 85.7 us  [per_device(): lax.all_to_all(half, BOTH, split_axis=0, concat_axis=0, tiled=True)]
    all_gather x1, waiting for transfers between devices: 141 us -> 136 us  [per_device(): factor = lax.all_gather(line, 'aux', axis=0, tiled=True)]
  transfers between devices with their start and end apart: 8 -> 8, of which waited for: 5 -> 5; matrix products, arithmetic and copies ran while one was open for 2% -> 1% of each run, Pallas kernels for 25% -> 23%
where the time goes in v11:
time: 456 us; the launch traced here: 454 us
  waiting for transfers between devices  280 us (61%)
  Pallas kernels  112 us (25%)
  starting transfers between devices  28.4 us (6%)
  blocking collectives  13.6 us (3%)
  between operations  13.5 us (3%)
    all_gather x1, waiting for transfers between devices, per_device(): factor = lax.all_gather(line, 'aux', axis=0, tiled=True)  136 us
    all_to_all x3, waiting for transfers between devices, per_device(): lax.all_to_all(half, BOTH, split_axis=0, concat_axis=0, tiled=True)  85.7 us
    ppermute x1, waiting for transfers between devices, line_forward(): return lax.ppermute(jnp.stack([nearer, far]), 'occ', [(1, 0), (2, 3)])  58.4 us
    pallas_call x3, Pallas kernels, fit_exchange(): pl.pallas_call(functools.partial(fit_kernel, aux_total // 8), out_shape=j...  51.8 us
    pallas_call x3, Pallas kernels, half_transform(): pl.pallas_call(functools.partial(half_kernel, low_block), out_shape=jax.S...  40.1 us
    pallas_call x3, Pallas kernels, factor_rows(): pl.pallas_call(functools.partial(factor_kernel, start), out_shape=(jax.Sh...  19.8 us
    all_to_all x3, starting transfers between devices, per_device(): lax.all_to_all(half, BOTH, split_axis=0, concat_axis=0, tiled=True)  15.2 us
    all_to_all x1, blocking collectives, per_device(): lax.all_to_all(shares, BOTH, split_axis=0, concat_axis=0, tiled=True)  13.6 us
  transfers between devices with their start and end apart: 8, of which 5 were waited for; matrix products, arithmetic and copies ran while one was open for 1% of the time, Pallas kernels for 23%

profile of v11, /device:TPU:0, one launch (start us, length us, event | category | flops | bytes accessed | tf_op | source)
XLA Modules:
  0.0 454.3 jit_solution(11009898835270904423)
XLA Ops:
  6.5 5.0 %collective-permute-start = (bf16[128,2048]{1,0:T(8,128)(2,1)}, bf16[128,2048]{1,0:T(8,128)(2,1)S(1)}, u32[]{:S(2)}, u32[]{:S(2)}) collective-permute-start(bf16[128,2048]{1,0:T(8,128)(2,1)} %param.13), channel_id=1, source_target_pairs={{0,1},{1,2},{2,3},{4,5},{5,6},{6,7},{8,9},{9,10},{10,11},{12,13},{... | collective-permute-start | bytes 1572872 | tf_op jit(solution)/shard_map/ppermute | solution.py:324
  11.5 1.3 collective-permute-start.1
  12.8 5.6 %collective-permute-start.2 = (bf16[128,2048]{1,0:T(8,128)(2,1)}, bf16[128,2048]{1,0:T(8,128)(2,1)S(1)}, u32[]{:S(2)}, u32[]{:S(2)}) collective-permute-start(bf16[128,2048]{1,0:T(8,128)(2,1)} %param.13), channel_id=1, source_target_pairs={{0,2},{3,1},{4,6},{7,5},{8,10},{11,9},{12,14},{15,13},{16,18},{19,... | collective-permute-start | bytes 1572872 | tf_op jit(solution)/shard_map/ppermute | solution.py:323
  18.4 5.6 %factor_rows.3 = (bf16[128,256]{1,0:T(8,128)(2,1)}, f32[256,256]{1,0:T(8,128)}, f32[8,256]{1,0:T(8,128)}) custom-call(bf16[256,384]{1,0:T(8,128)(2,1)} %refs_0_.4), custom_call_target="tpu_custom_call" | custom-call | tf_op jit(solution)/shard_map/factor_rows/pallas_call | solution.py:113
  23.9 13.4 %half_transform.3 = bf16[16,4,128,256]{3,2,1,0:T(8,128)(2,1)} custom-call(s32[4,8]{1,0:T(4,128)} %bitcast.15, s32[8]{0:T(128)} %count_ref.5, bf16[128,256]{1,0:T(8,128)(2,1)} %get-tuple-element.63.basis_ref, bf16[8,4,16,128,128]{4,3,2,1,0:T(8,128)(2,1)} %refs_1_.5, bf16[8,4,16,128,128]{4,3,2,1,0:T(8,128)(2,1)} %refs_1_.5, ...), custom_call_target="tpu_custom_call" | custom-call | flops 2147483648 | bytes 20971520 | tf_op jit(solution)/shard_map/half_transform/pallas_call | solution.py:182
  37.4 0.0 collective-permute-done
  37.4 0.0 collective-permute-done.1
  37.4 0.0 collective-permute-done.2
  37.4 5.8 %all-to-all-start.1 = ((bf16[16,4,128,256]{3,2,1,0:T(8,128)(2,1)}), bf16[16,4,128,256]{3,2,1,0:T(8,128)(2,1)}, u32[]{:S(2)}, u32[]{:S(2)}) async-start(bf16[16,4,128,256]{3,2,1,0:T(8,128)(2,1)} %half_transform.3), calls=%async_computation.1 | async-start | bytes 8388608 | tf_op jit(solution)/shard_map/all_to_all | solution.py:382
  43.2 0.1 select_bitcast_fusion
  43.2 0.1 pad_maximum_fusion.1
  43.3 1.3 collective-permute-start.3
  44.6 10.8 %factor_rows.4 = (bf16[320,256]{1,0:T(8,128)(2,1)}, f32[256,256]{1,0:T(8,128)}, f32[8,256]{1,0:T(8,128)}) custom-call(f32[256,256]{1,0:T(8,128)} %get-tuple-element.66.refs_0_, f32[8,256]{1,0:T(8,128)} %get-tuple-element.67.refs_1_), custom_call_target="tpu_custom_call" | custom-call | tf_op jit(solution)/shard_map/factor_rows/pallas_call | solution.py:113
  55.4 16.7 %half_transform.4 = bf16[16,10,128,256]{3,2,1,0:T(8,128)(2,1)} custom-call(s32[4,8]{1,0:T(4,128)} %bitcast.16, s32[8]{0:T(128)} %count_ref.5, bf16[320,256]{1,0:T(8,128)(2,1)} %get-tuple-element.68.basis_ref, bf16[8,4,16,128,128]{4,3,2,1,0:T(8,128)(2,1)} %refs_1_.5, bf16[8,4,16,128,128]{4,3,2,1,0:T(8,128)(2,1)} %refs_1_.5, ...), custom_call_target="tpu_custom_call" | custom-call | flops 5368709120 | bytes 27262976 | tf_op jit(solution)/shard_map/half_transform/pallas_call | solution.py:182
  72.1 58.4 %collective-permute-done.3 = bf16[2,128,2048]{2,1,0:T(8,128)(2,1)S(1)} collective-permute-done((bf16[2,128,2048]{2,1,0:T(8,128)(2,1)S(1)}, bf16[2,128,2048]{2,1,0:T(8,128)(2,1)S(1)}, u32[]{:S(2)}, u32[]{:S(2)}) %collective-permute-start.3) | collective-permute-done | bytes 1048608 | tf_op jit(solution)/shard_map/ppermute | solution.py:331
  130.5 0.0 copy-start
  130.5 7.1 %all-to-all-done.1.half_ref = bf16[16,4,128,256]{3,2,1,0:T(8,128)(2,1)} async-done(((bf16[16,4,128,256]{3,2,1,0:T(8,128)(2,1)}), bf16[16,4,128,256]{3,2,1,0:T(8,128)(2,1)}, u32[]{:S(2)}, u32[]{:S(2)}) %all-to-all-start.1) | async-done | bytes 4194336 | tf_op jit(solution)/shard_map/all_to_all | solution.py:382
  137.6 4.9 %all-to-all-start = ((bf16[16,10,128,256]{3,2,1,0:T(8,128)(2,1)}), bf16[16,10,128,256]{3,2,1,0:T(8,128)(2,1)}, u32[]{:S(2)}, u32[]{:S(2)}) async-start(bf16[16,10,128,256]{3,2,1,0:T(8,128)(2,1)} %half_transform.4), calls=%async_computation | async-start | bytes 20971520 | tf_op jit(solution)/shard_map/all_to_all | solution.py:382
  142.4 0.0 all-gather.2.cloned.1.call-start
  142.5 0.0 copy-done
  142.5 2.7 conditional.1
  142.5 0.8 copy.6
  143.3 0.8 copy.7
  144.1 1.1 slice_bitcast_fusion
  145.2 3.1 pad_maximum_fusion
  148.2 0.0 all-gather.2.cloned.1.call-update
  148.3 3.5 factor_rows.5
  151.7 9.9 %half_transform.5 = bf16[16,2,128,256]{3,2,1,0:T(8,128)(2,1)} custom-call(s32[4,8]{1,0:T(4,128)} %bitcast.17, s32[8]{0:T(128)} %count_ref.5, bf16[64,256]{1,0:T(8,128)(2,1)} %get-tuple-element.76.basis_ref, bf16[8,4,16,128,128]{4,3,2,1,0:T(8,128)(2,1)} %refs_1_.5, bf16[8,4,16,128,128]{4,3,2,1,0:T(8,128)(2,1)} %refs_1_.5), custom_call_target="tpu_custom_call" | custom-call | flops 1073741824 | bytes 18874368 | tf_op jit(solution)/shard_map/half_transform/pallas_call | solution.py:182
  161.7 135.9 %all-gather.2.cloned.1.call-done.factor_ref = bf16[2048,2048]{1,0:T(8,128)(2,1)} async-done(((bf16[512,2048]{1,0:T(8,128)(2,1)}), bf16[2048,2048]{1,0:T(8,128)(2,1)}) %all-gather.2.cloned.1.call-update) | async-done | bytes 8388624 | tf_op jit(solution)/shard_map/all_gather | solution.py:374
  297.5 0.7 broadcast_in_dim.3.before_ref
  298.2 13.4 %fit_exchange.3.before_ref = f32[256,256]{1,0:T(8,128)} custom-call(f32[256,256]{1,0:T(8,128)} %broadcast_in_dim.3.before_ref, bf16[2048,2048]{1,0:T(8,128)(2,1)} %all-gather.2.cloned.1.call-done.factor_ref, bf16[16,4,128,256]{3,2,1,0:T(8,128)(2,1)} %all-to-all-done.1.half_ref), custom_call_target="tpu_custom_call" | custom-call | flops 5905580032 | bytes 12582912 | tf_op jit(solution)/shard_map/fit_exchange/pallas_call | solution.py:294
  311.7 60.0 %all-to-all-done.half_ref = bf16[16,10,128,256]{3,2,1,0:T(8,128)(2,1)} async-done(((bf16[16,10,128,256]{3,2,1,0:T(8,128)(2,1)}), bf16[16,10,128,256]{3,2,1,0:T(8,128)(2,1)}, u32[]{:S(2)}, u32[]{:S(2)}) %all-to-all-start) | async-done | bytes 10485792 | tf_op jit(solution)/shard_map/all_to_all | solution.py:382
  371.7 4.6 %all-to-all-start.2 = ((bf16[16,2,128,256]{3,2,1,0:T(8,128)(2,1)}), bf16[16,2,128,256]{3,2,1,0:T(8,128)(2,1)}, u32[]{:S(2)}, u32[]{:S(2)}) async-start(bf16[16,2,128,256]{3,2,1,0:T(8,128)(2,1)} %half_transform.5), calls=%async_computation.2 | async-start | bytes 4194304 | tf_op jit(solution)/shard_map/all_to_all | solution.py:382
  376.3 30.6 %fit_exchange.4.before_ref = f32[256,256]{1,0:T(8,128)} custom-call(f32[256,256]{1,0:T(8,128)} %fit_exchange.3.before_ref, bf16[2048,2048]{1,0:T(8,128)(2,1)} %all-gather.2.cloned.1.call-done.factor_ref, bf16[16,10,128,256]{3,2,1,0:T(8,128)(2,1)} %all-to-all-done.half_ref), custom_call_target="tpu_custom_call" | custom-call | flops 14763950080 | bytes 18874368 | tf_op jit(solution)/shard_map/fit_exchange/pallas_call | solution.py:294
  406.9 18.6 %all-to-all-done.2.half_ref = bf16[16,2,128,256]{3,2,1,0:T(8,128)(2,1)} async-done(((bf16[16,2,128,256]{3,2,1,0:T(8,128)(2,1)}), bf16[16,2,128,256]{3,2,1,0:T(8,128)(2,1)}, u32[]{:S(2)}, u32[]{:S(2)}) %all-to-all-start.2) | async-done | bytes 2097184 | tf_op jit(solution)/shard_map/all_to_all | solution.py:382
  425.5 7.7 %fit_exchange.5 = f32[256,256]{1,0:T(8,128)} custom-call(f32[256,256]{1,0:T(8,128)} %fit_exchange.4.before_ref, bf16[2048,2048]{1,0:T(8,128)(2,1)} %all-gather.2.cloned.1.call-done.factor_ref, bf16[16,2,128,256]{3,2,1,0:T(8,128)(2,1)} %all-to-all-done.2.half_ref), custom_call_target="tpu_custom_call" | custom-call | flops 2952790016 | bytes 10485760 | tf_op jit(solution)/shard_map/fit_exchange/pallas_call | solution.py:294
  433.3 13.6 %all_to_all.20 = f32[16,16,256]{2,1,0:T(8,128)S(1)} all-to-all(f32[16,16,256]{2,1,0:T(8,128)} %bitcast.14), channel_id=1, replica_groups=mesh['grp'=2,'aux'=4,'occ'=4] {'aux','occ'}, dimensions={0} | all-to-all | bytes 524288 | tf_op jit(solution)/shard_map/all_to_all | solution.py:387
  446.8 0.6 reduce_sum.9
Async XLA Ops:
  6.5 30.8 %collective-permute-start = (bf16[128,2048]{1,0:T(8,128)(2,1)}, bf16[128,2048]{1,0:T(8,128)(2,1)S(1)}, u32[]{:S(2)}, u32[]{:S(2)}) collective-permute-start(bf16[128,2048]{1,0:T(8,128)(2,1)} %param.13), channel_id=1, source_target_pairs={{0,1},{1,2},{2,3},{4,5},{5,6},{6,7},{8,9},{9,10},{10,11},{12,13},{... | collective-permute-start | bytes 1572872 | tf_op jit(solution)/shard_map/ppermute | solution.py:324
  11.5 25.9 %collective-permute-start.1 = (bf16[128,2048]{1,0:T(8,128)(2,1)}, bf16[128,2048]{1,0:T(8,128)(2,1)S(1)}, u32[]{:S(2)}, u32[]{:S(2)}) collective-permute-start(bf16[128,2048]{1,0:T(8,128)(2,1)} %param.13), channel_id=1, source_target_pairs={{3,2},{2,1},{1,0},{7,6},{6,5},{5,4},{11,10},{10,9},{9,8},{15,14},{... | collective-permute-start | bytes 1572872 | tf_op jit(solution)/shard_map/ppermute | solution.py:325
  12.8 24.6 %collective-permute-start.2 = (bf16[128,2048]{1,0:T(8,128)(2,1)}, bf16[128,2048]{1,0:T(8,128)(2,1)S(1)}, u32[]{:S(2)}, u32[]{:S(2)}) collective-permute-start(bf16[128,2048]{1,0:T(8,128)(2,1)} %param.13), channel_id=1, source_target_pairs={{0,2},{3,1},{4,6},{7,5},{8,10},{11,9},{12,14},{15,13},{16,18},{19,... | collective-permute-start | bytes 1572872 | tf_op jit(solution)/shard_map/ppermute | solution.py:323
  37.4 100.2 %all-to-all-start.1 = ((bf16[16,4,128,256]{3,2,1,0:T(8,128)(2,1)}), bf16[16,4,128,256]{3,2,1,0:T(8,128)(2,1)}, u32[]{:S(2)}, u32[]{:S(2)}) async-start(bf16[16,4,128,256]{3,2,1,0:T(8,128)(2,1)} %half_transform.3), calls=%async_computation.1 | async-start | bytes 8388608 | tf_op jit(solution)/shard_map/all_to_all | solution.py:382
  43.3 87.2 %collective-permute-start.3 = (bf16[2,128,2048]{2,1,0:T(8,128)(2,1)S(1)}, bf16[2,128,2048]{2,1,0:T(8,128)(2,1)S(1)}, u32[]{:S(2)}, u32[]{:S(2)}) collective-permute-start(bf16[2,128,2048]{2,1,0:T(8,128)(2,1)S(1)} %pad_maximum_fusion.1), channel_id=1, source_target_pairs={{1,0},{2,3},{5,4},{6,7},{9,8},{10,11},{13,12},{14,15},{17,16},{18,... | collective-permute-start | bytes 3145736 | tf_op jit(solution)/shard_map/ppermute | solution.py:331
  130.5 12.0 %copy-start = (bf16[128,2048]{1,0:T(8,128)(2,1)S(1)}, bf16[128,2048]{1,0:T(8,128)(2,1)}, u32[]{:S(2)}) copy-start(bf16[128,2048]{1,0:T(8,128)(2,1)} %param.13) | copy-start | bytes 1572868
  137.6 234.1 %all-to-all-start = ((bf16[16,10,128,256]{3,2,1,0:T(8,128)(2,1)}), bf16[16,10,128,256]{3,2,1,0:T(8,128)(2,1)}, u32[]{:S(2)}, u32[]{:S(2)}) async-start(bf16[16,10,128,256]{3,2,1,0:T(8,128)(2,1)} %half_transform.4), calls=%async_computation | async-start | bytes 20971520 | tf_op jit(solution)/shard_map/all_to_all | solution.py:382
  142.4 155.1 %all-gather.2.cloned.1.call-start = ((), (), s32[]{:S(2)}) async-start(), calls=%async_computation.4 | async-start | bytes 10485760 | tf_op jit(solution)/shard_map/all_gather | solution.py:374
  371.7 53.9 %all-to-all-start.2 = ((bf16[16,2,128,256]{3,2,1,0:T(8,128)(2,1)}), bf16[16,2,128,256]{3,2,1,0:T(8,128)(2,1)}, u32[]{:S(2)}, u32[]{:S(2)}) async-start(bf16[16,2,128,256]{3,2,1,0:T(8,128)(2,1)} %half_transform.5), calls=%async_computation.2 | async-start | bytes 4194304 | tf_op jit(solution)/shard_map/all_to_all | solution.py:382
Sparse Core Ops, SparseCore 0:
  148.4 149.0 all-gather.1

commit v12 on v11

--- a/solution.py
+++ b/solution.py
@@ -265,12 +265,19 @@
         for k in range(width):
             half_copy(step, number, k).wait()
         pl.when(step == 0)(lambda number=number: factor_copy(number).wait())
-        columns = columns_ref[lax.rem(step, 2), : (number + 1) * sources]
-        fitted = jnp.dot(
-            lower_ref[low:high, :high],
-            columns.reshape(high, columns.shape[-1]),
-            preferred_element_type=jnp.float32,
-        ).astype(jnp.bfloat16)
+        fitted = None
+        middle = (number + 1) // 2
+        for first, last in ((0, middle), (middle, number + 1)):
+            if first == last:
+                continue
+            columns = columns_ref[lax.rem(step, 2), first * sources : last * sources]
+            product = jnp.dot(
+                lower_ref[low:high, first * step_rows : last * step_rows],
+                columns.reshape((last - first) * step_rows, columns.shape[-1]),
+                preferred_element_type=jnp.float32,
+            )
+            fitted = product if fitted is None else fitted + product
+        fitted = fitted.astype(jnp.bfloat16)
         for k in range(width):
             one = fitted[:, k * basis_total : (k + 1) * basis_total]
             total = total + lax.dot_general(
@@ -320,10 +327,13 @@
 
 
 def line_near(block):
-    far = lax.ppermute(block, "occ", [(0, 2), (3, 1)])
     up = lax.ppermute(block, "occ", [(0, 1), (1, 2), (2, 3)])
     down = lax.ppermute(block, "occ", [(3, 2), (2, 1), (1, 0)])
-    return up, down, far
+    return up, down
+
+
+def line_far(block):
+    return lax.ppermute(block, "occ", [(0, 2), (3, 1)])
 
 
 def line_forward(up, down, far):
@@ -363,6 +373,9 @@
     for chunk, own in enumerate(chunk_sizes(basis_total // devices)):
         width = own * devices
         rows, state = factor_rows(start, width, basis_total, state)
+        if chunk == 0 and in_line:
+            rows, block = lax.optimization_barrier((rows, metric))
+            near += (line_far(block),)
         half = half_transform(integrals, pair_list, pair_count, rows, start, devices)
         if chunk == 0:
             half, state, near = lax.optimization_barrier((half, state, near))

time: 456 us -> 456 us (level)
  Pallas kernels: 112 us -> 117 us
  waiting for transfers between devices: 280 us -> 275 us
    pallas_call x3, Pallas kernels: 51.8 us -> 57.2 us  [fit_exchange(): pl.pallas_call(functools.partial(fit_kernel, aux_total // 8), out_shape=j...]
    all_to_all x3, waiting for transfers between devices: 85.7 us -> 81 us  [per_device(): lax.all_to_all(half, BOTH, split_axis=0, concat_axis=0, tiled=True)]
  transfers between devices with their start and end apart: 8 -> 8, of which waited for: 5 -> 5; matrix products, arithmetic and copies ran while one was open for 1% -> 1% of each run, Pallas kernels for 23% -> 24%
where the time goes in v12:
time: 456 us; the launch traced here: 455 us
  waiting for transfers between devices  275 us (60%)
  Pallas kernels  117 us (26%)
  starting transfers between devices  28.4 us (6%)
  blocking collectives  13.6 us (3%)
  between operations  13.5 us (3%)
    all_gather x1, waiting for transfers between devices, per_device(): factor = lax.all_gather(line, 'aux', axis=0, tiled=True)  136 us
    all_to_all x3, waiting for transfers between devices, per_device(): lax.all_to_all(half, BOTH, split_axis=0, concat_axis=0, tiled=True)  81 us
    ppermute x1, waiting for transfers between devices, line_forward(): return lax.ppermute(jnp.stack([nearer, far]), 'occ', [(1, 0), (2, 3)])  58.4 us
    pallas_call x3, Pallas kernels, fit_exchange(): pl.pallas_call(functools.partial(fit_kernel, aux_total // 8), out_shape=j...  57.2 us
    pallas_call x3, Pallas kernels, half_transform(): pl.pallas_call(functools.partial(half_kernel, low_block), out_shape=jax.S...  40.1 us
    pallas_call x3, Pallas kernels, factor_rows(): pl.pallas_call(functools.partial(factor_kernel, start), out_shape=(jax.Sh...  19.8 us
    all_to_all x3, starting transfers between devices, per_device(): lax.all_to_all(half, BOTH, split_axis=0, concat_axis=0, tiled=True)  15.2 us
    all_to_all x1, blocking collectives, per_device(): lax.all_to_all(shares, BOTH, split_axis=0, concat_axis=0, tiled=True)  13.6 us
  transfers between devices with their start and end apart: 8, of which 5 were waited for; matrix products, arithmetic and copies ran while one was open for 1% of the time, Pallas kernels for 24%

profile of v12, /device:TPU:0, one launch (start us, length us, event | category | flops | bytes accessed | tf_op | source)
XLA Modules:
  0.0 455.0 jit_solution(9601698217642393828)
XLA Ops:
  6.5 5.0 %collective-permute-start = (bf16[128,2048]{1,0:T(8,128)(2,1)}, bf16[128,2048]{1,0:T(8,128)(2,1)S(1)}, u32[]{:S(2)}, u32[]{:S(2)}) collective-permute-start(bf16[128,2048]{1,0:T(8,128)(2,1)} %param.13), channel_id=1, source_target_pairs={{0,1},{1,2},{2,3},{4,5},{5,6},{6,7},{8,9},{9,10},{10,11},{12,13},{... | collective-permute-start | bytes 1572872 | tf_op jit(solution)/shard_map/ppermute | solution.py:330
  11.5 1.3 collective-permute-start.1
  12.8 5.5 %factor_rows.3 = (bf16[128,256]{1,0:T(8,128)(2,1)}, f32[256,256]{1,0:T(8,128)}, f32[8,256]{1,0:T(8,128)}) custom-call(bf16[256,384]{1,0:T(8,128)(2,1)} %refs_0_.4), custom_call_target="tpu_custom_call" | custom-call | tf_op jit(solution)/shard_map/factor_rows/pallas_call | solution.py:113
  18.3 5.6 %collective-permute-start.2 = (bf16[128,2048]{1,0:T(8,128)(2,1)}, bf16[128,2048]{1,0:T(8,128)(2,1)S(1)}, u32[]{:S(2)}, u32[]{:S(2)}) collective-permute-start(bf16[128,2048]{1,0:T(8,128)(2,1)} %param.13), channel_id=1, source_target_pairs={{0,2},{3,1},{4,6},{7,5},{8,10},{11,9},{12,14},{15,13},{16,18},{19,... | collective-permute-start | bytes 1572872 | tf_op jit(solution)/shard_map/ppermute | solution.py:336
  23.9 13.4 %half_transform.3 = bf16[16,4,128,256]{3,2,1,0:T(8,128)(2,1)} custom-call(s32[4,8]{1,0:T(4,128)} %bitcast.15, s32[8]{0:T(128)} %count_ref.5, bf16[128,256]{1,0:T(8,128)(2,1)} %get-tuple-element.66.basis_ref, bf16[8,4,16,128,128]{4,3,2,1,0:T(8,128)(2,1)} %refs_1_.5, bf16[8,4,16,128,128]{4,3,2,1,0:T(8,128)(2,1)} %refs_1_.5, ...), custom_call_target="tpu_custom_call" | custom-call | flops 2147483648 | bytes 20971520 | tf_op jit(solution)/shard_map/half_transform/pallas_call | solution.py:182
  37.4 0.0 collective-permute-done
  37.4 0.0 collective-permute-done.1
  37.4 0.0 collective-permute-done.2
  37.4 5.8 %all-to-all-start.1 = ((bf16[16,4,128,256]{3,2,1,0:T(8,128)(2,1)}), bf16[16,4,128,256]{3,2,1,0:T(8,128)(2,1)}, u32[]{:S(2)}, u32[]{:S(2)}) async-start(bf16[16,4,128,256]{3,2,1,0:T(8,128)(2,1)} %half_transform.3), calls=%async_computation.1 | async-start | bytes 8388608 | tf_op jit(solution)/shard_map/all_to_all | solution.py:395
  43.2 0.1 select_bitcast_fusion
  43.2 0.1 pad_maximum_fusion.1
  43.3 1.3 collective-permute-start.3
  44.6 10.8 %factor_rows.4 = (bf16[320,256]{1,0:T(8,128)(2,1)}, f32[256,256]{1,0:T(8,128)}, f32[8,256]{1,0:T(8,128)}) custom-call(f32[256,256]{1,0:T(8,128)} %get-tuple-element.70.refs_0_, f32[8,256]{1,0:T(8,128)} %get-tuple-element.71.refs_1_), custom_call_target="tpu_custom_call" | custom-call | tf_op jit(solution)/shard_map/factor_rows/pallas_call | solution.py:113
  55.4 16.7 %half_transform.4 = bf16[16,10,128,256]{3,2,1,0:T(8,128)(2,1)} custom-call(s32[4,8]{1,0:T(4,128)} %bitcast.16, s32[8]{0:T(128)} %count_ref.5, bf16[320,256]{1,0:T(8,128)(2,1)} %get-tuple-element.72.basis_ref, bf16[8,4,16,128,128]{4,3,2,1,0:T(8,128)(2,1)} %refs_1_.5, bf16[8,4,16,128,128]{4,3,2,1,0:T(8,128)(2,1)} %refs_1_.5, ...), custom_call_target="tpu_custom_call" | custom-call | flops 5368709120 | bytes 27262976 | tf_op jit(solution)/shard_map/half_transform/pallas_call | solution.py:182
  72.1 58.4 %collective-permute-done.3 = bf16[2,128,2048]{2,1,0:T(8,128)(2,1)S(1)} collective-permute-done((bf16[2,128,2048]{2,1,0:T(8,128)(2,1)S(1)}, bf16[2,128,2048]{2,1,0:T(8,128)(2,1)S(1)}, u32[]{:S(2)}, u32[]{:S(2)}) %collective-permute-start.3) | collective-permute-done | bytes 1048608 | tf_op jit(solution)/shard_map/ppermute | solution.py:341
  130.5 0.0 copy-start
  130.5 7.1 %all-to-all-done.1.half_ref = bf16[16,4,128,256]{3,2,1,0:T(8,128)(2,1)} async-done(((bf16[16,4,128,256]{3,2,1,0:T(8,128)(2,1)}), bf16[16,4,128,256]{3,2,1,0:T(8,128)(2,1)}, u32[]{:S(2)}, u32[]{:S(2)}) %all-to-all-start.1) | async-done | bytes 4194336 | tf_op jit(solution)/shard_map/all_to_all | solution.py:395
  137.6 4.9 %all-to-all-start = ((bf16[16,10,128,256]{3,2,1,0:T(8,128)(2,1)}), bf16[16,10,128,256]{3,2,1,0:T(8,128)(2,1)}, u32[]{:S(2)}, u32[]{:S(2)}) async-start(bf16[16,10,128,256]{3,2,1,0:T(8,128)(2,1)} %half_transform.4), calls=%async_computation | async-start | bytes 20971520 | tf_op jit(solution)/shard_map/all_to_all | solution.py:395
  142.4 0.0 all-gather.2.cloned.1.call-start
  142.5 0.0 copy-done
  142.5 2.7 conditional.1
  142.5 0.8 copy.6
  143.3 0.8 copy.7
  144.1 1.1 slice_bitcast_fusion
  145.2 3.1 pad_maximum_fusion
  148.2 0.0 all-gather.2.cloned.1.call-update
  148.3 3.5 factor_rows.5
  151.7 9.9 %half_transform.5 = bf16[16,2,128,256]{3,2,1,0:T(8,128)(2,1)} custom-call(s32[4,8]{1,0:T(4,128)} %bitcast.17, s32[8]{0:T(128)} %count_ref.5, bf16[64,256]{1,0:T(8,128)(2,1)} %get-tuple-element.80.basis_ref, bf16[8,4,16,128,128]{4,3,2,1,0:T(8,128)(2,1)} %refs_1_.5, bf16[8,4,16,128,128]{4,3,2,1,0:T(8,128)(2,1)} %refs_1_.5), custom_call_target="tpu_custom_call" | custom-call | flops 1073741824 | bytes 18874368 | tf_op jit(solution)/shard_map/half_transform/pallas_call | solution.py:182
  161.7 135.9 %all-gather.2.cloned.1.call-done.factor_ref = bf16[2048,2048]{1,0:T(8,128)(2,1)} async-done(((bf16[512,2048]{1,0:T(8,128)(2,1)}), bf16[2048,2048]{1,0:T(8,128)(2,1)}) %all-gather.2.cloned.1.call-update) | async-done | bytes 8388624 | tf_op jit(solution)/shard_map/all_gather | solution.py:387
  297.5 0.7 broadcast_in_dim.3.before_ref
  298.2 14.8 %fit_exchange.3.before_ref = f32[256,256]{1,0:T(8,128)} custom-call(f32[256,256]{1,0:T(8,128)} %broadcast_in_dim.3.before_ref, bf16[2048,2048]{1,0:T(8,128)(2,1)} %all-gather.2.cloned.1.call-done.factor_ref, bf16[16,4,128,256]{3,2,1,0:T(8,128)(2,1)} %all-to-all-done.1.half_ref), custom_call_target="tpu_custom_call" | custom-call | flops 5905580032 | bytes 12582912 | tf_op jit(solution)/shard_map/fit_exchange/pallas_call | solution.py:301
  313.0 58.7 %all-to-all-done.half_ref = bf16[16,10,128,256]{3,2,1,0:T(8,128)(2,1)} async-done(((bf16[16,10,128,256]{3,2,1,0:T(8,128)(2,1)}), bf16[16,10,128,256]{3,2,1,0:T(8,128)(2,1)}, u32[]{:S(2)}, u32[]{:S(2)}) %all-to-all-start) | async-done | bytes 10485792 | tf_op jit(solution)/shard_map/all_to_all | solution.py:395
  371.7 4.6 %all-to-all-start.2 = ((bf16[16,2,128,256]{3,2,1,0:T(8,128)(2,1)}), bf16[16,2,128,256]{3,2,1,0:T(8,128)(2,1)}, u32[]{:S(2)}, u32[]{:S(2)}) async-start(bf16[16,2,128,256]{3,2,1,0:T(8,128)(2,1)} %half_transform.5), calls=%async_computation.2 | async-start | bytes 4194304 | tf_op jit(solution)/shard_map/all_to_all | solution.py:395
  376.3 34.0 %fit_exchange.4.before_ref = f32[256,256]{1,0:T(8,128)} custom-call(f32[256,256]{1,0:T(8,128)} %fit_exchange.3.before_ref, bf16[2048,2048]{1,0:T(8,128)(2,1)} %all-gather.2.cloned.1.call-done.factor_ref, bf16[16,10,128,256]{3,2,1,0:T(8,128)(2,1)} %all-to-all-done.half_ref), custom_call_target="tpu_custom_call" | custom-call | flops 14763950080 | bytes 18874368 | tf_op jit(solution)/shard_map/fit_exchange/pallas_call | solution.py:301
  410.3 15.3 %all-to-all-done.2.half_ref = bf16[16,2,128,256]{3,2,1,0:T(8,128)(2,1)} async-done(((bf16[16,2,128,256]{3,2,1,0:T(8,128)(2,1)}), bf16[16,2,128,256]{3,2,1,0:T(8,128)(2,1)}, u32[]{:S(2)}, u32[]{:S(2)}) %all-to-all-start.2) | async-done | bytes 2097184 | tf_op jit(solution)/shard_map/all_to_all | solution.py:395
  425.5 8.4 %fit_exchange.5 = f32[256,256]{1,0:T(8,128)} custom-call(f32[256,256]{1,0:T(8,128)} %fit_exchange.4.before_ref, bf16[2048,2048]{1,0:T(8,128)(2,1)} %all-gather.2.cloned.1.call-done.factor_ref, bf16[16,2,128,256]{3,2,1,0:T(8,128)(2,1)} %all-to-all-done.2.half_ref), custom_call_target="tpu_custom_call" | custom-call | flops 2952790016 | bytes 10485760 | tf_op jit(solution)/shard_map/fit_exchange/pallas_call | solution.py:301
  433.9 13.6 %all_to_all.20 = f32[16,16,256]{2,1,0:T(8,128)S(1)} all-to-all(f32[16,16,256]{2,1,0:T(8,128)} %bitcast.14), channel_id=1, replica_groups=mesh['grp'=2,'aux'=4,'occ'=4] {'aux','occ'}, dimensions={0} | all-to-all | bytes 524288 | tf_op jit(solution)/shard_map/all_to_all | solution.py:400
  447.5 0.6 reduce_sum.9
Async XLA Ops:
  6.5 30.8 %collective-permute-start = (bf16[128,2048]{1,0:T(8,128)(2,1)}, bf16[128,2048]{1,0:T(8,128)(2,1)S(1)}, u32[]{:S(2)}, u32[]{:S(2)}) collective-permute-start(bf16[128,2048]{1,0:T(8,128)(2,1)} %param.13), channel_id=1, source_target_pairs={{0,1},{1,2},{2,3},{4,5},{5,6},{6,7},{8,9},{9,10},{10,11},{12,13},{... | collective-permute-start | bytes 1572872 | tf_op jit(solution)/shard_map/ppermute | solution.py:330
  11.5 25.9 %collective-permute-start.1 = (bf16[128,2048]{1,0:T(8,128)(2,1)}, bf16[128,2048]{1,0:T(8,128)(2,1)S(1)}, u32[]{:S(2)}, u32[]{:S(2)}) collective-permute-start(bf16[128,2048]{1,0:T(8,128)(2,1)} %param.13), channel_id=1, source_target_pairs={{3,2},{2,1},{1,0},{7,6},{6,5},{5,4},{11,10},{10,9},{9,8},{15,14},{... | collective-permute-start | bytes 1572872 | tf_op jit(solution)/shard_map/ppermute | solution.py:331
  18.3 19.0 %collective-permute-start.2 = (bf16[128,2048]{1,0:T(8,128)(2,1)}, bf16[128,2048]{1,0:T(8,128)(2,1)S(1)}, u32[]{:S(2)}, u32[]{:S(2)}) collective-permute-start(bf16[128,2048]{1,0:T(8,128)(2,1)} %param.13), channel_id=1, source_target_pairs={{0,2},{3,1},{4,6},{7,5},{8,10},{11,9},{12,14},{15,13},{16,18},{19,... | collective-permute-start | bytes 1572872 | tf_op jit(solution)/shard_map/ppermute | solution.py:336
  37.4 100.2 %all-to-all-start.1 = ((bf16[16,4,128,256]{3,2,1,0:T(8,128)(2,1)}), bf16[16,4,128,256]{3,2,1,0:T(8,128)(2,1)}, u32[]{:S(2)}, u32[]{:S(2)}) async-start(bf16[16,4,128,256]{3,2,1,0:T(8,128)(2,1)} %half_transform.3), calls=%async_computation.1 | async-start | bytes 8388608 | tf_op jit(solution)/shard_map/all_to_all | solution.py:395
  43.3 87.2 %collective-permute-start.3 = (bf16[2,128,2048]{2,1,0:T(8,128)(2,1)S(1)}, bf16[2,128,2048]{2,1,0:T(8,128)(2,1)S(1)}, u32[]{:S(2)}, u32[]{:S(2)}) collective-permute-start(bf16[2,128,2048]{2,1,0:T(8,128)(2,1)S(1)} %pad_maximum_fusion.1), channel_id=1, source_target_pairs={{1,0},{2,3},{5,4},{6,7},{9,8},{10,11},{13,12},{14,15},{17,16},{18,... | collective-permute-start | bytes 3145736 | tf_op jit(solution)/shard_map/ppermute | solution.py:341
  130.5 12.0 %copy-start = (bf16[128,2048]{1,0:T(8,128)(2,1)S(1)}, bf16[128,2048]{1,0:T(8,128)(2,1)}, u32[]{:S(2)}) copy-start(bf16[128,2048]{1,0:T(8,128)(2,1)} %param.13) | copy-start | bytes 1572868
  137.6 234.1 %all-to-all-start = ((bf16[16,10,128,256]{3,2,1,0:T(8,128)(2,1)}), bf16[16,10,128,256]{3,2,1,0:T(8,128)(2,1)}, u32[]{:S(2)}, u32[]{:S(2)}) async-start(bf16[16,10,128,256]{3,2,1,0:T(8,128)(2,1)} %half_transform.4), calls=%async_computation | async-start | bytes 20971520 | tf_op jit(solution)/shard_map/all_to_all | solution.py:395
  142.4 155.1 %all-gather.2.cloned.1.call-start = ((), (), s32[]{:S(2)}) async-start(), calls=%async_computation.4 | async-start | bytes 10485760 | tf_op jit(solution)/shard_map/all_gather | solution.py:387
  371.7 53.9 %all-to-all-start.2 = ((bf16[16,2,128,256]{3,2,1,0:T(8,128)(2,1)}), bf16[16,2,128,256]{3,2,1,0:T(8,128)(2,1)}, u32[]{:S(2)}, u32[]{:S(2)}) async-start(bf16[16,2,128,256]{3,2,1,0:T(8,128)(2,1)} %half_transform.5), calls=%async_computation.2 | async-start | bytes 4194304 | tf_op jit(solution)/shard_map/all_to_all | solution.py:395
Sparse Core Ops, SparseCore 0:
  148.4 149.0 all-gather.1

commit v13 on v11

--- a/solution.py
+++ b/solution.py
@@ -123,39 +123,41 @@
     return rows, (rest, diagonals)
 
 
-def half_kernel(low_block, list_ref, count_ref, basis_ref, *refs):
+def half_kernel(low_block, together, list_ref, count_ref, basis_ref, *refs):
     tile_refs, (out_ref, rows_ref) = refs[:-2], refs[-2:]
-    block = pl.program_id(0)
     aux_width, size_block = tile_refs[0].shape[2:4]
     vectors = basis_ref.shape[0] // 2
     side = basis_ref.shape[1] // size_block
     columns = range(low_block, side)
-    for m in range(side):
-        basis = []
-        for n in columns:
-            used = jnp.bool_(False)
-            for slot in range(list_ref.shape[0]):
-                hit = jnp.logical_and(
-                    list_ref[slot, block] == m * side + n, slot < count_ref[block]
-                )
-                used = jnp.logical_or(used, hit)
-            part = basis_ref[:, n * size_block : (n + 1) * size_block]
-            basis.append(jnp.where(used, part, jnp.zeros_like(part)))
-        tiles = [
-            tile_refs[m * len(columns) + i][0, 0].reshape(aux_width * size_block, size_block)
-            for i in range(len(columns))
-        ]
-        product = lax.dot_general(
-            jnp.concatenate(basis, axis=1),
-            jnp.concatenate(tiles, axis=1),
-            (((1,), (1,)), ((), ())),
-            preferred_element_type=jnp.float32,
-        )
-        product = product[:vectors] + product[vectors:]
-        for p in range(aux_width):
-            rows_ref[m, pl.ds(p, vectors, stride=aux_width), :] = product[
-                :, p * size_block : (p + 1) * size_block
+    for here in range(together):
+        block = pl.program_id(0) * together + here
+        for m in range(side):
+            basis = []
+            for n in columns:
+                used = jnp.bool_(False)
+                for slot in range(list_ref.shape[0]):
+                    hit = jnp.logical_and(
+                        list_ref[slot, block] == m * side + n, slot < count_ref[block]
+                    )
+                    used = jnp.logical_or(used, hit)
+                part = basis_ref[:, n * size_block : (n + 1) * size_block]
+                basis.append(jnp.where(used, part, jnp.zeros_like(part)))
+            low = (here * side + m) * len(columns)
+            tiles = [
+                tile_ref[0, 0].reshape(aux_width * size_block, size_block)
+                for tile_ref in tile_refs[low : low + len(columns)]
             ]
+            product = lax.dot_general(
+                jnp.concatenate(basis, axis=1),
+                jnp.concatenate(tiles, axis=1),
+                (((1,), (1,)), ((), ())),
+                preferred_element_type=jnp.float32,
+            )
+            product = product[:vectors] + product[vectors:]
+            for p in range(aux_width):
+                rows_ref[
+                    m, pl.ds(here * aux_width + p, vectors, stride=together * aux_width), :
+                ] = product[:, p * size_block : (p + 1) * size_block]
     for m in range(side):
         out_ref[..., m * size_block : (m + 1) * size_block] = (
             rows_ref[m].astype(jnp.bfloat16).reshape(out_ref.shape[:-1] + (size_block,))
@@ -169,8 +171,11 @@
     side = basis_total // size_block
     low_block = start // size_block
 
-    def tile_spec(pair):
-        def place(b, list_ref, count_ref):
+    together = 2 if blocks % 2 == 0 else 1
+
+    def tile_spec(here, pair):
+        def place(step, list_ref, count_ref):
+            b = step * together + here
             slot_of = jnp.int32(0)
             for slot in range(1, slots):
                 slot_of = jnp.where(list_ref[slot, b] == pair, slot, slot_of)
@@ -178,22 +183,28 @@
 
         return pl.BlockSpec((1, 1, aux_width, size_block, size_block), place)
 
-    tiles = [tile_spec(m * side + n) for m in range(side) for n in range(low_block, side)]
+    tiles = [
+        tile_spec(here, m * side + n)
+        for here in range(together)
+        for m in range(side)
+        for n in range(low_block, side)
+    ]
     return pl.pallas_call(
-        functools.partial(half_kernel, low_block),
+        functools.partial(half_kernel, low_block, together),
         out_shape=jax.ShapeDtypeStruct(
             (devices, own, blocks * aux_width, basis_total), jnp.bfloat16
         ),
         grid_spec=pltpu.PrefetchScalarGridSpec(
             num_scalar_prefetch=2,
-            grid=(blocks,),
+            grid=(blocks // together,),
             in_specs=[pl.BlockSpec(basis_rows.shape, lambda b, *_: (0, 0))] + tiles,
             out_specs=pl.BlockSpec(
-                (devices, own, aux_width, basis_total), lambda b, *_: (0, 0, b, 0)
+                (devices, own, together * aux_width, basis_total), lambda b, *_: (0, 0, b, 0)
             ),
             scratch_shapes=[
                 pltpu.VMEM(
-                    (basis_total // size_block, vectors * aux_width, size_block), jnp.float32
+                    (basis_total // size_block, vectors * together * aux_width, size_block),
+                    jnp.float32,
                 ),
             ],
         ),

time: 456 us -> 455 us (level)
  waiting for transfers between devices: 280 us -> 275 us
    ppermute x1, waiting for transfers between devices: 58.4 us -> 52.1 us  [line_forward(): return lax.ppermute(jnp.stack([nearer, far]), 'occ', [(1, 0), (2, 3)])]
    pallas_call x3, Pallas kernels: 40.1 us -> 44.8 us  [half_transform(): pl.pallas_call(functools.partial(half_kernel, low_block, together), out_s...]
  transfers between devices with their start and end apart: 8 -> 8, of which waited for: 5 -> 5; matrix products, arithmetic and copies ran while one was open for 1% -> 1% of each run, Pallas kernels for 23% -> 24%
where the time goes in v13:
time: 455 us; the launch traced here: 454 us
  waiting for transfers between devices  275 us (60%)
  Pallas kernels  116 us (25%)
  starting transfers between devices  28.8 us (6%)
  blocking collectives  13.6 us (3%)
  between operations  13.5 us (3%)
    all_gather x1, waiting for transfers between devices, per_device(): factor = lax.all_gather(line, 'aux', axis=0, tiled=True)  137 us
    all_to_all x3, waiting for transfers between devices, per_device(): lax.all_to_all(half, BOTH, split_axis=0, concat_axis=0, tiled=True)  85.6 us
    ppermute x1, waiting for transfers between devices, line_forward(): return lax.ppermute(jnp.stack([nearer, far]), 'occ', [(1, 0), (2, 3)])  52.1 us
    pallas_call x3, Pallas kernels, fit_exchange(): pl.pallas_call(functools.partial(fit_kernel, aux_total // 8), out_shape=j...  51.8 us
    pallas_call x3, Pallas kernels, half_transform(): pl.pallas_call(functools.partial(half_kernel, low_block, together), out_s...  44.8 us
    pallas_call x3, Pallas kernels, factor_rows(): pl.pallas_call(functools.partial(factor_kernel, start), out_shape=(jax.Sh...  19.8 us
    all_to_all x3, starting transfers between devices, per_device(): lax.all_to_all(half, BOTH, split_axis=0, concat_axis=0, tiled=True)  15.6 us
    all_to_all x1, blocking collectives, per_device(): lax.all_to_all(shares, BOTH, split_axis=0, concat_axis=0, tiled=True)  13.6 us
  transfers between devices with their start and end apart: 8, of which 5 were waited for; matrix products, arithmetic and copies ran while one was open for 1% of the time, Pallas kernels for 24%

profile of v13, /device:TPU:0, one launch (start us, length us, event | category | flops | bytes accessed | tf_op | source)
XLA Modules:
  0.0 454.3 jit_solution(13276284801656518047)
XLA Ops:
  6.5 5.0 %collective-permute-start = (bf16[128,2048]{1,0:T(8,128)(2,1)}, bf16[128,2048]{1,0:T(8,128)(2,1)S(1)}, u32[]{:S(2)}, u32[]{:S(2)}) collective-permute-start(bf16[128,2048]{1,0:T(8,128)(2,1)} %param.13), channel_id=1, source_target_pairs={{0,1},{1,2},{2,3},{4,5},{5,6},{6,7},{8,9},{9,10},{10,11},{12,13},{... | collective-permute-start | bytes 1572872 | tf_op jit(solution)/shard_map/ppermute | solution.py:335
  11.5 1.3 collective-permute-start.1
  12.8 5.6 %collective-permute-start.2 = (bf16[128,2048]{1,0:T(8,128)(2,1)}, bf16[128,2048]{1,0:T(8,128)(2,1)S(1)}, u32[]{:S(2)}, u32[]{:S(2)}) collective-permute-start(bf16[128,2048]{1,0:T(8,128)(2,1)} %param.13), channel_id=1, source_target_pairs={{0,2},{3,1},{4,6},{7,5},{8,10},{11,9},{12,14},{15,13},{16,18},{19,... | collective-permute-start | bytes 1572872 | tf_op jit(solution)/shard_map/ppermute | solution.py:334
  18.4 5.6 %factor_rows.3 = (bf16[128,256]{1,0:T(8,128)(2,1)}, f32[256,256]{1,0:T(8,128)}, f32[8,256]{1,0:T(8,128)}) custom-call(bf16[256,384]{1,0:T(8,128)(2,1)} %refs_0_.4), custom_call_target="tpu_custom_call" | custom-call | tf_op jit(solution)/shard_map/factor_rows/pallas_call | solution.py:113
  23.9 13.1 %half_transform.3 = bf16[16,4,128,256]{3,2,1,0:T(8,128)(2,1)} custom-call(s32[4,8]{1,0:T(4,128)} %bitcast.15, s32[8]{0:T(128)} %count_ref.5, bf16[128,256]{1,0:T(8,128)(2,1)} %get-tuple-element.63.basis_ref, bf16[8,4,16,128,128]{4,3,2,1,0:T(8,128)(2,1)} %refs_3_.5, bf16[8,4,16,128,128]{4,3,2,1,0:T(8,128)(2,1)} %refs_3_.5, ...), custom_call_target="tpu_custom_call" | custom-call | flops 2147483648 | bytes 20971520 | tf_op jit(solution)/shard_map/half_transform/pallas_call | solution.py:192
  37.0 0.0 collective-permute-done
  37.0 0.0 collective-permute-done.1
  37.0 0.0 collective-permute-done.2
  37.0 6.1 %all-to-all-start.1 = ((bf16[16,4,128,256]{3,2,1,0:T(8,128)(2,1)}), bf16[16,4,128,256]{3,2,1,0:T(8,128)(2,1)}, u32[]{:S(2)}, u32[]{:S(2)}) async-start(bf16[16,4,128,256]{3,2,1,0:T(8,128)(2,1)} %half_transform.3), calls=%async_computation.1 | async-start | bytes 8388608 | tf_op jit(solution)/shard_map/all_to_all | solution.py:393
  43.2 0.1 select_bitcast_fusion
  43.2 0.1 pad_maximum_fusion.1
  43.3 1.3 collective-permute-start.3
  44.6 10.8 %factor_rows.4 = (bf16[320,256]{1,0:T(8,128)(2,1)}, f32[256,256]{1,0:T(8,128)}, f32[8,256]{1,0:T(8,128)}) custom-call(f32[256,256]{1,0:T(8,128)} %get-tuple-element.66.refs_0_, f32[8,256]{1,0:T(8,128)} %get-tuple-element.67.refs_1_), custom_call_target="tpu_custom_call" | custom-call | tf_op jit(solution)/shard_map/factor_rows/pallas_call | solution.py:113
  55.4 23.0 %half_transform.4 = bf16[16,10,128,256]{3,2,1,0:T(8,128)(2,1)} custom-call(s32[4,8]{1,0:T(4,128)} %bitcast.16, s32[8]{0:T(128)} %count_ref.5, bf16[320,256]{1,0:T(8,128)(2,1)} %get-tuple-element.68.basis_ref, bf16[8,4,16,128,128]{4,3,2,1,0:T(8,128)(2,1)} %refs_3_.5, bf16[8,4,16,128,128]{4,3,2,1,0:T(8,128)(2,1)} %refs_3_.5, ...), custom_call_target="tpu_custom_call" | custom-call | flops 5368709120 | bytes 27262976 | tf_op jit(solution)/shard_map/half_transform/pallas_call | solution.py:192
  78.4 52.1 %collective-permute-done.3 = bf16[2,128,2048]{2,1,0:T(8,128)(2,1)S(1)} collective-permute-done((bf16[2,128,2048]{2,1,0:T(8,128)(2,1)S(1)}, bf16[2,128,2048]{2,1,0:T(8,128)(2,1)S(1)}, u32[]{:S(2)}, u32[]{:S(2)}) %collective-permute-start.3) | collective-permute-done | bytes 1048608 | tf_op jit(solution)/shard_map/ppermute | solution.py:342
  130.5 0.0 copy-start
  130.5 7.1 %all-to-all-done.1.half_ref = bf16[16,4,128,256]{3,2,1,0:T(8,128)(2,1)} async-done(((bf16[16,4,128,256]{3,2,1,0:T(8,128)(2,1)}), bf16[16,4,128,256]{3,2,1,0:T(8,128)(2,1)}, u32[]{:S(2)}, u32[]{:S(2)}) %all-to-all-start.1) | async-done | bytes 4194336 | tf_op jit(solution)/shard_map/all_to_all | solution.py:393
  137.6 4.9 %all-to-all-start = ((bf16[16,10,128,256]{3,2,1,0:T(8,128)(2,1)}), bf16[16,10,128,256]{3,2,1,0:T(8,128)(2,1)}, u32[]{:S(2)}, u32[]{:S(2)}) async-start(bf16[16,10,128,256]{3,2,1,0:T(8,128)(2,1)} %half_transform.4), calls=%async_computation | async-start | bytes 20971520 | tf_op jit(solution)/shard_map/all_to_all | solution.py:393
  142.4 0.0 all-gather.2.cloned.1.call-start
  142.5 0.0 copy-done
  142.5 2.7 conditional.1
  142.5 0.8 copy.6
  143.3 0.8 copy.7
  144.1 1.1 slice_bitcast_fusion
  145.2 3.1 pad_maximum_fusion
  148.2 0.0 all-gather.2.cloned.1.call-update
  148.3 3.5 factor_rows.5
  151.7 8.7 %half_transform.5 = bf16[16,2,128,256]{3,2,1,0:T(8,128)(2,1)} custom-call(s32[4,8]{1,0:T(4,128)} %bitcast.17, s32[8]{0:T(128)} %count_ref.5, bf16[64,256]{1,0:T(8,128)(2,1)} %get-tuple-element.76.basis_ref, bf16[8,4,16,128,128]{4,3,2,1,0:T(8,128)(2,1)} %refs_3_.5, bf16[8,4,16,128,128]{4,3,2,1,0:T(8,128)(2,1)} %refs_3_.5, ...), custom_call_target="tpu_custom_call" | custom-call | flops 1073741824 | bytes 18874368 | tf_op jit(solution)/shard_map/half_transform/pallas_call | solution.py:192
  160.5 137.0 %all-gather.2.cloned.1.call-done.factor_ref = bf16[2048,2048]{1,0:T(8,128)(2,1)} async-done(((bf16[512,2048]{1,0:T(8,128)(2,1)}), bf16[2048,2048]{1,0:T(8,128)(2,1)}) %all-gather.2.cloned.1.call-update) | async-done | bytes 8388624 | tf_op jit(solution)/shard_map/all_gather | solution.py:385
  297.5 0.7 broadcast_in_dim.3.before_ref
  298.2 13.4 %fit_exchange.3.before_ref = f32[256,256]{1,0:T(8,128)} custom-call(f32[256,256]{1,0:T(8,128)} %broadcast_in_dim.3.before_ref, bf16[2048,2048]{1,0:T(8,128)(2,1)} %all-gather.2.cloned.1.call-done.factor_ref, bf16[16,4,128,256]{3,2,1,0:T(8,128)(2,1)} %all-to-all-done.1.half_ref), custom_call_target="tpu_custom_call" | custom-call | flops 5905580032 | bytes 12582912 | tf_op jit(solution)/shard_map/fit_exchange/pallas_call | solution.py:305
  311.7 60.0 %all-to-all-done.half_ref = bf16[16,10,128,256]{3,2,1,0:T(8,128)(2,1)} async-done(((bf16[16,10,128,256]{3,2,1,0:T(8,128)(2,1)}), bf16[16,10,128,256]{3,2,1,0:T(8,128)(2,1)}, u32[]{:S(2)}, u32[]{:S(2)}) %all-to-all-start) | async-done | bytes 10485792 | tf_op jit(solution)/shard_map/all_to_all | solution.py:393
  371.7 4.7 %all-to-all-start.2 = ((bf16[16,2,128,256]{3,2,1,0:T(8,128)(2,1)}), bf16[16,2,128,256]{3,2,1,0:T(8,128)(2,1)}, u32[]{:S(2)}, u32[]{:S(2)}) async-start(bf16[16,2,128,256]{3,2,1,0:T(8,128)(2,1)} %half_transform.5), calls=%async_computation.2 | async-start | bytes 4194304 | tf_op jit(solution)/shard_map/all_to_all | solution.py:393
  376.3 30.6 %fit_exchange.4.before_ref = f32[256,256]{1,0:T(8,128)} custom-call(f32[256,256]{1,0:T(8,128)} %fit_exchange.3.before_ref, bf16[2048,2048]{1,0:T(8,128)(2,1)} %all-gather.2.cloned.1.call-done.factor_ref, bf16[16,10,128,256]{3,2,1,0:T(8,128)(2,1)} %all-to-all-done.half_ref), custom_call_target="tpu_custom_call" | custom-call | flops 14763950080 | bytes 18874368 | tf_op jit(solution)/shard_map/fit_exchange/pallas_call | solution.py:305
  407.0 18.6 %all-to-all-done.2.half_ref = bf16[16,2,128,256]{3,2,1,0:T(8,128)(2,1)} async-done(((bf16[16,2,128,256]{3,2,1,0:T(8,128)(2,1)}), bf16[16,2,128,256]{3,2,1,0:T(8,128)(2,1)}, u32[]{:S(2)}, u32[]{:S(2)}) %all-to-all-start.2) | async-done | bytes 2097184 | tf_op jit(solution)/shard_map/all_to_all | solution.py:393
  425.5 7.7 %fit_exchange.5 = f32[256,256]{1,0:T(8,128)} custom-call(f32[256,256]{1,0:T(8,128)} %fit_exchange.4.before_ref, bf16[2048,2048]{1,0:T(8,128)(2,1)} %all-gather.2.cloned.1.call-done.factor_ref, bf16[16,2,128,256]{3,2,1,0:T(8,128)(2,1)} %all-to-all-done.2.half_ref), custom_call_target="tpu_custom_call" | custom-call | flops 2952790016 | bytes 10485760 | tf_op jit(solution)/shard_map/fit_exchange/pallas_call | solution.py:305
  433.3 13.6 %all_to_all.20 = f32[16,16,256]{2,1,0:T(8,128)S(1)} all-to-all(f32[16,16,256]{2,1,0:T(8,128)} %bitcast.14), channel_id=1, replica_groups=mesh['grp'=2,'aux'=4,'occ'=4] {'aux','occ'}, dimensions={0} | all-to-all | bytes 524288 | tf_op jit(solution)/shard_map/all_to_all | solution.py:398
  446.8 0.6 reduce_sum.9
Async XLA Ops:
  6.5 30.5 %collective-permute-start = (bf16[128,2048]{1,0:T(8,128)(2,1)}, bf16[128,2048]{1,0:T(8,128)(2,1)S(1)}, u32[]{:S(2)}, u32[]{:S(2)}) collective-permute-start(bf16[128,2048]{1,0:T(8,128)(2,1)} %param.13), channel_id=1, source_target_pairs={{0,1},{1,2},{2,3},{4,5},{5,6},{6,7},{8,9},{9,10},{10,11},{12,13},{... | collective-permute-start | bytes 1572872 | tf_op jit(solution)/shard_map/ppermute | solution.py:335
  11.5 25.5 %collective-permute-start.1 = (bf16[128,2048]{1,0:T(8,128)(2,1)}, bf16[128,2048]{1,0:T(8,128)(2,1)S(1)}, u32[]{:S(2)}, u32[]{:S(2)}) collective-permute-start(bf16[128,2048]{1,0:T(8,128)(2,1)} %param.13), channel_id=1, source_target_pairs={{3,2},{2,1},{1,0},{7,6},{6,5},{5,4},{11,10},{10,9},{9,8},{15,14},{... | collective-permute-start | bytes 1572872 | tf_op jit(solution)/shard_map/ppermute | solution.py:336
  12.8 24.2 %collective-permute-start.2 = (bf16[128,2048]{1,0:T(8,128)(2,1)}, bf16[128,2048]{1,0:T(8,128)(2,1)S(1)}, u32[]{:S(2)}, u32[]{:S(2)}) collective-permute-start(bf16[128,2048]{1,0:T(8,128)(2,1)} %param.13), channel_id=1, source_target_pairs={{0,2},{3,1},{4,6},{7,5},{8,10},{11,9},{12,14},{15,13},{16,18},{19,... | collective-permute-start | bytes 1572872 | tf_op jit(solution)/shard_map/ppermute | solution.py:334
  37.0 100.5 %all-to-all-start.1 = ((bf16[16,4,128,256]{3,2,1,0:T(8,128)(2,1)}), bf16[16,4,128,256]{3,2,1,0:T(8,128)(2,1)}, u32[]{:S(2)}, u32[]{:S(2)}) async-start(bf16[16,4,128,256]{3,2,1,0:T(8,128)(2,1)} %half_transform.3), calls=%async_computation.1 | async-start | bytes 8388608 | tf_op jit(solution)/shard_map/all_to_all | solution.py:393
  43.3 87.2 %collective-permute-start.3 = (bf16[2,128,2048]{2,1,0:T(8,128)(2,1)S(1)}, bf16[2,128,2048]{2,1,0:T(8,128)(2,1)S(1)}, u32[]{:S(2)}, u32[]{:S(2)}) collective-permute-start(bf16[2,128,2048]{2,1,0:T(8,128)(2,1)S(1)} %pad_maximum_fusion.1), channel_id=1, source_target_pairs={{1,0},{2,3},{5,4},{6,7},{9,8},{10,11},{13,12},{14,15},{17,16},{18,... | collective-permute-start | bytes 3145736 | tf_op jit(solution)/shard_map/ppermute | solution.py:342
  130.5 12.0 %copy-start = (bf16[128,2048]{1,0:T(8,128)(2,1)S(1)}, bf16[128,2048]{1,0:T(8,128)(2,1)}, u32[]{:S(2)}) copy-start(bf16[128,2048]{1,0:T(8,128)(2,1)} %param.13) | copy-start | bytes 1572868
  137.6 234.1 %all-to-all-start = ((bf16[16,10,128,256]{3,2,1,0:T(8,128)(2,1)}), bf16[16,10,128,256]{3,2,1,0:T(8,128)(2,1)}, u32[]{:S(2)}, u32[]{:S(2)}) async-start(bf16[16,10,128,256]{3,2,1,0:T(8,128)(2,1)} %half_transform.4), calls=%async_computation | async-start | bytes 20971520 | tf_op jit(solution)/shard_map/all_to_all | solution.py:393
  142.4 155.1 %all-gather.2.cloned.1.call-start = ((), (), s32[]{:S(2)}) async-start(), calls=%async_computation.4 | async-start | bytes 10485760 | tf_op jit(solution)/shard_map/all_gather | solution.py:385
  371.7 53.9 %all-to-all-start.2 = ((bf16[16,2,128,256]{3,2,1,0:T(8,128)(2,1)}), bf16[16,2,128,256]{3,2,1,0:T(8,128)(2,1)}, u32[]{:S(2)}, u32[]{:S(2)}) async-start(bf16[16,2,128,256]{3,2,1,0:T(8,128)(2,1)} %half_transform.5), calls=%async_computation.2 | async-start | bytes 4194304 | tf_op jit(solution)/shard_map/all_to_all | solution.py:393
Sparse Core Ops, SparseCore 0:
  148.4 149.0 all-gather.1

commit v14 on v11

--- a/solution.py
+++ b/solution.py
@@ -383,8 +383,11 @@
         start += width
     for piece in arrived[-2:]:
         total = fit_exchange(factor, piece, total)
-    shares = total.reshape(devices, basis_total // devices, basis_total)
-    return jnp.sum(lax.all_to_all(shares, BOTH, split_axis=0, concat_axis=0, tiled=True), axis=0)
+    for axis in BOTH:
+        count = lax.axis_size(axis)
+        shares = total.reshape(count, total.shape[0] // count, basis_total)
+        total = jnp.sum(lax.all_to_all(shares, axis, split_axis=0, concat_axis=0, tiled=True), axis=0)
+    return total
 
 
 def solution(mesh):

time: 456 us -> 460 us (level)
    all_to_all x1 -> x2, blocking collectives: 13.6 us -> 17.5 us  [per_device(): lax.all_to_all(shares, axis, split_axis=0, concat_axis=0, tiled=True)]
where the time goes in v14:
time: 460 us; the launch traced here: 458 us
  waiting for transfers between devices  280 us (61%)
  Pallas kernels  112 us (24%)
  starting transfers between devices  28.4 us (6%)
  blocking collectives  17.5 us (4%)
  between operations  13.5 us (3%)
    all_gather x1, waiting for transfers between devices, per_device(): factor = lax.all_gather(line, 'aux', axis=0, tiled=True)  136 us
    all_to_all x3, waiting for transfers between devices, per_device(): lax.all_to_all(half, BOTH, split_axis=0, concat_axis=0, tiled=True)  85.7 us
    ppermute x1, waiting for transfers between devices, line_forward(): return lax.ppermute(jnp.stack([nearer, far]), 'occ', [(1, 0), (2, 3)])  58.3 us
    pallas_call x3, Pallas kernels, fit_exchange(): pl.pallas_call(functools.partial(fit_kernel, aux_total // 8), out_shape=j...  51.8 us
    pallas_call x3, Pallas kernels, half_transform(): pl.pallas_call(functools.partial(half_kernel, low_block), out_shape=jax.S...  40 us
    pallas_call x3, Pallas kernels, factor_rows(): pl.pallas_call(functools.partial(factor_kernel, start), out_shape=(jax.Sh...  19.8 us
    all_to_all x2, blocking collectives, per_device(): lax.all_to_all(shares, axis, split_axis=0, concat_axis=0, tiled=True)  17.5 us
    all_to_all x3, starting transfers between devices, per_device(): lax.all_to_all(half, BOTH, split_axis=0, concat_axis=0, tiled=True)  15.2 us
  transfers between devices with their start and end apart: 8, of which 5 were waited for; matrix products, arithmetic and copies ran while one was open for 1% of the time, Pallas kernels for 23%

profile of v14, /device:TPU:0, one launch (start us, length us, event | category | flops | bytes accessed | tf_op | source)
XLA Modules:
  0.0 458.3 jit_solution(10260946120123173865)
XLA Ops:
  6.5 5.0 %collective-permute-start = (bf16[128,2048]{1,0:T(8,128)(2,1)}, bf16[128,2048]{1,0:T(8,128)(2,1)S(1)}, u32[]{:S(2)}, u32[]{:S(2)}) collective-permute-start(bf16[128,2048]{1,0:T(8,128)(2,1)} %param.13), channel_id=1, source_target_pairs={{0,1},{1,2},{2,3},{4,5},{5,6},{6,7},{8,9},{9,10},{10,11},{12,13},{... | collective-permute-start | bytes 1572872 | tf_op jit(solution)/shard_map/ppermute | solution.py:324
  11.5 1.3 collective-permute-start.1
  12.8 5.6 %collective-permute-start.2 = (bf16[128,2048]{1,0:T(8,128)(2,1)}, bf16[128,2048]{1,0:T(8,128)(2,1)S(1)}, u32[]{:S(2)}, u32[]{:S(2)}) collective-permute-start(bf16[128,2048]{1,0:T(8,128)(2,1)} %param.13), channel_id=1, source_target_pairs={{0,2},{3,1},{4,6},{7,5},{8,10},{11,9},{12,14},{15,13},{16,18},{19,... | collective-permute-start | bytes 1572872 | tf_op jit(solution)/shard_map/ppermute | solution.py:323
  18.4 5.5 %factor_rows.3 = (bf16[128,256]{1,0:T(8,128)(2,1)}, f32[256,256]{1,0:T(8,128)}, f32[8,256]{1,0:T(8,128)}) custom-call(bf16[256,384]{1,0:T(8,128)(2,1)} %refs_0_.4), custom_call_target="tpu_custom_call" | custom-call | tf_op jit(solution)/shard_map/factor_rows/pallas_call | solution.py:113
  23.9 13.4 %half_transform.3 = bf16[16,4,128,256]{3,2,1,0:T(8,128)(2,1)} custom-call(s32[4,8]{1,0:T(4,128)} %bitcast.17, s32[8]{0:T(128)} %count_ref.5, bf16[128,256]{1,0:T(8,128)(2,1)} %get-tuple-element.63.basis_ref, bf16[8,4,16,128,128]{4,3,2,1,0:T(8,128)(2,1)} %refs_1_.5, bf16[8,4,16,128,128]{4,3,2,1,0:T(8,128)(2,1)} %refs_1_.5, ...), custom_call_target="tpu_custom_call" | custom-call | flops 2147483648 | bytes 20971520 | tf_op jit(solution)/shard_map/half_transform/pallas_call | solution.py:182
  37.3 0.0 collective-permute-done
  37.3 0.0 collective-permute-done.1
  37.3 0.0 collective-permute-done.2
  37.4 5.8 %all-to-all-start.1 = ((bf16[16,4,128,256]{3,2,1,0:T(8,128)(2,1)}), bf16[16,4,128,256]{3,2,1,0:T(8,128)(2,1)}, u32[]{:S(2)}, u32[]{:S(2)}) async-start(bf16[16,4,128,256]{3,2,1,0:T(8,128)(2,1)} %half_transform.3), calls=%async_computation.1 | async-start | bytes 8388608 | tf_op jit(solution)/shard_map/all_to_all | solution.py:382
  43.2 0.1 select_bitcast_fusion
  43.2 0.1 pad_maximum_fusion.1
  43.3 1.3 collective-permute-start.3
  44.6 10.8 %factor_rows.4 = (bf16[320,256]{1,0:T(8,128)(2,1)}, f32[256,256]{1,0:T(8,128)}, f32[8,256]{1,0:T(8,128)}) custom-call(f32[256,256]{1,0:T(8,128)} %get-tuple-element.66.refs_0_, f32[8,256]{1,0:T(8,128)} %get-tuple-element.67.refs_1_), custom_call_target="tpu_custom_call" | custom-call | tf_op jit(solution)/shard_map/factor_rows/pallas_call | solution.py:113
  55.4 16.7 %half_transform.4 = bf16[16,10,128,256]{3,2,1,0:T(8,128)(2,1)} custom-call(s32[4,8]{1,0:T(4,128)} %bitcast.18, s32[8]{0:T(128)} %count_ref.5, bf16[320,256]{1,0:T(8,128)(2,1)} %get-tuple-element.68.basis_ref, bf16[8,4,16,128,128]{4,3,2,1,0:T(8,128)(2,1)} %refs_1_.5, bf16[8,4,16,128,128]{4,3,2,1,0:T(8,128)(2,1)} %refs_1_.5, ...), custom_call_target="tpu_custom_call" | custom-call | flops 5368709120 | bytes 27262976 | tf_op jit(solution)/shard_map/half_transform/pallas_call | solution.py:182
  72.2 58.3 %collective-permute-done.3 = bf16[2,128,2048]{2,1,0:T(8,128)(2,1)S(1)} collective-permute-done((bf16[2,128,2048]{2,1,0:T(8,128)(2,1)S(1)}, bf16[2,128,2048]{2,1,0:T(8,128)(2,1)S(1)}, u32[]{:S(2)}, u32[]{:S(2)}) %collective-permute-start.3) | collective-permute-done | bytes 1048608 | tf_op jit(solution)/shard_map/ppermute | solution.py:331
  130.5 0.0 copy-start
  130.5 7.1 %all-to-all-done.1.half_ref = bf16[16,4,128,256]{3,2,1,0:T(8,128)(2,1)} async-done(((bf16[16,4,128,256]{3,2,1,0:T(8,128)(2,1)}), bf16[16,4,128,256]{3,2,1,0:T(8,128)(2,1)}, u32[]{:S(2)}, u32[]{:S(2)}) %all-to-all-start.1) | async-done | bytes 4194336 | tf_op jit(solution)/shard_map/all_to_all | solution.py:382
  137.6 4.8 %all-to-all-start = ((bf16[16,10,128,256]{3,2,1,0:T(8,128)(2,1)}), bf16[16,10,128,256]{3,2,1,0:T(8,128)(2,1)}, u32[]{:S(2)}, u32[]{:S(2)}) async-start(bf16[16,10,128,256]{3,2,1,0:T(8,128)(2,1)} %half_transform.4), calls=%async_computation | async-start | bytes 20971520 | tf_op jit(solution)/shard_map/all_to_all | solution.py:382
  142.4 0.0 all-gather.2.cloned.1.call-start
  142.5 0.0 copy-done
  142.5 2.7 conditional.1
  142.5 0.8 copy.6
  143.3 0.8 copy.7
  144.1 1.1 slice_bitcast_fusion
  145.2 3.1 pad_maximum_fusion
  148.3 0.0 all-gather.2.cloned.1.call-update
  148.3 3.5 factor_rows.5
  151.8 9.9 %half_transform.5 = bf16[16,2,128,256]{3,2,1,0:T(8,128)(2,1)} custom-call(s32[4,8]{1,0:T(4,128)} %bitcast.19, s32[8]{0:T(128)} %count_ref.5, bf16[64,256]{1,0:T(8,128)(2,1)} %get-tuple-element.76.basis_ref, bf16[8,4,16,128,128]{4,3,2,1,0:T(8,128)(2,1)} %refs_1_.5, bf16[8,4,16,128,128]{4,3,2,1,0:T(8,128)(2,1)} %refs_1_.5), custom_call_target="tpu_custom_call" | custom-call | flops 1073741824 | bytes 18874368 | tf_op jit(solution)/shard_map/half_transform/pallas_call | solution.py:182
  161.6 135.9 %all-gather.2.cloned.1.call-done.factor_ref = bf16[2048,2048]{1,0:T(8,128)(2,1)} async-done(((bf16[512,2048]{1,0:T(8,128)(2,1)}), bf16[2048,2048]{1,0:T(8,128)(2,1)}) %all-gather.2.cloned.1.call-update) | async-done | bytes 8388624 | tf_op jit(solution)/shard_map/all_gather | solution.py:374
  297.5 0.7 broadcast_in_dim.3.before_ref
  298.2 13.4 %fit_exchange.3.before_ref = f32[256,256]{1,0:T(8,128)} custom-call(f32[256,256]{1,0:T(8,128)} %broadcast_in_dim.3.before_ref, bf16[2048,2048]{1,0:T(8,128)(2,1)} %all-gather.2.cloned.1.call-done.factor_ref, bf16[16,4,128,256]{3,2,1,0:T(8,128)(2,1)} %all-to-all-done.1.half_ref), custom_call_target="tpu_custom_call" | custom-call | flops 5905580032 | bytes 12582912 | tf_op jit(solution)/shard_map/fit_exchange/pallas_call | solution.py:294
  311.6 60.0 %all-to-all-done.half_ref = bf16[16,10,128,256]{3,2,1,0:T(8,128)(2,1)} async-done(((bf16[16,10,128,256]{3,2,1,0:T(8,128)(2,1)}), bf16[16,10,128,256]{3,2,1,0:T(8,128)(2,1)}, u32[]{:S(2)}, u32[]{:S(2)}) %all-to-all-start) | async-done | bytes 10485792 | tf_op jit(solution)/shard_map/all_to_all | solution.py:382
  371.6 4.6 %all-to-all-start.2 = ((bf16[16,2,128,256]{3,2,1,0:T(8,128)(2,1)}), bf16[16,2,128,256]{3,2,1,0:T(8,128)(2,1)}, u32[]{:S(2)}, u32[]{:S(2)}) async-start(bf16[16,2,128,256]{3,2,1,0:T(8,128)(2,1)} %half_transform.5), calls=%async_computation.2 | async-start | bytes 4194304 | tf_op jit(solution)/shard_map/all_to_all | solution.py:382
  376.3 30.6 %fit_exchange.4.before_ref = f32[256,256]{1,0:T(8,128)} custom-call(f32[256,256]{1,0:T(8,128)} %fit_exchange.3.before_ref, bf16[2048,2048]{1,0:T(8,128)(2,1)} %all-gather.2.cloned.1.call-done.factor_ref, bf16[16,10,128,256]{3,2,1,0:T(8,128)(2,1)} %all-to-all-done.half_ref), custom_call_target="tpu_custom_call" | custom-call | flops 14763950080 | bytes 18874368 | tf_op jit(solution)/shard_map/fit_exchange/pallas_call | solution.py:294
  406.9 18.6 %all-to-all-done.2.half_ref = bf16[16,2,128,256]{3,2,1,0:T(8,128)(2,1)} async-done(((bf16[16,2,128,256]{3,2,1,0:T(8,128)(2,1)}), bf16[16,2,128,256]{3,2,1,0:T(8,128)(2,1)}, u32[]{:S(2)}, u32[]{:S(2)}) %all-to-all-start.2) | async-done | bytes 2097184 | tf_op jit(solution)/shard_map/all_to_all | solution.py:382
  425.5 7.8 %fit_exchange.5 = f32[256,256]{1,0:T(8,128)} custom-call(f32[256,256]{1,0:T(8,128)} %fit_exchange.4.before_ref, bf16[2048,2048]{1,0:T(8,128)(2,1)} %all-gather.2.cloned.1.call-done.factor_ref, bf16[16,2,128,256]{3,2,1,0:T(8,128)(2,1)} %all-to-all-done.2.half_ref), custom_call_target="tpu_custom_call" | custom-call | flops 2952790016 | bytes 10485760 | tf_op jit(solution)/shard_map/fit_exchange/pallas_call | solution.py:294
  433.3 9.4 %all_to_all.25 = f32[4,64,256]{2,1,0:T(8,128)S(1)} all-to-all(f32[4,64,256]{2,1,0:T(8,128)} %bitcast.15), channel_id=1, replica_groups=mesh['grp'=2,'aux'=4,'occ'=4] {'aux'}, dimensions={0} | all-to-all | bytes 524288 | tf_op jit(solution)/shard_map/all_to_all | solution.py:389
  442.7 8.1 %all_to_all.26 = f32[4,16,256]{2,1,0:T(8,128)S(1)} all-to-all(f32[4,16,256]{2,1,0:T(8,128)S(1)} %bitcast.16), channel_id=1, replica_groups=mesh['grp'=2,'aux'=4,'occ'=4] {'occ'}, dimensions={0} | all-to-all | bytes 131072 | tf_op jit(solution)/shard_map/all_to_all | solution.py:389
  450.8 0.6 reduce_sum.19
  (1 shorter events, 0.0 us)
Async XLA Ops:
  6.5 30.8 %collective-permute-start = (bf16[128,2048]{1,0:T(8,128)(2,1)}, bf16[128,2048]{1,0:T(8,128)(2,1)S(1)}, u32[]{:S(2)}, u32[]{:S(2)}) collective-permute-start(bf16[128,2048]{1,0:T(8,128)(2,1)} %param.13), channel_id=1, source_target_pairs={{0,1},{1,2},{2,3},{4,5},{5,6},{6,7},{8,9},{9,10},{10,11},{12,13},{... | collective-permute-start | bytes 1572872 | tf_op jit(solution)/shard_map/ppermute | solution.py:324
  11.5 25.8 %collective-permute-start.1 = (bf16[128,2048]{1,0:T(8,128)(2,1)}, bf16[128,2048]{1,0:T(8,128)(2,1)S(1)}, u32[]{:S(2)}, u32[]{:S(2)}) collective-permute-start(bf16[128,2048]{1,0:T(8,128)(2,1)} %param.13), channel_id=1, source_target_pairs={{3,2},{2,1},{1,0},{7,6},{6,5},{5,4},{11,10},{10,9},{9,8},{15,14},{... | collective-permute-start | bytes 1572872 | tf_op jit(solution)/shard_map/ppermute | solution.py:325
  12.8 24.6 %collective-permute-start.2 = (bf16[128,2048]{1,0:T(8,128)(2,1)}, bf16[128,2048]{1,0:T(8,128)(2,1)S(1)}, u32[]{:S(2)}, u32[]{:S(2)}) collective-permute-start(bf16[128,2048]{1,0:T(8,128)(2,1)} %param.13), channel_id=1, source_target_pairs={{0,2},{3,1},{4,6},{7,5},{8,10},{11,9},{12,14},{15,13},{16,18},{19,... | collective-permute-start | bytes 1572872 | tf_op jit(solution)/shard_map/ppermute | solution.py:323
  37.4 100.2 %all-to-all-start.1 = ((bf16[16,4,128,256]{3,2,1,0:T(8,128)(2,1)}), bf16[16,4,128,256]{3,2,1,0:T(8,128)(2,1)}, u32[]{:S(2)}, u32[]{:S(2)}) async-start(bf16[16,4,128,256]{3,2,1,0:T(8,128)(2,1)} %half_transform.3), calls=%async_computation.1 | async-start | bytes 8388608 | tf_op jit(solution)/shard_map/all_to_all | solution.py:382
  43.3 87.2 %collective-permute-start.3 = (bf16[2,128,2048]{2,1,0:T(8,128)(2,1)S(1)}, bf16[2,128,2048]{2,1,0:T(8,128)(2,1)S(1)}, u32[]{:S(2)}, u32[]{:S(2)}) collective-permute-start(bf16[2,128,2048]{2,1,0:T(8,128)(2,1)S(1)} %pad_maximum_fusion.1), channel_id=1, source_target_pairs={{1,0},{2,3},{5,4},{6,7},{9,8},{10,11},{13,12},{14,15},{17,16},{18,... | collective-permute-start | bytes 3145736 | tf_op jit(solution)/shard_map/ppermute | solution.py:331
  130.5 12.0 %copy-start = (bf16[128,2048]{1,0:T(8,128)(2,1)S(1)}, bf16[128,2048]{1,0:T(8,128)(2,1)}, u32[]{:S(2)}) copy-start(bf16[128,2048]{1,0:T(8,128)(2,1)} %param.13) | copy-start | bytes 1572868
  137.6 234.0 %all-to-all-start = ((bf16[16,10,128,256]{3,2,1,0:T(8,128)(2,1)}), bf16[16,10,128,256]{3,2,1,0:T(8,128)(2,1)}, u32[]{:S(2)}, u32[]{:S(2)}) async-start(bf16[16,10,128,256]{3,2,1,0:T(8,128)(2,1)} %half_transform.4), calls=%async_computation | async-start | bytes 20971520 | tf_op jit(solution)/shard_map/all_to_all | solution.py:382
  142.4 155.1 %all-gather.2.cloned.1.call-start = ((), (), s32[]{:S(2)}) async-start(), calls=%async_computation.5 | async-start | bytes 10485760 | tf_op jit(solution)/shard_map/all_gather | solution.py:374
  371.6 53.9 %all-to-all-start.2 = ((bf16[16,2,128,256]{3,2,1,0:T(8,128)(2,1)}), bf16[16,2,128,256]{3,2,1,0:T(8,128)(2,1)}, u32[]{:S(2)}, u32[]{:S(2)}) async-start(bf16[16,2,128,256]{3,2,1,0:T(8,128)(2,1)} %half_transform.5), calls=%async_computation.2 | async-start | bytes 4194304 | tf_op jit(solution)/shard_map/all_to_all | solution.py:382
Sparse Core Ops, SparseCore 0:
  148.4 149.0 all-gather.1

commit v15 on v11

--- a/solution.py
+++ b/solution.py
@@ -320,25 +320,26 @@
 
 
 def line_near(block):
-    far = lax.ppermute(block, "occ", [(0, 2), (3, 1)])
-    up = lax.ppermute(block, "occ", [(0, 1), (1, 2), (2, 3)])
-    down = lax.ppermute(block, "occ", [(3, 2), (2, 1), (1, 0)])
-    return up, down, far
-
-
-def line_forward(up, down, far):
-    nearer = jnp.where(lax.axis_index("occ") < 2, down, up)
-    return lax.ppermute(jnp.stack([nearer, far]), "occ", [(1, 0), (2, 3)])
-
-
-def line_order(block, up, down, far, later):
+    before = lax.ppermute(block, "occ", [(i, (i + 1) % 4) for i in range(4)])
+    after = lax.ppermute(block, "occ", [(i, (i + 3) % 4) for i in range(4)])
+    return before, after
+
+
+def line_forward(before, after):
+    even = lax.axis_index("occ") % 2 == 0
+    return lax.ppermute(
+        jnp.where(even, before, after), "occ", [(i, i ^ 1) for i in range(4)]
+    )
+
+
+def line_order(block, before, after, opposite):
     order = lax.switch(
         lax.axis_index("occ"),
         [
-            lambda: (block, down, later[0], later[1]),
-            lambda: (up, block, down, far),
-            lambda: (far, up, block, down),
-            lambda: (later[1], later[0], up, block),
+            lambda: (block, after, opposite, before),
+            lambda: (before, block, after, opposite),
+            lambda: (opposite, before, block, after),
+            lambda: (after, opposite, before, block),
         ],
     )
     return jnp.concatenate(order)

time: 456 us -> 452 us (level)
  starting transfers between devices: 28.4 us -> 20.9 us
  waiting for transfers between devices: 280 us -> 286 us
    all_to_all x3, waiting for transfers between devices: 85.7 us -> 93.2 us  [per_device(): lax.all_to_all(half, BOTH, split_axis=0, concat_axis=0, tiled=True)]
    ppermute x4 -> x3, starting transfers between devices: 13.1 us -> 6.84 us  [the longest x1 5.05 us: line_near(): after = lax.ppermute(block, 'occ', [(i, (i + 3) % 4) for i in range(4)])]
    ppermute x4 -> x3, waiting for transfers between devices: 58.4 us -> 54.9 us  [the longest x1 50.3 us: line_forward(): lax.ppermute(jnp.where(even, before, after), 'occ', [(i, i ^ 1) for i in...]
  transfers between devices with their start and end apart: 8 -> 7, of which waited for: 5 -> 6; matrix products, arithmetic and copies ran while one was open for 1% -> 1% of each run, Pallas kernels for 23% -> 23%
where the time goes in v15:
time: 452 us; the launch traced here: 451 us
  waiting for transfers between devices  286 us (63%)
  Pallas kernels  112 us (25%)
  starting transfers between devices  20.9 us (5%)
  blocking collectives  13.6 us (3%)
  between operations  13.5 us (3%)
    all_gather x1, waiting for transfers between devices, per_device(): factor = lax.all_gather(line, 'aux', axis=0, tiled=True)  138 us
    all_to_all x3, waiting for transfers between devices, per_device(): lax.all_to_all(half, BOTH, split_axis=0, concat_axis=0, tiled=True)  93.2 us
    pallas_call x3, Pallas kernels, fit_exchange(): pl.pallas_call(functools.partial(fit_kernel, aux_total // 8), out_shape=j...  51.8 us
    ppermute x1, waiting for transfers between devices, line_forward(): lax.ppermute(jnp.where(even, before, after), 'occ', [(i, i ^ 1) for i in...  50.3 us
    pallas_call x3, Pallas kernels, half_transform(): pl.pallas_call(functools.partial(half_kernel, low_block), out_shape=jax.S...  40.1 us
    pallas_call x3, Pallas kernels, factor_rows(): pl.pallas_call(functools.partial(factor_kernel, start), out_shape=(jax.Sh...  19.8 us
    all_to_all x3, starting transfers between devices, per_device(): lax.all_to_all(half, BOTH, split_axis=0, concat_axis=0, tiled=True)  14 us
    all_to_all x1, blocking collectives, per_device(): lax.all_to_all(shares, BOTH, split_axis=0, concat_axis=0, tiled=True)  13.6 us
  transfers between devices with their start and end apart: 7, of which 6 were waited for; matrix products, arithmetic and copies ran while one was open for 1% of the time, Pallas kernels for 23%

profile of v15, /device:TPU:0, one launch (start us, length us, event | category | flops | bytes accessed | tf_op | source)
XLA Modules:
  0.0 450.8 jit_solution(6320706163301373707)
XLA Ops:
  6.5 5.0 %collective-permute-start.1 = (bf16[128,2048]{1,0:T(8,128)(2,1)}, bf16[128,2048]{1,0:T(8,128)(2,1)S(1)}, u32[]{:S(2)}, u32[]{:S(2)}) collective-permute-start(bf16[128,2048]{1,0:T(8,128)(2,1)} %param.13), channel_id=1, source_target_pairs={{0,3},{1,0},{2,1},{3,2},{4,7},{5,4},{6,5},{7,6},{8,11},{9,8},{10,9... | collective-permute-start | bytes 1572872 | tf_op jit(solution)/shard_map/ppermute | solution.py:324
  11.6 0.0 collective-permute-start
  11.6 5.5 %factor_rows.3 = (bf16[128,256]{1,0:T(8,128)(2,1)}, f32[256,256]{1,0:T(8,128)}, f32[8,256]{1,0:T(8,128)}) custom-call(bf16[256,384]{1,0:T(8,128)(2,1)} %refs_0_.4), custom_call_target="tpu_custom_call" | custom-call | tf_op jit(solution)/shard_map/factor_rows/pallas_call | solution.py:113
  17.1 13.4 %half_transform.3 = bf16[16,4,128,256]{3,2,1,0:T(8,128)(2,1)} custom-call(s32[4,8]{1,0:T(4,128)} %bitcast.3, s32[8]{0:T(128)} %count_ref.5, bf16[128,256]{1,0:T(8,128)(2,1)} %get-tuple-element.60.basis_ref, bf16[8,4,16,128,128]{4,3,2,1,0:T(8,128)(2,1)} %refs_1_.5, bf16[8,4,16,128,128]{4,3,2,1,0:T(8,128)(2,1)} %refs_1_.5, ...), custom_call_target="tpu_custom_call" | custom-call | flops 2147483648 | bytes 20971520 | tf_op jit(solution)/shard_map/half_transform/pallas_call | solution.py:182
  30.5 0.0 collective-permute-done.1
  30.5 4.6 %collective-permute-done = bf16[128,2048]{1,0:T(8,128)(2,1)S(1)} collective-permute-done((bf16[128,2048]{1,0:T(8,128)(2,1)}, bf16[128,2048]{1,0:T(8,128)(2,1)S(1)}, u32[]{:S(2)}, u32[]{:S(2)}) %collective-permute-start) | collective-permute-done | bytes 524320 | tf_op jit(solution)/shard_map/ppermute | solution.py:323
  35.1 4.5 %all-to-all-start.1 = ((bf16[16,4,128,256]{3,2,1,0:T(8,128)(2,1)}), bf16[16,4,128,256]{3,2,1,0:T(8,128)(2,1)}, u32[]{:S(2)}, u32[]{:S(2)}) async-start(bf16[16,4,128,256]{3,2,1,0:T(8,128)(2,1)} %half_transform.3), calls=%async_computation.1 | async-start | bytes 8388608 | tf_op jit(solution)/shard_map/all_to_all | solution.py:383
  39.7 0.1 broadcast_select_fusion
  39.8 1.8 collective-permute-start.2
  41.5 10.8 %factor_rows.4 = (bf16[320,256]{1,0:T(8,128)(2,1)}, f32[256,256]{1,0:T(8,128)}, f32[8,256]{1,0:T(8,128)}) custom-call(f32[256,256]{1,0:T(8,128)} %get-tuple-element.63.refs_0_, f32[8,256]{1,0:T(8,128)} %get-tuple-element.64.refs_1_), custom_call_target="tpu_custom_call" | custom-call | tf_op jit(solution)/shard_map/factor_rows/pallas_call | solution.py:113
  52.3 16.8 %half_transform.4 = bf16[16,10,128,256]{3,2,1,0:T(8,128)(2,1)} custom-call(s32[4,8]{1,0:T(4,128)} %bitcast.4, s32[8]{0:T(128)} %count_ref.5, bf16[320,256]{1,0:T(8,128)(2,1)} %get-tuple-element.65.basis_ref, bf16[8,4,16,128,128]{4,3,2,1,0:T(8,128)(2,1)} %refs_1_.5, bf16[8,4,16,128,128]{4,3,2,1,0:T(8,128)(2,1)} %refs_1_.5, ...), custom_call_target="tpu_custom_call" | custom-call | flops 5368709120 | bytes 27262976 | tf_op jit(solution)/shard_map/half_transform/pallas_call | solution.py:182
  69.1 50.3 %collective-permute-done.2 = bf16[128,2048]{1,0:T(8,128)(2,1)S(1)} collective-permute-done((bf16[128,2048]{1,0:T(8,128)(2,1)S(1)}, bf16[128,2048]{1,0:T(8,128)(2,1)S(1)}, u32[]{:S(2)}, u32[]{:S(2)}) %collective-permute-start.2) | collective-permute-done | bytes 524320 | tf_op jit(solution)/shard_map/ppermute | solution.py:330
  119.4 0.0 copy-start
  119.4 14.7 %all-to-all-done.1.half_ref = bf16[16,4,128,256]{3,2,1,0:T(8,128)(2,1)} async-done(((bf16[16,4,128,256]{3,2,1,0:T(8,128)(2,1)}), bf16[16,4,128,256]{3,2,1,0:T(8,128)(2,1)}, u32[]{:S(2)}, u32[]{:S(2)}) %all-to-all-start.1) | async-done | bytes 4194336 | tf_op jit(solution)/shard_map/all_to_all | solution.py:383
  134.1 4.8 %all-to-all-start = ((bf16[16,10,128,256]{3,2,1,0:T(8,128)(2,1)}), bf16[16,10,128,256]{3,2,1,0:T(8,128)(2,1)}, u32[]{:S(2)}, u32[]{:S(2)}) async-start(bf16[16,10,128,256]{3,2,1,0:T(8,128)(2,1)} %half_transform.4), calls=%async_computation | async-start | bytes 20971520 | tf_op jit(solution)/shard_map/all_to_all | solution.py:383
  138.9 0.0 all-gather.2.cloned.1.call-start
  138.9 0.0 copy-done
  139.0 0.9 conditional.1
  139.1 0.8 copy.8
  139.9 2.6 pad_maximum_fusion
  142.5 0.0 all-gather.2.cloned.1.call-update
  142.5 3.5 factor_rows.5
  146.0 9.9 %half_transform.5 = bf16[16,2,128,256]{3,2,1,0:T(8,128)(2,1)} custom-call(s32[4,8]{1,0:T(4,128)} %bitcast.5, s32[8]{0:T(128)} %count_ref.5, bf16[64,256]{1,0:T(8,128)(2,1)} %get-tuple-element.72.basis_ref, bf16[8,4,16,128,128]{4,3,2,1,0:T(8,128)(2,1)} %refs_1_.5, bf16[8,4,16,128,128]{4,3,2,1,0:T(8,128)(2,1)} %refs_1_.5), custom_call_target="tpu_custom_call" | custom-call | flops 1073741824 | bytes 18874368 | tf_op jit(solution)/shard_map/half_transform/pallas_call | solution.py:182
  155.9 138.1 %all-gather.2.cloned.1.call-done.factor_ref = bf16[2048,2048]{1,0:T(8,128)(2,1)} async-done(((bf16[512,2048]{1,0:T(8,128)(2,1)}), bf16[2048,2048]{1,0:T(8,128)(2,1)}) %all-gather.2.cloned.1.call-update) | async-done | bytes 8388624 | tf_op jit(solution)/shard_map/all_gather | solution.py:375
  294.0 0.7 broadcast_in_dim.3.before_ref
  294.7 13.4 %fit_exchange.3.before_ref = f32[256,256]{1,0:T(8,128)} custom-call(f32[256,256]{1,0:T(8,128)} %broadcast_in_dim.3.before_ref, bf16[2048,2048]{1,0:T(8,128)(2,1)} %all-gather.2.cloned.1.call-done.factor_ref, bf16[16,4,128,256]{3,2,1,0:T(8,128)(2,1)} %all-to-all-done.1.half_ref), custom_call_target="tpu_custom_call" | custom-call | flops 5905580032 | bytes 12582912 | tf_op jit(solution)/shard_map/fit_exchange/pallas_call | solution.py:294
  308.1 60.0 %all-to-all-done.half_ref = bf16[16,10,128,256]{3,2,1,0:T(8,128)(2,1)} async-done(((bf16[16,10,128,256]{3,2,1,0:T(8,128)(2,1)}), bf16[16,10,128,256]{3,2,1,0:T(8,128)(2,1)}, u32[]{:S(2)}, u32[]{:S(2)}) %all-to-all-start) | async-done | bytes 10485792 | tf_op jit(solution)/shard_map/all_to_all | solution.py:383
  368.1 4.6 %all-to-all-start.2 = ((bf16[16,2,128,256]{3,2,1,0:T(8,128)(2,1)}), bf16[16,2,128,256]{3,2,1,0:T(8,128)(2,1)}, u32[]{:S(2)}, u32[]{:S(2)}) async-start(bf16[16,2,128,256]{3,2,1,0:T(8,128)(2,1)} %half_transform.5), calls=%async_computation.2 | async-start | bytes 4194304 | tf_op jit(solution)/shard_map/all_to_all | solution.py:383
  372.7 30.6 %fit_exchange.4.before_ref = f32[256,256]{1,0:T(8,128)} custom-call(f32[256,256]{1,0:T(8,128)} %fit_exchange.3.before_ref, bf16[2048,2048]{1,0:T(8,128)(2,1)} %all-gather.2.cloned.1.call-done.factor_ref, bf16[16,10,128,256]{3,2,1,0:T(8,128)(2,1)} %all-to-all-done.half_ref), custom_call_target="tpu_custom_call" | custom-call | flops 14763950080 | bytes 18874368 | tf_op jit(solution)/shard_map/fit_exchange/pallas_call | solution.py:294
  403.4 18.6 %all-to-all-done.2.half_ref = bf16[16,2,128,256]{3,2,1,0:T(8,128)(2,1)} async-done(((bf16[16,2,128,256]{3,2,1,0:T(8,128)(2,1)}), bf16[16,2,128,256]{3,2,1,0:T(8,128)(2,1)}, u32[]{:S(2)}, u32[]{:S(2)}) %all-to-all-start.2) | async-done | bytes 2097184 | tf_op jit(solution)/shard_map/all_to_all | solution.py:383
  422.0 7.8 %fit_exchange.5 = f32[256,256]{1,0:T(8,128)} custom-call(f32[256,256]{1,0:T(8,128)} %fit_exchange.4.before_ref, bf16[2048,2048]{1,0:T(8,128)(2,1)} %all-gather.2.cloned.1.call-done.factor_ref, bf16[16,2,128,256]{3,2,1,0:T(8,128)(2,1)} %all-to-all-done.2.half_ref), custom_call_target="tpu_custom_call" | custom-call | flops 2952790016 | bytes 10485760 | tf_op jit(solution)/shard_map/fit_exchange/pallas_call | solution.py:294
  429.7 13.6 %all_to_all.20 = f32[16,16,256]{2,1,0:T(8,128)S(1)} all-to-all(f32[16,16,256]{2,1,0:T(8,128)} %bitcast.2), channel_id=1, replica_groups=mesh['grp'=2,'aux'=4,'occ'=4] {'aux','occ'}, dimensions={0} | all-to-all | bytes 524288 | tf_op jit(solution)/shard_map/all_to_all | solution.py:388
  443.3 0.6 reduce_sum.9
  (2 shorter events, 0.1 us)
Async XLA Ops:
  6.5 24.0 %collective-permute-start.1 = (bf16[128,2048]{1,0:T(8,128)(2,1)}, bf16[128,2048]{1,0:T(8,128)(2,1)S(1)}, u32[]{:S(2)}, u32[]{:S(2)}) collective-permute-start(bf16[128,2048]{1,0:T(8,128)(2,1)} %param.13), channel_id=1, source_target_pairs={{0,3},{1,0},{2,1},{3,2},{4,7},{5,4},{6,5},{7,6},{8,11},{9,8},{10,9... | collective-permute-start | bytes 1572872 | tf_op jit(solution)/shard_map/ppermute | solution.py:324
  11.6 23.5 %collective-permute-start = (bf16[128,2048]{1,0:T(8,128)(2,1)}, bf16[128,2048]{1,0:T(8,128)(2,1)S(1)}, u32[]{:S(2)}, u32[]{:S(2)}) collective-permute-start(bf16[128,2048]{1,0:T(8,128)(2,1)} %param.13), channel_id=1, source_target_pairs={{0,1},{1,2},{2,3},{3,0},{4,5},{5,6},{6,7},{7,4},{8,9},{9,10},{10,1... | collective-permute-start | bytes 1572872 | tf_op jit(solution)/shard_map/ppermute | solution.py:323
  35.1 98.9 %all-to-all-start.1 = ((bf16[16,4,128,256]{3,2,1,0:T(8,128)(2,1)}), bf16[16,4,128,256]{3,2,1,0:T(8,128)(2,1)}, u32[]{:S(2)}, u32[]{:S(2)}) async-start(bf16[16,4,128,256]{3,2,1,0:T(8,128)(2,1)} %half_transform.3), calls=%async_computation.1 | async-start | bytes 8388608 | tf_op jit(solution)/shard_map/all_to_all | solution.py:383
  39.8 79.6 %collective-permute-start.2 = (bf16[128,2048]{1,0:T(8,128)(2,1)S(1)}, bf16[128,2048]{1,0:T(8,128)(2,1)S(1)}, u32[]{:S(2)}, u32[]{:S(2)}) collective-permute-start(bf16[128,2048]{1,0:T(8,128)(2,1)S(1)} %broadcast_select_fusion), channel_id=1, source_target_pairs={{0,1},{1,0},{2,3},{3,2},{4,5},{5,4},{6,7},{7,6},{8,9},{9,8},{10,11... | collective-permute-start | bytes 1572872 | tf_op jit(solution)/shard_map/ppermute | solution.py:330
  119.4 19.6 %copy-start = (bf16[128,2048]{1,0:T(8,128)(2,1)S(1)}, bf16[128,2048]{1,0:T(8,128)(2,1)}, u32[]{:S(2)}) copy-start(bf16[128,2048]{1,0:T(8,128)(2,1)} %param.13) | copy-start | bytes 1572868
  134.1 234.0 %all-to-all-start = ((bf16[16,10,128,256]{3,2,1,0:T(8,128)(2,1)}), bf16[16,10,128,256]{3,2,1,0:T(8,128)(2,1)}, u32[]{:S(2)}, u32[]{:S(2)}) async-start(bf16[16,10,128,256]{3,2,1,0:T(8,128)(2,1)} %half_transform.4), calls=%async_computation | async-start | bytes 20971520 | tf_op jit(solution)/shard_map/all_to_all | solution.py:383
  138.9 155.1 %all-gather.2.cloned.1.call-start = ((), (), s32[]{:S(2)}) async-start(), calls=%async_computation.4 | async-start | bytes 10485760 | tf_op jit(solution)/shard_map/all_gather | solution.py:375
  368.1 53.9 %all-to-all-start.2 = ((bf16[16,2,128,256]{3,2,1,0:T(8,128)(2,1)}), bf16[16,2,128,256]{3,2,1,0:T(8,128)(2,1)}, u32[]{:S(2)}, u32[]{:S(2)}) async-start(bf16[16,2,128,256]{3,2,1,0:T(8,128)(2,1)} %half_transform.5), calls=%async_computation.2 | async-start | bytes 4194304 | tf_op jit(solution)/shard_map/all_to_all | solution.py:383
Sparse Core Ops, SparseCore 0:
  142.6 151.3 all-gather.1
